TPU v7x, 32 devices: a whole 2x2x4 slice. The times are simulated.
32 devices in a mesh: seq: 4 (over x, core), chan: 8 (over z, y).
Axes of the slice: x: 2, y: 2, z: 4, core: 2. Of those that a mesh axis runs over, the one named last changes fastest.
Arguments:
- projections: bfloat16 [3, 2048, 8192], P(None, 'chan', 'seq'), may hold values from -6 to 6
- filter_taps: float32 [2048, 8192], P('chan', 'seq'), may hold values from -1.3 to 1.3
- skip_gain: float32 [2048], P('chan'), may hold values from -1 to 1
- head_weight: bfloat16 [2048, 3840], P('chan'), may hold values from -0.75 to 0.75
- head_bias: float32 [3840], replicated, may hold values from -1 to 1
- counts: int32 [256, 3840], P('seq'), may hold values from 0 to 11
Outputs:
- mean_loss: float32 [], replicated
- feature_grads: float32 [3, 2048, 8192], P(None, 'chan', 'seq')
All inputs are finite; a program needn't handle non-finite values.
Results may differ from a plain program's by a relative error of at most 0.007.
Values may be sent and summed in bfloat16 or wider, within the bound.
No kernel may reach another device: no remote copies, remote signals or barrier semaphores. Data moves between devices by JAX's collectives and lax.ppermute only.
A program may use at most 128 MiB of HBM per device.

v0:
```python
import math

import jax
import jax.numpy as jnp
from jax import lax
from jax.sharding import PartitionSpec as P

POOL = 32


total_weight = 0.2
rate_floor = 0.5


def split_length(padded_len):
    best = 1
    factor = 1
    while factor * factor <= padded_len:
        if padded_len % factor == 0:
            best = factor
        factor = factor + 1
    return (padded_len // best, best)


def dft_tables(outer, inner, padded_len):
    outer_idx = jnp.arange(outer, dtype=jnp.int32)
    inner_idx = jnp.arange(inner, dtype=jnp.int32)
    outer_angle = (
        2.0
        * math.pi
        * (outer_idx[:, None] * outer_idx[None, :] % outer).astype(jnp.float32)
        / outer
    )
    inner_angle = (
        2.0
        * math.pi
        * (inner_idx[:, None] * inner_idx[None, :] % inner).astype(jnp.float32)
        / inner
    )
    twist_angle = (
        2.0
        * math.pi
        * (outer_idx[:, None] * inner_idx[None, :] % padded_len).astype(jnp.float32)
        / padded_len
    )
    return (
        jnp.cos(outer_angle),
        -jnp.sin(outer_angle),
        jnp.cos(inner_angle),
        -jnp.sin(inner_angle),
        jnp.cos(twist_angle),
        -jnp.sin(twist_angle),
    )


def forward(real_in, tables):
    outer_re, outer_im, inner_re, inner_im, twist_re, twist_im = tables
    highest = lax.Precision.HIGHEST
    first_re = jnp.einsum("ka,mab->mkb", outer_re, real_in, precision=highest)
    first_im = jnp.einsum("ka,mab->mkb", outer_im, real_in, precision=highest)
    turned_re = first_re * twist_re - first_im * twist_im
    turned_im = first_re * twist_im + first_im * twist_re
    spec_re = jnp.einsum("mkb,bj->mkj", turned_re, inner_re, precision=highest) - jnp.einsum(
        "mkb,bj->mkj", turned_im, inner_im, precision=highest
    )
    spec_im = jnp.einsum("mkb,bj->mkj", turned_re, inner_im, precision=highest) + jnp.einsum(
        "mkb,bj->mkj", turned_im, inner_re, precision=highest
    )
    return (spec_re, spec_im)


def inverse(spec_re, spec_im, tables, padded_len):
    outer_re, outer_im, inner_re, inner_im, twist_re, twist_im = tables
    highest = lax.Precision.HIGHEST
    back_re = jnp.einsum("mkj,bj->mkb", spec_re, inner_re, precision=highest) + jnp.einsum(
        "mkj,bj->mkb", spec_im, inner_im, precision=highest
    )
    back_im = jnp.einsum("mkj,bj->mkb", spec_im, inner_re, precision=highest) - jnp.einsum(
        "mkj,bj->mkb", spec_re, inner_im, precision=highest
    )
    turned_re = back_re * twist_re + back_im * twist_im
    turned_im = back_im * twist_re - back_re * twist_im
    result = jnp.einsum("ka,mkb->mab", outer_re, turned_re, precision=highest) + jnp.einsum(
        "ka,mkb->mab", outer_im, turned_im, precision=highest
    )
    return result / padded_len


def to_pencil(stacked):
    return lax.all_to_all(stacked, "seq", split_axis=1, concat_axis=2, tiled=True)


def from_pencil(pencil_rows):
    return lax.all_to_all(pencil_rows, "seq", split_axis=1, concat_axis=0, tiled=True)


def pad_fold(pencil, outer, inner):
    padded = jnp.concatenate([pencil, jnp.zeros_like(pencil)], axis=2)
    return padded.reshape(-1, outer, inner)


def per_device(projections, filter_taps, skip_gain, head_weight, head_bias, counts):
    query = projections[0].astype(jnp.float32)
    keyed = projections[1].astype(jnp.float32)
    valued = projections[2].astype(jnp.float32)
    channels, width = keyed.shape
    bins = width // POOL
    seq_count = lax.axis_size("seq")
    tracks = head_weight.shape[1]
    key_value = keyed * valued
    pencil = to_pencil(jnp.stack([key_value, filter_taps], axis=0))
    pencil_ch = pencil.shape[1]
    length = pencil.shape[2]
    padded_len = 2 * length
    outer, inner = split_length(padded_len)
    tables = dft_tables(outer, inner, padded_len)
    spec_re, spec_im = forward(pad_fold(pencil, outer, inner), tables)
    signal_re = spec_re[:pencil_ch]
    signal_im = spec_im[:pencil_ch]
    taps_re = spec_re[pencil_ch:]
    taps_im = spec_im[pencil_ch:]
    prod_re = signal_re * taps_re - signal_im * taps_im
    prod_im = signal_re * taps_im + signal_im * taps_re
    conv_pencil = inverse(prod_re, prod_im, tables, padded_len).reshape(pencil_ch, padded_len)[
        :, :length
    ]
    conv = from_pencil(conv_pencil)
    mixed = conv + skip_gain[:, None] * key_value
    output = query * mixed
    pooled = output.reshape(channels, bins, POOL).mean(axis=2).astype(jnp.bfloat16)
    partial_value = jnp.einsum("cb,ct->bt", pooled, head_weight, preferred_element_type=jnp.float32)
    logits = lax.psum(partial_value, "chan") + head_bias[None, :]
    rates = jax.nn.softplus(logits) + rate_floor
    observed = counts.astype(jnp.float32)
    local_log = jnp.sum(observed * jnp.log(rates))
    pred_total, obs_total, log_sum = lax.psum(
        (jnp.sum(rates, axis=0), jnp.sum(observed, axis=0), local_log), "seq"
    )
    log_pred = jnp.log(pred_total)
    loss_sum = (
        jnp.sum(total_weight * (pred_total - obs_total * log_pred) + obs_total * log_pred) - log_sum
    )
    ratio = obs_total / pred_total
    grad_rates = total_weight * (1.0 - ratio)[None, :] + ratio[None, :] - observed / rates
    grad_logits = (grad_rates * jax.nn.sigmoid(logits)).astype(jnp.bfloat16)
    grad_pooled = jnp.einsum(
        "bt,ct->cb", grad_logits, head_weight, preferred_element_type=jnp.float32
    )
    mean_loss = loss_sum / (bins * seq_count * tracks)
    grad_output = jnp.broadcast_to(grad_pooled[:, :, None] / POOL, (channels, bins, POOL)).reshape(
        channels, width
    )
    grad_query = grad_output * mixed
    gated = grad_output * query
    back_pencil = to_pencil(gated[None])
    back_re, back_im = forward(pad_fold(back_pencil, outer, inner), tables)
    corr_re = taps_re * back_re + taps_im * back_im
    corr_im = taps_re * back_im - taps_im * back_re
    corr_pencil = inverse(corr_re, corr_im, tables, padded_len).reshape(pencil_ch, padded_len)[
        :, :length
    ]
    grad_kv = from_pencil(corr_pencil) + skip_gain[:, None] * gated
    return (mean_loss, jnp.stack([grad_query, grad_kv * valued, grad_kv * keyed], axis=0))


def solution(mesh):
    placed = (
        P(None, "chan", "seq"),
        P("chan", "seq"),
        P("chan"),
        P("chan", None),
        P(),
        P("seq", None),
    )
    return jax.shard_map(
        per_device,
        mesh=mesh,
        in_specs=placed,
        out_specs=(P(), P(None, "chan", "seq")),
        check_vma=False,
    )
```

profile of v0, /device:TPU:1, one launch (start us, length us, event | category | flops | bytes accessed | tf_op | source)
XLA Modules:
  0.0 561.9 jit_solution(10187353011130561504)
XLA Ops:
  23.3 7.4 %copy.85 = f32[2,256,2048]{2,0,1:T(2,128)} copy(f32[2,256,2048]{1,2,0:T(8,128)} %pad_maximum_fusion.1) | data formatting | bytes 8388608 | tf_op jit(solution)/shard_map/stack | solution.py:111
  30.7 4.9 all-to-all-start
  36.1 47.2 %all-to-all-done = f32[2,256,2048]{2,0,1:T(2,128)} async-done(((f32[2,256,2048]{2,0,1:T(2,128)}), f32[2,256,2048]{2,0,1:T(2,128)}, u32[]{:S(2)}, u32[]{:S(2)}) %all-to-all-start) | async-done | bytes 4194336 | tf_op jit(solution)/shard_map/all_to_all | solution.py:90
  89.1 4.7 copy.136
  93.8 18.0 %fusion.64 = f32[128,128,128]{2,1,0:T(8,128)S(1)} fusion(f32[128,128,128]{2,1,0:T(8,128)} %bitcast.172), kind=kOutput, calls=%fused_computation.97 | convolution fusion | flops 3221471232 | bytes 16777216 | tf_op jit(solution)/shard_map/ka,mab->mkb/dot_general | solution.py:60
  111.8 13.6 %fusion.82 = f32[128,128,128]{2,1,0:T(8,128)S(1)} fusion(f32[128,128,128]{2,1,0:T(8,128)S(1)} %bitcast.175), kind=kOutput, calls=%fused_computation.115 | convolution fusion | flops 3221454848 | bytes 16777216 | tf_op jit(solution)/shard_map/ka,mab->mkb/dot_general | solution.py:59
  125.4 16.1 %fusion.22 = f32[128,128,128]{2,1,0:T(8,128)} fusion(f32[128,128,128]{2,1,0:T(8,128)S(1)} %fusion.64, f32[128,128,128]{2,1,0:T(8,128)S(1)} %fusion.82, f32[128,128]{0,1:T(8,128)S(1)} %copy.91, f32[128,128]{0,1:T(8,128)S(1)} %copy.89), kind=kOutput, calls=%fused_computation.44 | convolution fusion | flops 3227762688 | bytes 25296896 | tf_op jit(solution)/shard_map/mkb,bj->mkj/dot_general | solution.py:66
  141.5 16.0 %fusion.24 = f32[128,128,128]{2,1,0:T(8,128)} fusion(f32[128,128,128]{2,1,0:T(8,128)S(1)} %fusion.64, f32[128,128,128]{2,1,0:T(8,128)S(1)} %fusion.82, f32[128,128]{0,1:T(8,128)S(1)} %copy.91, f32[128,128]{0,1:T(8,128)S(1)} %copy.89), kind=kOutput, calls=%fused_computation.45 | convolution fusion | flops 3227746304 | bytes 25296896 | tf_op jit(solution)/shard_map/mkb,bj->mkj/dot_general | solution.py:63
  157.6 19.1 %convolution_add_fusion = f32[128,128,128]{2,1,0:T(8,128)} fusion(f32[128,128,128]{2,1,0:T(8,128)} %fusion.22, f32[128,128,128]{2,1,0:T(8,128)S(1)} %fusion.64, f32[128,128,128]{2,1,0:T(8,128)} %copy-done.2, f32[128,128]{0,1:T(8,128)S(1)} %copy.91, f32[128,128]{0,1:T(8,128)S(1)} %copy.89), kind=kOutput, calls=%fused_computation.39 | convolution fusion | flops 3229843456 | bytes 33685504 | tf_op jit(solution)/shard_map/mkb,bj->mkj/dot_general | solution.py:66
  176.7 18.7 %convolution_subtract_fusion = f32[128,128,128]{2,1,0:T(8,128)} fusion(f32[128,128,128]{2,1,0:T(8,128)} %fusion.24, f32[128,128,128]{2,1,0:T(8,128)S(1)} %fusion.64, f32[128,128,128]{2,1,0:T(8,128)} %copy-done.2, f32[128,128]{0,1:T(8,128)S(1)} %copy.91, f32[128,128]{0,1:T(8,128)S(1)} %copy.89), kind=kOutput, calls=%fused_computation.40 | convolution fusion | flops 3229859840 | bytes 33685504 | tf_op jit(solution)/shard_map/mkb,bj->mkj/dot_general | solution.py:63
  195.3 6.9 %multiply_add_fusion.1 = (f32[64,128,128]{2,1,0:T(8,128)S(1)}, f32[64,128,128]{2,1,0:T(8,128)S(1)}) fusion(f32[128,128,128]{2,1,0:T(8,128)} %convolution_add_fusion, f32[128,128,128]{2,1,0:T(8,128)} %convolution_subtract_fusion), kind=kLoop, calls=%fused_computation.37 | loop fusion | flops 6291456 | bytes 25165824 | tf_op jit(solution)/shard_map/add | solution.py:123
  218.1 7.4 %fusion.12 = f32[64,128,128]{2,1,0:T(8,128)S(1)} fusion(f32[64,128,128]{2,1,0:T(8,128)S(1)} %convolution_add_fusion.3, f32[64,128,128]{2,1,0:T(8,128)S(1)} %convolution_subtract_fusion.3, f32[128,128]{1,0:T(8,128)S(1)} %get-tuple-element.26, f32[128,128]{1,0:T(8,128)S(1)} %get-tuple-element.27), kind=kOutput, calls=%fused_computation.29 | convolution fusion | flops 1614004224 | bytes 12713984 | tf_op jit(solution)/shard_map/ka,mkb->mab/dot_general | solution.py:83
  225.5 9.3 %multiply_bitcast_fusion.1 = f32[64,128,128]{1,2,0:T(8,128)} fusion(f32[64,128,128]{2,1,0:T(8,128)S(1)} %fusion.12, f32[64,128,128]{2,1,0:T(8,128)S(1)} %convolution_subtract_fusion.3, f32[64,128,128]{2,1,0:T(8,128)S(1)} %convolution_add_fusion.3, f32[128,128]{1,0:T(8,128)S(1)} %get-tuple-element.26, f32[128,128]{1,0:T(8,128)S(1)} %get-tuple-element.27), kind=kOutput, calls=%fused_computation.28 | convolution fusion | flops 1616084992 | bytes 16908288 | tf_op jit(solution)/shard_map/ka,mkb->mab/dot_general | solution.py:83
  234.8 5.6 copy.98
  246.6 5.6 all-to-all-start.1
  253.7 23.5 %all-to-all-done.1 = f32[64,4,2048]{2,0,1:T(8,128)} async-done(((f32[64,4,2048]{2,0,1:T(8,128)}), f32[64,4,2048]{2,0,1:T(8,128)}, u32[]{:S(2)}, u32[]{:S(2)}) %all-to-all-start.1) | async-done | bytes 2097184 | tf_op jit(solution)/shard_map/all_to_all | solution.py:94
  277.1 4.7 copy.100
  281.9 5.3 all_to_all.63
  291.7 77.4 %all-reduce.5.cloned.1.call-done = f32[64,3840]{1,0:T(8,128)} async-done(((f32[64,3840]{1,0:T(8,128)}), f32[64,3840]{1,0:T(8,128)}) %all-reduce.5.cloned.1.call-update) | async-done | bytes 983056 | tf_op jit(solution)/shard_map/psum | solution.py:132
  372.0 12.8 %all-reduce.2 = (f32[3840]{0:T(1024)S(1)}, f32[3840]{0:T(1024)S(1)}, f32[]{:T(128)}) all-reduce(f32[3840]{0:T(1024)S(1)} %get-tuple-element.9, f32[3840]{0:T(1024)S(1)} %get-tuple-element.10, f32[]{:T(128)} %get-tuple-element.8), channel_id=1, replica_groups=mesh['seq'=4,'chan'=8] {'seq'}, use_global_device_ids=true, to_apply=%region_3.4 | all-reduce | flops 7681 | bytes 61448 | tf_op jit(solution)/shard_map/psum | solution.py:136
  389.4 6.1 %copy.102 = f32[1,256,2048]{2,0,1:T(1,128)} copy(f32[1,256,2048]{1,2,0:T(8,128)} %bitcast_multiply_fusion.8) | data formatting | bytes 4194304 | tf_op jit(solution)/shard_map/mul | solution.py:154
  395.5 28.7 %all_to_all.77 = f32[1,256,2048]{2,0,1:T(1,128)S(1)} all-to-all(f32[1,256,2048]{2,0,1:T(1,128)} %copy.102), channel_id=1, replica_groups=mesh['seq'=4,'chan'=8] {'seq'}, dimensions={1} | all-to-all | bytes 4194304 | tf_op jit(solution)/shard_map/all_to_all | solution.py:90
  439.6 5.6 fusion.42
  445.2 5.6 %convolution_add_fusion.2 = f32[64,128,128]{2,1,0:T(8,128)} fusion(f32[64,128,128]{2,1,0:T(8,128)S(1)} %fusion.40, f32[64,128,128]{1,2,0:T(8,128)S(1)} %fusion.57, f32[64,128,128]{1,2,0:T(8,128)S(1)} %fusion.73, f32[128,128]{1,0:T(8,128)S(1)} %get-tuple-element.26, f32[128,128]{1,0:T(8,128)S(1)} %get-tuple-element.27), kind=kOutput, calls=%fused_computation.51 | convolution fusion | flops 1615036416 | bytes 16908288 | tf_op jit(solution)/shard_map/mkb,bj->mkj/dot_general | solution.py:66
  450.8 10.0 %multiply_subtract_fusion = (f32[64,128,128]{2,1,0:T(8,128)}, f32[64,128,128]{2,1,0:T(8,128)}) fusion(f32[64,128,128]{2,1,0:T(8,128)} %convolution_add_fusion.2, f32[128,128,128]{2,1,0:T(8,128)S(1)} %bitcast.177, f32[128,128,128]{2,1,0:T(8,128)} %convolution_subtract_fusion, f32[64,128,128]{2,1,0:T(8,128)} %fusion.42, f32[64,128,128]{1,2,0:T(8,128)S(1)} %fusion.57, ...), kind=kOutput, calls=%fused_computation.25 | convolution fusion | flops 1621344256 | bytes 33685504 | tf_op jit(solution)/shard_map/mkb,bj->mkj/dot_general | solution.py:63
  460.8 6.4 %fusion.67 = f32[64,128,128]{2,1,0:T(8,128)S(1)} fusion(f32[64,128,128]{2,1,0:T(8,128)} %get-tuple-element.14), kind=kOutput, calls=%fused_computation.100 | convolution fusion | flops 1610842112 | bytes 8388608 | tf_op jit(solution)/shard_map/mkj,bj->mkb/dot_general | solution.py:78
  478.9 7.6 %fusion.4 = f32[64,128,128]{2,1,0:T(8,128)S(1)} fusion(f32[64,128,128]{2,1,0:T(8,128)S(1)} %convolution_add_fusion.1, f32[64,128,128]{2,1,0:T(8,128)S(1)} %convolution_subtract_fusion.1, f32[128,128]{1,0:T(8,128)S(1)} %get-tuple-element.26, f32[128,128]{1,0:T(8,128)S(1)} %get-tuple-element.27), kind=kOutput, calls=%fused_computation.17 | convolution fusion | flops 1614004224 | bytes 12713984 | tf_op jit(solution)/shard_map/ka,mkb->mab/dot_general | solution.py:83
  486.5 8.9 %multiply_bitcast_fusion = f32[64,128,128]{1,2,0:T(8,128)} fusion(f32[64,128,128]{2,1,0:T(8,128)S(1)} %fusion.4, f32[64,128,128]{2,1,0:T(8,128)S(1)} %convolution_subtract_fusion.1, f32[64,128,128]{2,1,0:T(8,128)S(1)} %convolution_add_fusion.1, f32[128,128]{1,0:T(8,128)S(1)} %get-tuple-element.26, f32[128,128]{1,0:T(8,128)S(1)} %get-tuple-element.27), kind=kOutput, calls=%fused_computation.16 | convolution fusion | flops 1616084992 | bytes 16908288 | tf_op jit(solution)/shard_map/ka,mkb->mab/dot_general | solution.py:83
  495.4 5.8 %copy.110 = f32[64,128,128]{2,1,0:T(8,128)} copy(f32[64,128,128]{1,2,0:T(8,128)} %multiply_bitcast_fusion) | data formatting | bytes 8388608 | tf_op jit(solution)/shard_map/div | solution.py:86
  507.4 5.5 all-to-all-start.3
  517.0 20.7 %all-to-all-done.3 = f32[64,4,2048]{2,0,1:T(8,128)} async-done(((f32[64,4,2048]{2,0,1:T(8,128)}), f32[64,4,2048]{2,0,1:T(8,128)}, u32[]{:S(2)}, u32[]{:S(2)}) %all-to-all-start.3) | async-done | bytes 2097184 | tf_op jit(solution)/shard_map/all_to_all | solution.py:94
  547.1 6.6 %copy.113 = f32[3,256,2048]{2,1,0:T(8,128)} copy(f32[3,256,2048]{1,2,0:T(8,128)} %pad_maximum_fusion) | data formatting | bytes 12582912
  (77 shorter events, 103.3 us)
Async XLA Ops:
  7.2 283.0 %copy-start = (bf16[256,3840]{1,0:T(8,128)(2,1)S(1)}, bf16[256,3840]{1,0:T(8,128)(2,1)}, u32[]{:S(2)}) copy-start(bf16[256,3840]{1,0:T(8,128)(2,1)} %param.9) | copy-start | bytes 5898244
  15.4 7.9 %copy-start.6 = (bf16[1,256,2048]{1,2,0:T(8,128)(2,1)}, bf16[1,256,2048]{1,2,0:T(8,128)(2,1)S(1)}, u32[]{:S(2)}) copy-start(bf16[1,256,2048]{1,2,0:T(8,128)(2,1)S(1)} %copy.130) | copy-start | bytes 3145732
  18.1 3.0 copy-start.8
  19.7 1.4 copy-start.5
  30.7 52.6 %all-to-all-start = ((f32[2,256,2048]{2,0,1:T(2,128)}), f32[2,256,2048]{2,0,1:T(2,128)}, u32[]{:S(2)}, u32[]{:S(2)}) async-start(f32[2,256,2048]{2,0,1:T(2,128)} %copy.85), calls=%async_computation | async-start | bytes 8388608 | tf_op jit(solution)/shard_map/all_to_all | solution.py:90
  93.8 18.0 %slice-start = ((s8[8388608]{0:T(1024)(128)(4,1)}), s8[4194304]{0:T(1024)(128)(4,1)S(1)}, s32[]{:S(2)}) async-start(s8[8388608]{0:T(1024)(128)(4,1)} %bitcast.173), calls=%async_computation.5 | async-start | bytes 8388608
  93.8 18.0 %slice-start.1 = ((s8[8388608]{0:T(1024)(128)(4,1)}), s8[4194304]{0:T(1024)(128)(4,1)S(1)}, s32[]{:S(2)}) async-start(s8[8388608]{0:T(1024)(128)(4,1)} %bitcast.173), calls=%async_computation.6 | async-start | bytes 8388608
  125.4 16.1 %copy-start.2 = (f32[128,128,128]{2,1,0:T(8,128)}, f32[128,128,128]{2,1,0:T(8,128)S(1)}, u32[]{:S(2)}) copy-start(f32[128,128,128]{2,1,0:T(8,128)S(1)} %fusion.82) | copy-start | bytes 25165828
  246.6 30.5 %all-to-all-start.1 = ((f32[64,4,2048]{2,0,1:T(8,128)}), f32[64,4,2048]{2,0,1:T(8,128)}, u32[]{:S(2)}, u32[]{:S(2)}) async-start(f32[64,4,2048]{2,0,1:T(8,128)} %bitcast.191), calls=%async_computation.1 | async-start | bytes 4194304 | tf_op jit(solution)/shard_map/all_to_all | solution.py:94
  252.2 116.9 %all-reduce.5.cloned.1.call-start = ((), (), s32[]{:S(2)}) async-start(), calls=%async_computation.4 | async-start | bytes 1966080 | tf_op jit(solution)/shard_map/psum | solution.py:132
  281.9 5.3 copy-start.10
  287.2 81.8 %copy-start.9 = (f32[3840]{0:T(1024)S(1)}, f32[3840]{0:T(1024)}, u32[]{:S(2)}) copy-start(f32[3840]{0:T(1024)} %param.10) | copy-start | bytes 46084
  439.6 11.2 %slice-start.2 = ((s8[8388608]{0:T(1024)(128)(4,1)}), s8[4194304]{0:T(1024)(128)(4,1)S(1)}, s32[]{:S(2)}) async-start(s8[8388608]{0:T(1024)(128)(4,1)} %bitcast.176), calls=%async_computation.7 | async-start | bytes 8388608
  445.2 5.6 %slice-start.3 = ((s8[8388608]{0:T(1024)(128)(4,1)}), s8[4194304]{0:T(1024)(128)(4,1)S(1)}, s32[]{:S(2)}) async-start(s8[8388608]{0:T(1024)(128)(4,1)} %bitcast.176), calls=%async_computation.8 | async-start | bytes 8388608
  460.8 6.4 %copy-start.4 = (f32[64,128,128]{2,1,0:T(8,128)S(1)}, f32[64,128,128]{2,1,0:T(8,128)}, u32[]{:S(2)}) copy-start(f32[64,128,128]{2,1,0:T(8,128)} %get-tuple-element.15) | copy-start | bytes 12582916
  471.1 3.9 copy-start.3
  507.4 30.4 %all-to-all-start.3 = ((f32[64,4,2048]{2,0,1:T(8,128)}), f32[64,4,2048]{2,0,1:T(8,128)}, u32[]{:S(2)}, u32[]{:S(2)}) async-start(f32[64,4,2048]{2,0,1:T(8,128)} %bitcast.190), calls=%async_computation.3 | async-start | bytes 4194304 | tf_op jit(solution)/shard_map/all_to_all | solution.py:94
  512.8 27.8 %copy-start.7 = (bf16[1,256,2048]{1,2,0:T(8,128)(2,1)S(1)}, bf16[1,256,2048]{1,2,0:T(8,128)(2,1)}, u32[]{:S(2)}) copy-start(bf16[1,256,2048]{1,2,0:T(8,128)(2,1)} %copy-done.6) | copy-start | bytes 3145732
  544.0 9.7 %copy-start.1 = (bf16[256,3840]{1,0:T(8,128)(2,1)S(1)}, bf16[256,3840]{1,0:T(8,128)(2,1)}, u32[]{:S(2)}) copy-start(bf16[256,3840]{1,0:T(8,128)(2,1)} %param.9) | copy-start | bytes 5898244
Sparse Core Ops, SparseCore 0:
  291.8 77.2 all-reduce.4
where the time goes:
time: 570 us; the launch traced here: 562 us
  matrix products  207 us (36%)
  waiting for transfers between devices  169 us (30%)
  local copies, waits for them, and re-layouts  86.5 us (15%)
  blocking collectives  41.5 us (7%)
  other arithmetic  25.5 us (4%)
  between operations  17 us (3%)
  starting transfers between devices  15.9 us (3%)
    psum x1, waiting for transfers between devices, per_device(): logits = lax.psum(partial_value, 'chan') + head_bias[None, :]  77.4 us
    all_to_all x1, waiting for transfers between devices, to_pencil(): lax.all_to_all(stacked, 'seq', split_axis=1, concat_axis=2, tiled=True)  47.2 us
    all_to_all x2, waiting for transfers between devices, from_pencil(): lax.all_to_all(pencil_rows, 'seq', split_axis=1, concat_axis=0, tiled=True)  44.2 us
    unnamed x41, local copies, waits for them, and re-layouts  32.4 us
    all_to_all x1, blocking collectives, to_pencil(): lax.all_to_all(stacked, 'seq', split_axis=1, concat_axis=2, tiled=True)  28.7 us
    dot_general x2, matrix products, forward(): jnp.einsum('mkb,bj->mkj', turned_im, inner_im, precision=highest)  28.6 us
    dot_general x2, matrix products, forward(): jnp.einsum('mkb,bj->mkj', turned_im, inner_re, precision=highest)  24.7 us
    dot_general x2, matrix products, forward(): first_im = jnp.einsum('ka,mab->mkb', outer_im, real_in, precision=highest)  22.4 us
  transfers between devices with their start and end apart: 4, of which 4 were waited for; matrix products, arithmetic and copies ran while one was open for 1% of the time, Pallas kernels for 0%

commit v1 on v0

v1 whole, which is shorter than its diff:
```python
import math

import jax
import jax.numpy as jnp
import ml_dtypes
import numpy as np
from jax import lax
from jax.experimental import pallas as pl
from jax.experimental.pallas import tpu as pltpu
from jax.sharding import PartitionSpec as P

POOL = 32
LANES = 128
ROWS = 16
SHIFT = 0.25

total_weight = 0.2
rate_floor = 0.5

VMEM_LIMIT = 48 * 1024 * 1024


def split_bf16(table):
    high = table.astype(ml_dtypes.bfloat16)
    low = (table - high.astype(np.float64)).astype(ml_dtypes.bfloat16)
    return high, low


def radices(outer):
    first = 1
    while first * first < outer:
        first *= 2
    return first, outer // first


def transform_tables(length):
    outer = length // LANES
    idx = np.arange(LANES)
    angle = 2.0 * np.pi * (np.outer(idx, idx) % LANES) / LANES
    wr, wi = np.cos(angle), -np.sin(angle)
    forward = np.block([[wr, wi], [-wi, wr]])
    backward = np.block([[wr, -wi], [wi, wr]]) / length
    k1 = np.arange(outer)[:, None]
    twist = 2.0 * np.pi * (k1 - SHIFT) * idx[None, :] / length
    f_hi, f_lo = split_bf16(forward)
    b_hi, b_lo = split_bf16(backward)
    return dict(
        fwd=np.stack([f_hi, f_lo]),
        bwd=np.stack([b_hi, b_lo]),
        twist=np.stack([np.cos(twist), -np.sin(twist)]).astype(np.float32),
    )


def pool_tables():
    per = LANES // POOL
    lane = np.arange(LANES)
    hit = (lane[:, None] // POOL) == (lane[None, :] % per)
    gather = np.concatenate([hit, hit], axis=0) / POOL
    spread = np.concatenate([hit.T, hit.T], axis=0) / POOL
    return gather.astype(ml_dtypes.bfloat16), spread.astype(ml_dtypes.bfloat16)


def times(value, angle):
    re, im = value
    c, s = math.cos(angle), math.sin(angle)
    tiny = 1e-12
    if im is None:
        if abs(s) < tiny and c > 0:
            return (re, None)
        return (re * c, re * s)
    if abs(s) < tiny:
        return (re, im) if c > 0 else (-re, -im)
    if abs(c) < tiny:
        return (-im, re) if s > 0 else (im, -re)
    return (re * c - im * s, re * s + im * c)


def add(a, b):
    if a[1] is None and b[1] is None:
        return (a[0] + b[0], None)
    if a[1] is None:
        return (a[0] + b[0], b[1])
    if b[1] is None:
        return (a[0] + b[0], a[1])
    return (a[0] + b[0], a[1] + b[1])


def sub(a, b):
    if a[1] is None and b[1] is None:
        return (a[0] - b[0], None)
    if a[1] is None:
        return (a[0] - b[0], -b[1])
    if b[1] is None:
        return (a[0] - b[0], a[1])
    return (a[0] - b[0], a[1] - b[1])


def small_dft(values, sign):
    count = len(values)
    if count == 1:
        return values
    even = small_dft(values[0::2], sign)
    odd = small_dft(values[1::2], sign)
    out = [None] * count
    half = count // 2
    for k in range(half):
        turned = times(odd[k], sign * 2.0 * math.pi * k / count)
        out[k] = add(even[k], turned)
        out[k + half] = sub(even[k], turned)
    return out


def dot(a, b):
    return jnp.dot(a, b, preferred_element_type=jnp.float32)


def split(value):
    high = value.astype(jnp.bfloat16)
    return high, (value - high.astype(jnp.float32)).astype(jnp.bfloat16)


def lane_transform(re_parts, im_parts, lhs, table_ref):
    for i, (re, im) in enumerate(zip(re_parts, im_parts)):
        rows = pl.ds(i * ROWS, ROWS)
        re_hi, re_lo = split(re)
        im_hi, im_lo = split(im)
        lhs[0, rows, :LANES] = re_hi
        lhs[0, rows, LANES:] = im_hi
        lhs[1, rows, :LANES] = re_lo
        lhs[1, rows, LANES:] = im_lo
    high = lhs[0]
    return dot(high, table_ref[0]) + (dot(lhs[1], table_ref[0]) + dot(high, table_ref[1]))


def first_pass(load, store, outer):
    ra, rb = radices(outer)
    for b in range(rb):
        values = [times((load(rb * a + b), None), 2.0 * math.pi * a * SHIFT / ra) for a in range(ra)]
        out = small_dft(values, -1)
        for alpha in range(ra):
            re, im = times(out[alpha], -2.0 * math.pi * b * (alpha - SHIFT) / outer)
            store(b, alpha, re, im)


def second_pass(parts, alpha, outer, twist_ref):
    ra, rb = radices(outer)
    values = [(parts[0, b, alpha], parts[1, b, alpha]) for b in range(rb)]
    out = small_dft(values, -1)
    res, ims = [], []
    for beta in range(rb):
        k1 = alpha + ra * beta
        tr = twist_ref[0, k1 : k1 + 1, :]
        ti = twist_ref[1, k1 : k1 + 1, :]
        re, im = out[beta]
        res.append(re * tr - im * ti)
        ims.append(re * ti + im * tr)
    return res, ims


def back_second_pass(spectrum, alpha, outer, twist_ref, store):
    ra, rb = radices(outer)
    values = []
    for beta in range(rb):
        k1 = alpha + ra * beta
        tr = twist_ref[0, k1 : k1 + 1, :]
        ti = twist_ref[1, k1 : k1 + 1, :]
        re = spectrum[beta * ROWS : (beta + 1) * ROWS, :LANES]
        im = spectrum[beta * ROWS : (beta + 1) * ROWS, LANES:]
        values.append((re * tr + im * ti, im * tr - re * ti))
    out = small_dft(values, +1)
    for b in range(rb):
        re, im = times(out[b], 2.0 * math.pi * b * (alpha - SHIFT) / outer)
        store(b, alpha, re, im)


def back_first_pass(parts, outer, emit):
    ra, rb = radices(outer)
    for b in range(rb):
        values = [(parts[0, b, alpha], parts[1, b, alpha]) for alpha in range(ra)]
        out = small_dft(values, +1)
        for a in range(ra):
            angle = -2.0 * math.pi * a * SHIFT / ra
            re, im = out[a]
            c, s = math.cos(angle), math.sin(angle)
            emit(rb * a + b, re if a == 0 else re * c - im * s)


def keep(parts):
    def store(b, alpha, re, im):
        parts[0, b, alpha] = re
        parts[1, b, alpha] = im

    return store


def conv_kernel(peers, outer, me_ref, *refs):
    pieces = refs[:peers]
    skip_ref, fwd_ref, bwd_ref, twist_ref = refs[peers : peers + 4]
    outs = refs[peers + 4 : 2 * peers + 4]
    mixed_ref, spec_ref = refs[2 * peers + 4 : 2 * peers + 6]
    rows_in, parts_x, parts_h, parts_y, lhs, rows_out = refs[2 * peers + 6 :]
    me = me_ref[0]
    ra, rb = radices(outer)
    per = outer // peers
    width = per * LANES
    for k in range(peers):
        rows_in[me ^ k] = pieces[k][...]

    def loader(which):
        def load(n1):
            lanes = slice((n1 % per) * LANES, (n1 % per + 1) * LANES)
            return rows_in[n1 // per, which, :, lanes].astype(jnp.float32)

        return load

    load_x = loader(0)
    first_pass(load_x, keep(parts_x), outer)
    first_pass(loader(1), keep(parts_h), outer)
    chunk = rb * ROWS
    for alpha in range(ra):
        x = lane_transform(*second_pass(parts_x, alpha, outer, twist_ref), lhs.at[3 * alpha], fwd_ref)
        h = lane_transform(*second_pass(parts_h, alpha, outer, twist_ref), lhs.at[3 * alpha + 1], fwd_ref)
        spec_ref[0, alpha * chunk : (alpha + 1) * chunk, :] = h
        xr, xi, hr, hi = x[:, :LANES], x[:, LANES:], h[:, :LANES], h[:, LANES:]
        pr = xr * hr - xi * hi
        pi = xr * hi + xi * hr
        rows = [slice(i * ROWS, (i + 1) * ROWS) for i in range(rb)]
        y = lane_transform([pr[r] for r in rows], [pi[r] for r in rows], lhs.at[3 * alpha + 2], bwd_ref)
        back_second_pass(y, alpha, outer, twist_ref, keep(parts_y))
    skip = jnp.broadcast_to(skip_ref[...], (ROWS, LANES))

    def emit(n1, value):
        mixed = value + skip * load_x(n1)
        lanes = slice((n1 % per) * LANES, (n1 % per + 1) * LANES)
        mixed_ref[:, n1 * LANES : (n1 + 1) * LANES] = mixed
        rows_out[n1 // per, :, lanes] = mixed.astype(jnp.bfloat16)

    back_first_pass(parts_y, outer, emit)
    for k in range(peers):
        outs[k][...] = rows_out[me ^ k]


def pool_kernel(peers, outer, me_ref, *refs):
    queries = refs[:peers]
    mixed_ref, gather_ref, pooled_ref, rows_in, lhs = refs[peers:]
    me = me_ref[0]
    per = outer // peers
    for k in range(peers):
        rows_in[me ^ k] = queries[k][...]
    for n1 in range(outer):
        lanes = slice((n1 % per) * LANES, (n1 % per + 1) * LANES)
        query = rows_in[n1 // per, :, lanes].astype(jnp.float32)
        high, low = split(query * mixed_ref[:, n1 * LANES : (n1 + 1) * LANES])
        lhs[n1 * ROWS : (n1 + 1) * ROWS, :LANES] = high
        lhs[n1 * ROWS : (n1 + 1) * ROWS, LANES:] = low
    sums = dot(lhs[...], gather_ref[...])
    each = LANES // POOL
    held = LANES // each
    place = lax.broadcasted_iota(jnp.int32, (ROWS, LANES), 1) // each
    for tile in range(-(-outer // held)):
        total = jnp.zeros((ROWS, LANES), jnp.float32)
        count = min(held, outer - tile * held)
        for j in range(count):
            n1 = tile * held + j
            total = jnp.where(place == j, sums[n1 * ROWS : (n1 + 1) * ROWS], total)
        used = count * each
        pooled_ref[:, tile * LANES : tile * LANES + used] = total[:, :used].astype(jnp.bfloat16)


def corr_kernel(peers, outer, me_ref, *refs):
    queries = refs[:peers]
    grad_ref, spec_ref, skip_ref, fwd_ref, bwd_ref, twist_ref, spread_ref = refs[peers : peers + 7]
    outs = refs[peers + 7 : 2 * peers + 7]
    rows_in, lhs_g, gated, parts_g, parts_y, lhs, rows_out = refs[2 * peers + 7 :]
    me = me_ref[0]
    ra, rb = radices(outer)
    per = outer // peers
    for k in range(peers):
        rows_in[me ^ k] = queries[k][...]
    each = LANES // POOL
    held = LANES // each
    place = lax.broadcasted_iota(jnp.int32, (ROWS, LANES), 1) // each
    zero = jnp.zeros((ROWS, LANES), jnp.float32)
    for tile in range(-(-outer // held)):
        count = min(held, outer - tile * held)
        used = count * each
        part = grad_ref[:, tile * LANES : tile * LANES + used]
        if used < LANES:
            part = jnp.concatenate([part, jnp.zeros((ROWS, LANES - used), jnp.float32)], axis=1)
        high = part.astype(jnp.bfloat16).astype(jnp.float32)
        low = part - high
        for j in range(count):
            rows = pl.ds((tile * held + j) * ROWS, ROWS)
            lhs_g[rows, :LANES] = jnp.where(place == j, high, zero).astype(jnp.bfloat16)
            lhs_g[rows, LANES:] = jnp.where(place == j, low, zero).astype(jnp.bfloat16)
    gated[...] = dot(lhs_g[...], spread_ref[...])
    for n1 in range(outer):
        lanes = slice((n1 % per) * LANES, (n1 % per + 1) * LANES)
        rows = pl.ds(n1 * ROWS, ROWS)
        gated[rows, :] = gated[rows, :] * rows_in[n1 // per, :, lanes].astype(jnp.float32)

    def load_g(n1):
        return gated[n1 * ROWS : (n1 + 1) * ROWS, :]

    first_pass(load_g, keep(parts_g), outer)
    chunk = rb * ROWS
    for alpha in range(ra):
        g = lane_transform(*second_pass(parts_g, alpha, outer, twist_ref), lhs.at[2 * alpha], fwd_ref)
        h = spec_ref[0, alpha * chunk : (alpha + 1) * chunk, :]
        gr, gi, hr, hi = g[:, :LANES], g[:, LANES:], h[:, :LANES], h[:, LANES:]
        pr = gr * hr + gi * hi
        pi = gi * hr - gr * hi
        rows = [slice(i * ROWS, (i + 1) * ROWS) for i in range(rb)]
        y = lane_transform([pr[r] for r in rows], [pi[r] for r in rows], lhs.at[2 * alpha + 1], bwd_ref)
        back_second_pass(y, alpha, outer, twist_ref, keep(parts_y))
    skip = jnp.broadcast_to(skip_ref[...], (ROWS, LANES))

    def emit(n1, value):
        lanes = slice((n1 % per) * LANES, (n1 % per + 1) * LANES)
        rows_out[n1 // per, :, lanes] = (value + skip * load_g(n1)).astype(jnp.bfloat16)

    back_first_pass(parts_y, outer, emit)
    for k in range(peers):
        outs[k][...] = rows_out[me ^ k]


def whole(array):
    rank = array.ndim
    return pl.BlockSpec(array.shape, lambda i, me: (0,) * rank)


def by_rows(width):
    return pl.BlockSpec((ROWS, width), lambda i, me: (i, 0))


def call(kernel, name, me, steps, inputs, in_specs, out_shapes, out_specs, scratch, flops):
    moved = sum(x.size * x.dtype.itemsize for x in inputs)
    moved += sum(math.prod(o.shape) * o.dtype.itemsize for o in out_shapes)
    return pl.pallas_call(
        kernel,
        name=name,
        grid_spec=pltpu.PrefetchScalarGridSpec(
            num_scalar_prefetch=1,
            grid=(steps,),
            in_specs=in_specs,
            out_specs=out_specs,
            scratch_shapes=scratch,
        ),
        out_shape=out_shapes,
        compiler_params=pltpu.CompilerParams(
            dimension_semantics=("arbitrary",), vmem_limit_bytes=VMEM_LIMIT
        ),
        cost_estimate=pl.CostEstimate(flops=flops, bytes_accessed=moved, transcendentals=0),
    )(me, *inputs)


def convolve(me, pieces, skip, tables):
    peers = len(pieces)
    rows, width = pieces[0].shape[1:]
    length = width * peers
    outer = length // LANES
    ra, rb = radices(outer)
    chunk = rb * ROWS
    steps = rows // ROWS
    f32, bf16 = jnp.float32, jnp.bfloat16
    fwd, bwd, twist = tables["fwd"], tables["bwd"], tables["twist"]
    out_shapes = [jax.ShapeDtypeStruct((rows, width), bf16)] * peers + [
        jax.ShapeDtypeStruct((rows, length), f32),
        jax.ShapeDtypeStruct((steps, outer * ROWS, 2 * LANES), f32),
    ]
    out_specs = [by_rows(width)] * peers + [
        by_rows(length),
        pl.BlockSpec((1, outer * ROWS, 2 * LANES), lambda i, me: (i, 0, 0)),
    ]
    in_specs = [pl.BlockSpec((2, ROWS, width), lambda i, me: (0, i, 0))] * peers + [
        pl.BlockSpec((ROWS, 1), lambda i, me: (i, 0)),
        whole(fwd),
        whole(bwd),
        whole(twist),
    ]
    parts = pltpu.VMEM((2, rb, ra, ROWS, LANES), f32)
    scratch = [
        pltpu.VMEM((peers, 2, ROWS, width), bf16),
        parts,
        parts,
        parts,
        pltpu.VMEM((3 * ra, 2, chunk, 2 * LANES), bf16),
        pltpu.VMEM((peers, ROWS, width), bf16),
    ]

    def kernel(*refs):
        conv_kernel(peers, outer, *refs)

    out = call(
        kernel, "long_convolution", me, steps, [*pieces, skip, fwd, bwd, twist], in_specs, out_shapes, out_specs,
        scratch, 2 * 9 * rows * outer * (2 * LANES) ** 2,
    )
    return out[:peers], out[peers], out[peers + 1]


def pool(me, queries, mixed, gather):
    peers = len(queries)
    rows, width = queries[0].shape
    length = width * peers
    outer = length // LANES
    bins = length // POOL
    bf16 = jnp.bfloat16

    def kernel(*refs):
        pool_kernel(peers, outer, *refs)

    return call(
        kernel, "pool_bins", me, rows // ROWS, [*queries, mixed, gather],
        [by_rows(width)] * peers + [by_rows(length), whole(gather)],
        [jax.ShapeDtypeStruct((rows, bins), bf16)], [by_rows(bins)],
        [pltpu.VMEM((peers, ROWS, width), bf16), pltpu.VMEM((outer * ROWS, 2 * LANES), bf16)],
        2 * rows * outer * 2 * LANES * LANES,
    )[0]


def correlate(me, queries, grad_pooled, spec, skip, tables, spread):
    peers = len(queries)
    rows, width = queries[0].shape
    length = width * peers
    outer = length // LANES
    bins = length // POOL
    ra, rb = radices(outer)
    chunk = rb * ROWS
    f32, bf16 = jnp.float32, jnp.bfloat16
    fwd, bwd, twist = tables["fwd"], tables["bwd"], tables["twist"]
    in_specs = [by_rows(width)] * peers + [
        by_rows(bins),
        pl.BlockSpec((1, outer * ROWS, 2 * LANES), lambda i, me: (i, 0, 0)),
        pl.BlockSpec((ROWS, 1), lambda i, me: (i, 0)),
        whole(fwd),
        whole(bwd),
        whole(twist),
        whole(spread),
    ]
    parts = pltpu.VMEM((2, rb, ra, ROWS, LANES), f32)
    scratch = [
        pltpu.VMEM((peers, ROWS, width), bf16),
        pltpu.VMEM((outer * ROWS, 2 * LANES), bf16),
        pltpu.VMEM((outer * ROWS, LANES), f32),
        parts,
        parts,
        pltpu.VMEM((2 * ra, 2, chunk, 2 * LANES), bf16),
        pltpu.VMEM((peers, ROWS, width), bf16),
    ]

    def kernel(*refs):
        corr_kernel(peers, outer, *refs)

    return call(
        kernel, "long_correlation", me, rows // ROWS,
        [*queries, grad_pooled, spec, skip, fwd, bwd, twist, spread], in_specs,
        [jax.ShapeDtypeStruct((rows, width), bf16)] * peers, [by_rows(width)] * peers,
        scratch, 2 * 7 * rows * outer * (2 * LANES) ** 2,
    )


def swap(value, k, count):
    if k == 0:
        return value
    return lax.ppermute(value, "seq", [(i, i ^ k) for i in range(count)])


def pad_rows(value, rows):
    short = rows - value.shape[-2]
    if short == 0:
        return value
    widths = [(0, 0)] * value.ndim
    widths[-2] = (0, short)
    return jnp.pad(value, widths)


def per_device(projections, filter_taps, skip_gain, head_weight, head_bias, counts):
    f32, bf16 = jnp.float32, jnp.bfloat16
    _, channels, width = projections.shape
    peers = lax.axis_size("seq")
    groups = lax.axis_size("chan")
    seat = lax.axis_index("seq")
    group = lax.axis_index("chan")
    bins = width // POOL
    length = width * peers
    tracks = head_weight.shape[1]
    own_tracks = tracks // groups
    pencil = channels // peers
    rows = -(-pencil // ROWS) * ROWS
    me = jnp.asarray(seat, jnp.int32).reshape(1)
    tables = transform_tables(length)
    gather, spread = pool_tables()

    def block(array, k):
        return lax.dynamic_index_in_dim(array, seat ^ k, axis=-3, keepdims=False)

    query = projections[0]
    key_value = projections[1].astype(f32) * projections[2].astype(f32)
    stacked = jnp.stack([key_value.astype(bf16), filter_taps.astype(bf16)])
    stacked = stacked.reshape(2, peers, pencil, width)
    pieces = [pad_rows(swap(block(stacked, k), k, peers), rows) for k in range(peers)]
    query_blocks = query.reshape(peers, pencil, width)
    queries = [pad_rows(swap(block(query_blocks, k), k, peers), rows) for k in range(peers)]
    skip = pad_rows(block(skip_gain.reshape(peers, pencil, 1), 0), rows)

    half = channels // 2
    by_track = head_weight.reshape(2, half, groups, own_tracks).transpose(0, 2, 1, 3)
    mine = lax.dynamic_index_in_dim(by_track, seat & 1, axis=0, keepdims=False)
    mine = lax.all_to_all(mine, "chan", split_axis=0, concat_axis=0, tiled=True)
    other = swap(mine, 1, peers)
    mine = mine.reshape(groups * half, own_tracks)
    other = other.reshape(groups * half, own_tracks)

    mixed_out, mixed, spec = convolve(me, pieces, skip, tables)
    mixed_home = [swap(mixed_out[k][:pencil], k, peers) for k in range(peers)]
    pooled = pool(me, queries, mixed, gather)[:pencil]

    sent = pooled.reshape(pencil, peers, bins).transpose(1, 0, 2)
    sent = jnp.broadcast_to(sent[None], (groups, peers, pencil, bins))
    got = lax.all_to_all(
        sent.reshape(groups * peers, pencil, bins), ("chan", "seq"), split_axis=0, concat_axis=0, tiled=True
    )
    got = got.reshape(groups, 2, half, bins)
    low_half = got[:, 0].reshape(groups * half, bins)
    high_half = got[:, 1].reshape(groups * half, bins)
    odd = (seat & 1) == 1
    pooled_mine = jnp.where(odd, high_half, low_half)
    pooled_other = jnp.where(odd, low_half, high_half)

    def project(x, w):
        return lax.dot_general(x, w, (((0,), (0,)), ((), ())), preferred_element_type=f32)

    own_bias = lax.dynamic_slice_in_dim(head_bias, group * own_tracks, own_tracks)
    own_counts = lax.dynamic_slice_in_dim(counts, group * own_tracks, own_tracks, axis=1)
    logits = project(pooled_mine, mine) + project(pooled_other, other) + own_bias[None, :]
    rates = jax.nn.softplus(logits) + rate_floor
    observed = own_counts.astype(f32)
    partial_sums = jnp.stack(
        [jnp.sum(rates, axis=0), jnp.sum(observed, axis=0), jnp.sum(observed * jnp.log(rates), axis=0)]
    )
    pred_total, obs_total, log_sum = jnp.sum(lax.all_gather(partial_sums, "seq"), axis=0)
    log_pred = jnp.log(pred_total)
    loss_part = jnp.sum(
        total_weight * (pred_total - obs_total * log_pred) + obs_total * log_pred - log_sum
    )
    mean_loss = lax.psum(loss_part, "chan") / (bins * peers * tracks)
    ratio = obs_total / pred_total
    grad_rates = total_weight * (1.0 - ratio)[None, :] + ratio[None, :] - observed / rates
    grad_logits = (grad_rates * jax.nn.sigmoid(logits)).astype(bf16)

    def spread_back(w):
        return lax.dot_general(w, grad_logits, (((1,), (1,)), ((), ())), preferred_element_type=f32)

    part_mine = spread_back(mine).astype(bf16).reshape(groups, 1, half, bins)
    part_other = spread_back(other).astype(bf16).reshape(groups, 1, half, bins)
    part = jnp.concatenate(
        [jnp.where(odd, part_other, part_mine), jnp.where(odd, part_mine, part_other)], axis=1
    )
    back = lax.all_to_all(
        part.reshape(groups * peers, pencil, bins), ("chan", "seq"), split_axis=0, concat_axis=0, tiled=True
    )
    grad_pooled = jnp.sum(back.reshape(groups, peers, pencil, bins).astype(f32), axis=0)
    grad_home = [swap(block(grad_pooled, k), k, peers) for k in range(peers)]
    grad_rows = pad_rows(grad_pooled.transpose(1, 0, 2).reshape(pencil, peers * bins), rows)

    corr_out = correlate(me, queries, grad_rows, spec, skip, tables, spread)
    corr_home = [swap(corr_out[k][:pencil], k, peers) for k in range(peers)]

    def assemble(parts):
        out = jnp.zeros((peers,) + parts[0].shape, parts[0].dtype)
        for k, part in enumerate(parts):
            out = lax.dynamic_update_index_in_dim(out, part, seat ^ k, axis=0)
        return out.reshape((channels,) + parts[0].shape[1:])

    grad_output = jnp.repeat(assemble(grad_home) / POOL, POOL, axis=1)
    grad_kv = assemble(corr_home).astype(f32)
    grad_query = grad_output * assemble(mixed_home).astype(f32)
    grads = jnp.stack(
        [grad_query, grad_kv * projections[2].astype(f32), grad_kv * projections[1].astype(f32)], axis=0
    )
    return mean_loss, grads


def solution(mesh):
    placed = (
        P(None, "chan", "seq"),
        P("chan", "seq"),
        P("chan"),
        P("chan", None),
        P(),
        P("seq", None),
    )
    return jax.shard_map(
        per_device,
        mesh=mesh,
        in_specs=placed,
        out_specs=(P(), P(None, "chan", "seq")),
        check_vma=False,
    )
```

time: 570 us -> 167 us (0.29); the launches traced: 562 us -> 165 us
  matrix products: 207 us -> 6.7 us
  waiting for transfers between devices: 169 us -> 40.9 us
  local copies, waits for them, and re-layouts: 86.5 us -> 23.1 us
  blocking collectives: 41.5 us -> 21.1 us
  starting transfers between devices: 15.9 us -> 31.1 us
  between operations: 17 us -> 2.89 us
  other arithmetic: 25.5 us -> 38.4 us
    dot_general x26 -> x4, matrix products: 207 us -> 6.7 us  [the longest x2 3.37 us: project(): lax.dot_general(x, w, (((0,), (0,)), ((), ())), preferred_element_type=f32)]
    psum x1 -> x0, waiting for transfers between devices: 77.4 us -> none  [per_device(): logits = lax.psum(partial_value, 'chan') + head_bias[None, :]]
    all_to_all x3, waiting for transfers between devices: 91.4 us -> 15 us  [the longest x1 8.66 us: per_device(): lax.all_to_all(part.reshape(groups * peers, pencil, bins), ('chan', 'seq'...]
    all_to_all x1 -> x0, blocking collectives: 28.7 us -> none  [to_pencil(): lax.all_to_all(stacked, 'seq', split_axis=1, concat_axis=2, tiled=True)]
    pallas_call x0 -> x2, other arithmetic: none -> 27.1 us  [call(): pl.pallas_call(kernel, name=name, grid_spec=pltpu.PrefetchScalarGridSpec(...]
    unnamed x41 -> x22, local copies, waits for them, and re-layouts: 32.4 us -> 6.44 us
    ppermute x0 -> x16, waiting for transfers between devices: none -> 25.9 us  [swap(): return lax.ppermute(value, 'seq', [(i, i ^ k) for i in range(count)])]
    all_to_all x9 -> x0, local copies, waits for them, and re-layouts: 24 us -> none  [the longest x6 18.9 us: from_pencil(): lax.all_to_all(pencil_rows, 'seq', split_axis=1, concat_axis=0, tiled=True)]
  transfers between devices with their start and end apart: 4 -> 19, of which waited for: 4 -> 5; matrix products, arithmetic and copies ran while one was open for 1% -> 33% of each run, Pallas kernels for 0% -> 1%
where the time goes in v1:
time: 167 us; the launch traced here: 165 us
  waiting for transfers between devices  40.9 us (24%)
  other arithmetic  38.4 us (23%)
  starting transfers between devices  31.1 us (19%)
  local copies, waits for them, and re-layouts  23.1 us (14%)
  blocking collectives  21.1 us (13%)
  matrix products  6.7 us (4%)
  between operations  2.89 us (2%)
    pallas_call x2, other arithmetic, call(): pl.pallas_call(kernel, name=name, grid_spec=pltpu.PrefetchScalarGridSpec(...  27.1 us
    ppermute x16, waiting for transfers between devices, swap(): return lax.ppermute(value, 'seq', [(i, i ^ k) for i in range(count)])  25.9 us
    psum x1, blocking collectives, per_device(): mean_loss = lax.psum(loss_part, 'chan') / (bins * peers * tracks)  15.5 us
    ppermute x16, starting transfers between devices, swap(): return lax.ppermute(value, 'seq', [(i, i ^ k) for i in range(count)])  15 us
    all_to_all x1, waiting for transfers between devices, per_device(): lax.all_to_all(part.reshape(groups * peers, pencil, bins), ('chan', 'seq'...  8.66 us
    all_to_all x1, starting transfers between devices, per_device(): mine = lax.all_to_all(mine, 'chan', split_axis=0, concat_axis=0, tiled=True)  6.65 us
    unnamed x22, local copies, waits for them, and re-layouts  6.44 us
    all_to_all x1, waiting for transfers between devices, per_device(): lax.all_to_all(sent.reshape(groups * peers, pencil, bins), ('chan', 'seq'...  6.32 us
  transfers between devices with their start and end apart: 19, of which 5 were waited for; matrix products, arithmetic and copies ran while one was open for 33% of the time, Pallas kernels for 1%

profile of v1, /device:TPU:1, one launch (start us, length us, event | category | flops | bytes accessed | tf_op | source)
XLA Modules:
  0.0 165.5 jit_solution(10606993357897807573)
XLA Ops:
  0.6 4.8 %reshape.154 = bf16[2,128,8,480]{3,2,1,0:T(8,128)(2,1)S(1)} reshape(bf16[256,3840]{1,0:T(8,128)(2,1)} %param.14) | data formatting | bytes 3932160 | tf_op jit(solution)/shard_map/reshape | solution.py:507
  5.5 1.6 copy.74
  8.2 6.6 %all-to-all-start.1 = ((bf16[8,128,480]{1,2,0:T(8,128)(2,1)}), bf16[8,128,480]{1,2,0:T(8,128)(2,1)}, u32[]{:S(2)}, u32[]{:S(2)}) async-start(bf16[8,128,480]{1,2,0:T(8,128)(2,1)} %bitcast.130), calls=%async_computation.1 | async-start | bytes 1966080 | tf_op jit(solution)/shard_map/all_to_all | solution.py:509
  14.9 2.7 %convert_element_type.67 = bf16[256,2048]{1,0:T(8,128)(2,1)} convert(f32[256,2048]{1,0:T(8,128)} %param.12) | non-fusion elementwise | flops 524288 | bytes 3145728 | tf_op jit(solution)/shard_map/convert_element_type | solution.py:499
  18.8 1.4 fusion.12
  21.1 1.2 collective-permute-start.4
  23.2 1.2 collective-permute-start.1
  25.3 9.7 %collective-permute-done.4 = bf16[2,64,2048]{2,1,0:T(8,128)(2,1)} collective-permute-done((bf16[2,64,2048]{2,1,0:T(8,128)(2,1)}, bf16[2,64,2048]{2,1,0:T(8,128)(2,1)}, u32[]{:S(2)}, u32[]{:S(2)}) %collective-permute-start.4) | collective-permute-done | bytes 524320 | tf_op jit(solution)/shard_map/ppermute | solution.py:465
  35.0 11.7 %collective-permute-done.5 = bf16[2,64,2048]{2,1,0:T(8,128)(2,1)} collective-permute-done((bf16[2,64,2048]{2,1,0:T(8,128)(2,1)}, bf16[2,64,2048]{2,1,0:T(8,128)(2,1)}, u32[]{:S(2)}, u32[]{:S(2)}) %collective-permute-start.5) | collective-permute-done | bytes 524320 | tf_op jit(solution)/shard_map/ppermute | solution.py:465
  46.9 15.6 %long_convolution.1 = (bf16[4,64,2048]{2,1,0:T(8,128)(2,1)S(1)}, f32[64,8192]{1,0:T(8,128)S(1)}, bf16[64,2048]{1,0:T(8,128)(2,1)}, bf16[64,2048]{1,0:T(8,128)(2,...) fusion(bf16[4,64,2048]{2,1,0:T(8,128)(2,1)S(1)} %broadcast.36.clone, s32[]{:T(128)S(6)} %select_n.104, ...), kind=kCustom, calls=%fused_computation.46 | custom fusion | flops 4831838208 | bytes 10059784 | tf_op jit(solution)/shard_map/long_convolution/pallas_call | solution.py:339
  62.5 1.3 pool_bins.1
  64.1 1.1 reshape.155
  65.2 6.3 %all-to-all-start = ((bf16[32,2,2048]{2,1,0:T(2,128)(2,1)}), bf16[32,2,2048]{2,1,0:T(2,128)(2,1)S(1)}, u32[]{:S(2)}, u32[]{:S(2)}) async-start(bf16[32,2,2048]{2,1,0:T(2,128)(2,1)} %reshape.155), calls=%async_computation | async-start | bytes 524288 | tf_op jit(solution)/shard_map/all_to_all | solution.py:520
  72.5 1.5 collective-permute-start.11
  75.4 6.3 %all-to-all-done = bf16[32,2,2048]{2,1,0:T(2,128)(2,1)S(1)} async-done(((bf16[32,2,2048]{2,1,0:T(2,128)(2,1)}), bf16[32,2,2048]{2,1,0:T(2,128)(2,1)S(1)}, u32[]{:S(2)}, u32[]{:S(2)}) %all-to-all-start) | async-done | bytes 262176 | tf_op jit(solution)/shard_map/all_to_all | solution.py:520
  82.1 1.6 fusion.5
  83.7 1.8 %convert_reduce_fusion.1 = (f32[480]{0:T(512)S(1)}, f32[480]{0:T(512)S(1)}, f32[480]{0:T(512)S(1)}, f32[64,480]{1,0:T(8,128)S(1)}) fusion(s32[64,3840]{1,0:T(8,128)} %param.16, s32[]{:T(128)S(6)} %select_n.113, f32[480]{0:T(512)S(1)} %dynamic_slice.63, f32[64,480]{1,0:T(8,128)S(1)} %fusion.5, bf16[1024,64]{1,0:T(8,128)(2,1)S(1)} %bitcast.138, ...), kind=kOutput, calls=%fused_computation.56 | convolution fusion | flops 63343200 | bytes 1490436 | tf_op jit(solution)/shard_map/dot_general | solution.py:531
  85.5 5.6 %all-gather.1 = f32[4,3,480]{2,1,0:T(4,128)S(1)} all-gather(f32[1,3,480]{2,1,0:T(4,128)S(1)} %maximum_bitcast_fusion), channel_id=2, replica_groups=mesh['seq'=4,'chan'=8] {'seq'}, dimensions={0}, use_global_device_ids=true | all-gather | bytes 28800 | tf_op jit(solution)/shard_map/all_gather | solution.py:541
  91.1 1.7 %convolution_convert_fusion = bf16[1024,64]{0,1:T(8,128)(2,1)S(1)} fusion(f32[64,480]{1,0:T(8,128)S(1)} %get-tuple-element.69, s32[64,3840]{1,0:T(8,128)} %param.16, s32[]{:T(128)S(6)} %select_n.113, f32[480]{0:T(512)S(1)} %bitcast.145, bf16[8,128,480]{1,2,0:T(8,128)(2,1)} %all-to-all-done.1), kind=kOutput, calls=%fused_computation.14 | convolution fusion | flops 63440896 | bytes 1369988 | tf_op jit(solution)/shard_map/dot_general | solution.py:552
  92.8 1.7 %broadcast_select_fusion.3 = (bf16[1024,64]{0,1:T(8,128)(2,1)S(1)}, bf16[1024,64]{0,1:T(8,128)(2,1)S(1)}) fusion(bf16[1024,64]{0,1:T(8,128)(2,1)S(1)} %convolution_convert_fusion, pred[]{:T(512)S(6)} %eq.3, f32[64,480]{1,0:T(8,128)S(1)} %get-tuple-element.69, s32[64,3840]{1,0:T(8,128)} %param.16, s32[]{:T(128)S(6)} %select_n.113, f32[480]{0:T(512)S(1)} %bitcast.146, ...), kind=kOutput, calls=%fused_computation.58 | convolution fusion | flops 63571968 | bytes 1632133 | tf_op jit(solution)/shard_map/dot_general | solution.py:552
  95.8 1.1 reshape.157
  96.9 3.2 %all-to-all-start.2 = ((bf16[32,2,2048]{2,1,0:T(2,128)(2,1)}), bf16[32,2,2048]{2,1,0:T(2,128)(2,1)S(1)}, u32[]{:S(2)}, u32[]{:S(2)}) async-start(bf16[32,2,2048]{2,1,0:T(2,128)(2,1)} %reshape.157), calls=%async_computation.2 | async-start | bytes 524288 | tf_op jit(solution)/shard_map/all_to_all | solution.py:559
  101.7 8.7 %all-to-all-done.2 = bf16[32,2,2048]{2,1,0:T(2,128)(2,1)S(1)} async-done(((bf16[32,2,2048]{2,1,0:T(2,128)(2,1)}), bf16[32,2,2048]{2,1,0:T(2,128)(2,1)S(1)}, u32[]{:S(2)}, u32[]{:S(2)}) %all-to-all-start.2) | async-done | bytes 262176 | tf_op jit(solution)/shard_map/all_to_all | solution.py:559
  112.1 1.6 collective-permute-start.9
  113.8 15.5 %psum.7 = f32[]{:T(128)} all-reduce(f32[]{:T(128)} %subtract_reduce_fusion), channel_id=1, replica_groups=mesh['seq'=4,'chan'=8] {'chan'}, use_global_device_ids=true, to_apply=%region_5.6 | all-reduce | flops 1 | bytes 8 | tf_op jit(solution)/shard_map/psum | solution.py:546
  130.2 11.5 %long_correlation.1 = (bf16[4,64,2048]{2,1,0:T(8,128)(2,1)S(1)}, bf16[64,2048]{1,0:T(8,128)(2,1)}, bf16[64,2048]{1,0:T(8,128)(2,1)}, bf16[64,2048]{1,0:T(8,128)(2,1)}) fusion(bf16[4,64,2048]{2,1,0:T(8,128)(2,1)S(1)} %broadcast.36, s32[]{:T(128)S(6)} %select_n.104, s32[1]{0:T(128)} %bitcast.refs_0_, bf16[64,2048]{1,0:T(8,128)(2,1)S(1)} %get-tuple-element.56.refs_1_, ...), kind=kCustom, calls=%fused_computation.42 | custom fusion | flops 3758096384 | bytes 7045128 | tf_op jit(solution)/shard_map/long_correlation/pallas_call | solution.py:339
  141.7 4.0 %collective-permute-start.13 = (bf16[64,2048]{1,0:T(8,128)(2,1)}, bf16[64,2048]{1,0:T(8,128)(2,1)}, u32[]{:S(2)}, u32[]{:S(2)}) collective-permute-start(bf16[64,2048]{1,0:T(8,128)(2,1)} %get-tuple-element.27), channel_id=1, source_target_pairs={{0,8},{8,0},{16,24},{24,16},{1,9},{9,1},{17,25},{25,17},{2,10},{10... | collective-permute-start | bytes 786440 | tf_op jit(solution)/shard_map/ppermute | solution.py:465
  149.1 1.5 broadcast_in_dim.56
  150.6 1.9 %copy.68 = f32[1,256,2048]{2,1,0:T(8,128)S(1)} copy(f32[1,256,2048]{1,2,0:T(8,128)} %bitcast.124) | data formatting | bytes 4194304 | tf_op jit(solution)/shard_map/reshape | solution.py:575
  152.5 1.6 convert_multiply_fusion.3
  155.2 4.4 %collective-permute-done.15 = bf16[64,2048]{1,0:T(8,128)(2,1)} collective-permute-done((bf16[64,2048]{1,0:T(8,128)(2,1)}, bf16[64,2048]{1,0:T(8,128)(2,1)}, u32[]{:S(2)}, u32[]{:S(2)}) %collective-permute-start.15) | collective-permute-done | bytes 262176 | tf_op jit(solution)/shard_map/ppermute | solution.py:465
  161.2 3.1 %pad_maximum_fusion = f32[3,256,2048]{2,1,0:T(8,128)} fusion(f32[1,256,2048]{2,1,0:T(8,128)S(1)} %get-tuple-element.48, f32[1,256,2048]{2,1,0:T(8,128)S(1)} %get-tuple-element.47, f32[1,256,2048]{2,1,0:T(8,128)S(1)} %convert_multiply_fusion.3), kind=kLoop, calls=%fused_computation | loop fusion | flops 3145728 | bytes 12582912 | tf_op jit(solution)/shard_map/stack | solution.py:578
  (85 shorter events, 19.1 us)
Async XLA Ops:
  8.2 9.4 %copy-start.1 = (bf16[3,256,2048]{2,1,0:T(8,128)(2,1)S(1)}, bf16[3,256,2048]{2,1,0:T(8,128)(2,1)}, u32[]{:S(2)}) copy-start(bf16[3,256,2048]{2,1,0:T(8,128)(2,1)} %param.11) | copy-start | bytes 9437188
  8.2 56.9 %all-to-all-start.1 = ((bf16[8,128,480]{1,2,0:T(8,128)(2,1)}), bf16[8,128,480]{1,2,0:T(8,128)(2,1)}, u32[]{:S(2)}, u32[]{:S(2)}) async-start(bf16[8,128,480]{1,2,0:T(8,128)(2,1)} %bitcast.130), calls=%async_computation.1 | async-start | bytes 1966080 | tf_op jit(solution)/shard_map/all_to_all | solution.py:509
  17.6 1.2 copy-start.4
  20.2 2.6 %slice-start = ((bf16[3,256,2048]{2,1,0:T(8,128)(2,1)}), bf16[1,256,2048]{2,1,0:T(8,128)(2,1)S(1)}, s32[]{:S(2)}) async-start(bf16[3,256,2048]{2,1,0:T(8,128)(2,1)} %param.11), calls=%async_computation.3 | async-start | bytes 2097152 | tf_op jit(solution)/shard_map/slice | solution.py:497
  20.2 4.3 %collective-permute-start.3 = (bf16[2,64,2048]{2,1,0:T(8,128)(2,1)}, bf16[2,64,2048]{2,1,0:T(8,128)(2,1)}, u32[]{:S(2)}, u32[]{:S(2)}) collective-permute-start(bf16[2,64,2048]{2,1,0:T(8,128)(2,1)} %get-tuple-element.51), channel_id=1, source_target_pairs={{0,8},{8,0},{16,24},{24,16},{1,9},{9,1},{17,25},{25,17},{2,10},{10... | collective-permute-start | bytes 1572872 | tf_op jit(solution)/shard_map/ppermute | solution.py:465
  21.1 13.9 %collective-permute-start.4 = (bf16[2,64,2048]{2,1,0:T(8,128)(2,1)}, bf16[2,64,2048]{2,1,0:T(8,128)(2,1)}, u32[]{:S(2)}, u32[]{:S(2)}) collective-permute-start(bf16[2,64,2048]{2,1,0:T(8,128)(2,1)} %get-tuple-element.52), channel_id=1, source_target_pairs={{0,16},{8,24},{16,0},{24,8},{1,17},{9,25},{17,1},{25,9},{2,18},{10... | collective-permute-start | bytes 1572872 | tf_op jit(solution)/shard_map/ppermute | solution.py:465
  22.3 2.0 %copy-start.6 = (f32[256]{0:T(256)S(1)}, f32[256]{0:T(256)}, u32[]{:S(2)}) copy-start(f32[256]{0:T(256)} %param.13) | copy-start | bytes 3076
  22.3 24.4 %collective-permute-start.5 = (bf16[2,64,2048]{2,1,0:T(8,128)(2,1)}, bf16[2,64,2048]{2,1,0:T(8,128)(2,1)}, u32[]{:S(2)}, u32[]{:S(2)}) collective-permute-start(bf16[2,64,2048]{2,1,0:T(8,128)(2,1)} %get-tuple-element.49), channel_id=1, source_target_pairs={{0,24},{8,16},{16,8},{24,0},{1,25},{9,17},{17,9},{25,1},{2,26},{10... | collective-permute-start | bytes 1572872 | tf_op jit(solution)/shard_map/ppermute | solution.py:465
  22.8 24.1 %copy-start.5 = (bf16[2,64,2048]{2,1,0:T(8,128)(2,1)S(1)}, bf16[2,64,2048]{2,1,0:T(8,128)(2,1)}, u32[]{:S(2)}) copy-start(bf16[2,64,2048]{2,1,0:T(8,128)(2,1)} %get-tuple-element.50) | copy-start | bytes 1572868
  22.8 24.1 %copy-start.7 = (f32[2,64,128]{2,1,0:T(8,128)S(1)}, f32[2,64,128]{2,1,0:T(8,128)}, u32[]{:S(2)}) copy-start(f32[2,64,128]{2,1,0:T(8,128)} %constant.120.clone) | copy-start | bytes 196612
  22.9 39.6 %collective-permute-start = (bf16[64,2048]{1,0:T(8,128)(2,1)S(1)}, bf16[64,2048]{1,0:T(8,128)(2,1)S(1)}, u32[]{:S(2)}, u32[]{:S(2)}) collective-permute-start(bf16[64,2048]{1,0:T(8,128)(2,1)S(1)} %get-tuple-element.55), channel_id=1, source_target_pairs={{0,8},{8,0},{16,24},{24,16},{1,9},{9,1},{17,25},{25,17},{2,10},{10... | collective-permute-start | bytes 786440 | tf_op jit(solution)/shard_map/ppermute | solution.py:465
  23.2 39.3 %collective-permute-start.1 = (bf16[64,2048]{1,0:T(8,128)(2,1)S(1)}, bf16[64,2048]{1,0:T(8,128)(2,1)S(1)}, u32[]{:S(2)}, u32[]{:S(2)}) collective-permute-start(bf16[64,2048]{1,0:T(8,128)(2,1)S(1)} %get-tuple-element.54), channel_id=1, source_target_pairs={{0,16},{8,24},{16,0},{24,8},{1,17},{9,25},{17,1},{25,9},{2,18},{10... | collective-permute-start | bytes 786440 | tf_op jit(solution)/shard_map/ppermute | solution.py:465
  24.5 38.0 %collective-permute-start.2 = (bf16[64,2048]{1,0:T(8,128)(2,1)S(1)}, bf16[64,2048]{1,0:T(8,128)(2,1)S(1)}, u32[]{:S(2)}, u32[]{:S(2)}) collective-permute-start(bf16[64,2048]{1,0:T(8,128)(2,1)S(1)} %get-tuple-element.53), channel_id=1, source_target_pairs={{0,24},{8,16},{16,8},{24,0},{1,25},{9,17},{17,9},{25,1},{2,26},{10... | collective-permute-start | bytes 786440 | tf_op jit(solution)/shard_map/ppermute | solution.py:465
  46.9 15.7 %copy-start = (bf16[256,128]{1,0:T(8,128)(2,1)S(1)}, bf16[256,128]{1,0:T(8,128)(2,1)}, u32[]{:S(2)}) copy-start(bf16[256,128]{1,0:T(8,128)(2,1)} %constant.121.clone.refs_6_) | copy-start | bytes 196612
  62.5 11.9 %collective-permute-start.10 = (bf16[64,2048]{1,0:T(8,128)(2,1)}, bf16[64,2048]{1,0:T(8,128)(2,1)}, u32[]{:S(2)}, u32[]{:S(2)}) collective-permute-start(bf16[64,2048]{1,0:T(8,128)(2,1)} %get-tuple-element.37), channel_id=1, source_target_pairs={{0,8},{8,0},{16,24},{24,16},{1,9},{9,1},{17,25},{25,17},{2,10},{10... | collective-permute-start | bytes 786440 | tf_op jit(solution)/shard_map/ppermute | solution.py:465
  65.2 16.5 %all-to-all-start = ((bf16[32,2,2048]{2,1,0:T(2,128)(2,1)}), bf16[32,2,2048]{2,1,0:T(2,128)(2,1)S(1)}, u32[]{:S(2)}, u32[]{:S(2)}) async-start(bf16[32,2,2048]{2,1,0:T(2,128)(2,1)} %reshape.155), calls=%async_computation | async-start | bytes 524288 | tf_op jit(solution)/shard_map/all_to_all | solution.py:520
  71.4 12.3 %collective-permute-start.6 = (bf16[8,128,480]{1,2,0:T(8,128)(2,1)}, bf16[8,128,480]{1,2,0:T(8,128)(2,1)}, u32[]{:S(2)}, u32[]{:S(2)}) collective-permute-start(bf16[8,128,480]{1,2,0:T(8,128)(2,1)} %all-to-all-done.1), channel_id=1, source_target_pairs={{0,8},{8,0},{16,24},{24,16},{1,9},{9,1},{17,25},{25,17},{2,10},{10... | collective-permute-start | bytes 2949128 | tf_op jit(solution)/shard_map/ppermute | solution.py:465
  72.5 27.6 %collective-permute-start.11 = (bf16[64,2048]{1,0:T(8,128)(2,1)}, bf16[64,2048]{1,0:T(8,128)(2,1)}, u32[]{:S(2)}, u32[]{:S(2)}) collective-permute-start(bf16[64,2048]{1,0:T(8,128)(2,1)} %get-tuple-element.39), channel_id=1, source_target_pairs={{0,16},{8,24},{16,0},{24,8},{1,17},{9,25},{17,1},{25,9},{2,18},{10... | collective-permute-start | bytes 786440 | tf_op jit(solution)/shard_map/ppermute | solution.py:465
  74.0 39.7 %collective-permute-start.12 = (bf16[64,2048]{1,0:T(8,128)(2,1)}, bf16[64,2048]{1,0:T(8,128)(2,1)S(1)}, u32[]{:S(2)}, u32[]{:S(2)}) collective-permute-start(bf16[64,2048]{1,0:T(8,128)(2,1)} %get-tuple-element.41), channel_id=1, source_target_pairs={{0,24},{8,16},{16,8},{24,0},{1,25},{9,17},{17,9},{25,1},{2,26},{10... | collective-permute-start | bytes 786440 | tf_op jit(solution)/shard_map/ppermute | solution.py:465
  96.9 13.5 %all-to-all-start.2 = ((bf16[32,2,2048]{2,1,0:T(2,128)(2,1)}), bf16[32,2,2048]{2,1,0:T(2,128)(2,1)S(1)}, u32[]{:S(2)}, u32[]{:S(2)}) async-start(bf16[32,2,2048]{2,1,0:T(2,128)(2,1)} %reshape.157), calls=%async_computation.2 | async-start | bytes 524288 | tf_op jit(solution)/shard_map/all_to_all | solution.py:559
  111.5 35.1 %collective-permute-start.7 = (f32[64,64]{0,1:T(8,128)}, f32[64,64]{0,1:T(8,128)}, u32[]{:S(2)}, u32[]{:S(2)}) collective-permute-start(f32[64,64]{0,1:T(8,128)} %get-tuple-element.63), channel_id=1, source_target_pairs={{0,8},{8,0},{16,24},{24,16},{1,9},{9,1},{17,25},{25,17},{2,10},{10... | collective-permute-start | bytes 49160 | tf_op jit(solution)/shard_map/ppermute | solution.py:465
  112.1 36.4 %collective-permute-start.8 = (f32[64,64]{0,1:T(8,128)}, f32[64,64]{0,1:T(8,128)S(1)}, u32[]{:S(2)}, u32[]{:S(2)}) collective-permute-start(f32[64,64]{0,1:T(8,128)} %get-tuple-element.62), channel_id=1, source_target_pairs={{0,16},{8,24},{16,0},{24,8},{1,17},{9,25},{17,1},{25,9},{2,18},{10... | collective-permute-start | bytes 49160 | tf_op jit(solution)/shard_map/ppermute | solution.py:465
  112.1 36.6 %collective-permute-start.9 = (f32[64,64]{0,1:T(8,128)}, f32[64,64]{0,1:T(8,128)S(1)}, u32[]{:S(2)}, u32[]{:S(2)}) collective-permute-start(f32[64,64]{0,1:T(8,128)} %get-tuple-element.61), channel_id=1, source_target_pairs={{0,24},{8,16},{16,8},{24,0},{1,25},{9,17},{17,9},{25,1},{2,26},{10... | collective-permute-start | bytes 49160 | tf_op jit(solution)/shard_map/ppermute | solution.py:465
  113.8 16.3 %copy-start.3 = (bf16[4,64,2048]{2,1,0:T(8,128)(2,1)}, bf16[4,64,2048]{2,1,0:T(8,128)(2,1)S(1)}, u32[]{:S(2)}) copy-start(bf16[4,64,2048]{2,1,0:T(8,128)(2,1)S(1)} %bitcast_dynamic-update-slice_fusion.4) | copy-start | bytes 3145732
  141.7 12.5 %collective-permute-start.13 = (bf16[64,2048]{1,0:T(8,128)(2,1)}, bf16[64,2048]{1,0:T(8,128)(2,1)}, u32[]{:S(2)}, u32[]{:S(2)}) collective-permute-start(bf16[64,2048]{1,0:T(8,128)(2,1)} %get-tuple-element.27), channel_id=1, source_target_pairs={{0,8},{8,0},{16,24},{24,16},{1,9},{9,1},{17,25},{25,17},{2,10},{10... | collective-permute-start | bytes 786440 | tf_op jit(solution)/shard_map/ppermute | solution.py:465
  145.6 9.5 %collective-permute-start.14 = (bf16[64,2048]{1,0:T(8,128)(2,1)}, bf16[64,2048]{1,0:T(8,128)(2,1)S(1)}, u32[]{:S(2)}, u32[]{:S(2)}) collective-permute-start(bf16[64,2048]{1,0:T(8,128)(2,1)} %get-tuple-element.29), channel_id=1, source_target_pairs={{0,16},{8,24},{16,0},{24,8},{1,17},{9,25},{17,1},{25,9},{2,18},{10... | collective-permute-start | bytes 786440 | tf_op jit(solution)/shard_map/ppermute | solution.py:465
  146.7 13.0 %collective-permute-start.15 = (bf16[64,2048]{1,0:T(8,128)(2,1)}, bf16[64,2048]{1,0:T(8,128)(2,1)}, u32[]{:S(2)}, u32[]{:S(2)}) collective-permute-start(bf16[64,2048]{1,0:T(8,128)(2,1)} %get-tuple-element.31), channel_id=1, source_target_pairs={{0,24},{8,16},{16,8},{24,0},{1,25},{9,17},{17,9},{25,1},{2,26},{10... | collective-permute-start | bytes 786440 | tf_op jit(solution)/shard_map/ppermute | solution.py:465
  152.5 8.1 %copy-start.2 = (bf16[3,256,2048]{2,1,0:T(8,128)(2,1)S(1)}, bf16[3,256,2048]{2,1,0:T(8,128)(2,1)}, u32[]{:S(2)}) copy-start(bf16[3,256,2048]{2,1,0:T(8,128)(2,1)} %param.11) | copy-start | bytes 9437188

commit v2 on v1

--- a/solution.py
+++ b/solution.py
@@ -18,6 +18,8 @@
 rate_floor = 0.5
 
 VMEM_LIMIT = 48 * 1024 * 1024
+CHUNKS = 2
+MOST_GROUPS = 16
 
 
 def split_bf16(table):
@@ -196,13 +198,10 @@
 def conv_kernel(peers, outer, me_ref, *refs):
     pieces = refs[:peers]
     skip_ref, fwd_ref, bwd_ref, twist_ref = refs[peers : peers + 4]
-    outs = refs[peers + 4 : 2 * peers + 4]
-    mixed_ref, spec_ref = refs[2 * peers + 4 : 2 * peers + 6]
-    rows_in, parts_x, parts_h, parts_y, lhs, rows_out = refs[2 * peers + 6 :]
+    mixed_ref, spec_ref, rows_in, parts_x, parts_h, parts_y, lhs = refs[-7:]
     me = me_ref[0]
     ra, rb = radices(outer)
     per = outer // peers
-    width = per * LANES
     for k in range(peers):
         rows_in[me ^ k] = pieces[k][...]
 
@@ -230,41 +229,59 @@
     skip = jnp.broadcast_to(skip_ref[...], (ROWS, LANES))
 
     def emit(n1, value):
-        mixed = value + skip * load_x(n1)
-        lanes = slice((n1 % per) * LANES, (n1 % per + 1) * LANES)
-        mixed_ref[:, n1 * LANES : (n1 + 1) * LANES] = mixed
-        rows_out[n1 // per, :, lanes] = mixed.astype(jnp.bfloat16)
+        mixed_ref[:, n1 * LANES : (n1 + 1) * LANES] = value + skip * load_x(n1)
 
     back_first_pass(parts_y, outer, emit)
-    for k in range(peers):
-        outs[k][...] = rows_out[me ^ k]
-
-
-def pool_kernel(peers, outer, me_ref, *refs):
-    queries = refs[:peers]
-    mixed_ref, gather_ref, pooled_ref, rows_in, lhs = refs[peers:]
-    me = me_ref[0]
-    per = outer // peers
-    for k in range(peers):
-        rows_in[me ^ k] = queries[k][...]
+
+
+def pool_rows(rows_in, mixed_ref, rows_out, row, gather_ref, lhs, per, outer):
     for n1 in range(outer):
         lanes = slice((n1 % per) * LANES, (n1 % per + 1) * LANES)
-        query = rows_in[n1 // per, :, lanes].astype(jnp.float32)
-        high, low = split(query * mixed_ref[:, n1 * LANES : (n1 + 1) * LANES])
+        query = rows_in[n1 // per, row : row + ROWS, lanes].astype(jnp.float32)
+        mixed = mixed_ref[row : row + ROWS, n1 * LANES : (n1 + 1) * LANES]
+        rows_out[n1 // per, row : row + ROWS, lanes] = mixed.astype(jnp.bfloat16)
+        high, low = split(query * mixed)
         lhs[n1 * ROWS : (n1 + 1) * ROWS, :LANES] = high
         lhs[n1 * ROWS : (n1 + 1) * ROWS, LANES:] = low
     sums = dot(lhs[...], gather_ref[...])
     each = LANES // POOL
     held = LANES // each
     place = lax.broadcasted_iota(jnp.int32, (ROWS, LANES), 1) // each
+    tiles = []
     for tile in range(-(-outer // held)):
         total = jnp.zeros((ROWS, LANES), jnp.float32)
-        count = min(held, outer - tile * held)
-        for j in range(count):
+        for j in range(min(held, outer - tile * held)):
             n1 = tile * held + j
             total = jnp.where(place == j, sums[n1 * ROWS : (n1 + 1) * ROWS], total)
-        used = count * each
-        pooled_ref[:, tile * LANES : tile * LANES + used] = total[:, :used].astype(jnp.bfloat16)
+        tiles.append(total)
+    return jnp.concatenate(tiles, axis=1)
+
+
+def pool_kernel(peers, outer, me_ref, *refs):
+    queries = refs[:peers]
+    mixed_ref, gather_ref = refs[peers : peers + 2]
+    outs = refs[peers + 2 : 2 * peers + 2]
+    pooled_ref, rows_in, rows_out, lhs = refs[2 * peers + 2 :]
+    me = me_ref[0]
+    per = outer // peers
+    for k in range(peers):
+        rows_in[me ^ k] = queries[k][...]
+    rows = mixed_ref.shape[0]
+    bins = outer * LANES // POOL
+    if rows == ROWS:
+        pooled = pool_rows(rows_in, mixed_ref, rows_out, 0, gather_ref, lhs.at[0], per, outer)
+        pooled_ref[...] = pooled[:, :bins].astype(jnp.bfloat16)
+    else:
+        left = pool_rows(rows_in, mixed_ref, rows_out, 0, gather_ref, lhs.at[0], per, outer)
+        right = pool_rows(rows_in, mixed_ref, rows_out, ROWS, gather_ref, lhs.at[1], per, outer)
+        each = bins // peers
+        for seat in range(peers):
+            mine = slice(seat * each, (seat + 1) * each)
+            pair = jnp.concatenate([left[:, mine], right[:, mine]], axis=1).astype(jnp.bfloat16)
+            for group in range(pooled_ref.shape[0]):
+                pooled_ref[group, seat] = pair
+    for k in range(peers):
+        outs[k][...] = rows_out[me ^ k]
 
 
 def corr_kernel(peers, outer, me_ref, *refs):
@@ -329,11 +346,11 @@
     return pl.BlockSpec(array.shape, lambda i, me: (0,) * rank)
 
 
-def by_rows(width):
-    return pl.BlockSpec((ROWS, width), lambda i, me: (i, 0))
-
-
-def call(kernel, name, me, steps, inputs, in_specs, out_shapes, out_specs, scratch, flops):
+def by_rows(width, rows=ROWS, start=0):
+    return pl.BlockSpec((rows, width), lambda i, me: (start + i, 0))
+
+
+def call(kernel, name, me, steps, inputs, in_specs, out_shapes, out_specs, scratch, flops, aliases=None):
     moved = sum(x.size * x.dtype.itemsize for x in inputs)
     moved += sum(math.prod(o.shape) * o.dtype.itemsize for o in out_shapes)
     return pl.pallas_call(
@@ -347,6 +364,7 @@
             scratch_shapes=scratch,
         ),
         out_shape=out_shapes,
+        input_output_aliases=aliases or {},
         compiler_params=pltpu.CompilerParams(
             dimension_semantics=("arbitrary",), vmem_limit_bytes=VMEM_LIMIT
         ),
@@ -354,7 +372,11 @@
     )(me, *inputs)
 
 
-def convolve(me, pieces, skip, tables):
+def shape(dims, dtype):
+    return jax.ShapeDtypeStruct(dims, dtype)
+
+
+def convolve(me, pieces, skip, tables, total_rows, start, before):
     peers = len(pieces)
     rows, width = pieces[0].shape[1:]
     length = width * peers
@@ -362,76 +384,91 @@
     ra, rb = radices(outer)
     chunk = rb * ROWS
     steps = rows // ROWS
+    first = start // ROWS
     f32, bf16 = jnp.float32, jnp.bfloat16
     fwd, bwd, twist = tables["fwd"], tables["bwd"], tables["twist"]
-    out_shapes = [jax.ShapeDtypeStruct((rows, width), bf16)] * peers + [
-        jax.ShapeDtypeStruct((rows, length), f32),
-        jax.ShapeDtypeStruct((steps, outer * ROWS, 2 * LANES), f32),
-    ]
-    out_specs = [by_rows(width)] * peers + [
-        by_rows(length),
-        pl.BlockSpec((1, outer * ROWS, 2 * LANES), lambda i, me: (i, 0, 0)),
-    ]
+    inputs = [*pieces, skip, fwd, bwd, twist]
     in_specs = [pl.BlockSpec((2, ROWS, width), lambda i, me: (0, i, 0))] * peers + [
-        pl.BlockSpec((ROWS, 1), lambda i, me: (i, 0)),
+        by_rows(1, start=first),
         whole(fwd),
         whole(bwd),
         whole(twist),
     ]
+    aliases = {}
+    if before is not None:
+        aliases = {1 + len(inputs): 0}
+        inputs.append(before)
+        in_specs.append(pl.BlockSpec(memory_space=pl.ANY))
     parts = pltpu.VMEM((2, rb, ra, ROWS, LANES), f32)
-    scratch = [
-        pltpu.VMEM((peers, 2, ROWS, width), bf16),
-        parts,
-        parts,
-        parts,
-        pltpu.VMEM((3 * ra, 2, chunk, 2 * LANES), bf16),
-        pltpu.VMEM((peers, ROWS, width), bf16),
-    ]
 
     def kernel(*refs):
         conv_kernel(peers, outer, *refs)
 
-    out = call(
-        kernel, "long_convolution", me, steps, [*pieces, skip, fwd, bwd, twist], in_specs, out_shapes, out_specs,
-        scratch, 2 * 9 * rows * outer * (2 * LANES) ** 2,
-    )
-    return out[:peers], out[peers], out[peers + 1]
-
-
-def pool(me, queries, mixed, gather):
+    return call(
+        kernel, "long_convolution", me, steps, inputs, in_specs,
+        [shape((total_rows, length), f32), shape((steps, outer * ROWS, 2 * LANES), f32)],
+        [by_rows(length, start=first), pl.BlockSpec((1, outer * ROWS, 2 * LANES), lambda i, me: (i, 0, 0))],
+        [
+            pltpu.VMEM((peers, 2, ROWS, width), bf16),
+            parts,
+            parts,
+            parts,
+            pltpu.VMEM((3 * ra, 2, chunk, 2 * LANES), bf16),
+        ],
+        2 * 9 * rows * outer * (2 * LANES) ** 2, aliases,
+    )
+
+
+def pool(me, queries, mixed, gather, groups):
     peers = len(queries)
     rows, width = queries[0].shape
     length = width * peers
     outer = length // LANES
     bins = length // POOL
     bf16 = jnp.bfloat16
+    if groups:
+        step = 2 * ROWS
+        pooled_shape = shape((groups, peers, rows // 2, LANES), bf16)
+        pooled_spec = pl.BlockSpec((groups, peers, ROWS, LANES), lambda i, me: (0, 0, i, 0))
+    else:
+        step = ROWS
+        pooled_shape = shape((rows, bins), bf16)
+        pooled_spec = by_rows(bins)
 
     def kernel(*refs):
         pool_kernel(peers, outer, *refs)
 
-    return call(
-        kernel, "pool_bins", me, rows // ROWS, [*queries, mixed, gather],
-        [by_rows(width)] * peers + [by_rows(length), whole(gather)],
-        [jax.ShapeDtypeStruct((rows, bins), bf16)], [by_rows(bins)],
-        [pltpu.VMEM((peers, ROWS, width), bf16), pltpu.VMEM((outer * ROWS, 2 * LANES), bf16)],
+    out = call(
+        kernel, "pool_bins", me, rows // step, [*queries, mixed, gather],
+        [by_rows(width, step)] * peers + [by_rows(length, step), whole(gather)],
+        [shape((rows, width), bf16)] * peers + [pooled_shape],
+        [by_rows(width, step)] * peers + [pooled_spec],
+        [
+            pltpu.VMEM((peers, step, width), bf16),
+            pltpu.VMEM((peers, step, width), bf16),
+            pltpu.VMEM((step // ROWS, outer * ROWS, 2 * LANES), bf16),
+        ],
         2 * rows * outer * 2 * LANES * LANES,
-    )[0]
-
-
-def correlate(me, queries, grad_pooled, spec, skip, tables, spread):
+    )
+    return out[:peers], out[peers]
+
+
+def correlate(me, queries, grad_pooled, spec, skip, tables, spread, start):
     peers = len(queries)
-    rows, width = queries[0].shape
+    width = queries[0].shape[1]
+    rows = spec.shape[0] * ROWS
     length = width * peers
     outer = length // LANES
     bins = length // POOL
     ra, rb = radices(outer)
     chunk = rb * ROWS
+    first = start // ROWS
     f32, bf16 = jnp.float32, jnp.bfloat16
     fwd, bwd, twist = tables["fwd"], tables["bwd"], tables["twist"]
-    in_specs = [by_rows(width)] * peers + [
-        by_rows(bins),
+    in_specs = [by_rows(width, start=first)] * peers + [
+        by_rows(bins, start=first),
         pl.BlockSpec((1, outer * ROWS, 2 * LANES), lambda i, me: (i, 0, 0)),
-        pl.BlockSpec((ROWS, 1), lambda i, me: (i, 0)),
+        by_rows(1, start=first),
         whole(fwd),
         whole(bwd),
         whole(twist),
@@ -454,9 +491,231 @@
     return call(
         kernel, "long_correlation", me, rows // ROWS,
         [*queries, grad_pooled, spec, skip, fwd, bwd, twist, spread], in_specs,
-        [jax.ShapeDtypeStruct((rows, width), bf16)] * peers, [by_rows(width)] * peers,
+        [shape((rows, width), bf16)] * peers, [by_rows(width)] * peers,
         scratch, 2 * 7 * rows * outer * (2 * LANES) ** 2,
     )
+
+
+def lay_out(me, projections, filter_taps, peers, chunks):
+    _, channels, width = projections.shape
+    pencil = channels // peers
+    rows = pencil // chunks
+    bf16 = jnp.bfloat16
+
+    def kernel(me_ref, keyed_ref, valued_ref, taps_ref, *outs):
+        for k in range(peers):
+
+            @pl.when(pl.program_id(0) == k)
+            def _():
+                for j in range(chunks):
+                    part = slice(j * rows, (j + 1) * rows)
+                    keyed = keyed_ref[0, part, :].astype(jnp.float32)
+                    valued = valued_ref[0, part, :].astype(jnp.float32)
+                    outs[j * peers + k][0] = (keyed * valued).astype(bf16)
+                    outs[j * peers + k][1] = taps_ref[part, :].astype(bf16)
+
+    piece = shape((2, rows, width), bf16)
+    out = call(
+        kernel, "lay_out", me, peers, [projections, projections, filter_taps],
+        [
+            pl.BlockSpec((1, pencil, width), lambda i, me: (1, me[0] ^ i, 0)),
+            pl.BlockSpec((1, pencil, width), lambda i, me: (2, me[0] ^ i, 0)),
+            pl.BlockSpec((pencil, width), lambda i, me: (me[0] ^ i, 0)),
+        ],
+        [piece] * (peers * chunks),
+        [pl.BlockSpec(piece.shape, lambda i, me: (0, 0, 0))] * (peers * chunks),
+        [], channels * width,
+    )
+    return [out[j * peers : (j + 1) * peers] for j in range(chunks)]
+
+
+def by_track(me, head_weight, groups):
+    channels, tracks = head_weight.shape
+    half, own = channels // 2, tracks // groups
+
+    def kernel(me_ref, weight_ref, out_ref):
+        for group in range(groups):
+            out_ref[group] = weight_ref[:, group * own : (group + 1) * own]
+
+    out = shape((groups, half, own), head_weight.dtype)
+    return call(
+        kernel, "by_track", me, 1, [head_weight],
+        [pl.BlockSpec((half, tracks), lambda i, me: (me[0] & 1, 0))],
+        [out], [pl.BlockSpec(out.shape, lambda i, me: (0, 0, 0))], [], half * tracks,
+    )[0]
+
+
+def weight_pair(weight_ref, seats, pencil):
+    groups, _, own = weight_ref.shape
+    rows = weight_ref[...].reshape(groups, seats, pencil // (2 * ROWS), 2, ROWS, own)
+    count = groups * seats * pencil // 2
+    return rows[:, :, :, 0].reshape(count, own), rows[:, :, :, 1].reshape(count, own)
+
+
+def head_rates(me, got, mine, other, bias, counts):
+    groups, peers, half_rows, _ = got.shape
+    own = mine.shape[2]
+    seats = peers // 2
+    pencil = 2 * half_rows
+    bins = LANES // 2
+    f32 = jnp.float32
+
+    def kernel(me_ref, got_ref, mine_ref, other_ref, bias_ref, counts_ref, logits_ref, sums_ref):
+        odd = me_ref[0] & 1
+        total = jnp.broadcast_to(bias_ref[...], (bins, own))
+        for weight_ref, place in ((mine_ref, odd), (other_ref, 1 - odd)):
+            block = got_ref[:, pl.ds(place * seats, seats)].reshape(groups * seats * half_rows, LANES)
+            turned = block.astype(f32).T.astype(jnp.bfloat16)
+            left, right = weight_pair(weight_ref, seats, pencil)
+            total = total + dot(turned[:bins], left) + dot(turned[bins:], right)
+        logits_ref[...] = total
+        rates = jax.nn.softplus(total) + rate_floor
+        observed = counts_ref[...].astype(f32)
+        sums_ref[0:1, :] = jnp.sum(rates, axis=0, keepdims=True)
+        sums_ref[1:2, :] = jnp.sum(observed, axis=0, keepdims=True)
+        sums_ref[2:3, :] = jnp.sum(observed * jnp.log(rates), axis=0, keepdims=True)
+        sums_ref[3:8, :] = jnp.zeros((5, own), f32)
+
+    inputs = [got, mine, other, bias, counts]
+    return call(
+        kernel, "head_rates", me, 1, inputs, [whole(x) for x in inputs],
+        [shape((bins, own), f32), shape((8, own), f32)],
+        [pl.BlockSpec((bins, own), lambda i, me: (0, 0)), pl.BlockSpec((8, own), lambda i, me: (0, 0))],
+        [], 2 * bins * groups * peers * pencil * own,
+    )
+
+
+def head_grads(me, logits, sums, mine, other, counts, peers):
+    groups, half, own = mine.shape
+    seats = peers // 2
+    pencil = half // seats
+    bins = LANES // 2
+    f32, bf16 = jnp.float32, jnp.bfloat16
+
+    def kernel(me_ref, logits_ref, sums_ref, mine_ref, other_ref, counts_ref, out_ref, loss_ref):
+        odd = me_ref[0] & 1
+        totals = sums_ref[0]
+        for seat in range(1, peers):
+            totals = totals + sums_ref[seat]
+        pred_total, obs_total, log_sum = totals[0:1], totals[1:2], totals[2:3]
+        log_pred = jnp.log(pred_total)
+        terms = total_weight * (pred_total - obs_total * log_pred) + obs_total * log_pred - log_sum
+        loss_ref[...] = jnp.broadcast_to(jnp.sum(terms, axis=1, keepdims=True), loss_ref.shape)
+        ratio = obs_total / pred_total
+        logits_here = logits_ref[...]
+        rates = jax.nn.softplus(logits_here) + rate_floor
+        observed = counts_ref[...].astype(f32)
+        grad_rates = total_weight * (1.0 - ratio) + ratio - observed / rates
+        grads = (grad_rates * jax.nn.sigmoid(logits_here)).astype(bf16)
+        none = jnp.zeros_like(grads)
+        in_left = jnp.concatenate([grads, none], axis=0)
+        in_right = jnp.concatenate([none, grads], axis=0)
+        across = (((1,), (1,)), ((), ()))
+        for weight_ref, place in ((mine_ref, odd), (other_ref, 1 - odd)):
+            left, right = weight_pair(weight_ref, seats, pencil)
+            part = lax.dot_general(left, in_left, across, preferred_element_type=f32)
+            part = part + lax.dot_general(right, in_right, across, preferred_element_type=f32)
+            out_ref[:, pl.ds(place * seats, seats)] = part.astype(bf16).reshape(groups, seats, pencil // 2, LANES)
+
+    inputs = [logits, sums, mine, other, counts]
+    out = shape((groups, peers, pencil // 2, LANES), bf16)
+    return call(
+        kernel, "head_grads", me, 1, inputs, [whole(x) for x in inputs],
+        [out, shape((8, LANES), f32)],
+        [pl.BlockSpec(out.shape, lambda i, me: (0, 0, 0, 0)), pl.BlockSpec((8, LANES), lambda i, me: (0, 0))],
+        [], 4 * bins * groups * peers * pencil * own,
+    )
+
+
+def sum_grads(me, back):
+    groups, peers, half_rows, _ = back.shape
+    bins = LANES // 2
+    f32 = jnp.float32
+
+    def kernel(me_ref, back_ref, rows_ref, *refs):
+        outs, total_ref = refs[:peers], refs[peers]
+        for seat in range(peers):
+            total = back_ref[0, seat].astype(f32)
+            for group in range(1, groups):
+                total = total + back_ref[group, seat].astype(f32)
+            total_ref[seat] = total
+            for i in range(half_rows // ROWS):
+                pair = total[i * ROWS : (i + 1) * ROWS]
+                lanes = slice(seat * bins, (seat + 1) * bins)
+                rows_ref[2 * i * ROWS : (2 * i + 1) * ROWS, lanes] = pair[:, :bins]
+                rows_ref[(2 * i + 1) * ROWS : (2 * i + 2) * ROWS, lanes] = pair[:, bins:]
+        for k in range(peers):
+            outs[k][...] = total_ref[me_ref[0] ^ k]
+
+    packed = shape((half_rows, LANES), f32)
+    out = call(
+        kernel, "sum_grads", me, 1, [back], [whole(back)],
+        [shape((2 * half_rows, peers * bins), f32)] + [packed] * peers,
+        [pl.BlockSpec((2 * half_rows, peers * bins), lambda i, me: (0, 0))]
+        + [pl.BlockSpec(packed.shape, lambda i, me: (0, 0))] * peers,
+        [pltpu.VMEM((peers, half_rows, LANES), f32)], back.size,
+    )
+    return out[0], out[1:]
+
+
+def finish(me, projections, mixed_home, grad_home, corr_home, spread, chunk, chunks, before):
+    peers = len(mixed_home)
+    _, channels, width = projections.shape
+    pencil = channels // peers
+    rows = pencil // chunks
+    bins = width // POOL
+    tiles = width // LANES
+    each = LANES // POOL
+    f32, bf16 = jnp.float32, jnp.bfloat16
+
+    def kernel(me_ref, keyed_ref, valued_ref, spread_ref, *refs):
+        mixed_refs, grad_refs, corr_refs = refs[:peers], refs[peers : 2 * peers], refs[2 * peers : 3 * peers]
+        out_ref, lhs = refs[-2:]
+        place = lax.broadcasted_iota(jnp.int32, (ROWS, LANES), 1) // each
+        zero = jnp.zeros((ROWS, LANES), f32)
+        for k in range(peers):
+
+            @pl.when(pl.program_id(0) == k)
+            def _():
+                for i in range(rows // ROWS):
+                    part = slice(i * ROWS, (i + 1) * ROWS)
+                    source = (chunk * rows + i * ROWS) // (2 * ROWS) * ROWS
+                    side = (chunk * rows // ROWS + i) % 2
+                    pair = grad_refs[k][source : source + ROWS, :]
+                    high = pair.astype(bf16).astype(f32)
+                    low = pair - high
+                    for t in range(tiles):
+                        here = place == t + side * tiles
+                        lhs[t * ROWS : (t + 1) * ROWS, :LANES] = jnp.where(here, high, zero).astype(bf16)
+                        lhs[t * ROWS : (t + 1) * ROWS, LANES:] = jnp.where(here, low, zero).astype(bf16)
+                    grad = dot(lhs[...], spread_ref[...])
+                    for t in range(tiles):
+                        lanes = slice(t * LANES, (t + 1) * LANES)
+                        mixed = mixed_refs[k][part, lanes].astype(f32)
+                        out_ref[0, part, lanes] = grad[t * ROWS : (t + 1) * ROWS] * mixed
+                    corr = corr_refs[k][part, :].astype(f32)
+                    out_ref[1, part, :] = corr * valued_ref[0, part, :].astype(f32)
+                    out_ref[2, part, :] = corr * keyed_ref[0, part, :].astype(f32)
+
+    inputs = [projections, projections, spread, *mixed_home, *grad_home, *corr_home]
+    in_specs = [
+        pl.BlockSpec((1, rows, width), lambda i, me: (1, (me[0] ^ i) * chunks + chunk, 0)),
+        pl.BlockSpec((1, rows, width), lambda i, me: (2, (me[0] ^ i) * chunks + chunk, 0)),
+        whole(spread),
+    ]
+    in_specs += [pl.BlockSpec((rows, width), lambda i, me: (chunk, 0))] * peers
+    in_specs += [whole(x) for x in [*grad_home, *corr_home]]
+    aliases = {}
+    if before is not None:
+        aliases = {1 + len(inputs): 0}
+        inputs.append(before)
+        in_specs.append(pl.BlockSpec(memory_space=pl.ANY))
+    return call(
+        kernel, "finish", me, peers, inputs, in_specs,
+        [shape((3, channels, width), f32)],
+        [pl.BlockSpec((3, rows, width), lambda i, me: (0, (me[0] ^ i) * chunks + chunk, 0))],
+        [pltpu.VMEM((tiles * ROWS, 2 * LANES), bf16)], 4 * channels * width, aliases,
+    )[0]
 
 
 def swap(value, k, count):
@@ -474,7 +733,98 @@
     return jnp.pad(value, widths)
 
 
+def aligned(projections, filter_taps, skip_gain, head_weight, head_bias, counts):
+    f32 = jnp.float32
+    _, channels, width = projections.shape
+    peers = lax.axis_size("seq")
+    groups = lax.axis_size("chan")
+    seat = lax.axis_index("seq")
+    group = lax.axis_index("chan")
+    bins = width // POOL
+    length = width * peers
+    tracks = head_weight.shape[1]
+    own_tracks = tracks // groups
+    pencil = channels // peers
+    chunks = CHUNKS
+    rows = pencil // chunks
+    me = jnp.asarray(seat, jnp.int32).reshape(1)
+    tables = transform_tables(length)
+    gather, spread = pool_tables()
+
+    laid = lay_out(me, projections, filter_taps, peers, chunks)
+    pieces = [[swap(laid[j][k], k, peers) for k in range(peers)] for j in range(chunks)]
+    skip = lax.dynamic_index_in_dim(skip_gain.reshape(peers, pencil, 1), seat, axis=0, keepdims=False)
+
+    me_late, _ = lax.optimization_barrier((me, laid[chunks - 1][0]))
+    mine = by_track(me_late, head_weight, groups)
+    mine = lax.all_to_all(mine, "chan", split_axis=0, concat_axis=0, tiled=True)
+    other = swap(mine, 1, peers)
+
+    mixed, specs = None, []
+    for j in range(chunks):
+        mixed, spec = convolve(me, pieces[j], skip, tables, pencil, j * rows, mixed)
+        specs.append(spec)
+        if j == 0:
+            seat_late, _ = lax.optimization_barrier((seat, spec))
+            query_blocks = projections[0].reshape(peers, pencil, width)
+            queries = [
+                swap(lax.dynamic_index_in_dim(query_blocks, seat_late ^ k, axis=0, keepdims=False), k, peers)
+                for k in range(peers)
+            ]
+    mixed_out, sent = pool(me, queries, mixed, gather, groups)
+    mixed_home = [swap(mixed_out[k], k, peers) for k in range(peers)]
+
+    def exchange(blocks):
+        flat = blocks.reshape(groups * peers, pencil // 2, LANES)
+        flat = lax.all_to_all(flat, ("chan", "seq"), split_axis=0, concat_axis=0, tiled=True)
+        return flat.reshape(blocks.shape)
+
+    got = exchange(sent)
+    own_bias = lax.dynamic_slice_in_dim(head_bias, group * own_tracks, own_tracks).reshape(1, own_tracks)
+    own_counts = lax.dynamic_slice_in_dim(counts, group * own_tracks, own_tracks, axis=1)
+    logits, sums = head_rates(me, got, mine, other, own_bias, own_counts)
+    all_sums = lax.all_gather(sums, "seq")
+    part, loss = head_grads(me, logits, all_sums, mine, other, own_counts, peers)
+    back = exchange(part)
+    step = 1
+    while step < groups:
+        loss = loss + lax.ppermute(loss, "chan", [(i, i ^ step) for i in range(groups)])
+        step *= 2
+    mean_loss = loss[0, 0] / (bins * peers * tracks)
+
+    grad_rows, grad_out = sum_grads(me, back)
+    grad_home = [swap(grad_out[k], k, peers) for k in range(peers)]
+    grads = None
+    corr_home = []
+    for j in range(chunks):
+        corr = correlate(me, queries, grad_rows, specs[j], skip, tables, spread, j * rows)
+        corr_home.append([swap(corr[k], k, peers) for k in range(peers)])
+    for j in range(chunks):
+        grads = finish(me, projections, mixed_home, grad_home, corr_home[j], spread, j, chunks, grads)
+    return mean_loss, grads
+
+
+def power_of_two(value):
+    return value & (value - 1) == 0
+
+
 def per_device(projections, filter_taps, skip_gain, head_weight, head_bias, counts):
+    channels, width = projections.shape[1:]
+    peers, groups = lax.axis_size("seq"), lax.axis_size("chan")
+    pencil = channels // peers
+    fits = (
+        pencil % (2 * ROWS * CHUNKS) == 0
+        and 2 * (width // POOL) == LANES
+        and power_of_two(peers)
+        and peers > 1
+        and power_of_two(groups)
+        and groups <= MOST_GROUPS
+    )
+    run = aligned if fits else general
+    return run(projections, filter_taps, skip_gain, head_weight, head_bias, counts)
+
+
+def general(projections, filter_taps, skip_gain, head_weight, head_bias, counts):
     f32, bf16 = jnp.float32, jnp.bfloat16
     _, channels, width = projections.shape
     peers = lax.axis_size("seq")
@@ -511,9 +861,10 @@
     mine = mine.reshape(groups * half, own_tracks)
     other = other.reshape(groups * half, own_tracks)
 
-    mixed_out, mixed, spec = convolve(me, pieces, skip, tables)
+    mixed, spec = convolve(me, pieces, skip, tables, rows, 0, None)
+    mixed_out, pooled = pool(me, queries, mixed, gather, 0)
+    pooled = pooled[:pencil]
     mixed_home = [swap(mixed_out[k][:pencil], k, peers) for k in range(peers)]
-    pooled = pool(me, queries, mixed, gather)[:pencil]
 
     sent = pooled.reshape(pencil, peers, bins).transpose(1, 0, 2)
     sent = jnp.broadcast_to(sent[None], (groups, peers, pencil, bins))
@@ -563,7 +914,7 @@
     grad_home = [swap(block(grad_pooled, k), k, peers) for k in range(peers)]
     grad_rows = pad_rows(grad_pooled.transpose(1, 0, 2).reshape(pencil, peers * bins), rows)
 
-    corr_out = correlate(me, queries, grad_rows, spec, skip, tables, spread)
+    corr_out = correlate(me, queries, grad_rows, spec, skip, tables, spread, 0)
     corr_home = [swap(corr_out[k][:pencil], k, peers) for k in range(peers)]
 
     def assemble(parts):

time: 167 us -> 139 us (0.83)
  other arithmetic: 38.4 us -> 0.01 us
  Pallas kernels: 1.29 us -> 37.3 us
  waiting for transfers between devices: 40.9 us -> 22.1 us
  blocking collectives: 21.1 us -> 5.8 us
  local copies, waits for them, and re-layouts: 23.1 us -> 32.7 us
  matrix products: 6.7 us -> 0 us
  starting transfers between devices: 31.1 us -> 36.8 us
    pallas_call x1 -> x12, Pallas kernels: 1.29 us -> 37.3 us  [call(): pl.pallas_call(kernel, name=name, grid_spec=pltpu.PrefetchScalarGridSpec(...]
    pallas_call x2 -> x0, other arithmetic: 27.1 us -> none  [call(): pl.pallas_call(kernel, name=name, grid_spec=pltpu.PrefetchScalarGridSpec(...]
    unnamed x22 -> x86, local copies, waits for them, and re-layouts: 6.44 us -> 26.8 us
    psum x1 -> x0, blocking collectives: 15.5 us -> none  [per_device(): mean_loss = lax.psum(loss_part, 'chan') / (bins * peers * tracks)]
    ppermute x16 -> x22, waiting for transfers between devices: 25.9 us -> 12.4 us  [swap(): return lax.ppermute(value, 'seq', [(i, i ^ k) for i in range(count)])]
    all_to_all x3, waiting for transfers between devices: 15 us -> 6.64 us  [the longest x2 6.63 us: exchange(): lax.all_to_all(flat, ('chan', 'seq'), split_axis=0, concat_axis=0, tiled=...]
    reshape x7 -> x1, local copies, waits for them, and re-layouts: 7.43 us -> 0.08 us  [aligned(): skip_gain.reshape(peers, pencil, 1)]
    dot_general x4 -> x0, matrix products: 6.7 us -> none  [the longest x2 3.37 us: project(): lax.dot_general(x, w, (((0,), (0,)), ((), ())), preferred_element_type=f32)]
  transfers between devices with their start and end apart: 19 -> 28, of which waited for: 5 -> 8; matrix products, arithmetic and copies ran while one was open for 33% -> 3% of each run, Pallas kernels for 1% -> 21%
where the time goes in v2:
time: 139 us; the launch traced here: 138 us
  Pallas kernels  37.3 us (27%)
  starting transfers between devices  36.8 us (26%)
  local copies, waits for them, and re-layouts  32.7 us (24%)
  waiting for transfers between devices  22.1 us (16%)
  blocking collectives  5.8 us (4%)
  between operations  2.77 us (2%)
    pallas_call x12, Pallas kernels, call(): pl.pallas_call(kernel, name=name, grid_spec=pltpu.PrefetchScalarGridSpec(...  37.3 us
    unnamed x86, local copies, waits for them, and re-layouts  26.8 us
    ppermute x22, starting transfers between devices, swap(): return lax.ppermute(value, 'seq', [(i, i ^ k) for i in range(count)])  17.2 us
    ppermute x22, waiting for transfers between devices, swap(): return lax.ppermute(value, 'seq', [(i, i ^ k) for i in range(count)])  12.4 us
    all_to_all x2, starting transfers between devices, exchange(): lax.all_to_all(flat, ('chan', 'seq'), split_axis=0, concat_axis=0, tiled=...  8.43 us
    all_to_all x2, waiting for transfers between devices, exchange(): lax.all_to_all(flat, ('chan', 'seq'), split_axis=0, concat_axis=0, tiled=...  6.63 us
    all_to_all x1, starting transfers between devices, aligned(): mine = lax.all_to_all(mine, 'chan', split_axis=0, concat_axis=0, tiled=True)  6.51 us
    all_gather x1, blocking collectives, aligned(): all_sums = lax.all_gather(sums, 'seq')  5.8 us
  transfers between devices with their start and end apart: 28, of which 8 were waited for; matrix products, arithmetic and copies ran while one was open for 3% of the time, Pallas kernels for 21%

profile of v2, /device:TPU:1, one launch (start us, length us, event | category | flops | bytes accessed | tf_op | source)
XLA Modules:
  0.0 137.6 jit_solution(1892050055977502744)
XLA Ops:
  0.7 1.7 %copy-done.4 = f32[256,2048]{1,0:T(8,128)S(1)} copy-done((f32[256,2048]{1,0:T(8,128)S(1)}, f32[256,2048]{1,0:T(8,128)}, u32[]{:S(2)}) %copy-start.4) | copy-done | bytes 2097176
  2.3 3.3 %lay_out.1 = (bf16[2,32,2048]{2,1,0:T(8,128)(2,1)S(1)}, bf16[2,32,2048]{2,1,0:T(8,128)(2,1)S(1)}, bf16[2,32,2048]{2,1,0:T(8,128)(2,1)S(1)}, bf16[2,32,2048]{2,1,...) custom-call(s32[1]{0:T(128)} %bitcast.me_ref.refs_0_, ...), custom_call_target="tpu_custom_call" | custom-call | flops 524288 | bytes 10485760 | tf_op jit(solution)/shard_map/lay_out/pallas_call | solution.py:356
  8.7 6.5 %all-to-all-start.1 = ((bf16[8,128,480]{1,2,0:T(8,128)(2,1)}), bf16[8,128,480]{1,2,0:T(8,128)(2,1)}, u32[]{:S(2)}, u32[]{:S(2)}) async-start(bf16[8,128,480]{1,2,0:T(8,128)(2,1)} %copy.21), calls=%async_computation.1 | async-start | bytes 1966080 | tf_op jit(solution)/shard_map/all_to_all | solution.py:760
  20.9 3.4 %collective-permute-done.1.refs_3_ = bf16[2,32,2048]{2,1,0:T(8,128)(2,1)S(1)} collective-permute-done((bf16[2,32,2048]{2,1,0:T(8,128)(2,1)}, bf16[2,32,2048]{2,1,0:T(8,128)(2,1)S(1)}, u32[]{:S(2)}, u32[]{:S(2)}) %collective-permute-start.1) | collective-permute-done | bytes 262176 | tf_op jit(solution)/shard_map/ppermute | solution.py:724
  25.0 5.8 %collective-permute-done.2.refs_4_ = bf16[2,32,2048]{2,1,0:T(8,128)(2,1)S(1)} collective-permute-done((bf16[2,32,2048]{2,1,0:T(8,128)(2,1)S(1)}, bf16[2,32,2048]{2,1,0:T(8,128)(2,1)S(1)}, u32[]{:S(2)}, u32[]{:S(2)}) %collective-permute-start.2) | collective-permute-done | bytes 262176 | tf_op jit(solution)/shard_map/ppermute | solution.py:724
  36.3 6.8 %long_convolution.2 = (f32[64,8192]{1,0:T(8,128)S(1)}, f32[2,1024,256]{2,1,0:T(8,128)S(1)}) custom-call(s32[1]{0:T(128)} %bitcast.me_ref.refs_0_, bf16[2,32,2048]{2,1,0:T(8,128)(2,1)S(1)} %get-tuple-element.38.refs_1_, bf16[2,32,2048]{2,1,0:T(8,128)(2,1)S(1)} %copy-done.24, bf16[2,32,2048]{2,1,0:T(8,128)(2,1)S(1)} %copy-done.27, ...), custom_call_target="tpu_custom_call" | custom-call | flops 2415919104 | bytes 5832960 | tf_op jit(solution)/shard_map/long_convolution/pallas_call | solution.py:356
  43.1 1.3 copy-done.2
  44.4 1.3 copy-done.38
  45.9 1.7 %collective-permute-start.5 = (bf16[64,2048]{1,0:T(8,128)(2,1)S(1)}, bf16[64,2048]{1,0:T(8,128)(2,1)S(1)}, u32[]{:S(2)}, u32[]{:S(2)}) collective-permute-start(bf16[64,2048]{1,0:T(8,128)(2,1)S(1)} %get-tuple-element.74), channel_id=1, source_target_pairs={{0,24},{8,16},{16,8},{24,0},{1,25},{9,17},{17,9},{25,1},{2,26},{10... | collective-permute-start | bytes 786440 | tf_op jit(solution)/shard_map/ppermute | solution.py:724
  50.0 7.7 %long_convolution.3 = (f32[64,8192]{1,0:T(8,128)S(1)}, f32[2,1024,256]{2,1,0:T(8,128)S(1)}) custom-call(s32[1]{0:T(128)} %bitcast.me_ref.refs_0_, bf16[2,32,2048]{2,1,0:T(8,128)(2,1)S(1)} %get-tuple-element.44.refs_1_, bf16[2,32,2048]{2,1,0:T(8,128)(2,1)} %collective-permute-done.6.refs_2_, ...), custom_call_target="tpu_custom_call", output_to_operand_aliasing={{0}: (9, {})} | custom-call | flops 2415919104 | bytes 7930112 | tf_op jit(solution)/shard_map/long_convolution/pallas_call | solution.py:356
  57.7 1.3 copy-done.40
  60.1 1.8 %pool_bins.1 = (bf16[64,2048]{1,0:T(8,128)(2,1)S(1)}, bf16[64,2048]{1,0:T(8,128)(2,1)S(1)}, bf16[64,2048]{1,0:T(8,128)(2,1)S(1)}, bf16[64,2048]{1,0:T(8,128)(2,1)S(1)}, bf16[8,4,32,128]{3,2,1,0:T(8,128)(2,1)}) custom-call(s32[1]{0:T(128)} %bitcast.me_ref.refs_0_, bf16[64,2048]{1,0:T(8,128)(2,1)S(1)} %get-tuple-element.77.refs_1_, ...), custom_call_target="tpu_custom_call" | custom-call | flops 268435456 | bytes 4521984 | tf_op jit(solution)/shard_map/pool_bins/pallas_call | solution.py:356
  63.3 5.9 %all-to-all-start = ((bf16[32,32,128]{2,1,0:T(8,128)(2,1)}), bf16[32,32,128]{2,1,0:T(8,128)(2,1)}, u32[]{:S(2)}, u32[]{:S(2)}) async-start(bf16[32,32,128]{2,1,0:T(8,128)(2,1)} %bitcast.7), calls=%async_computation | async-start | bytes 524288 | tf_op jit(solution)/shard_map/all_to_all | solution.py:779
  70.2 1.5 %copy.22.mine_ref = bf16[8,128,480]{2,1,0:T(8,128)(2,1)S(1)} copy(bf16[8,128,480]{1,2,0:T(8,128)(2,1)} %all-to-all-done.1) | data formatting | bytes 1966080 | tf_op jit(solution)/shard_map/all_to_all | solution.py:760
  71.7 1.5 %copy.23.other_ref = bf16[8,128,480]{2,1,0:T(8,128)(2,1)S(1)} copy(bf16[8,128,480]{1,2,0:T(8,128)(2,1)} %collective-permute-done.9) | data formatting | bytes 1966080 | tf_op jit(solution)/shard_map/ppermute | solution.py:724
  73.2 6.4 %all-to-all-done = bf16[32,32,128]{2,1,0:T(8,128)(2,1)} async-done(((bf16[32,32,128]{2,1,0:T(8,128)(2,1)}), bf16[32,32,128]{2,1,0:T(8,128)(2,1)}, u32[]{:S(2)}, u32[]{:S(2)}) %all-to-all-start) | async-done | bytes 262176 | tf_op jit(solution)/shard_map/all_to_all | solution.py:779
  79.6 1.6 %head_rates.1 = (f32[64,480]{1,0:T(8,128)S(1)}, f32[8,480]{1,0:T(8,128)S(1)}) custom-call(s32[1]{0:T(128)} %bitcast.me_ref.refs_0_, bf16[8,4,32,128]{3,2,1,0:T(8,128)(2,1)} %bitcast.8.got_ref, bf16[8,128,480]{2,1,0:T(8,128)(2,1)S(1)} %copy.22.mine_ref, bf16[8,128,480]{2,1,0:T(8,128)(2,1)S(1)} %copy.23.other_ref, f32[1,480]{1,0:T(1,128)S(1)} %bitcast.23, ...), custom_call_target="tpu_custom_call" | custom-call | flops 125829120 | bytes 2491264 | tf_op jit(solution)/shard_map/head_rates/pallas_call | solution.py:356
  81.2 5.8 %all-gather = f32[32,480]{1,0:T(8,128)S(1)} all-gather(f32[8,480]{1,0:T(8,128)S(1)} %get-tuple-element.53), channel_id=2, replica_groups=mesh['seq'=4,'chan'=8] {'seq'}, dimensions={0}, use_global_device_ids=true | all-gather | bytes 76800 | tf_op jit(solution)/shard_map/all_gather | solution.py:786
  88.5 2.5 %all-to-all-start.2 = ((bf16[32,32,128]{2,1,0:T(8,128)(2,1)}), bf16[32,32,128]{2,1,0:T(8,128)(2,1)S(1)}, u32[]{:S(2)}, u32[]{:S(2)}) async-start(bf16[32,32,128]{2,1,0:T(8,128)(2,1)} %bitcast.21), calls=%async_computation.2 | async-start | bytes 524288 | tf_op jit(solution)/shard_map/all_to_all | solution.py:779
  94.5 1.5 %collective-permute-done.10 = f32[8,128]{1,0:T(8,128)S(1)} collective-permute-done((f32[8,128]{1,0:T(8,128)S(1)}, f32[8,128]{1,0:T(8,128)S(1)}, u32[]{:S(2)}, u32[]{:S(2)}) %collective-permute-start.10) | collective-permute-done | bytes 4128 | tf_op jit(solution)/shard_map/ppermute | solution.py:791
  97.2 1.6 %collective-permute-done.11 = f32[8,128]{1,0:T(8,128)S(1)} collective-permute-done((f32[8,128]{1,0:T(8,128)S(1)}, f32[8,128]{1,0:T(8,128)S(1)}, u32[]{:S(2)}, u32[]{:S(2)}) %collective-permute-start.11) | collective-permute-done | bytes 4128 | tf_op jit(solution)/shard_map/ppermute | solution.py:791
  98.9 2.1 %collective-permute-start.12 = (f32[8,128]{1,0:T(8,128)S(1)}, f32[8,128]{1,0:T(8,128)S(1)}, u32[]{:S(2)}, u32[]{:S(2)}) collective-permute-start(f32[8,128]{1,0:T(8,128)S(1)} %add.37), channel_id=1, source_target_pairs={{0,4},{1,5},{2,6},{3,7},{4,0},{5,1},{6,2},{7,3},{8,12},{9,13},{10,... | collective-permute-start | bytes 12296 | tf_op jit(solution)/shard_map/ppermute | solution.py:791
  101.3 1.9 %collective-permute-start.16 = (f32[32,128]{1,0:T(8,128)S(1)}, f32[32,128]{1,0:T(8,128)S(1)}, u32[]{:S(2)}, u32[]{:S(2)}) collective-permute-start(f32[32,128]{1,0:T(8,128)S(1)} %get-tuple-element.61), channel_id=1, source_target_pairs={{0,8},{8,0},{16,24},{24,16},{1,9},{9,1},{17,25},{25,17},{2,10},{10... | collective-permute-start | bytes 49160 | tf_op jit(solution)/shard_map/ppermute | solution.py:724
  110.5 1.6 %copy-done.39 = f32[2,1024,256]{2,1,0:T(8,128)S(1)} copy-done((f32[2,1024,256]{2,1,0:T(8,128)S(1)}, f32[2,1024,256]{2,1,0:T(8,128)}, u32[]{:S(2)}) %copy-start.39) | copy-done | bytes 2097176
  112.1 4.8 %long_correlation.3 = (bf16[32,2048]{1,0:T(8,128)(2,1)S(1)}, bf16[32,2048]{1,0:T(8,128)(2,1)S(1)}, bf16[32,2048]{1,0:T(8,128)(2,1)S(1)}, bf16[32,2048]{1,0:T(8,128)(2,1)S(1)}) custom-call(s32[1]{0:T(128)} %bitcast.me_ref.refs_0_, bf16[64,2048]{1,0:T(8,128)(2,1)S(1)} %copy-done.7, bf16[64,2048]{1,0:T(8,128)(2,1)S(1)} %copy-done.15, ...), custom_call_target="tpu_custom_call" | custom-call | flops 1879048192 | bytes 4391168 | tf_op jit(solution)/shard_map/long_correlation/pallas_call | solution.py:356
  117.0 1.4 %collective-permute-start.17 = (f32[32,128]{1,0:T(8,128)S(1)}, f32[32,128]{1,0:T(8,128)S(1)}, u32[]{:S(2)}, u32[]{:S(2)}) collective-permute-start(f32[32,128]{1,0:T(8,128)S(1)} %get-tuple-element.62), channel_id=1, source_target_pairs={{0,16},{8,24},{16,0},{24,8},{1,17},{9,25},{17,1},{25,9},{2,18},{10... | collective-permute-start | bytes 49160 | tf_op jit(solution)/shard_map/ppermute | solution.py:724
  118.9 1.3 collective-permute-start.23
  120.8 4.8 %long_correlation.2 = (bf16[32,2048]{1,0:T(8,128)(2,1)S(1)}, bf16[32,2048]{1,0:T(8,128)(2,1)S(1)}, bf16[32,2048]{1,0:T(8,128)(2,1)S(1)}, bf16[32,2048]{1,0:T(8,128)(2,1)S(1)}) custom-call(s32[1]{0:T(128)} %bitcast.me_ref.refs_0_, bf16[64,2048]{1,0:T(8,128)(2,1)S(1)} %copy-done.7, bf16[64,2048]{1,0:T(8,128)(2,1)S(1)} %copy-done.15, ...), custom_call_target="tpu_custom_call" | custom-call | flops 1879048192 | bytes 4391168 | tf_op jit(solution)/shard_map/long_correlation/pallas_call | solution.py:356
  125.8 1.4 %collective-permute-start.20 = (bf16[32,2048]{1,0:T(8,128)(2,1)S(1)}, bf16[32,2048]{1,0:T(8,128)(2,1)S(1)}, u32[]{:S(2)}, u32[]{:S(2)}) collective-permute-start(bf16[32,2048]{1,0:T(8,128)(2,1)S(1)} %get-tuple-element.68), channel_id=1, source_target_pairs={{0,16},{8,24},{16,0},{24,8},{1,17},{9,25},{17,1},{25,9},{2,18},{10... | collective-permute-start | bytes 393224 | tf_op jit(solution)/shard_map/ppermute | solution.py:724
  129.1 2.6 %finish.2.refs_12_ = f32[3,256,2048]{2,1,0:T(8,128)} custom-call(s32[1]{0:T(128)} %bitcast.me_ref.refs_0_, bf16[3,256,2048]{2,1,0:T(8,128)(2,1)S(1)} %copy-done.1, bf16[3,256,2048]{2,1,0:T(8,128)(2,1)S(1)} %copy-done.1, bf16[256,128]{1,0:T(8,128)(2,1)S(1)} %copy-done.8, bf16[64,2048]{1,0:T(8,128)(2,1)S(1)} %get-tuple-element.55.refs_0_, ...), custom_call_target="tpu_custom_call" | custom-call | flops 2097152 | bytes 14286848 | tf_op jit(solution)/shard_map/finish/pallas_call | solution.py:356
  131.8 2.1 %collective-permute-done.21.refs_11_ = bf16[32,2048]{1,0:T(8,128)(2,1)S(1)} collective-permute-done((bf16[32,2048]{1,0:T(8,128)(2,1)S(1)}, bf16[32,2048]{1,0:T(8,128)(2,1)S(1)}, u32[]{:S(2)}, u32[]{:S(2)}) %collective-permute-start.21) | collective-permute-done | bytes 131104 | tf_op jit(solution)/shard_map/ppermute | solution.py:724
  133.9 2.6 %finish.3 = f32[3,256,2048]{2,1,0:T(8,128)} custom-call(s32[1]{0:T(128)} %bitcast.me_ref.refs_0_, bf16[3,256,2048]{2,1,0:T(8,128)(2,1)S(1)} %copy-done.1, bf16[3,256,2048]{2,1,0:T(8,128)(2,1)S(1)} %copy-done.1, bf16[256,128]{1,0:T(8,128)(2,1)S(1)} %copy-done.8, bf16[64,2048]{1,0:T(8,128)(2,1)S(1)} %get-tuple-element.55.refs_0_, ...), custom_call_target="tpu_custom_call", output_to_operand_aliasing={{}: (16, {})} | custom-call | flops 2097152 | bytes 20578304 | tf_op jit(solution)/shard_map/finish/pallas_call | solution.py:356
  (138 shorter events, 37.2 us)
Async XLA Ops:
  0.6 69.4 %copy-start = (s32[64,3840]{1,0:T(8,128)S(1)}, s32[64,3840]{1,0:T(8,128)}, u32[]{:S(2)}) copy-start(s32[64,3840]{1,0:T(8,128)} %param.16) | copy-start | bytes 2949124
  8.7 22.9 %copy-start.36 = (f32[2,64,128]{2,1,0:T(8,128)S(1)}, f32[2,64,128]{2,1,0:T(8,128)}, u32[]{:S(2)}) copy-start(f32[2,64,128]{2,1,0:T(8,128)} %constant.51.clone.refs_8_.refs_10_) | copy-start | bytes 196612
  8.7 37.1 %all-to-all-start.1 = ((bf16[8,128,480]{1,2,0:T(8,128)(2,1)}), bf16[8,128,480]{1,2,0:T(8,128)(2,1)}, u32[]{:S(2)}, u32[]{:S(2)}) async-start(bf16[8,128,480]{1,2,0:T(8,128)(2,1)} %copy.21), calls=%async_computation.1 | async-start | bytes 1966080 | tf_op jit(solution)/shard_map/all_to_all | solution.py:760
  15.2 4.2 %collective-permute-start = (bf16[2,32,2048]{2,1,0:T(8,128)(2,1)}, bf16[2,32,2048]{2,1,0:T(8,128)(2,1)S(1)}, u32[]{:S(2)}, u32[]{:S(2)}) collective-permute-start(bf16[2,32,2048]{2,1,0:T(8,128)(2,1)} %copy-done.25), channel_id=1, source_target_pairs={{0,8},{8,0},{16,24},{24,16},{1,9},{9,1},{17,25},{25,17},{2,10},{10... | collective-permute-start | bytes 786440 | tf_op jit(solution)/shard_map/ppermute | solution.py:724
  16.1 8.2 %collective-permute-start.1 = (bf16[2,32,2048]{2,1,0:T(8,128)(2,1)}, bf16[2,32,2048]{2,1,0:T(8,128)(2,1)S(1)}, u32[]{:S(2)}, u32[]{:S(2)}) collective-permute-start(bf16[2,32,2048]{2,1,0:T(8,128)(2,1)} %copy-done.22), channel_id=1, source_target_pairs={{0,16},{8,24},{16,0},{24,8},{1,17},{9,25},{17,1},{25,9},{2,18},{10... | collective-permute-start | bytes 786440 | tf_op jit(solution)/shard_map/ppermute | solution.py:724
  17.4 13.5 %collective-permute-start.2 = (bf16[2,32,2048]{2,1,0:T(8,128)(2,1)S(1)}, bf16[2,32,2048]{2,1,0:T(8,128)(2,1)S(1)}, u32[]{:S(2)}, u32[]{:S(2)}) collective-permute-start(bf16[2,32,2048]{2,1,0:T(8,128)(2,1)S(1)} %get-tuple-element.41), channel_id=1, source_target_pairs={{0,24},{8,16},{16,8},{24,0},{1,25},{9,17},{17,9},{25,1},{2,26},{10... | collective-permute-start | bytes 786440 | tf_op jit(solution)/shard_map/ppermute | solution.py:724
  17.9 29.7 %collective-permute-start.6 = (bf16[2,32,2048]{2,1,0:T(8,128)(2,1)S(1)}, bf16[2,32,2048]{2,1,0:T(8,128)(2,1)}, u32[]{:S(2)}, u32[]{:S(2)}) collective-permute-start(bf16[2,32,2048]{2,1,0:T(8,128)(2,1)S(1)} %get-tuple-element.45), channel_id=1, source_target_pairs={{0,8},{8,0},{16,24},{24,16},{1,9},{9,1},{17,25},{25,17},{2,10},{10... | collective-permute-start | bytes 786440 | tf_op jit(solution)/shard_map/ppermute | solution.py:724
  18.0 29.8 %collective-permute-start.7 = (bf16[2,32,2048]{2,1,0:T(8,128)(2,1)}, bf16[2,32,2048]{2,1,0:T(8,128)(2,1)}, u32[]{:S(2)}, u32[]{:S(2)}) collective-permute-start(bf16[2,32,2048]{2,1,0:T(8,128)(2,1)} %get-tuple-element.46), channel_id=1, source_target_pairs={{0,16},{8,24},{16,0},{24,8},{1,17},{9,25},{17,1},{25,9},{2,18},{10... | collective-permute-start | bytes 786440 | tf_op jit(solution)/shard_map/ppermute | solution.py:724
  19.4 28.7 %copy-start.17 = (f32[64,1]{1,0:T(8,128)}, f32[64,1]{1,0:T(8,128)S(1)}, u32[]{:S(2)}) copy-start(f32[64,1]{1,0:T(8,128)S(1)} %copy.19.refs_5_.refs_7_) | copy-start | bytes 772
  20.1 27.9 %collective-permute-start.8 = (bf16[2,32,2048]{2,1,0:T(8,128)(2,1)S(1)}, bf16[2,32,2048]{2,1,0:T(8,128)(2,1)}, u32[]{:S(2)}, u32[]{:S(2)}) collective-permute-start(bf16[2,32,2048]{2,1,0:T(8,128)(2,1)S(1)} %get-tuple-element.47), channel_id=1, source_target_pairs={{0,24},{8,16},{16,8},{24,0},{1,25},{9,17},{17,9},{25,1},{2,26},{10... | collective-permute-start | bytes 786440 | tf_op jit(solution)/shard_map/ppermute | solution.py:724
  45.7 25.9 %collective-permute-start.9 = (bf16[8,128,480]{1,2,0:T(8,128)(2,1)}, bf16[8,128,480]{1,2,0:T(8,128)(2,1)}, u32[]{:S(2)}, u32[]{:S(2)}) collective-permute-start(bf16[8,128,480]{1,2,0:T(8,128)(2,1)} %all-to-all-done.1), channel_id=1, source_target_pairs={{0,8},{8,0},{16,24},{24,16},{1,9},{9,1},{17,25},{25,17},{2,10},{10... | collective-permute-start | bytes 2949128 | tf_op jit(solution)/shard_map/ppermute | solution.py:724
  45.9 13.2 %collective-permute-start.5 = (bf16[64,2048]{1,0:T(8,128)(2,1)S(1)}, bf16[64,2048]{1,0:T(8,128)(2,1)S(1)}, u32[]{:S(2)}, u32[]{:S(2)}) collective-permute-start(bf16[64,2048]{1,0:T(8,128)(2,1)S(1)} %get-tuple-element.74), channel_id=1, source_target_pairs={{0,24},{8,16},{16,8},{24,0},{1,25},{9,17},{17,9},{25,1},{2,26},{10... | collective-permute-start | bytes 786440 | tf_op jit(solution)/shard_map/ppermute | solution.py:724
  47.5 12.5 %collective-permute-start.4 = (bf16[64,2048]{1,0:T(8,128)(2,1)S(1)}, bf16[64,2048]{1,0:T(8,128)(2,1)S(1)}, u32[]{:S(2)}, u32[]{:S(2)}) collective-permute-start(bf16[64,2048]{1,0:T(8,128)(2,1)S(1)} %get-tuple-element.75), channel_id=1, source_target_pairs={{0,16},{8,24},{16,0},{24,8},{1,17},{9,25},{17,1},{25,9},{2,18},{10... | collective-permute-start | bytes 786440 | tf_op jit(solution)/shard_map/ppermute | solution.py:724
  47.8 12.3 %collective-permute-start.3 = (bf16[64,2048]{1,0:T(8,128)(2,1)S(1)}, bf16[64,2048]{1,0:T(8,128)(2,1)S(1)}, u32[]{:S(2)}, u32[]{:S(2)}) collective-permute-start(bf16[64,2048]{1,0:T(8,128)(2,1)S(1)} %get-tuple-element.76), channel_id=1, source_target_pairs={{0,8},{8,0},{16,24},{24,16},{1,9},{9,1},{17,25},{25,17},{2,10},{10... | collective-permute-start | bytes 786440 | tf_op jit(solution)/shard_map/ppermute | solution.py:724
  63.3 16.2 %all-to-all-start = ((bf16[32,32,128]{2,1,0:T(8,128)(2,1)}), bf16[32,32,128]{2,1,0:T(8,128)(2,1)}, u32[]{:S(2)}, u32[]{:S(2)}) async-start(bf16[32,32,128]{2,1,0:T(8,128)(2,1)} %bitcast.7), calls=%async_computation | async-start | bytes 524288 | tf_op jit(solution)/shard_map/all_to_all | solution.py:779
  81.2 22.0 %copy-start.8 = (bf16[256,128]{1,0:T(8,128)(2,1)S(1)}, bf16[256,128]{1,0:T(8,128)(2,1)}, u32[]{:S(2)}) copy-start(bf16[256,128]{1,0:T(8,128)(2,1)} %constant.53.clone.refs_11_.spread_ref) | copy-start | bytes 196612
  88.5 12.8 %all-to-all-start.2 = ((bf16[32,32,128]{2,1,0:T(8,128)(2,1)}), bf16[32,32,128]{2,1,0:T(8,128)(2,1)S(1)}, u32[]{:S(2)}, u32[]{:S(2)}) async-start(bf16[32,32,128]{2,1,0:T(8,128)(2,1)} %bitcast.21), calls=%async_computation.2 | async-start | bytes 524288 | tf_op jit(solution)/shard_map/all_to_all | solution.py:779
  91.0 26.0 %collective-permute-start.13 = (bf16[64,2048]{1,0:T(8,128)(2,1)}, bf16[64,2048]{1,0:T(8,128)(2,1)S(1)}, u32[]{:S(2)}, u32[]{:S(2)}) collective-permute-start(bf16[64,2048]{1,0:T(8,128)(2,1)} %copy-done.21), channel_id=1, source_target_pairs={{0,8},{8,0},{16,24},{24,16},{1,9},{9,1},{17,25},{25,17},{2,10},{10... | collective-permute-start | bytes 786440 | tf_op jit(solution)/shard_map/ppermute | solution.py:724
  91.5 26.9 %collective-permute-start.14 = (bf16[64,2048]{1,0:T(8,128)(2,1)}, bf16[64,2048]{1,0:T(8,128)(2,1)S(1)}, u32[]{:S(2)}, u32[]{:S(2)}) collective-permute-start(bf16[64,2048]{1,0:T(8,128)(2,1)} %copy-done.20), channel_id=1, source_target_pairs={{0,16},{8,24},{16,0},{24,8},{1,17},{9,25},{17,1},{25,9},{2,18},{10... | collective-permute-start | bytes 786440 | tf_op jit(solution)/shard_map/ppermute | solution.py:724
  92.6 26.0 %collective-permute-start.15 = (bf16[64,2048]{1,0:T(8,128)(2,1)}, bf16[64,2048]{1,0:T(8,128)(2,1)S(1)}, u32[]{:S(2)}, u32[]{:S(2)}) collective-permute-start(bf16[64,2048]{1,0:T(8,128)(2,1)} %copy-done.19), channel_id=1, source_target_pairs={{0,24},{8,16},{16,8},{24,0},{1,25},{9,17},{17,9},{25,1},{2,26},{10... | collective-permute-start | bytes 786440 | tf_op jit(solution)/shard_map/ppermute | solution.py:724
  93.2 2.8 %collective-permute-start.10 = (f32[8,128]{1,0:T(8,128)S(1)}, f32[8,128]{1,0:T(8,128)S(1)}, u32[]{:S(2)}, u32[]{:S(2)}) collective-permute-start(f32[8,128]{1,0:T(8,128)S(1)} %get-tuple-element.54), channel_id=1, source_target_pairs={{0,1},{1,0},{2,3},{3,2},{4,5},{5,4},{6,7},{7,6},{8,9},{9,8},{10,11... | collective-permute-start | bytes 12296 | tf_op jit(solution)/shard_map/ppermute | solution.py:791
  96.0 2.9 %collective-permute-start.11 = (f32[8,128]{1,0:T(8,128)S(1)}, f32[8,128]{1,0:T(8,128)S(1)}, u32[]{:S(2)}, u32[]{:S(2)}) collective-permute-start(f32[8,128]{1,0:T(8,128)S(1)} %add.36), channel_id=1, source_target_pairs={{0,2},{1,3},{2,0},{3,1},{4,6},{5,7},{6,4},{7,5},{8,10},{9,11},{10,... | collective-permute-start | bytes 12296 | tf_op jit(solution)/shard_map/ppermute | solution.py:791
  98.9 20.0 %collective-permute-start.12 = (f32[8,128]{1,0:T(8,128)S(1)}, f32[8,128]{1,0:T(8,128)S(1)}, u32[]{:S(2)}, u32[]{:S(2)}) collective-permute-start(f32[8,128]{1,0:T(8,128)S(1)} %add.37), channel_id=1, source_target_pairs={{0,4},{1,5},{2,6},{3,7},{4,0},{5,1},{6,2},{7,3},{8,12},{9,13},{10,... | collective-permute-start | bytes 12296 | tf_op jit(solution)/shard_map/ppermute | solution.py:791
  101.3 18.9 %collective-permute-start.16 = (f32[32,128]{1,0:T(8,128)S(1)}, f32[32,128]{1,0:T(8,128)S(1)}, u32[]{:S(2)}, u32[]{:S(2)}) collective-permute-start(f32[32,128]{1,0:T(8,128)S(1)} %get-tuple-element.61), channel_id=1, source_target_pairs={{0,8},{8,0},{16,24},{24,16},{1,9},{9,1},{17,25},{25,17},{2,10},{10... | collective-permute-start | bytes 49160 | tf_op jit(solution)/shard_map/ppermute | solution.py:724
  117.0 8.7 %collective-permute-start.17 = (f32[32,128]{1,0:T(8,128)S(1)}, f32[32,128]{1,0:T(8,128)S(1)}, u32[]{:S(2)}, u32[]{:S(2)}) collective-permute-start(f32[32,128]{1,0:T(8,128)S(1)} %get-tuple-element.62), channel_id=1, source_target_pairs={{0,16},{8,24},{16,0},{24,8},{1,17},{9,25},{17,1},{25,9},{2,18},{10... | collective-permute-start | bytes 49160 | tf_op jit(solution)/shard_map/ppermute | solution.py:724
  118.3 7.4 %collective-permute-start.18 = (f32[32,128]{1,0:T(8,128)S(1)}, f32[32,128]{1,0:T(8,128)S(1)}, u32[]{:S(2)}, u32[]{:S(2)}) collective-permute-start(f32[32,128]{1,0:T(8,128)S(1)} %get-tuple-element.63), channel_id=1, source_target_pairs={{0,24},{8,16},{16,8},{24,0},{1,25},{9,17},{17,9},{25,1},{2,26},{10... | collective-permute-start | bytes 49160 | tf_op jit(solution)/shard_map/ppermute | solution.py:724
  118.7 8.5 %collective-permute-start.22 = (bf16[32,2048]{1,0:T(8,128)(2,1)S(1)}, bf16[32,2048]{1,0:T(8,128)(2,1)S(1)}, u32[]{:S(2)}, u32[]{:S(2)}) collective-permute-start(bf16[32,2048]{1,0:T(8,128)(2,1)S(1)} %get-tuple-element.71), channel_id=1, source_target_pairs={{0,8},{8,0},{16,24},{24,16},{1,9},{9,1},{17,25},{25,17},{2,10},{10... | collective-permute-start | bytes 393224 | tf_op jit(solution)/shard_map/ppermute | solution.py:724
  118.9 10.2 %collective-permute-start.23 = (bf16[32,2048]{1,0:T(8,128)(2,1)S(1)}, bf16[32,2048]{1,0:T(8,128)(2,1)S(1)}, u32[]{:S(2)}, u32[]{:S(2)}) collective-permute-start(bf16[32,2048]{1,0:T(8,128)(2,1)S(1)} %get-tuple-element.72), channel_id=1, source_target_pairs={{0,16},{8,24},{16,0},{24,8},{1,17},{9,25},{17,1},{25,9},{2,18},{10... | collective-permute-start | bytes 393224 | tf_op jit(solution)/shard_map/ppermute | solution.py:724
  120.2 8.9 %collective-permute-start.24 = (bf16[32,2048]{1,0:T(8,128)(2,1)S(1)}, bf16[32,2048]{1,0:T(8,128)(2,1)S(1)}, u32[]{:S(2)}, u32[]{:S(2)}) collective-permute-start(bf16[32,2048]{1,0:T(8,128)(2,1)S(1)} %get-tuple-element.73), channel_id=1, source_target_pairs={{0,24},{8,16},{16,8},{24,0},{1,25},{9,17},{17,9},{25,1},{2,26},{10... | collective-permute-start | bytes 393224 | tf_op jit(solution)/shard_map/ppermute | solution.py:724
  125.7 6.1 %collective-permute-start.19 = (bf16[32,2048]{1,0:T(8,128)(2,1)S(1)}, bf16[32,2048]{1,0:T(8,128)(2,1)S(1)}, u32[]{:S(2)}, u32[]{:S(2)}) collective-permute-start(bf16[32,2048]{1,0:T(8,128)(2,1)S(1)} %get-tuple-element.67), channel_id=1, source_target_pairs={{0,8},{8,0},{16,24},{24,16},{1,9},{9,1},{17,25},{25,17},{2,10},{10... | collective-permute-start | bytes 393224 | tf_op jit(solution)/shard_map/ppermute | solution.py:724
  125.8 6.0 %collective-permute-start.20 = (bf16[32,2048]{1,0:T(8,128)(2,1)S(1)}, bf16[32,2048]{1,0:T(8,128)(2,1)S(1)}, u32[]{:S(2)}, u32[]{:S(2)}) collective-permute-start(bf16[32,2048]{1,0:T(8,128)(2,1)S(1)} %get-tuple-element.68), channel_id=1, source_target_pairs={{0,16},{8,24},{16,0},{24,8},{1,17},{9,25},{17,1},{25,9},{2,18},{10... | collective-permute-start | bytes 393224 | tf_op jit(solution)/shard_map/ppermute | solution.py:724
  127.2 6.7 %collective-permute-start.21 = (bf16[32,2048]{1,0:T(8,128)(2,1)S(1)}, bf16[32,2048]{1,0:T(8,128)(2,1)S(1)}, u32[]{:S(2)}, u32[]{:S(2)}) collective-permute-start(bf16[32,2048]{1,0:T(8,128)(2,1)S(1)} %get-tuple-element.69), channel_id=1, source_target_pairs={{0,24},{8,16},{16,8},{24,0},{1,25},{9,17},{17,9},{25,1},{2,26},{10... | collective-permute-start | bytes 393224 | tf_op jit(solution)/shard_map/ppermute | solution.py:724
  (40 other events, 129.5 us)

commit v3 on v2

--- a/solution.py
+++ b/solution.py
@@ -17,7 +17,9 @@
 total_weight = 0.2
 rate_floor = 0.5
 
-VMEM_LIMIT = 48 * 1024 * 1024
+MICROSECOND = 1.0e9
+
+VMEM_LIMIT = 20 * 1024 * 1024
 CHUNKS = 2
 MOST_GROUPS = 16
 
@@ -350,9 +352,17 @@
     return pl.BlockSpec((rows, width), lambda i, me: (start + i, 0))
 
 
-def call(kernel, name, me, steps, inputs, in_specs, out_shapes, out_specs, scratch, flops, aliases=None):
+def call(kernel, name, me, steps, inputs, in_specs, out_shapes, out_specs, scratch, flops, aliases=None, near=(), vmem=()):
     moved = sum(x.size * x.dtype.itemsize for x in inputs)
     moved += sum(math.prod(o.shape) * o.dtype.itemsize for o in out_shapes)
+    def space(i):
+        return pltpu.VMEM if i in vmem else pltpu.HBM
+
+    count = len(inputs)
+    inputs = [x if i in near else pltpu.with_memory_space_constraint(x, space(i)) for i, x in enumerate(inputs)]
+    out_shapes = [
+        o if count + i in near else space(count + i)(o.shape, o.dtype) for i, o in enumerate(out_shapes)
+    ]
     return pl.pallas_call(
         kernel,
         name=name,
@@ -368,7 +378,7 @@
         compiler_params=pltpu.CompilerParams(
             dimension_semantics=("arbitrary",), vmem_limit_bytes=VMEM_LIMIT
         ),
-        cost_estimate=pl.CostEstimate(flops=flops, bytes_accessed=moved, transcendentals=0),
+        cost_estimate=pl.CostEstimate(flops=int(flops), bytes_accessed=moved, transcendentals=0),
     )(me, *inputs)
 
 
@@ -415,7 +425,7 @@
             parts,
             pltpu.VMEM((3 * ra, 2, chunk, 2 * LANES), bf16),
         ],
-        2 * 9 * rows * outer * (2 * LANES) ** 2, aliases,
+        rows * outer * 0.004 * MICROSECOND, aliases, (peers,), range(peers + 4, len(inputs) + 1),
     )
 
 
@@ -448,7 +458,7 @@
             pltpu.VMEM((peers, step, width), bf16),
             pltpu.VMEM((step // ROWS, outer * ROWS, 2 * LANES), bf16),
         ],
-        2 * rows * outer * 2 * LANES * LANES,
+        rows * outer * 0.001 * MICROSECOND, vmem=(peers,),
     )
     return out[:peers], out[peers]
 
@@ -492,69 +502,116 @@
         kernel, "long_correlation", me, rows // ROWS,
         [*queries, grad_pooled, spec, skip, fwd, bwd, twist, spread], in_specs,
         [shape((rows, width), bf16)] * peers, [by_rows(width)] * peers,
-        scratch, 2 * 7 * rows * outer * (2 * LANES) ** 2,
-    )
-
-
-def lay_out(me, projections, filter_taps, peers, chunks):
+        scratch, rows * outer * 0.004 * MICROSECOND, near=(peers, peers + 2),
+    )
+
+
+def lay_out(me, projections, filter_taps, peers, chunk, chunks):
+    last = chunk == chunks - 1
     _, channels, width = projections.shape
     pencil = channels // peers
     rows = pencil // chunks
-    bf16 = jnp.bfloat16
-
-    def kernel(me_ref, keyed_ref, valued_ref, taps_ref, *outs):
-        for k in range(peers):
-
-            @pl.when(pl.program_id(0) == k)
-            def _():
-                for j in range(chunks):
-                    part = slice(j * rows, (j + 1) * rows)
-                    keyed = keyed_ref[0, part, :].astype(jnp.float32)
-                    valued = valued_ref[0, part, :].astype(jnp.float32)
-                    outs[j * peers + k][0] = (keyed * valued).astype(bf16)
-                    outs[j * peers + k][1] = taps_ref[part, :].astype(bf16)
-
-    piece = shape((2, rows, width), bf16)
-    out = call(
-        kernel, "lay_out", me, peers, [projections, projections, filter_taps],
+    f32, bf16 = jnp.float32, jnp.bfloat16
+    order = list(range(peers))[::-1]
+
+    def kernel(me_ref, proj_ref, taps_ref, *refs):
+        outs = refs[:peers]
+        queries = refs[peers:-7]
+        pair, taps, laid, passing, sems, out_sems, query_sems = refs[-7:]
+
+        def take(k):
+            block = pl.ds(pl.multiple_of((me_ref[0] ^ k) * pencil, pencil), pencil)
+            return pltpu.make_async_copy(proj_ref.at[0, block], passing.at[k], query_sems.at[k, 0])
+
+        def hand_on(k):
+            return pltpu.make_async_copy(passing.at[k], queries[k], query_sems.at[k, 1])
+
+
+        def fetch(k):
+            here = pl.ds(pl.multiple_of((me_ref[0] ^ k) * pencil + chunk * rows, rows), rows)
+            return (
+                pltpu.make_async_copy(proj_ref.at[1, here], pair.at[k, 0], sems.at[k, 0]),
+                pltpu.make_async_copy(proj_ref.at[2, here], pair.at[k, 1], sems.at[k, 1]),
+                pltpu.make_async_copy(taps_ref.at[here], taps.at[k], sems.at[k, 2]),
+            )
+
+        def leave(k):
+            return pltpu.make_async_copy(laid.at[k], outs[k], out_sems.at[k])
+
+        for k in order:
+            for copy in fetch(k):
+                copy.start()
+        for k in range(len(queries)):
+            take(k).start()
+        for k in order:
+            keyed, valued, lags = fetch(k)
+            keyed.wait()
+            valued.wait()
+            laid[k, 0] = (pair[k, 0].astype(f32) * pair[k, 1].astype(f32)).astype(bf16)
+            lags.wait()
+            laid[k, 1] = taps[k].astype(bf16)
+            leave(k).start()
+        for k in range(len(queries)):
+            take(k).wait()
+            hand_on(k).start()
+        for k in order:
+            leave(k).wait()
+        for k in range(len(queries)):
+            hand_on(k).wait()
+
+    out_shapes = [shape((2, rows, width), bf16)] * peers
+    if last:
+        out_shapes += [shape((pencil, width), bf16)] * peers
+    return call(
+        kernel, "lay_out", me, 1, [projections, filter_taps],
+        [pl.BlockSpec(memory_space=pltpu.HBM)] * 2,
+        out_shapes,
+        [pl.BlockSpec(memory_space=pltpu.HBM)] * len(out_shapes),
         [
-            pl.BlockSpec((1, pencil, width), lambda i, me: (1, me[0] ^ i, 0)),
-            pl.BlockSpec((1, pencil, width), lambda i, me: (2, me[0] ^ i, 0)),
-            pl.BlockSpec((pencil, width), lambda i, me: (me[0] ^ i, 0)),
+            pltpu.VMEM((peers, 2, rows, width), bf16),
+            pltpu.VMEM((peers, rows, width), f32),
+            pltpu.VMEM((peers, 2, rows, width), bf16),
+            pltpu.VMEM((peers, pencil, width), bf16),
+            pltpu.SemaphoreType.DMA((peers, 3)),
+            pltpu.SemaphoreType.DMA((peers,)),
+            pltpu.SemaphoreType.DMA((peers, 2)),
         ],
-        [piece] * (peers * chunks),
-        [pl.BlockSpec(piece.shape, lambda i, me: (0, 0, 0))] * (peers * chunks),
-        [], channels * width,
-    )
-    return [out[j * peers : (j + 1) * peers] for j in range(chunks)]
+        rows * peers * 0.015 * MICROSECOND,
+    )
 
 
 def by_track(me, head_weight, groups):
     channels, tracks = head_weight.shape
     half, own = channels // 2, tracks // groups
+    padded = -(-own // LANES) * LANES
+    rows = 2 * ROWS
 
     def kernel(me_ref, weight_ref, out_ref):
         for group in range(groups):
-            out_ref[group] = weight_ref[:, group * own : (group + 1) * own]
-
-    out = shape((groups, half, own), head_weight.dtype)
+            out_ref[group, :, :own] = weight_ref[:, group * own : (group + 1) * own]
+            if padded > own:
+                out_ref[group, :, own:] = jnp.zeros((rows, padded - own), head_weight.dtype)
+
+    out = shape((groups, half, padded), head_weight.dtype)
+    steps = half // rows
     return call(
-        kernel, "by_track", me, 1, [head_weight],
-        [pl.BlockSpec((half, tracks), lambda i, me: (me[0] & 1, 0))],
-        [out], [pl.BlockSpec(out.shape, lambda i, me: (0, 0, 0))], [], half * tracks,
+        kernel, "by_track", me, steps, [head_weight],
+        [pl.BlockSpec((rows, tracks), lambda i, me: ((me[0] & 1) * steps + i, 0))],
+        [out], [pl.BlockSpec((groups, rows, padded), lambda i, me: (0, i, 0))], [], 2 * MICROSECOND,
     )[0]
 
 
-def weight_pair(weight_ref, seats, pencil):
-    groups, _, own = weight_ref.shape
-    rows = weight_ref[...].reshape(groups, seats, pencil // (2 * ROWS), 2, ROWS, own)
+def weight_pair(weight_ref, seats, pencil, own):
+    groups, _, padded = weight_ref.shape
+    rows = weight_ref[...].reshape(groups, seats, pencil // (2 * ROWS), 2, ROWS, padded)
     count = groups * seats * pencil // 2
-    return rows[:, :, :, 0].reshape(count, own), rows[:, :, :, 1].reshape(count, own)
+    left, right = rows[:, :, :, 0].reshape(count, padded), rows[:, :, :, 1].reshape(count, padded)
+    return left[:, :own], right[:, :own]
 
 
 def head_rates(me, got, mine, other, bias, counts):
     groups, peers, half_rows, _ = got.shape
-    own = mine.shape[2]
+    own = counts.shape[1]
     seats = peers // 2
     pencil = 2 * half_rows
     bins = LANES // 2
@@ -566,7 +623,7 @@
         for weight_ref, place in ((mine_ref, odd), (other_ref, 1 - odd)):
             block = got_ref[:, pl.ds(place * seats, seats)].reshape(groups * seats * half_rows, LANES)
             turned = block.astype(f32).T.astype(jnp.bfloat16)
-            left, right = weight_pair(weight_ref, seats, pencil)
+            left, right = weight_pair(weight_ref, seats, pencil, own)
             total = total + dot(turned[:bins], left) + dot(turned[bins:], right)
         logits_ref[...] = total
         rates = jax.nn.softplus(total) + rate_floor
@@ -581,12 +638,13 @@
         kernel, "head_rates", me, 1, inputs, [whole(x) for x in inputs],
         [shape((bins, own), f32), shape((8, own), f32)],
         [pl.BlockSpec((bins, own), lambda i, me: (0, 0)), pl.BlockSpec((8, own), lambda i, me: (0, 0))],
-        [], 2 * bins * groups * peers * pencil * own,
+        [], 2 * bins * groups * peers * pencil * own, near=range(7),
     )
 
 
 def head_grads(me, logits, sums, mine, other, counts, peers):
-    groups, half, own = mine.shape
+    groups, half, _ = mine.shape
+    own = counts.shape[1]
     seats = peers // 2
     pencil = half // seats
     bins = LANES // 2
@@ -612,7 +670,7 @@
         in_right = jnp.concatenate([none, grads], axis=0)
         across = (((1,), (1,)), ((), ()))
         for weight_ref, place in ((mine_ref, odd), (other_ref, 1 - odd)):
-            left, right = weight_pair(weight_ref, seats, pencil)
+            left, right = weight_pair(weight_ref, seats, pencil, own)
             part = lax.dot_general(left, in_left, across, preferred_element_type=f32)
             part = part + lax.dot_general(right, in_right, across, preferred_element_type=f32)
             out_ref[:, pl.ds(place * seats, seats)] = part.astype(bf16).reshape(groups, seats, pencil // 2, LANES)
@@ -623,7 +681,7 @@
         kernel, "head_grads", me, 1, inputs, [whole(x) for x in inputs],
         [out, shape((8, LANES), f32)],
         [pl.BlockSpec(out.shape, lambda i, me: (0, 0, 0, 0)), pl.BlockSpec((8, LANES), lambda i, me: (0, 0))],
-        [], 4 * bins * groups * peers * pencil * own,
+        [], 4 * bins * groups * peers * pencil * own, near=(0, 1, 2, 3, 4, 6),
     )
 
 
@@ -653,7 +711,7 @@
         [shape((2 * half_rows, peers * bins), f32)] + [packed] * peers,
         [pl.BlockSpec((2 * half_rows, peers * bins), lambda i, me: (0, 0))]
         + [pl.BlockSpec(packed.shape, lambda i, me: (0, 0))] * peers,
-        [pltpu.VMEM((peers, half_rows, LANES), f32)], back.size,
+        [pltpu.VMEM((peers, half_rows, LANES), f32)], back.size, near=(0, 1),
     )
     return out[0], out[1:]
 
@@ -663,58 +721,85 @@
     _, channels, width = projections.shape
     pencil = channels // peers
     rows = pencil // chunks
-    bins = width // POOL
     tiles = width // LANES
     each = LANES // POOL
     f32, bf16 = jnp.float32, jnp.bfloat16
 
-    def kernel(me_ref, keyed_ref, valued_ref, spread_ref, *refs):
-        mixed_refs, grad_refs, corr_refs = refs[:peers], refs[peers : 2 * peers], refs[2 * peers : 3 * peers]
-        out_ref, lhs = refs[-2:]
+    def kernel(me_ref, spread_ref, proj_ref, *refs):
+        grad_refs, mixed_refs, corr_refs = refs[:peers], refs[peers : 2 * peers], refs[2 * peers : 3 * peers]
+        out_ref, pair, far, done, lhs, sems, out_sems = refs[-7:]
         place = lax.broadcasted_iota(jnp.int32, (ROWS, LANES), 1) // each
         zero = jnp.zeros((ROWS, LANES), f32)
+
+        def here(k):
+            return pl.ds(pl.multiple_of((me_ref[0] ^ k) * pencil + chunk * rows, rows), rows)
+
+        def fetch(k):
+            return (
+                pltpu.make_async_copy(mixed_refs[k].at[pl.ds(chunk * rows, rows)], far.at[k, 0], sems.at[k, 0]),
+                pltpu.make_async_copy(corr_refs[k], far.at[k, 1], sems.at[k, 1]),
+                pltpu.make_async_copy(proj_ref.at[1, here(k)], pair.at[k, 0], sems.at[k, 2]),
+                pltpu.make_async_copy(proj_ref.at[2, here(k)], pair.at[k, 1], sems.at[k, 3]),
+            )
+
+        def leave(k, plane):
+            return pltpu.make_async_copy(done.at[k, plane], out_ref.at[plane, here(k)], out_sems.at[k, plane])
+
         for k in range(peers):
-
-            @pl.when(pl.program_id(0) == k)
-            def _():
-                for i in range(rows // ROWS):
-                    part = slice(i * ROWS, (i + 1) * ROWS)
-                    source = (chunk * rows + i * ROWS) // (2 * ROWS) * ROWS
-                    side = (chunk * rows // ROWS + i) % 2
-                    pair = grad_refs[k][source : source + ROWS, :]
-                    high = pair.astype(bf16).astype(f32)
-                    low = pair - high
-                    for t in range(tiles):
-                        here = place == t + side * tiles
-                        lhs[t * ROWS : (t + 1) * ROWS, :LANES] = jnp.where(here, high, zero).astype(bf16)
-                        lhs[t * ROWS : (t + 1) * ROWS, LANES:] = jnp.where(here, low, zero).astype(bf16)
-                    grad = dot(lhs[...], spread_ref[...])
-                    for t in range(tiles):
-                        lanes = slice(t * LANES, (t + 1) * LANES)
-                        mixed = mixed_refs[k][part, lanes].astype(f32)
-                        out_ref[0, part, lanes] = grad[t * ROWS : (t + 1) * ROWS] * mixed
-                    corr = corr_refs[k][part, :].astype(f32)
-                    out_ref[1, part, :] = corr * valued_ref[0, part, :].astype(f32)
-                    out_ref[2, part, :] = corr * keyed_ref[0, part, :].astype(f32)
-
-    inputs = [projections, projections, spread, *mixed_home, *grad_home, *corr_home]
-    in_specs = [
-        pl.BlockSpec((1, rows, width), lambda i, me: (1, (me[0] ^ i) * chunks + chunk, 0)),
-        pl.BlockSpec((1, rows, width), lambda i, me: (2, (me[0] ^ i) * chunks + chunk, 0)),
-        whole(spread),
-    ]
-    in_specs += [pl.BlockSpec((rows, width), lambda i, me: (chunk, 0))] * peers
-    in_specs += [whole(x) for x in [*grad_home, *corr_home]]
+            for copy in fetch(k):
+                copy.start()
+        for k in range(peers):
+            mixed_copy, corr_copy, keyed_copy, valued_copy = fetch(k)
+            corr_copy.wait()
+            keyed_copy.wait()
+            valued_copy.wait()
+            corr = far[k, 1].astype(f32)
+            done[k, 1] = corr * pair[k, 1].astype(f32)
+            leave(k, 1).start()
+            done[k, 2] = corr * pair[k, 0].astype(f32)
+            leave(k, 2).start()
+            mixed_copy.wait()
+            for i in range(rows // ROWS):
+                part = slice(i * ROWS, (i + 1) * ROWS)
+                source = (chunk * rows + i * ROWS) // (2 * ROWS) * ROWS
+                side = (chunk * rows // ROWS + i) % 2
+                grads = grad_refs[k][source : source + ROWS, :]
+                high = grads.astype(bf16).astype(f32)
+                low = grads - high
+                for t in range(tiles):
+                    near = place == t + side * tiles
+                    lhs[i, t * ROWS : (t + 1) * ROWS, :LANES] = jnp.where(near, high, zero).astype(bf16)
+                    lhs[i, t * ROWS : (t + 1) * ROWS, LANES:] = jnp.where(near, low, zero).astype(bf16)
+                grad = dot(lhs[i], spread_ref[...])
+                for t in range(tiles):
+                    lanes = slice(t * LANES, (t + 1) * LANES)
+                    done[k, 0, part, lanes] = grad[t * ROWS : (t + 1) * ROWS] * far[k, 0, part, lanes].astype(f32)
+            leave(k, 0).start()
+        for k in range(peers):
+            for plane in range(3):
+                leave(k, plane).wait()
+
+    inputs = [spread, projections, *grad_home, *mixed_home, *corr_home]
+    in_specs = [whole(spread), pl.BlockSpec(memory_space=pltpu.HBM)]
+    in_specs += [whole(x) for x in grad_home]
+    in_specs += [pl.BlockSpec(memory_space=pl.ANY)] * (2 * peers)
     aliases = {}
     if before is not None:
         aliases = {1 + len(inputs): 0}
         inputs.append(before)
         in_specs.append(pl.BlockSpec(memory_space=pl.ANY))
     return call(
-        kernel, "finish", me, peers, inputs, in_specs,
-        [shape((3, channels, width), f32)],
-        [pl.BlockSpec((3, rows, width), lambda i, me: (0, (me[0] ^ i) * chunks + chunk, 0))],
-        [pltpu.VMEM((tiles * ROWS, 2 * LANES), bf16)], 4 * channels * width, aliases,
+        kernel, "finish", me, 1, inputs, in_specs,
+        [shape((3, channels, width), f32)], [pl.BlockSpec(memory_space=pltpu.HBM)],
+        [
+            pltpu.VMEM((peers, 2, rows, width), bf16),
+            pltpu.VMEM((peers, 2, rows, width), bf16),
+            pltpu.VMEM((peers, 3, rows, width), f32),
+            pltpu.VMEM((rows // ROWS, tiles * ROWS, 2 * LANES), bf16),
+            pltpu.SemaphoreType.DMA((peers, 4)),
+            pltpu.SemaphoreType.DMA((peers, 3)),
+        ],
+        rows * peers * 0.03 * MICROSECOND, aliases, near=(0, *range(2, 2 + 3 * peers)),
     )[0]
 
 
@@ -751,26 +836,23 @@
     tables = transform_tables(length)
     gather, spread = pool_tables()
 
-    laid = lay_out(me, projections, filter_taps, peers, chunks)
+    laid, me_next = [], me
+    for j in range(chunks):
+        laid.append(lay_out(me_next, projections, filter_taps, peers, j, chunks))
+        me_next, _ = lax.optimization_barrier((me, laid[j]))
     pieces = [[swap(laid[j][k], k, peers) for k in range(peers)] for j in range(chunks)]
     skip = lax.dynamic_index_in_dim(skip_gain.reshape(peers, pencil, 1), seat, axis=0, keepdims=False)
 
-    me_late, _ = lax.optimization_barrier((me, laid[chunks - 1][0]))
-    mine = by_track(me_late, head_weight, groups)
+    mine = by_track(me_next, head_weight, groups)
     mine = lax.all_to_all(mine, "chan", split_axis=0, concat_axis=0, tiled=True)
-    other = swap(mine, 1, peers)
 
     mixed, specs = None, []
     for j in range(chunks):
         mixed, spec = convolve(me, pieces[j], skip, tables, pencil, j * rows, mixed)
         specs.append(spec)
         if j == 0:
-            seat_late, _ = lax.optimization_barrier((seat, spec))
-            query_blocks = projections[0].reshape(peers, pencil, width)
-            queries = [
-                swap(lax.dynamic_index_in_dim(query_blocks, seat_late ^ k, axis=0, keepdims=False), k, peers)
-                for k in range(peers)
-            ]
+            queries, _ = lax.optimization_barrier((laid[-1][peers:], pieces[0]))
+            queries = [swap(queries[k], k, peers) for k in range(peers)]
     mixed_out, sent = pool(me, queries, mixed, gather, groups)
     mixed_home = [swap(mixed_out[k], k, peers) for k in range(peers)]
 
@@ -780,6 +862,8 @@
         return flat.reshape(blocks.shape)
 
     got = exchange(sent)
+    mine, _ = lax.optimization_barrier((mine, sent))
+    other = swap(mine, 1, peers)
     own_bias = lax.dynamic_slice_in_dim(head_bias, group * own_tracks, own_tracks).reshape(1, own_tracks)
     own_counts = lax.dynamic_slice_in_dim(counts, group * own_tracks, own_tracks, axis=1)
     logits, sums = head_rates(me, got, mine, other, own_bias, own_counts)

time: 139 us -> 120 us (0.86)
  local copies, waits for them, and re-layouts: 32.7 us -> 3.17 us
  Pallas kernels: 37.3 us -> 53.4 us
  waiting for transfers between devices: 22.1 us -> 15.9 us
  starting transfers between devices: 36.8 us -> 38.4 us
    unnamed x86 -> x36, local copies, waits for them, and re-layouts: 26.8 us -> 1.59 us
    pallas_call x12 -> x13, Pallas kernels: 37.3 us -> 53.4 us  [call(): pl.pallas_call(kernel, name=name, grid_spec=pltpu.PrefetchScalarGridSpec(...]
    ppermute x22, waiting for transfers between devices: 12.4 us -> 3.67 us  [swap(): return lax.ppermute(value, 'seq', [(i, i ^ k) for i in range(count)])]
    all_to_all x2, waiting for transfers between devices: 6.63 us -> 9.37 us  [exchange(): lax.all_to_all(flat, ('chan', 'seq'), split_axis=0, concat_axis=0, tiled=...]
    ppermute x22, starting transfers between devices: 17.2 us -> 19.7 us  [swap(): return lax.ppermute(value, 'seq', [(i, i ^ k) for i in range(count)])]
    all_to_all x1 -> x0, local copies, waits for them, and re-layouts: 1.48 us -> none  [aligned(): mine = lax.all_to_all(mine, 'chan', split_axis=0, concat_axis=0, tiled=True)]
    ppermute x1 -> x0, local copies, waits for them, and re-layouts: 1.48 us -> none  [swap(): return lax.ppermute(value, 'seq', [(i, i ^ k) for i in range(count)])]
  transfers between devices with their start and end apart: 28 -> 28, of which waited for: 8 -> 5; matrix products, arithmetic and copies ran while one was open for 3% -> 1% of each run, Pallas kernels for 21% -> 38%
where the time goes in v3:
time: 120 us; the launch traced here: 119 us
  Pallas kernels  53.4 us (44%)
  starting transfers between devices  38.4 us (32%)
  waiting for transfers between devices  15.9 us (13%)
  blocking collectives  5.67 us (5%)
  local copies, waits for them, and re-layouts  3.17 us (3%)
  between operations  2.73 us (2%)
    pallas_call x13, Pallas kernels, call(): pl.pallas_call(kernel, name=name, grid_spec=pltpu.PrefetchScalarGridSpec(...  53.4 us
    ppermute x22, starting transfers between devices, swap(): return lax.ppermute(value, 'seq', [(i, i ^ k) for i in range(count)])  19.7 us
    all_to_all x2, waiting for transfers between devices, exchange(): lax.all_to_all(flat, ('chan', 'seq'), split_axis=0, concat_axis=0, tiled=...  9.37 us
    all_to_all x2, starting transfers between devices, exchange(): lax.all_to_all(flat, ('chan', 'seq'), split_axis=0, concat_axis=0, tiled=...  7.18 us
    ppermute x3, starting transfers between devices, aligned(): lax.ppermute(loss, 'chan', [(i, i ^ step) for i in range(groups)])  5.79 us
    all_to_all x1, starting transfers between devices, aligned(): mine = lax.all_to_all(mine, 'chan', split_axis=0, concat_axis=0, tiled=True)  5.7 us
    all_gather x1, blocking collectives, aligned(): all_sums = lax.all_gather(sums, 'seq')  5.67 us
    ppermute x22, waiting for transfers between devices, swap(): return lax.ppermute(value, 'seq', [(i, i ^ k) for i in range(count)])  3.67 us
  transfers between devices with their start and end apart: 28, of which 5 were waited for; matrix products, arithmetic and copies ran while one was open for 1% of the time, Pallas kernels for 38%

profile of v3, /device:TPU:1, one launch (start us, length us, event | category | flops | bytes accessed | tf_op | source)
XLA Modules:
  0.0 119.3 jit_solution(11164305663114072047)
XLA Ops:
  0.7 2.6 %lay_out.2 = (bf16[2,32,2048]{2,1,0:T(8,128)(2,1)}, bf16[2,32,2048]{2,1,0:T(8,128)(2,1)}, bf16[2,32,2048]{2,1,0:T(8,128)(2,1)}, bf16[2,32,2048]{2,1,0:T(8,128)(2,1)}) custom-call(s32[1]{0:T(128)} %bitcast.me_ref.refs_0_, bf16[3,256,2048]{2,1,0:T(8,128)(2,1)} %proj_ref.7, f32[256,2048]{1,0:T(8,128)} %taps_ref.3), custom_call_target="tpu_custom_call" | custom-call | flops 1920000000 | bytes 6291456 | tf_op jit(solution)/shard_map/lay_out/pallas_call | solution.py:366
  3.3 2.7 %collective-permute-start.1 = (bf16[2,32,2048]{2,1,0:T(8,128)(2,1)}, bf16[2,32,2048]{2,1,0:T(8,128)(2,1)}, u32[]{:S(2)}, u32[]{:S(2)}) collective-permute-start(bf16[2,32,2048]{2,1,0:T(8,128)(2,1)} %get-tuple-element.49), channel_id=1, source_target_pairs={{0,16},{8,24},{16,0},{24,8},{1,17},{9,25},{17,1},{25,9},{2,18},{10... | collective-permute-start | bytes 786440 | tf_op jit(solution)/shard_map/ppermute | solution.py:809
  6.1 3.1 %lay_out.3 = (bf16[2,32,2048]{2,1,0:T(8,128)(2,1)}, bf16[2,32,2048]{2,1,0:T(8,128)(2,1)}, bf16[2,32,2048]{2,1,0:T(8,128)(2,1)}, bf16[2,32,2048]{2,1,0:T(8,128)(2...) custom-call(s32[1]{0:T(128)} %bitcast.me_ref.refs_0_, ...), custom_call_target="tpu_custom_call" | custom-call | flops 1920000000 | bytes 7340032 | tf_op jit(solution)/shard_map/lay_out/pallas_call | solution.py:366
  9.6 1.4 %collective-permute-start.7 = (bf16[2,32,2048]{2,1,0:T(8,128)(2,1)}, bf16[2,32,2048]{2,1,0:T(8,128)(2,1)}, u32[]{:S(2)}, u32[]{:S(2)}) collective-permute-start(bf16[2,32,2048]{2,1,0:T(8,128)(2,1)} %get-tuple-element.62), channel_id=1, source_target_pairs={{0,16},{8,24},{16,0},{24,8},{1,17},{9,25},{17,1},{25,9},{2,18},{10... | collective-permute-start | bytes 786440 | tf_op jit(solution)/shard_map/ppermute | solution.py:809
  11.0 3.7 %by_track.1 = bf16[8,128,512]{2,1,0:T(8,128)(2,1)} custom-call(s32[1]{0:T(128)} %bitcast.me_ref.refs_0_, bf16[256,3840]{1,0:T(8,128)(2,1)} %weight_ref.1), custom_call_target="tpu_custom_call" | custom-call | flops 2000000000 | bytes 3014656 | tf_op jit(solution)/shard_map/by_track/pallas_call | solution.py:366
  14.7 5.7 %all-to-all-start.1 = ((bf16[8,128,512]{2,1,0:T(8,128)(2,1)}), bf16[8,128,512]{2,1,0:T(8,128)(2,1)S(1)}, u32[]{:S(2)}, u32[]{:S(2)}) async-start(bf16[8,128,512]{2,1,0:T(8,128)(2,1)} %by_track.1), calls=%async_computation.1 | async-start | bytes 2097152 | tf_op jit(solution)/shard_map/all_to_all | solution.py:847
  20.6 1.1 collective-permute-start.8
  21.8 1.3 %collective-permute-start.4 = (bf16[64,2048]{1,0:T(8,128)(2,1)S(1)}, bf16[64,2048]{1,0:T(8,128)(2,1)S(1)}, u32[]{:S(2)}, u32[]{:S(2)}) collective-permute-start(bf16[64,2048]{1,0:T(8,128)(2,1)S(1)} %copy-done.11), channel_id=1, source_target_pairs={{0,16},{8,24},{16,0},{24,8},{1,17},{9,25},{17,1},{25,9},{2,18},{10... | collective-permute-start | bytes 786440 | tf_op jit(solution)/shard_map/ppermute | solution.py:809
  23.1 8.4 %long_convolution.2 = (f32[64,8192]{1,0:T(8,128)S(1)}, f32[2,1024,256]{2,1,0:T(8,128)}) custom-call(s32[1]{0:T(128)} %bitcast.me_ref.refs_0_, bf16[2,32,2048]{2,1,0:T(8,128)(2,1)} %get-tuple-element.47.refs_1_, bf16[2,32,2048]{2,1,0:T(8,128)(2,1)} %copy-done.15, bf16[2,32,2048]{2,1,0:T(8,128)(2,1)} %collective-permute-done.1.refs_3_, ...), custom_call_target="tpu_custom_call" | custom-call | flops 8192000000 | bytes 5832960 | tf_op jit(solution)/shard_map/long_convolution/pallas_call | solution.py:366
  33.1 8.3 %long_convolution.3 = (f32[64,8192]{1,0:T(8,128)S(1)}, f32[2,1024,256]{2,1,0:T(8,128)}) custom-call(s32[1]{0:T(128)} %bitcast.me_ref.refs_0_, bf16[2,32,2048]{2,1,0:T(8,128)(2,1)} %get-tuple-element.60.refs_1_, bf16[2,32,2048]{2,1,0:T(8,128)(2,1)} %copy-done.14, ...), custom_call_target="tpu_custom_call", output_to_operand_aliasing={{0}: (9, {})} | custom-call | flops 8192000000 | bytes 7930112 | tf_op jit(solution)/shard_map/long_convolution/pallas_call | solution.py:366
  42.3 3.1 %pool_bins.1 = (bf16[64,2048]{1,0:T(8,128)(2,1)}, bf16[64,2048]{1,0:T(8,128)(2,1)}, bf16[64,2048]{1,0:T(8,128)(2,1)}, bf16[64,2048]{1,0:T(8,128)(2,1)}, bf16[8,4,32,128]{3,2,1,0:T(8,128)(2,1)}) custom-call(s32[1]{0:T(128)} %bitcast.me_ref.refs_0_, bf16[64,2048]{1,0:T(8,128)(2,1)} %get-tuple-element.56.refs_1_, bf16[64,2048]{1,0:T(8,128)(2,1)} %copy-done.7, ...), custom_call_target="tpu_custom_call" | custom-call | flops 4096000000 | bytes 4521984 | tf_op jit(solution)/shard_map/pool_bins/pallas_call | solution.py:366
  45.4 1.7 %collective-permute-start.9 = (bf16[8,128,512]{2,1,0:T(8,128)(2,1)S(1)}, bf16[8,128,512]{2,1,0:T(8,128)(2,1)S(1)}, u32[]{:S(2)}, u32[]{:S(2)}) collective-permute-start(bf16[8,128,512]{2,1,0:T(8,128)(2,1)S(1)} %all-to-all-done.1.mine_ref), channel_id=1, source_target_pairs={{0,8},{8,0},{16,24},{24,16},{1,9},{9,1},{17,25},{25,17},{2,10},{10... | collective-permute-start | bytes 3145736 | tf_op jit(solution)/shard_map/ppermute | solution.py:809
  47.1 4.7 %all-to-all-start = ((bf16[32,32,128]{2,1,0:T(8,128)(2,1)}), bf16[32,32,128]{2,1,0:T(8,128)(2,1)S(1)}, u32[]{:S(2)}, u32[]{:S(2)}) async-start(bf16[32,32,128]{2,1,0:T(8,128)(2,1)} %bitcast.15), calls=%async_computation | async-start | bytes 524288 | tf_op jit(solution)/shard_map/all_to_all | solution.py:861
  52.7 9.4 %all-to-all-done = bf16[32,32,128]{2,1,0:T(8,128)(2,1)S(1)} async-done(((bf16[32,32,128]{2,1,0:T(8,128)(2,1)}), bf16[32,32,128]{2,1,0:T(8,128)(2,1)S(1)}, u32[]{:S(2)}, u32[]{:S(2)}) %all-to-all-start) | async-done | bytes 262176 | tf_op jit(solution)/shard_map/all_to_all | solution.py:861
  62.7 5.7 %all-gather = f32[32,480]{1,0:T(8,128)S(1)} all-gather(f32[8,480]{1,0:T(8,128)S(1)} %get-tuple-element.70), channel_id=2, replica_groups=mesh['seq'=4,'chan'=8] {'seq'}, dimensions={0}, use_global_device_ids=true | all-gather | bytes 76800 | tf_op jit(solution)/shard_map/all_gather | solution.py:870
  68.4 1.5 %head_grads.1 = (bf16[8,4,32,128]{3,2,1,0:T(8,128)(2,1)}, f32[8,128]{1,0:T(8,128)S(1)}) custom-call(s32[1]{0:T(128)} %bitcast.me_ref.refs_0_, f32[64,480]{1,0:T(8,128)S(1)} %get-tuple-element.69.logits_ref, f32[4,8,480]{2,1,0:T(8,128)S(1)} %bitcast.12, bf16[8,128,512]{2,1,0:T(8,128)(2,1)S(1)} %all-to-all-done.1.mine_ref, ...), custom_call_target="tpu_custom_call" | custom-call | flops 251658240 | bytes 2670592 | tf_op jit(solution)/shard_map/head_grads/pallas_call | solution.py:366
  69.8 2.5 %all-to-all-start.2 = ((bf16[32,32,128]{2,1,0:T(8,128)(2,1)}), bf16[32,32,128]{2,1,0:T(8,128)(2,1)S(1)}, u32[]{:S(2)}, u32[]{:S(2)}) async-start(bf16[32,32,128]{2,1,0:T(8,128)(2,1)} %bitcast.14), calls=%async_computation.2 | async-start | bytes 524288 | tf_op jit(solution)/shard_map/all_to_all | solution.py:861
  72.4 1.3 %collective-permute-start.10 = (f32[8,128]{1,0:T(8,128)S(1)}, f32[8,128]{1,0:T(8,128)S(1)}, u32[]{:S(2)}, u32[]{:S(2)}) collective-permute-start(f32[8,128]{1,0:T(8,128)S(1)} %get-tuple-element.71), channel_id=1, source_target_pairs={{0,1},{1,0},{2,3},{3,2},{4,5},{5,4},{6,7},{7,6},{8,9},{9,8},{10,11... | collective-permute-start | bytes 12296 | tf_op jit(solution)/shard_map/ppermute | solution.py:875
  73.7 1.4 %collective-permute-done.10 = f32[8,128]{1,0:T(8,128)S(1)} collective-permute-done((f32[8,128]{1,0:T(8,128)S(1)}, f32[8,128]{1,0:T(8,128)S(1)}, u32[]{:S(2)}, u32[]{:S(2)}) %collective-permute-start.10) | collective-permute-done | bytes 4128 | tf_op jit(solution)/shard_map/ppermute | solution.py:875
  75.1 1.2 %collective-permute-start.11 = (f32[8,128]{1,0:T(8,128)S(1)}, f32[8,128]{1,0:T(8,128)S(1)}, u32[]{:S(2)}, u32[]{:S(2)}) collective-permute-start(f32[8,128]{1,0:T(8,128)S(1)} %add.19), channel_id=1, source_target_pairs={{0,2},{1,3},{2,0},{3,1},{4,6},{5,7},{6,4},{7,5},{8,10},{9,11},{10,... | collective-permute-start | bytes 12296 | tf_op jit(solution)/shard_map/ppermute | solution.py:875
  76.3 1.5 %collective-permute-done.11 = f32[8,128]{1,0:T(8,128)S(1)} collective-permute-done((f32[8,128]{1,0:T(8,128)S(1)}, f32[8,128]{1,0:T(8,128)S(1)}, u32[]{:S(2)}, u32[]{:S(2)}) %collective-permute-start.11) | collective-permute-done | bytes 4128 | tf_op jit(solution)/shard_map/ppermute | solution.py:875
  77.8 3.2 %collective-permute-start.12 = (f32[8,128]{1,0:T(8,128)S(1)}, f32[8,128]{1,0:T(8,128)S(1)}, u32[]{:S(2)}, u32[]{:S(2)}) collective-permute-start(f32[8,128]{1,0:T(8,128)S(1)} %add.20), channel_id=1, source_target_pairs={{0,4},{1,5},{2,6},{3,7},{4,0},{5,1},{6,2},{7,3},{8,12},{9,13},{10,... | collective-permute-start | bytes 12296 | tf_op jit(solution)/shard_map/ppermute | solution.py:875
  81.0 1.6 %collective-permute-start.16 = (bf16[64,2048]{1,0:T(8,128)(2,1)}, bf16[64,2048]{1,0:T(8,128)(2,1)S(1)}, u32[]{:S(2)}, u32[]{:S(2)}) collective-permute-start(bf16[64,2048]{1,0:T(8,128)(2,1)} %get-tuple-element.78), channel_id=1, source_target_pairs={{0,8},{8,0},{16,24},{24,16},{1,9},{9,1},{17,25},{25,17},{2,10},{10... | collective-permute-start | bytes 786440 | tf_op jit(solution)/shard_map/ppermute | solution.py:809
  82.6 1.6 %collective-permute-start.17 = (bf16[64,2048]{1,0:T(8,128)(2,1)}, bf16[64,2048]{1,0:T(8,128)(2,1)S(1)}, u32[]{:S(2)}, u32[]{:S(2)}) collective-permute-start(bf16[64,2048]{1,0:T(8,128)(2,1)} %get-tuple-element.79), channel_id=1, source_target_pairs={{0,16},{8,24},{16,0},{24,8},{1,17},{9,25},{17,1},{25,9},{2,18},{10... | collective-permute-start | bytes 786440 | tf_op jit(solution)/shard_map/ppermute | solution.py:809
  86.9 1.1 collective-permute-start.14
  87.9 7.0 %long_correlation.3 = (bf16[32,2048]{1,0:T(8,128)(2,1)}, bf16[32,2048]{1,0:T(8,128)(2,1)}, bf16[32,2048]{1,0:T(8,128)(2,1)}, bf16[32,2048]{1,0:T(8,128)(2,1)}) custom-call(s32[1]{0:T(128)} %bitcast.me_ref.refs_0_, bf16[64,2048]{1,0:T(8,128)(2,1)} %get-tuple-element.56.refs_1_, bf16[64,2048]{1,0:T(8,128)(2,1)} %copy-done.7, bf16[64,2048]{1,0:T(8,128)(2,1)} %copy-done.8, ...), custom_call_target="tpu_custom_call" | custom-call | flops 8192000000 | bytes 4391168 | tf_op jit(solution)/shard_map/long_correlation/pallas_call | solution.py:366
  96.8 1.9 %collective-permute-start.23 = (bf16[32,2048]{1,0:T(8,128)(2,1)}, bf16[32,2048]{1,0:T(8,128)(2,1)S(1)}, u32[]{:S(2)}, u32[]{:S(2)}) collective-permute-start(bf16[32,2048]{1,0:T(8,128)(2,1)} %get-tuple-element.90), channel_id=1, source_target_pairs={{0,16},{8,24},{16,0},{24,8},{1,17},{9,25},{17,1},{25,9},{2,18},{10... | collective-permute-start | bytes 393224 | tf_op jit(solution)/shard_map/ppermute | solution.py:809
  98.7 7.2 %long_correlation.2 = (bf16[32,2048]{1,0:T(8,128)(2,1)}, bf16[32,2048]{1,0:T(8,128)(2,1)}, bf16[32,2048]{1,0:T(8,128)(2,1)}, bf16[32,2048]{1,0:T(8,128)(2,1)}) custom-call(s32[1]{0:T(128)} %bitcast.me_ref.refs_0_, bf16[64,2048]{1,0:T(8,128)(2,1)} %get-tuple-element.56.refs_1_, bf16[64,2048]{1,0:T(8,128)(2,1)} %copy-done.7, bf16[64,2048]{1,0:T(8,128)(2,1)} %copy-done.8, ...), custom_call_target="tpu_custom_call" | custom-call | flops 8192000000 | bytes 4391168 | tf_op jit(solution)/shard_map/long_correlation/pallas_call | solution.py:366
  106.2 1.5 %collective-permute-start.20 = (bf16[32,2048]{1,0:T(8,128)(2,1)}, bf16[32,2048]{1,0:T(8,128)(2,1)S(1)}, u32[]{:S(2)}, u32[]{:S(2)}) collective-permute-start(bf16[32,2048]{1,0:T(8,128)(2,1)} %get-tuple-element.85), channel_id=1, source_target_pairs={{0,16},{8,24},{16,0},{24,8},{1,17},{9,25},{17,1},{25,9},{2,18},{10... | collective-permute-start | bytes 393224 | tf_op jit(solution)/shard_map/ppermute | solution.py:809
  108.2 3.7 %finish.2.refs_12_ = f32[3,256,2048]{2,1,0:T(8,128)} custom-call(s32[1]{0:T(128)} %bitcast.me_ref.refs_0_, bf16[256,128]{1,0:T(8,128)(2,1)S(1)} %copy-done.3, bf16[3,256,2048]{2,1,0:T(8,128)(2,1)} %proj_ref.7, f32[32,128]{1,0:T(8,128)S(1)} %copy-done.4, f32[32,128]{1,0:T(8,128)S(1)} %collective-permute-done.13.refs_1_, ...), custom_call_target="tpu_custom_call" | custom-call | flops 3840000000 | bytes 11141120 | tf_op jit(solution)/shard_map/finish/pallas_call | solution.py:366
  111.9 2.6 %collective-permute-done.21.refs_11_ = bf16[32,2048]{1,0:T(8,128)(2,1)S(1)} collective-permute-done((bf16[32,2048]{1,0:T(8,128)(2,1)}, bf16[32,2048]{1,0:T(8,128)(2,1)S(1)}, u32[]{:S(2)}, u32[]{:S(2)}) %collective-permute-start.21) | collective-permute-done | bytes 131104 | tf_op jit(solution)/shard_map/ppermute | solution.py:809
  114.5 3.7 %finish.3 = f32[3,256,2048]{2,1,0:T(8,128)} custom-call(s32[1]{0:T(128)} %bitcast.me_ref.refs_0_, bf16[256,128]{1,0:T(8,128)(2,1)S(1)} %copy-done.3, bf16[3,256,2048]{2,1,0:T(8,128)(2,1)} %proj_ref.7, f32[32,128]{1,0:T(8,128)S(1)} %copy-done.4, f32[32,128]{1,0:T(8,128)S(1)} %collective-permute-done.13.refs_1_, ...), custom_call_target="tpu_custom_call", output_to_operand_aliasing={{}: (15, {})} | custom-call | flops 3840000000 | bytes 17432576 | tf_op jit(solution)/shard_map/finish/pallas_call | solution.py:366
  (83 shorter events, 9.5 us)
Async XLA Ops:
  0.6 51.9 %copy-start = (s32[64,3840]{1,0:T(8,128)S(1)}, s32[64,3840]{1,0:T(8,128)}, u32[]{:S(2)}) copy-start(s32[64,3840]{1,0:T(8,128)} %param.16) | copy-start | bytes 2949124
  3.2 17.4 %collective-permute-start = (bf16[2,32,2048]{2,1,0:T(8,128)(2,1)}, bf16[2,32,2048]{2,1,0:T(8,128)(2,1)S(1)}, u32[]{:S(2)}, u32[]{:S(2)}) collective-permute-start(bf16[2,32,2048]{2,1,0:T(8,128)(2,1)} %get-tuple-element.48), channel_id=1, source_target_pairs={{0,8},{8,0},{16,24},{24,16},{1,9},{9,1},{17,25},{25,17},{2,10},{10... | collective-permute-start | bytes 786440 | tf_op jit(solution)/shard_map/ppermute | solution.py:809
  3.3 18.4 %collective-permute-start.1 = (bf16[2,32,2048]{2,1,0:T(8,128)(2,1)}, bf16[2,32,2048]{2,1,0:T(8,128)(2,1)}, u32[]{:S(2)}, u32[]{:S(2)}) collective-permute-start(bf16[2,32,2048]{2,1,0:T(8,128)(2,1)} %get-tuple-element.49), channel_id=1, source_target_pairs={{0,16},{8,24},{16,0},{24,8},{1,17},{9,25},{17,1},{25,9},{2,18},{10... | collective-permute-start | bytes 786440 | tf_op jit(solution)/shard_map/ppermute | solution.py:809
  6.0 15.7 %collective-permute-start.2 = (bf16[2,32,2048]{2,1,0:T(8,128)(2,1)}, bf16[2,32,2048]{2,1,0:T(8,128)(2,1)}, u32[]{:S(2)}, u32[]{:S(2)}) collective-permute-start(bf16[2,32,2048]{2,1,0:T(8,128)(2,1)} %get-tuple-element.50), channel_id=1, source_target_pairs={{0,24},{8,16},{16,8},{24,0},{1,25},{9,17},{17,9},{25,1},{2,26},{10... | collective-permute-start | bytes 786440 | tf_op jit(solution)/shard_map/ppermute | solution.py:809
  9.1 22.3 %collective-permute-start.6 = (bf16[2,32,2048]{2,1,0:T(8,128)(2,1)}, bf16[2,32,2048]{2,1,0:T(8,128)(2,1)S(1)}, u32[]{:S(2)}, u32[]{:S(2)}) collective-permute-start(bf16[2,32,2048]{2,1,0:T(8,128)(2,1)} %get-tuple-element.61), channel_id=1, source_target_pairs={{0,8},{8,0},{16,24},{24,16},{1,9},{9,1},{17,25},{25,17},{2,10},{10... | collective-permute-start | bytes 786440 | tf_op jit(solution)/shard_map/ppermute | solution.py:809
  9.6 22.8 %collective-permute-start.7 = (bf16[2,32,2048]{2,1,0:T(8,128)(2,1)}, bf16[2,32,2048]{2,1,0:T(8,128)(2,1)}, u32[]{:S(2)}, u32[]{:S(2)}) collective-permute-start(bf16[2,32,2048]{2,1,0:T(8,128)(2,1)} %get-tuple-element.62), channel_id=1, source_target_pairs={{0,16},{8,24},{16,0},{24,8},{1,17},{9,25},{17,1},{25,9},{2,18},{10... | collective-permute-start | bytes 786440 | tf_op jit(solution)/shard_map/ppermute | solution.py:809
  14.7 30.7 %all-to-all-start.1 = ((bf16[8,128,512]{2,1,0:T(8,128)(2,1)}), bf16[8,128,512]{2,1,0:T(8,128)(2,1)S(1)}, u32[]{:S(2)}, u32[]{:S(2)}) async-start(bf16[8,128,512]{2,1,0:T(8,128)(2,1)} %by_track.1), calls=%async_computation.1 | async-start | bytes 2097152 | tf_op jit(solution)/shard_map/all_to_all | solution.py:847
  20.6 10.9 %copy-start.10 = (bf16[64,2048]{1,0:T(8,128)(2,1)S(1)}, bf16[64,2048]{1,0:T(8,128)(2,1)}, u32[]{:S(2)}) copy-start(bf16[64,2048]{1,0:T(8,128)(2,1)} %get-tuple-element.59) | copy-start | bytes 786436
  20.6 11.8 %collective-permute-start.8 = (bf16[2,32,2048]{2,1,0:T(8,128)(2,1)S(1)}, bf16[2,32,2048]{2,1,0:T(8,128)(2,1)S(1)}, u32[]{:S(2)}, u32[]{:S(2)}) collective-permute-start(bf16[2,32,2048]{2,1,0:T(8,128)(2,1)S(1)} %copy-done.13), channel_id=1, source_target_pairs={{0,24},{8,16},{16,8},{24,0},{1,25},{9,17},{17,9},{25,1},{2,26},{10... | collective-permute-start | bytes 786440 | tf_op jit(solution)/shard_map/ppermute | solution.py:809
  21.7 19.7 %collective-permute-start.3 = (bf16[64,2048]{1,0:T(8,128)(2,1)S(1)}, bf16[64,2048]{1,0:T(8,128)(2,1)S(1)}, u32[]{:S(2)}, u32[]{:S(2)}) collective-permute-start(bf16[64,2048]{1,0:T(8,128)(2,1)S(1)} %copy-done.12), channel_id=1, source_target_pairs={{0,8},{8,0},{16,24},{24,16},{1,9},{9,1},{17,25},{25,17},{2,10},{10... | collective-permute-start | bytes 786440 | tf_op jit(solution)/shard_map/ppermute | solution.py:809
  21.8 19.6 %collective-permute-start.4 = (bf16[64,2048]{1,0:T(8,128)(2,1)S(1)}, bf16[64,2048]{1,0:T(8,128)(2,1)S(1)}, u32[]{:S(2)}, u32[]{:S(2)}) collective-permute-start(bf16[64,2048]{1,0:T(8,128)(2,1)S(1)} %copy-done.11), channel_id=1, source_target_pairs={{0,16},{8,24},{16,0},{24,8},{1,17},{9,25},{17,1},{25,9},{2,18},{10... | collective-permute-start | bytes 786440 | tf_op jit(solution)/shard_map/ppermute | solution.py:809
  31.5 10.0 %collective-permute-start.5 = (bf16[64,2048]{1,0:T(8,128)(2,1)S(1)}, bf16[64,2048]{1,0:T(8,128)(2,1)S(1)}, u32[]{:S(2)}, u32[]{:S(2)}) collective-permute-start(bf16[64,2048]{1,0:T(8,128)(2,1)S(1)} %copy-done.10), channel_id=1, source_target_pairs={{0,24},{8,16},{16,8},{24,0},{1,25},{9,17},{17,9},{25,1},{2,26},{10... | collective-permute-start | bytes 786440 | tf_op jit(solution)/shard_map/ppermute | solution.py:809
  45.4 16.6 %collective-permute-start.9 = (bf16[8,128,512]{2,1,0:T(8,128)(2,1)S(1)}, bf16[8,128,512]{2,1,0:T(8,128)(2,1)S(1)}, u32[]{:S(2)}, u32[]{:S(2)}) collective-permute-start(bf16[8,128,512]{2,1,0:T(8,128)(2,1)S(1)} %all-to-all-done.1.mine_ref), channel_id=1, source_target_pairs={{0,8},{8,0},{16,24},{24,16},{1,9},{9,1},{17,25},{25,17},{2,10},{10... | collective-permute-start | bytes 3145736 | tf_op jit(solution)/shard_map/ppermute | solution.py:809
  47.1 14.9 %all-to-all-start = ((bf16[32,32,128]{2,1,0:T(8,128)(2,1)}), bf16[32,32,128]{2,1,0:T(8,128)(2,1)S(1)}, u32[]{:S(2)}, u32[]{:S(2)}) async-start(bf16[32,32,128]{2,1,0:T(8,128)(2,1)} %bitcast.15), calls=%async_computation | async-start | bytes 524288 | tf_op jit(solution)/shard_map/all_to_all | solution.py:861
  69.8 15.6 %all-to-all-start.2 = ((bf16[32,32,128]{2,1,0:T(8,128)(2,1)}), bf16[32,32,128]{2,1,0:T(8,128)(2,1)S(1)}, u32[]{:S(2)}, u32[]{:S(2)}) async-start(bf16[32,32,128]{2,1,0:T(8,128)(2,1)} %bitcast.14), calls=%async_computation.2 | async-start | bytes 524288 | tf_op jit(solution)/shard_map/all_to_all | solution.py:861
  72.4 2.7 %collective-permute-start.10 = (f32[8,128]{1,0:T(8,128)S(1)}, f32[8,128]{1,0:T(8,128)S(1)}, u32[]{:S(2)}, u32[]{:S(2)}) collective-permute-start(f32[8,128]{1,0:T(8,128)S(1)} %get-tuple-element.71), channel_id=1, source_target_pairs={{0,1},{1,0},{2,3},{3,2},{4,5},{5,4},{6,7},{7,6},{8,9},{9,8},{10,11... | collective-permute-start | bytes 12296 | tf_op jit(solution)/shard_map/ppermute | solution.py:875
  75.1 2.8 %collective-permute-start.11 = (f32[8,128]{1,0:T(8,128)S(1)}, f32[8,128]{1,0:T(8,128)S(1)}, u32[]{:S(2)}, u32[]{:S(2)}) collective-permute-start(f32[8,128]{1,0:T(8,128)S(1)} %add.19), channel_id=1, source_target_pairs={{0,2},{1,3},{2,0},{3,1},{4,6},{5,7},{6,4},{7,5},{8,10},{9,11},{10,... | collective-permute-start | bytes 12296 | tf_op jit(solution)/shard_map/ppermute | solution.py:875
  77.8 6.4 %collective-permute-start.12 = (f32[8,128]{1,0:T(8,128)S(1)}, f32[8,128]{1,0:T(8,128)S(1)}, u32[]{:S(2)}, u32[]{:S(2)}) collective-permute-start(f32[8,128]{1,0:T(8,128)S(1)} %add.20), channel_id=1, source_target_pairs={{0,4},{1,5},{2,6},{3,7},{4,0},{5,1},{6,2},{7,3},{8,12},{9,13},{10,... | collective-permute-start | bytes 12296 | tf_op jit(solution)/shard_map/ppermute | solution.py:875
  81.0 13.8 %collective-permute-start.16 = (bf16[64,2048]{1,0:T(8,128)(2,1)}, bf16[64,2048]{1,0:T(8,128)(2,1)S(1)}, u32[]{:S(2)}, u32[]{:S(2)}) collective-permute-start(bf16[64,2048]{1,0:T(8,128)(2,1)} %get-tuple-element.78), channel_id=1, source_target_pairs={{0,8},{8,0},{16,24},{24,16},{1,9},{9,1},{17,25},{25,17},{2,10},{10... | collective-permute-start | bytes 786440 | tf_op jit(solution)/shard_map/ppermute | solution.py:809
  82.6 12.9 %collective-permute-start.17 = (bf16[64,2048]{1,0:T(8,128)(2,1)}, bf16[64,2048]{1,0:T(8,128)(2,1)S(1)}, u32[]{:S(2)}, u32[]{:S(2)}) collective-permute-start(bf16[64,2048]{1,0:T(8,128)(2,1)} %get-tuple-element.79), channel_id=1, source_target_pairs={{0,16},{8,24},{16,0},{24,8},{1,17},{9,25},{17,1},{25,9},{2,18},{10... | collective-permute-start | bytes 786440 | tf_op jit(solution)/shard_map/ppermute | solution.py:809
  84.2 12.6 %collective-permute-start.18 = (bf16[64,2048]{1,0:T(8,128)(2,1)}, bf16[64,2048]{1,0:T(8,128)(2,1)S(1)}, u32[]{:S(2)}, u32[]{:S(2)}) collective-permute-start(bf16[64,2048]{1,0:T(8,128)(2,1)} %get-tuple-element.80), channel_id=1, source_target_pairs={{0,24},{8,16},{16,8},{24,0},{1,25},{9,17},{17,9},{25,1},{2,26},{10... | collective-permute-start | bytes 786440 | tf_op jit(solution)/shard_map/ppermute | solution.py:809
  86.1 12.6 %collective-permute-start.13 = (f32[32,128]{1,0:T(8,128)}, f32[32,128]{1,0:T(8,128)S(1)}, u32[]{:S(2)}, u32[]{:S(2)}) collective-permute-start(f32[32,128]{1,0:T(8,128)} %get-tuple-element.74), channel_id=1, source_target_pairs={{0,8},{8,0},{16,24},{24,16},{1,9},{9,1},{17,25},{25,17},{2,10},{10... | collective-permute-start | bytes 49160 | tf_op jit(solution)/shard_map/ppermute | solution.py:809
  86.9 19.1 %collective-permute-start.14 = (f32[32,128]{1,0:T(8,128)}, f32[32,128]{1,0:T(8,128)S(1)}, u32[]{:S(2)}, u32[]{:S(2)}) collective-permute-start(f32[32,128]{1,0:T(8,128)} %get-tuple-element.75), channel_id=1, source_target_pairs={{0,16},{8,24},{16,0},{24,8},{1,17},{9,25},{17,1},{25,9},{2,18},{10... | collective-permute-start | bytes 49160 | tf_op jit(solution)/shard_map/ppermute | solution.py:809
  94.9 11.3 %collective-permute-start.15 = (f32[32,128]{1,0:T(8,128)S(1)}, f32[32,128]{1,0:T(8,128)S(1)}, u32[]{:S(2)}, u32[]{:S(2)}) collective-permute-start(f32[32,128]{1,0:T(8,128)S(1)} %copy-done.17), channel_id=1, source_target_pairs={{0,24},{8,16},{16,8},{24,0},{1,25},{9,17},{17,9},{25,1},{2,26},{10... | collective-permute-start | bytes 49160 | tf_op jit(solution)/shard_map/ppermute | solution.py:809
  95.5 12.2 %collective-permute-start.22 = (bf16[32,2048]{1,0:T(8,128)(2,1)}, bf16[32,2048]{1,0:T(8,128)(2,1)S(1)}, u32[]{:S(2)}, u32[]{:S(2)}) collective-permute-start(bf16[32,2048]{1,0:T(8,128)(2,1)} %get-tuple-element.89), channel_id=1, source_target_pairs={{0,8},{8,0},{16,24},{24,16},{1,9},{9,1},{17,25},{25,17},{2,10},{10... | collective-permute-start | bytes 393224 | tf_op jit(solution)/shard_map/ppermute | solution.py:809
  96.8 11.4 %collective-permute-start.23 = (bf16[32,2048]{1,0:T(8,128)(2,1)}, bf16[32,2048]{1,0:T(8,128)(2,1)S(1)}, u32[]{:S(2)}, u32[]{:S(2)}) collective-permute-start(bf16[32,2048]{1,0:T(8,128)(2,1)} %get-tuple-element.90), channel_id=1, source_target_pairs={{0,16},{8,24},{16,0},{24,8},{1,17},{9,25},{17,1},{25,9},{2,18},{10... | collective-permute-start | bytes 393224 | tf_op jit(solution)/shard_map/ppermute | solution.py:809
  98.7 9.5 %collective-permute-start.24 = (bf16[32,2048]{1,0:T(8,128)(2,1)}, bf16[32,2048]{1,0:T(8,128)(2,1)S(1)}, u32[]{:S(2)}, u32[]{:S(2)}) collective-permute-start(bf16[32,2048]{1,0:T(8,128)(2,1)} %get-tuple-element.91), channel_id=1, source_target_pairs={{0,24},{8,16},{16,8},{24,0},{1,25},{9,17},{17,9},{25,1},{2,26},{10... | collective-permute-start | bytes 393224 | tf_op jit(solution)/shard_map/ppermute | solution.py:809
  98.7 9.5 %copy-start.1 = (bf16[64,2048]{1,0:T(8,128)(2,1)S(1)}, bf16[64,2048]{1,0:T(8,128)(2,1)}, u32[]{:S(2)}) copy-start(bf16[64,2048]{1,0:T(8,128)(2,1)} %get-tuple-element.77.refs_4_) | copy-start | bytes 786436
  98.7 9.5 %copy-start.3 = (bf16[256,128]{1,0:T(8,128)(2,1)S(1)}, bf16[256,128]{1,0:T(8,128)(2,1)}, u32[]{:S(2)}) copy-start(bf16[256,128]{1,0:T(8,128)(2,1)} %constant.37.clone.refs_11_.spread_ref) | copy-start | bytes 196612
  105.9 5.9 %collective-permute-start.19 = (bf16[32,2048]{1,0:T(8,128)(2,1)}, bf16[32,2048]{1,0:T(8,128)(2,1)S(1)}, u32[]{:S(2)}, u32[]{:S(2)}) collective-permute-start(bf16[32,2048]{1,0:T(8,128)(2,1)} %get-tuple-element.84), channel_id=1, source_target_pairs={{0,8},{8,0},{16,24},{24,16},{1,9},{9,1},{17,25},{25,17},{2,10},{10... | collective-permute-start | bytes 393224 | tf_op jit(solution)/shard_map/ppermute | solution.py:809
  106.2 5.6 %collective-permute-start.20 = (bf16[32,2048]{1,0:T(8,128)(2,1)}, bf16[32,2048]{1,0:T(8,128)(2,1)S(1)}, u32[]{:S(2)}, u32[]{:S(2)}) collective-permute-start(bf16[32,2048]{1,0:T(8,128)(2,1)} %get-tuple-element.85), channel_id=1, source_target_pairs={{0,16},{8,24},{16,0},{24,8},{1,17},{9,25},{17,1},{25,9},{2,18},{10... | collective-permute-start | bytes 393224 | tf_op jit(solution)/shard_map/ppermute | solution.py:809
  107.7 6.8 %collective-permute-start.21 = (bf16[32,2048]{1,0:T(8,128)(2,1)}, bf16[32,2048]{1,0:T(8,128)(2,1)S(1)}, u32[]{:S(2)}, u32[]{:S(2)}) collective-permute-start(bf16[32,2048]{1,0:T(8,128)(2,1)} %get-tuple-element.86), channel_id=1, source_target_pairs={{0,24},{8,16},{16,8},{24,0},{1,25},{9,17},{17,9},{25,1},{2,26},{10... | collective-permute-start | bytes 393224 | tf_op jit(solution)/shard_map/ppermute | solution.py:809
  (14 other events, 64.4 us)

commit v4 on v3

--- a/solution.py
+++ b/solution.py
@@ -21,6 +21,7 @@
 
 VMEM_LIMIT = 20 * 1024 * 1024
 CHUNKS = 2
+SPECTRA = 4
 MOST_GROUPS = 16
 
 
@@ -49,8 +50,8 @@
     f_hi, f_lo = split_bf16(forward)
     b_hi, b_lo = split_bf16(backward)
     return dict(
-        fwd=np.stack([f_hi, f_lo]),
-        bwd=np.stack([b_hi, b_lo]),
+        fwd=[f_hi, f_lo],
+        bwd=[b_hi, b_lo],
         twist=np.stack([np.cos(twist), -np.sin(twist)]).astype(np.float32),
     )
 
@@ -123,17 +124,21 @@
     return high, (value - high.astype(jnp.float32)).astype(jnp.bfloat16)
 
 
-def lane_transform(re_parts, im_parts, lhs, table_ref):
+def put(re_parts, im_parts, lhs, start):
     for i, (re, im) in enumerate(zip(re_parts, im_parts)):
-        rows = pl.ds(i * ROWS, ROWS)
+        rows = pl.ds(start + i * ROWS, ROWS)
         re_hi, re_lo = split(re)
         im_hi, im_lo = split(im)
         lhs[0, rows, :LANES] = re_hi
         lhs[0, rows, LANES:] = im_hi
         lhs[1, rows, :LANES] = re_lo
         lhs[1, rows, LANES:] = im_lo
+
+
+def lane_transform(lhs, table_refs):
     high = lhs[0]
-    return dot(high, table_ref[0]) + (dot(lhs[1], table_ref[0]) + dot(high, table_ref[1]))
+    table_high, table_low = table_refs[0][...], table_refs[1][...]
+    return dot(high, table_high) + (dot(lhs[1], table_high) + dot(high, table_low))
 
 
 def first_pass(load, store, outer):
@@ -189,6 +194,11 @@
             emit(rb * a + b, re if a == 0 else re * c - im * s)
 
 
+def put_product(re, im, lhs, start):
+    rows = [slice(i, i + ROWS) for i in range(0, re.shape[0], ROWS)]
+    put([re[r] for r in rows], [im[r] for r in rows], lhs, start)
+
+
 def keep(parts):
     def store(b, alpha, re, im):
         parts[0, b, alpha] = re
@@ -199,8 +209,11 @@
 
 def conv_kernel(peers, outer, me_ref, *refs):
     pieces = refs[:peers]
-    skip_ref, fwd_ref, bwd_ref, twist_ref = refs[peers : peers + 4]
-    mixed_ref, spec_ref, rows_in, parts_x, parts_h, parts_y, lhs = refs[-7:]
+    skip_ref, *tables, twist_ref = refs[peers : peers + 6]
+    fwd_ref, bwd_ref = tables[:2], tables[2:]
+    mixed_ref = refs[-6 - SPECTRA]
+    spec_refs = refs[-5 - SPECTRA : -5]
+    rows_in, parts_x, parts_h, parts_y, lhs = refs[-5:]
     me = me_ref[0]
     ra, rb = radices(outer)
     per = outer // peers
@@ -219,15 +232,19 @@
     first_pass(loader(1), keep(parts_h), outer)
     chunk = rb * ROWS
     for alpha in range(ra):
-        x = lane_transform(*second_pass(parts_x, alpha, outer, twist_ref), lhs.at[3 * alpha], fwd_ref)
-        h = lane_transform(*second_pass(parts_h, alpha, outer, twist_ref), lhs.at[3 * alpha + 1], fwd_ref)
-        spec_ref[0, alpha * chunk : (alpha + 1) * chunk, :] = h
+        put(*second_pass(parts_x, alpha, outer, twist_ref), lhs.at[alpha], 0)
+        put(*second_pass(parts_h, alpha, outer, twist_ref), lhs.at[alpha], chunk)
+    for alpha in range(ra):
+        both = lane_transform(lhs.at[alpha], fwd_ref)
+        x, h = both[:chunk], both[chunk:]
+        each = ra // SPECTRA
+        spec_refs[alpha // each][0, alpha % each * chunk : (alpha % each + 1) * chunk, :] = h
         xr, xi, hr, hi = x[:, :LANES], x[:, LANES:], h[:, :LANES], h[:, LANES:]
-        pr = xr * hr - xi * hi
-        pi = xr * hi + xi * hr
-        rows = [slice(i * ROWS, (i + 1) * ROWS) for i in range(rb)]
-        y = lane_transform([pr[r] for r in rows], [pi[r] for r in rows], lhs.at[3 * alpha + 2], bwd_ref)
-        back_second_pass(y, alpha, outer, twist_ref, keep(parts_y))
+        put_product(xr * hr - xi * hi, xr * hi + xi * hr, lhs.at[ra + alpha // 2], alpha % 2 * chunk)
+    for pair in range(ra // 2):
+        y = lane_transform(lhs.at[ra + pair], bwd_ref)
+        for i in range(2):
+            back_second_pass(y[i * chunk : (i + 1) * chunk], 2 * pair + i, outer, twist_ref, keep(parts_y))
     skip = jnp.broadcast_to(skip_ref[...], (ROWS, LANES))
 
     def emit(n1, value):
@@ -286,11 +303,15 @@
         outs[k][...] = rows_out[me ^ k]
 
 
-def corr_kernel(peers, outer, me_ref, *refs):
+def corr_kernel(peers, outer, packed, me_ref, *refs):
+    if packed:
+        packed_ref, refs = refs[0], refs[1:]
     queries = refs[:peers]
-    grad_ref, spec_ref, skip_ref, fwd_ref, bwd_ref, twist_ref, spread_ref = refs[peers : peers + 7]
-    outs = refs[peers + 7 : 2 * peers + 7]
-    rows_in, lhs_g, gated, parts_g, parts_y, lhs, rows_out = refs[2 * peers + 7 :]
+    refs, spec_refs = refs[: peers] + refs[peers + SPECTRA :], refs[peers : peers + SPECTRA]
+    grad_ref, skip_ref, *tables, twist_ref, spread_ref = refs[peers : peers + 8]
+    fwd_ref, bwd_ref = tables[:2], tables[2:]
+    outs = refs[peers + 8 : 2 * peers + 8]
+    rows_in, lhs_g, gated, parts_g, parts_y, lhs, rows_out = refs[2 * peers + 8 :]
     me = me_ref[0]
     ra, rb = radices(outer)
     per = outer // peers
@@ -324,14 +345,20 @@
     first_pass(load_g, keep(parts_g), outer)
     chunk = rb * ROWS
     for alpha in range(ra):
-        g = lane_transform(*second_pass(parts_g, alpha, outer, twist_ref), lhs.at[2 * alpha], fwd_ref)
-        h = spec_ref[0, alpha * chunk : (alpha + 1) * chunk, :]
-        gr, gi, hr, hi = g[:, :LANES], g[:, LANES:], h[:, :LANES], h[:, LANES:]
-        pr = gr * hr + gi * hi
-        pi = gi * hr - gr * hi
-        rows = [slice(i * ROWS, (i + 1) * ROWS) for i in range(rb)]
-        y = lane_transform([pr[r] for r in rows], [pi[r] for r in rows], lhs.at[2 * alpha + 1], bwd_ref)
-        back_second_pass(y, alpha, outer, twist_ref, keep(parts_y))
+        put(*second_pass(parts_g, alpha, outer, twist_ref), lhs.at[alpha // 2], alpha % 2 * chunk)
+    for pair in range(ra // 2):
+        both = lane_transform(lhs.at[pair], fwd_ref)
+        for i in range(2):
+            alpha = 2 * pair + i
+            g = both[i * chunk : (i + 1) * chunk]
+            each = ra // SPECTRA
+            h = spec_refs[alpha // each][0, alpha % each * chunk : (alpha % each + 1) * chunk, :]
+            gr, gi, hr, hi = g[:, :LANES], g[:, LANES:], h[:, :LANES], h[:, LANES:]
+            put_product(gr * hr + gi * hi, gi * hr - gr * hi, lhs.at[ra // 2 + pair], i * chunk)
+    for pair in range(ra // 2):
+        y = lane_transform(lhs.at[ra // 2 + pair], bwd_ref)
+        for i in range(2):
+            back_second_pass(y[i * chunk : (i + 1) * chunk], 2 * pair + i, outer, twist_ref, keep(parts_y))
     skip = jnp.broadcast_to(skip_ref[...], (ROWS, LANES))
 
     def emit(n1, value):
@@ -339,12 +366,20 @@
         rows_out[n1 // per, :, lanes] = (value + skip * load_g(n1)).astype(jnp.bfloat16)
 
     back_first_pass(parts_y, outer, emit)
+    step, steps = pl.program_id(0), pl.num_programs(0)
     for k in range(peers):
-        outs[k][...] = rows_out[me ^ k]
+        outs[k][:, : per * LANES] = rows_out[me ^ k]
+        if packed:
+            half = steps // 2
+            for chunk_at in range(packed_ref.shape[1] // (half * ROWS)):
+                here = pl.ds((chunk_at * half + lax.rem(step, half)) * ROWS, ROWS)
+                high, low = (part.astype(jnp.float32) for part in split(packed_ref[me ^ k, here, :]))
+                lanes = slice((per + chunk_at) * LANES, (per + chunk_at + 1) * LANES)
+                outs[k][:, lanes] = jnp.where(step < half, high, low).astype(jnp.bfloat16)
 
 
 def whole(array):
-    rank = array.ndim
+    rank = len(array.shape)
     return pl.BlockSpec(array.shape, lambda i, me: (0,) * rank)
 
 
@@ -397,12 +432,10 @@
     first = start // ROWS
     f32, bf16 = jnp.float32, jnp.bfloat16
     fwd, bwd, twist = tables["fwd"], tables["bwd"], tables["twist"]
-    inputs = [*pieces, skip, fwd, bwd, twist]
+    inputs = [*pieces, skip, *fwd, *bwd, twist]
     in_specs = [pl.BlockSpec((2, ROWS, width), lambda i, me: (0, i, 0))] * peers + [
         by_rows(1, start=first),
-        whole(fwd),
-        whole(bwd),
-        whole(twist),
+        *[whole(table) for table in (*fwd, *bwd, twist)],
     ]
     aliases = {}
     if before is not None:
@@ -414,19 +447,21 @@
     def kernel(*refs):
         conv_kernel(peers, outer, *refs)
 
-    return call(
+    part = (1, outer * ROWS // SPECTRA, 2 * LANES)
+    out = call(
         kernel, "long_convolution", me, steps, inputs, in_specs,
-        [shape((total_rows, length), f32), shape((steps, outer * ROWS, 2 * LANES), f32)],
-        [by_rows(length, start=first), pl.BlockSpec((1, outer * ROWS, 2 * LANES), lambda i, me: (i, 0, 0))],
+        [shape((total_rows, length), f32)] + [shape((steps, *part[1:]), f32)] * SPECTRA,
+        [by_rows(length, start=first)] + [pl.BlockSpec(part, lambda i, me: (i, 0, 0))] * SPECTRA,
         [
             pltpu.VMEM((peers, 2, ROWS, width), bf16),
             parts,
             parts,
             parts,
-            pltpu.VMEM((3 * ra, 2, chunk, 2 * LANES), bf16),
+            pltpu.VMEM((ra + ra // 2, 2, 2 * chunk, 2 * LANES), bf16),
         ],
-        rows * outer * 0.004 * MICROSECOND, aliases, (peers,), range(peers + 4, len(inputs) + 1),
-    )
+        rows * outer * 0.004 * MICROSECOND, aliases, (peers,), range(peers + 6, len(inputs) + 1),
+    )
+    return out[0], out[1:]
 
 
 def pool(me, queries, mixed, gather, groups):
@@ -463,10 +498,10 @@
     return out[:peers], out[peers]
 
 
-def correlate(me, queries, grad_pooled, spec, skip, tables, spread, start):
+def correlate(me, queries, grad_pooled, spec, skip, tables, spread, start, packed):
     peers = len(queries)
     width = queries[0].shape[1]
-    rows = spec.shape[0] * ROWS
+    rows = spec[0].shape[0] * ROWS
     length = width * peers
     outer = length // LANES
     bins = length // POOL
@@ -476,13 +511,10 @@
     f32, bf16 = jnp.float32, jnp.bfloat16
     fwd, bwd, twist = tables["fwd"], tables["bwd"], tables["twist"]
     in_specs = [by_rows(width, start=first)] * peers + [
+        *[pl.BlockSpec((1, *part.shape[1:]), lambda i, me: (i, 0, 0)) for part in spec],
         by_rows(bins, start=first),
-        pl.BlockSpec((1, outer * ROWS, 2 * LANES), lambda i, me: (i, 0, 0)),
         by_rows(1, start=first),
-        whole(fwd),
-        whole(bwd),
-        whole(twist),
-        whole(spread),
+        *[whole(table) for table in (*fwd, *bwd, twist, spread)],
     ]
     parts = pltpu.VMEM((2, rb, ra, ROWS, LANES), f32)
     scratch = [
@@ -491,18 +523,24 @@
         pltpu.VMEM((outer * ROWS, LANES), f32),
         parts,
         parts,
-        pltpu.VMEM((2 * ra, 2, chunk, 2 * LANES), bf16),
+        pltpu.VMEM((ra, 2, 2 * chunk, 2 * LANES), bf16),
         pltpu.VMEM((peers, ROWS, width), bf16),
     ]
 
     def kernel(*refs):
-        corr_kernel(peers, outer, *refs)
-
+        corr_kernel(peers, outer, packed is not None, *refs)
+
+    inputs = [*queries, *spec, grad_pooled, skip, *fwd, *bwd, twist, spread]
+    sent = width
+    if packed is not None:
+        sent = width + packed.shape[1] // (rows // 2) * LANES
+        inputs = [packed, *inputs]
+        in_specs = [whole(packed), *in_specs]
+    near = len(inputs) - 8
     return call(
-        kernel, "long_correlation", me, rows // ROWS,
-        [*queries, grad_pooled, spec, skip, fwd, bwd, twist, spread], in_specs,
-        [shape((rows, width), bf16)] * peers, [by_rows(width)] * peers,
-        scratch, rows * outer * 0.004 * MICROSECOND, near=(peers, peers + 2),
+        kernel, "long_correlation", me, rows // ROWS, inputs, in_specs,
+        [shape((rows, sent), bf16)] * peers, [by_rows(sent)] * peers,
+        scratch, rows * outer * 0.004 * MICROSECOND, near=(0, near, near + 1) if packed is not None else (near, near + 1),
     )
 
 
@@ -584,20 +622,30 @@
     channels, tracks = head_weight.shape
     half, own = channels // 2, tracks // groups
     padded = -(-own // LANES) * LANES
-    rows = 2 * ROWS
-
-    def kernel(me_ref, weight_ref, out_ref):
+    dtype = head_weight.dtype
+    steps = half // ROWS
+
+    def kernel(me_ref, weight_ref, out_ref, rows_in, sems):
+        first = pl.multiple_of((me_ref[0] & 1) * half, half)
+
+        def fetch(i):
+            return pltpu.make_async_copy(
+                weight_ref.at[pl.ds(first + i * ROWS, ROWS)], rows_in.at[pl.ds(i * ROWS, ROWS)], sems.at[i]
+            )
+
+        for i in range(steps):
+            fetch(i).start()
+        for i in range(steps):
+            fetch(i).wait()
         for group in range(groups):
-            out_ref[group, :, :own] = weight_ref[:, group * own : (group + 1) * own]
+            out_ref[group, :, :own] = rows_in[:, group * own : (group + 1) * own]
             if padded > own:
-                out_ref[group, :, own:] = jnp.zeros((rows, padded - own), head_weight.dtype)
-
-    out = shape((groups, half, padded), head_weight.dtype)
-    steps = half // rows
+                out_ref[group, :, own:] = jnp.zeros((half, padded - own), dtype)
+
+    out = shape((groups, half, padded), dtype)
     return call(
-        kernel, "by_track", me, steps, [head_weight],
-        [pl.BlockSpec((rows, tracks), lambda i, me: ((me[0] & 1) * steps + i, 0))],
-        [out], [pl.BlockSpec((groups, rows, padded), lambda i, me: (0, i, 0))], [], 2 * MICROSECOND,
+        kernel, "by_track", me, 1, [head_weight], [pl.BlockSpec(memory_space=pltpu.HBM)], [out], [whole(out)],
+        [pltpu.VMEM((half, tracks), dtype), pltpu.SemaphoreType.DMA((steps,))], 2 * MICROSECOND, vmem=(1,),
     )[0]
 
 
@@ -690,99 +738,103 @@
     bins = LANES // 2
     f32 = jnp.float32
 
-    def kernel(me_ref, back_ref, rows_ref, *refs):
-        outs, total_ref = refs[:peers], refs[peers]
+    def kernel(me_ref, back_ref, rows_ref, packed_ref):
         for seat in range(peers):
             total = back_ref[0, seat].astype(f32)
             for group in range(1, groups):
                 total = total + back_ref[group, seat].astype(f32)
-            total_ref[seat] = total
+            packed_ref[seat] = total
             for i in range(half_rows // ROWS):
                 pair = total[i * ROWS : (i + 1) * ROWS]
                 lanes = slice(seat * bins, (seat + 1) * bins)
                 rows_ref[2 * i * ROWS : (2 * i + 1) * ROWS, lanes] = pair[:, :bins]
                 rows_ref[(2 * i + 1) * ROWS : (2 * i + 2) * ROWS, lanes] = pair[:, bins:]
-        for k in range(peers):
-            outs[k][...] = total_ref[me_ref[0] ^ k]
-
-    packed = shape((half_rows, LANES), f32)
-    out = call(
-        kernel, "sum_grads", me, 1, [back], [whole(back)],
-        [shape((2 * half_rows, peers * bins), f32)] + [packed] * peers,
-        [pl.BlockSpec((2 * half_rows, peers * bins), lambda i, me: (0, 0))]
-        + [pl.BlockSpec(packed.shape, lambda i, me: (0, 0))] * peers,
-        [pltpu.VMEM((peers, half_rows, LANES), f32)], back.size, near=(0, 1),
-    )
-    return out[0], out[1:]
-
-
-def finish(me, projections, mixed_home, grad_home, corr_home, spread, chunk, chunks, before):
-    peers = len(mixed_home)
+
+    rows, packed = shape((2 * half_rows, peers * bins), f32), shape((peers, half_rows, LANES), f32)
+    return call(
+        kernel, "sum_grads", me, 1, [back], [whole(back)], [rows, packed], [whole(rows), whole(packed)], [], back.size,
+        near=(0, 1, 2),
+    )
+
+
+def finish(me, projections, mixed_home, corr_home, spread, chunk, chunks, before):
+    peers = len(corr_home)
     _, channels, width = projections.shape
     pencil = channels // peers
     rows = pencil // chunks
     tiles = width // LANES
     each = LANES // POOL
     f32, bf16 = jnp.float32, jnp.bfloat16
+    with_query = bool(mixed_home)
+    payload = corr_home[0].shape[1]
 
     def kernel(me_ref, spread_ref, proj_ref, *refs):
-        grad_refs, mixed_refs, corr_refs = refs[:peers], refs[peers : 2 * peers], refs[2 * peers : 3 * peers]
-        out_ref, pair, far, done, lhs, sems, out_sems = refs[-7:]
+        mixed_refs, corr_refs = refs[: len(mixed_home)], refs[len(mixed_home) : len(mixed_home) + peers]
+        out_ref, pair, mixed_in, corr_in, done, query_done, lhs, sems, out_sems = refs[-9:]
         place = lax.broadcasted_iota(jnp.int32, (ROWS, LANES), 1) // each
         zero = jnp.zeros((ROWS, LANES), f32)
 
+        def block(k, start, count):
+            return pl.ds(pl.multiple_of((me_ref[0] ^ k) * pencil + start, ROWS), count)
+
         def here(k):
-            return pl.ds(pl.multiple_of((me_ref[0] ^ k) * pencil + chunk * rows, rows), rows)
+            return block(k, chunk * rows, rows)
 
         def fetch(k):
             return (
-                pltpu.make_async_copy(mixed_refs[k].at[pl.ds(chunk * rows, rows)], far.at[k, 0], sems.at[k, 0]),
-                pltpu.make_async_copy(corr_refs[k], far.at[k, 1], sems.at[k, 1]),
-                pltpu.make_async_copy(proj_ref.at[1, here(k)], pair.at[k, 0], sems.at[k, 2]),
-                pltpu.make_async_copy(proj_ref.at[2, here(k)], pair.at[k, 1], sems.at[k, 3]),
+                pltpu.make_async_copy(corr_refs[k], corr_in.at[k], sems.at[k, 0]),
+                pltpu.make_async_copy(proj_ref.at[1, here(k)], pair.at[k, 0], sems.at[k, 1]),
+                pltpu.make_async_copy(proj_ref.at[2, here(k)], pair.at[k, 1], sems.at[k, 2]),
             )
 
+        def fetch_mixed(k):
+            return pltpu.make_async_copy(mixed_refs[k], mixed_in.at[k], sems.at[k, 3])
+
         def leave(k, plane):
-            return pltpu.make_async_copy(done.at[k, plane], out_ref.at[plane, here(k)], out_sems.at[k, plane])
+            if plane == 0:
+                return pltpu.make_async_copy(query_done.at[k], out_ref.at[0, block(k, 0, pencil)], out_sems.at[k, 0])
+            return pltpu.make_async_copy(done.at[k, plane - 1], out_ref.at[plane, here(k)], out_sems.at[k, plane])
 
         for k in range(peers):
             for copy in fetch(k):
                 copy.start()
+            if with_query:
+                fetch_mixed(k).start()
         for k in range(peers):
-            mixed_copy, corr_copy, keyed_copy, valued_copy = fetch(k)
-            corr_copy.wait()
-            keyed_copy.wait()
-            valued_copy.wait()
-            corr = far[k, 1].astype(f32)
-            done[k, 1] = corr * pair[k, 1].astype(f32)
+            for copy in fetch(k):
+                copy.wait()
+            corr = corr_in[k, :, :width].astype(f32)
+            done[k, 0] = corr * pair[k, 1].astype(f32)
             leave(k, 1).start()
-            done[k, 2] = corr * pair[k, 0].astype(f32)
+            done[k, 1] = corr * pair[k, 0].astype(f32)
             leave(k, 2).start()
-            mixed_copy.wait()
-            for i in range(rows // ROWS):
+            if not with_query:
+                continue
+            fetch_mixed(k).wait()
+            for i in range(pencil // ROWS):
                 part = slice(i * ROWS, (i + 1) * ROWS)
-                source = (chunk * rows + i * ROWS) // (2 * ROWS) * ROWS
-                side = (chunk * rows // ROWS + i) % 2
-                grads = grad_refs[k][source : source + ROWS, :]
-                high = grads.astype(bf16).astype(f32)
-                low = grads - high
+                inside = i % (rows // ROWS)
+                source = inside // 2 * ROWS
+                lanes = slice(width + i // (rows // ROWS) * LANES, width + (i // (rows // ROWS) + 1) * LANES)
+                high = corr_in[k, source : source + ROWS, lanes].astype(f32)
+                low = corr_in[k, rows // 2 + source : rows // 2 + source + ROWS, lanes].astype(f32)
                 for t in range(tiles):
-                    near = place == t + side * tiles
+                    near = place == t + inside % 2 * tiles
                     lhs[i, t * ROWS : (t + 1) * ROWS, :LANES] = jnp.where(near, high, zero).astype(bf16)
                     lhs[i, t * ROWS : (t + 1) * ROWS, LANES:] = jnp.where(near, low, zero).astype(bf16)
                 grad = dot(lhs[i], spread_ref[...])
                 for t in range(tiles):
-                    lanes = slice(t * LANES, (t + 1) * LANES)
-                    done[k, 0, part, lanes] = grad[t * ROWS : (t + 1) * ROWS] * far[k, 0, part, lanes].astype(f32)
+                    at = slice(t * LANES, (t + 1) * LANES)
+                    query_done[k, part, at] = grad[t * ROWS : (t + 1) * ROWS] * mixed_in[k, part, at].astype(f32)
             leave(k, 0).start()
         for k in range(peers):
-            for plane in range(3):
+            for plane in range(0 if with_query else 1, 3):
                 leave(k, plane).wait()
 
-    inputs = [spread, projections, *grad_home, *mixed_home, *corr_home]
+    inputs = [spread, projections, *mixed_home, *corr_home]
     in_specs = [whole(spread), pl.BlockSpec(memory_space=pltpu.HBM)]
-    in_specs += [whole(x) for x in grad_home]
-    in_specs += [pl.BlockSpec(memory_space=pl.ANY)] * (2 * peers)
+    in_specs += [pl.BlockSpec(memory_space=pl.ANY)] * (len(inputs) - 2)
+    near = (0, *range(2, len(inputs)))
     aliases = {}
     if before is not None:
         aliases = {1 + len(inputs): 0}
@@ -793,13 +845,15 @@
         [shape((3, channels, width), f32)], [pl.BlockSpec(memory_space=pltpu.HBM)],
         [
             pltpu.VMEM((peers, 2, rows, width), bf16),
-            pltpu.VMEM((peers, 2, rows, width), bf16),
-            pltpu.VMEM((peers, 3, rows, width), f32),
-            pltpu.VMEM((rows // ROWS, tiles * ROWS, 2 * LANES), bf16),
+            pltpu.VMEM((peers, pencil if with_query else ROWS, width), bf16),
+            pltpu.VMEM((peers, rows, payload), bf16),
+            pltpu.VMEM((peers, 2, rows, width), f32),
+            pltpu.VMEM((peers, pencil if with_query else ROWS, width), f32),
+            pltpu.VMEM((pencil // ROWS, tiles * ROWS, 2 * LANES), bf16),
             pltpu.SemaphoreType.DMA((peers, 4)),
             pltpu.SemaphoreType.DMA((peers, 3)),
         ],
-        rows * peers * 0.03 * MICROSECOND, aliases, near=(0, *range(2, 2 + 3 * peers)),
+        rows * peers * 0.03 * MICROSECOND, aliases, near=near,
     )[0]
 
 
@@ -841,6 +895,8 @@
         laid.append(lay_out(me_next, projections, filter_taps, peers, j, chunks))
         me_next, _ = lax.optimization_barrier((me, laid[j]))
     pieces = [[swap(laid[j][k], k, peers) for k in range(peers)] for j in range(chunks)]
+    held_back, _ = lax.optimization_barrier((laid[-1][peers:], pieces[0]))
+    queries = [swap(held_back[k], k, peers) for k in range(peers)]
     skip = lax.dynamic_index_in_dim(skip_gain.reshape(peers, pencil, 1), seat, axis=0, keepdims=False)
 
     mine = by_track(me_next, head_weight, groups)
@@ -850,9 +906,6 @@
     for j in range(chunks):
         mixed, spec = convolve(me, pieces[j], skip, tables, pencil, j * rows, mixed)
         specs.append(spec)
-        if j == 0:
-            queries, _ = lax.optimization_barrier((laid[-1][peers:], pieces[0]))
-            queries = [swap(queries[k], k, peers) for k in range(peers)]
     mixed_out, sent = pool(me, queries, mixed, gather, groups)
     mixed_home = [swap(mixed_out[k], k, peers) for k in range(peers)]
 
@@ -876,15 +929,14 @@
         step *= 2
     mean_loss = loss[0, 0] / (bins * peers * tracks)
 
-    grad_rows, grad_out = sum_grads(me, back)
-    grad_home = [swap(grad_out[k], k, peers) for k in range(peers)]
+    grad_rows, packed = sum_grads(me, back)
     grads = None
     corr_home = []
     for j in range(chunks):
-        corr = correlate(me, queries, grad_rows, specs[j], skip, tables, spread, j * rows)
+        corr = correlate(me, queries, grad_rows, specs[j], skip, tables, spread, j * rows, None if j else packed)
         corr_home.append([swap(corr[k], k, peers) for k in range(peers)])
     for j in range(chunks):
-        grads = finish(me, projections, mixed_home, grad_home, corr_home[j], spread, j, chunks, grads)
+        grads = finish(me, projections, [] if j else mixed_home, corr_home[j], spread, j, chunks, grads)
     return mean_loss, grads
 
 
@@ -998,7 +1050,7 @@
     grad_home = [swap(block(grad_pooled, k), k, peers) for k in range(peers)]
     grad_rows = pad_rows(grad_pooled.transpose(1, 0, 2).reshape(pencil, peers * bins), rows)
 
-    corr_out = correlate(me, queries, grad_rows, spec, skip, tables, spread, 0)
+    corr_out = correlate(me, queries, grad_rows, spec, skip, tables, spread, 0, None)
     corr_home = [swap(corr_out[k][:pencil], k, peers) for k in range(peers)]
 
     def assemble(parts):

time: 120 us -> 114 us (0.950)
  Pallas kernels: 53.4 us -> 48.3 us
  starting transfers between devices: 38.4 us -> 36.7 us
  waiting for transfers between devices: 15.9 us -> 17.2 us
    pallas_call x13, Pallas kernels: 53.4 us -> 48.3 us  [call(): pl.pallas_call(kernel, name=name, grid_spec=pltpu.PrefetchScalarGridSpec(...]
    ppermute x22 -> x19, starting transfers between devices: 19.7 us -> 17.5 us  [swap(): return lax.ppermute(value, 'seq', [(i, i ^ k) for i in range(count)])]
    ppermute x22 -> x19, waiting for transfers between devices: 3.67 us -> 4.99 us  [swap(): return lax.ppermute(value, 'seq', [(i, i ^ k) for i in range(count)])]
  transfers between devices with their start and end apart: 28 -> 25, of which waited for: 5 -> 5; matrix products, arithmetic and copies ran while one was open for 1% -> 1% of each run, Pallas kernels for 38% -> 36%
where the time goes in v4:
time: 114 us
  Pallas kernels  48.3 us (42%)
  starting transfers between devices  36.7 us (32%)
  waiting for transfers between devices  17.2 us (15%)
  blocking collectives  5.67 us (5%)
  local copies, waits for them, and re-layouts  3.08 us (3%)
  between operations  2.73 us (2%)
    pallas_call x13, Pallas kernels, call(): pl.pallas_call(kernel, name=name, grid_spec=pltpu.PrefetchScalarGridSpec(...  48.3 us
    ppermute x19, starting transfers between devices, swap(): return lax.ppermute(value, 'seq', [(i, i ^ k) for i in range(count)])  17.5 us
    all_to_all x2, waiting for transfers between devices, exchange(): lax.all_to_all(flat, ('chan', 'seq'), split_axis=0, concat_axis=0, tiled=...  9.37 us
    all_to_all x2, starting transfers between devices, exchange(): lax.all_to_all(flat, ('chan', 'seq'), split_axis=0, concat_axis=0, tiled=...  7.7 us
    ppermute x3, starting transfers between devices, aligned(): lax.ppermute(loss, 'chan', [(i, i ^ step) for i in range(groups)])  5.8 us
    all_to_all x1, starting transfers between devices, aligned(): mine = lax.all_to_all(mine, 'chan', split_axis=0, concat_axis=0, tiled=True)  5.7 us
    all_gather x1, blocking collectives, aligned(): all_sums = lax.all_gather(sums, 'seq')  5.67 us
    ppermute x19, waiting for transfers between devices, swap(): return lax.ppermute(value, 'seq', [(i, i ^ k) for i in range(count)])  4.99 us
  transfers between devices with their start and end apart: 25, of which 5 were waited for; matrix products, arithmetic and copies ran while one was open for 1% of the time, Pallas kernels for 36%

profile of v4, /device:TPU:1, one launch (start us, length us, event | category | flops | bytes accessed | tf_op | source)
XLA Modules:
  0.0 113.8 jit_solution(7407583320267384020)
XLA Ops:
  0.7 2.6 %lay_out.2 = (bf16[2,32,2048]{2,1,0:T(8,128)(2,1)}, bf16[2,32,2048]{2,1,0:T(8,128)(2,1)}, bf16[2,32,2048]{2,1,0:T(8,128)(2,1)}, bf16[2,32,2048]{2,1,0:T(8,128)(2,1)}) custom-call(s32[1]{0:T(128)} %bitcast.me_ref.refs_0_, bf16[3,256,2048]{2,1,0:T(8,128)(2,1)} %proj_ref.7, f32[256,2048]{1,0:T(8,128)} %taps_ref.3), custom_call_target="tpu_custom_call" | custom-call | flops 1920000000 | bytes 6291456 | tf_op jit(solution)/shard_map/lay_out/pallas_call | solution.py:401
  3.3 2.7 %collective-permute-start.1 = (bf16[2,32,2048]{2,1,0:T(8,128)(2,1)}, bf16[2,32,2048]{2,1,0:T(8,128)(2,1)}, u32[]{:S(2)}, u32[]{:S(2)}) collective-permute-start(bf16[2,32,2048]{2,1,0:T(8,128)(2,1)} %get-tuple-element.52), channel_id=1, source_target_pairs={{0,16},{8,24},{16,0},{24,8},{1,17},{9,25},{17,1},{25,9},{2,18},{10... | collective-permute-start | bytes 786440 | tf_op jit(solution)/shard_map/ppermute | solution.py:863
  6.1 3.1 %lay_out.3 = (bf16[2,32,2048]{2,1,0:T(8,128)(2,1)}, bf16[2,32,2048]{2,1,0:T(8,128)(2,1)}, bf16[2,32,2048]{2,1,0:T(8,128)(2,1)}, bf16[2,32,2048]{2,1,0:T(8,128)(2...) custom-call(s32[1]{0:T(128)} %bitcast.me_ref.refs_0_, ...), custom_call_target="tpu_custom_call" | custom-call | flops 1920000000 | bytes 7340032 | tf_op jit(solution)/shard_map/lay_out/pallas_call | solution.py:401
  9.6 1.4 %collective-permute-start.7 = (bf16[2,32,2048]{2,1,0:T(8,128)(2,1)}, bf16[2,32,2048]{2,1,0:T(8,128)(2,1)S(1)}, u32[]{:S(2)}, u32[]{:S(2)}) collective-permute-start(bf16[2,32,2048]{2,1,0:T(8,128)(2,1)} %get-tuple-element.65), channel_id=1, source_target_pairs={{0,16},{8,24},{16,0},{24,8},{1,17},{9,25},{17,1},{25,9},{2,18},{10... | collective-permute-start | bytes 786440 | tf_op jit(solution)/shard_map/ppermute | solution.py:863
  11.1 2.7 %by_track.1 = bf16[8,128,512]{2,1,0:T(8,128)(2,1)} custom-call(s32[1]{0:T(128)} %bitcast.me_ref.refs_0_, bf16[256,3840]{1,0:T(8,128)(2,1)} %weight_ref.1), custom_call_target="tpu_custom_call" | custom-call | flops 2000000000 | bytes 3014656 | tf_op jit(solution)/shard_map/by_track/pallas_call | solution.py:401
  13.8 5.7 %all-to-all-start.1 = ((bf16[8,128,512]{2,1,0:T(8,128)(2,1)}), bf16[8,128,512]{2,1,0:T(8,128)(2,1)S(1)}, u32[]{:S(2)}, u32[]{:S(2)}) async-start(bf16[8,128,512]{2,1,0:T(8,128)(2,1)} %by_track.1), calls=%async_computation.1 | async-start | bytes 2097152 | tf_op jit(solution)/shard_map/all_to_all | solution.py:903
  19.7 1.1 collective-permute-start.8
  20.9 1.3 %collective-permute-start.4 = (bf16[64,2048]{1,0:T(8,128)(2,1)S(1)}, bf16[64,2048]{1,0:T(8,128)(2,1)S(1)}, u32[]{:S(2)}, u32[]{:S(2)}) collective-permute-start(bf16[64,2048]{1,0:T(8,128)(2,1)S(1)} %copy-done.10), channel_id=1, source_target_pairs={{0,16},{8,24},{16,0},{24,8},{1,17},{9,25},{17,1},{25,9},{2,18},{10... | collective-permute-start | bytes 786440 | tf_op jit(solution)/shard_map/ppermute | solution.py:863
  22.2 7.3 %long_convolution.2 = (f32[64,8192]{1,0:T(8,128)S(1)}, f32[2,256,256]{2,1,0:T(8,128)}, f32[2,256,256]{2,1,0:T(8,128)}, f32[2,256,256]{2,1,0:T(8,128)}, f32[2,256,256]{2,1,0:T(8,128)}) custom-call(s32[1]{0:T(128)} %bitcast.me_ref.refs_0_, bf16[2,32,2048]{2,1,0:T(8,128)(2,1)} %get-tuple-element.50.refs_1_, bf16[2,32,2048]{2,1,0:T(8,128)(2,1)} %collective-permute-done.refs_2_, ...), custom_call_target="tpu_custom_call" | custom-call | flops 8192000000 | bytes 5832960 | tf_op jit(solution)/shard_map/long_convolution/pallas_call | solution.py:401
  31.2 7.3 %long_convolution.3 = (f32[64,8192]{1,0:T(8,128)S(1)}, f32[2,256,256]{2,1,0:T(8,128)}, f32[2,256,256]{2,1,0:T(8,128)}, f32[2,256,256]{2,1,0:T(8,128)}, f32[2,256,256]{2,1,0:T(8,128)}) custom-call(s32[1]{0:T(128)} %bitcast.me_ref.refs_0_, bf16[2,32,2048]{2,1,0:T(8,128)(2,1)} %get-tuple-element.63.refs_1_, ...), custom_call_target="tpu_custom_call", output_to_operand_aliasing={{0}: (11, {})} | custom-call | flops 8192000000 | bytes 7930112 | tf_op jit(solution)/shard_map/long_convolution/pallas_call | solution.py:401
  38.5 2.4 %collective-permute-done.5.refs_4_.refs_5_ = bf16[64,2048]{1,0:T(8,128)(2,1)S(1)} collective-permute-done((bf16[64,2048]{1,0:T(8,128)(2,1)S(1)}, bf16[64,2048]{1,0:T(8,128)(2,1)S(1)}, u32[]{:S(2)}, u32[]{:S(2)}) %collective-permute-start.5) | collective-permute-done | bytes 262176 | tf_op jit(solution)/shard_map/ppermute | solution.py:863
  41.6 3.1 %pool_bins.1 = (bf16[64,2048]{1,0:T(8,128)(2,1)}, bf16[64,2048]{1,0:T(8,128)(2,1)}, bf16[64,2048]{1,0:T(8,128)(2,1)}, bf16[64,2048]{1,0:T(8,128)(2,1)}, bf16[8,4,32,128]{3,2,1,0:T(8,128)(2,1)}) custom-call(s32[1]{0:T(128)} %bitcast.me_ref.refs_0_, bf16[64,2048]{1,0:T(8,128)(2,1)} %get-tuple-element.59.refs_1_.refs_2_, bf16[64,2048]{1,0:T(8,128)(2,1)} %copy-done.6, ...), custom_call_target="tpu_custom_call" | custom-call | flops 4096000000 | bytes 4521984 | tf_op jit(solution)/shard_map/pool_bins/pallas_call | solution.py:401
  44.7 1.5 %collective-permute-start.9 = (bf16[8,128,512]{2,1,0:T(8,128)(2,1)S(1)}, bf16[8,128,512]{2,1,0:T(8,128)(2,1)S(1)}, u32[]{:S(2)}, u32[]{:S(2)}) collective-permute-start(bf16[8,128,512]{2,1,0:T(8,128)(2,1)S(1)} %all-to-all-done.1.mine_ref), channel_id=1, source_target_pairs={{0,8},{8,0},{16,24},{24,16},{1,9},{9,1},{17,25},{25,17},{2,10},{10... | collective-permute-start | bytes 3145736 | tf_op jit(solution)/shard_map/ppermute | solution.py:863
  46.2 5.2 %all-to-all-start = ((bf16[32,32,128]{2,1,0:T(8,128)(2,1)}), bf16[32,32,128]{2,1,0:T(8,128)(2,1)S(1)}, u32[]{:S(2)}, u32[]{:S(2)}) async-start(bf16[32,32,128]{2,1,0:T(8,128)(2,1)} %bitcast.15), calls=%async_computation | async-start | bytes 524288 | tf_op jit(solution)/shard_map/all_to_all | solution.py:914
  52.3 9.4 %all-to-all-done = bf16[32,32,128]{2,1,0:T(8,128)(2,1)S(1)} async-done(((bf16[32,32,128]{2,1,0:T(8,128)(2,1)}), bf16[32,32,128]{2,1,0:T(8,128)(2,1)S(1)}, u32[]{:S(2)}, u32[]{:S(2)}) %all-to-all-start) | async-done | bytes 262176 | tf_op jit(solution)/shard_map/all_to_all | solution.py:914
  62.3 5.7 %all-gather = f32[32,480]{1,0:T(8,128)S(1)} all-gather(f32[8,480]{1,0:T(8,128)S(1)} %get-tuple-element.73), channel_id=2, replica_groups=mesh['seq'=4,'chan'=8] {'seq'}, dimensions={0}, use_global_device_ids=true | all-gather | bytes 76800 | tf_op jit(solution)/shard_map/all_gather | solution.py:923
  68.0 1.5 %head_grads.1 = (bf16[8,4,32,128]{3,2,1,0:T(8,128)(2,1)}, f32[8,128]{1,0:T(8,128)S(1)}) custom-call(s32[1]{0:T(128)} %bitcast.me_ref.refs_0_, f32[64,480]{1,0:T(8,128)S(1)} %get-tuple-element.72.logits_ref, f32[4,8,480]{2,1,0:T(8,128)S(1)} %bitcast.12, bf16[8,128,512]{2,1,0:T(8,128)(2,1)S(1)} %all-to-all-done.1.mine_ref, ...), custom_call_target="tpu_custom_call" | custom-call | flops 251658240 | bytes 2670592 | tf_op jit(solution)/shard_map/head_grads/pallas_call | solution.py:401
  69.4 2.5 %all-to-all-start.2 = ((bf16[32,32,128]{2,1,0:T(8,128)(2,1)}), bf16[32,32,128]{2,1,0:T(8,128)(2,1)S(1)}, u32[]{:S(2)}, u32[]{:S(2)}) async-start(bf16[32,32,128]{2,1,0:T(8,128)(2,1)} %bitcast.14), calls=%async_computation.2 | async-start | bytes 524288 | tf_op jit(solution)/shard_map/all_to_all | solution.py:914
  72.0 1.3 %collective-permute-start.10 = (f32[8,128]{1,0:T(8,128)S(1)}, f32[8,128]{1,0:T(8,128)S(1)}, u32[]{:S(2)}, u32[]{:S(2)}) collective-permute-start(f32[8,128]{1,0:T(8,128)S(1)} %get-tuple-element.74), channel_id=1, source_target_pairs={{0,1},{1,0},{2,3},{3,2},{4,5},{5,4},{6,7},{7,6},{8,9},{9,8},{10,11... | collective-permute-start | bytes 12296 | tf_op jit(solution)/shard_map/ppermute | solution.py:928
  73.3 1.4 %collective-permute-done.10 = f32[8,128]{1,0:T(8,128)S(1)} collective-permute-done((f32[8,128]{1,0:T(8,128)S(1)}, f32[8,128]{1,0:T(8,128)S(1)}, u32[]{:S(2)}, u32[]{:S(2)}) %collective-permute-start.10) | collective-permute-done | bytes 4128 | tf_op jit(solution)/shard_map/ppermute | solution.py:928
  74.7 1.2 %collective-permute-start.11 = (f32[8,128]{1,0:T(8,128)S(1)}, f32[8,128]{1,0:T(8,128)S(1)}, u32[]{:S(2)}, u32[]{:S(2)}) collective-permute-start(f32[8,128]{1,0:T(8,128)S(1)} %add.19), channel_id=1, source_target_pairs={{0,2},{1,3},{2,0},{3,1},{4,6},{5,7},{6,4},{7,5},{8,10},{9,11},{10,... | collective-permute-start | bytes 12296 | tf_op jit(solution)/shard_map/ppermute | solution.py:928
  75.9 1.5 %collective-permute-done.11 = f32[8,128]{1,0:T(8,128)S(1)} collective-permute-done((f32[8,128]{1,0:T(8,128)S(1)}, f32[8,128]{1,0:T(8,128)S(1)}, u32[]{:S(2)}, u32[]{:S(2)}) %collective-permute-start.11) | collective-permute-done | bytes 4128 | tf_op jit(solution)/shard_map/ppermute | solution.py:928
  77.4 3.2 %collective-permute-start.12 = (f32[8,128]{1,0:T(8,128)S(1)}, f32[8,128]{1,0:T(8,128)S(1)}, u32[]{:S(2)}, u32[]{:S(2)}) collective-permute-start(f32[8,128]{1,0:T(8,128)S(1)} %add.20), channel_id=1, source_target_pairs={{0,4},{1,5},{2,6},{3,7},{4,0},{5,1},{6,2},{7,3},{8,12},{9,13},{10,... | collective-permute-start | bytes 12296 | tf_op jit(solution)/shard_map/ppermute | solution.py:928
  80.6 1.6 %collective-permute-start.16 = (bf16[64,2048]{1,0:T(8,128)(2,1)}, bf16[64,2048]{1,0:T(8,128)(2,1)S(1)}, u32[]{:S(2)}, u32[]{:S(2)}) collective-permute-start(bf16[64,2048]{1,0:T(8,128)(2,1)} %get-tuple-element.86), channel_id=1, source_target_pairs={{0,8},{8,0},{16,24},{24,16},{1,9},{9,1},{17,25},{25,17},{2,10},{10... | collective-permute-start | bytes 786440 | tf_op jit(solution)/shard_map/ppermute | solution.py:863
  82.2 1.6 %collective-permute-start.17 = (bf16[64,2048]{1,0:T(8,128)(2,1)}, bf16[64,2048]{1,0:T(8,128)(2,1)S(1)}, u32[]{:S(2)}, u32[]{:S(2)}) collective-permute-start(bf16[64,2048]{1,0:T(8,128)(2,1)} %get-tuple-element.87), channel_id=1, source_target_pairs={{0,16},{8,24},{16,0},{24,8},{1,17},{9,25},{17,1},{25,9},{2,18},{10... | collective-permute-start | bytes 786440 | tf_op jit(solution)/shard_map/ppermute | solution.py:863
  85.1 6.8 %long_correlation.3 = (bf16[32,2304]{1,0:T(8,128)(2,1)}, bf16[32,2304]{1,0:T(8,128)(2,1)}, bf16[32,2304]{1,0:T(8,128)(2,1)}, bf16[32,2304]{1,0:T(8,128)(2,1)}) custom-call(s32[1]{0:T(128)} %bitcast.me_ref.refs_0_, f32[4,32,128]{2,1,0:T(8,128)S(1)} %get-tuple-element.89.refs_1_, bf16[64,2048]{1,0:T(8,128)(2,1)} %get-tuple-element.59.refs_1_.refs_2_, ...), custom_call_target="tpu_custom_call" | custom-call | flops 8192000000 | bytes 4522240 | tf_op jit(solution)/shard_map/long_correlation/pallas_call | solution.py:401
  92.7 1.1 collective-permute-start.20
  94.5 6.9 %long_correlation.2 = (bf16[32,2048]{1,0:T(8,128)(2,1)}, bf16[32,2048]{1,0:T(8,128)(2,1)}, bf16[32,2048]{1,0:T(8,128)(2,1)}, bf16[32,2048]{1,0:T(8,128)(2,1)}) custom-call(s32[1]{0:T(128)} %bitcast.me_ref.refs_0_, bf16[64,2048]{1,0:T(8,128)(2,1)} %get-tuple-element.59.refs_1_.refs_2_, bf16[64,2048]{1,0:T(8,128)(2,1)} %copy-done.6, ...), custom_call_target="tpu_custom_call" | custom-call | flops 8192000000 | bytes 4391168 | tf_op jit(solution)/shard_map/long_correlation/pallas_call | solution.py:401
  101.6 1.2 %collective-permute-start.14 = (bf16[32,2048]{1,0:T(8,128)(2,1)}, bf16[32,2048]{1,0:T(8,128)(2,1)S(1)}, u32[]{:S(2)}, u32[]{:S(2)}) collective-permute-start(bf16[32,2048]{1,0:T(8,128)(2,1)} %get-tuple-element.83), channel_id=1, source_target_pairs={{0,16},{8,24},{16,0},{24,8},{1,17},{9,25},{17,1},{25,9},{2,18},{10... | collective-permute-start | bytes 393224 | tf_op jit(solution)/shard_map/ppermute | solution.py:863
  103.7 3.7 %finish.2.refs_4_ = f32[3,256,2048]{2,1,0:T(8,128)} custom-call(s32[1]{0:T(128)} %bitcast.me_ref.refs_0_, bf16[256,128]{1,0:T(8,128)(2,1)S(1)} %copy-done.2, bf16[3,256,2048]{2,1,0:T(8,128)(2,1)} %proj_ref.7, bf16[64,2048]{1,0:T(8,128)(2,1)S(1)} %copy-done.3, bf16[64,2048]{1,0:T(8,128)(2,1)S(1)} %collective-permute-done.16.refs_1_, ...), custom_call_target="tpu_custom_call" | custom-call | flops 3840000000 | bytes 11141120 | tf_op jit(solution)/shard_map/finish/pallas_call | solution.py:401
  107.3 2.5 %collective-permute-done.15.refs_3_ = bf16[32,2048]{1,0:T(8,128)(2,1)S(1)} collective-permute-done((bf16[32,2048]{1,0:T(8,128)(2,1)}, bf16[32,2048]{1,0:T(8,128)(2,1)S(1)}, u32[]{:S(2)}, u32[]{:S(2)}) %collective-permute-start.15) | collective-permute-done | bytes 131104 | tf_op jit(solution)/shard_map/ppermute | solution.py:863
  109.9 2.8 %finish.3 = f32[3,256,2048]{2,1,0:T(8,128)} custom-call(s32[1]{0:T(128)} %bitcast.me_ref.refs_0_, bf16[256,128]{1,0:T(8,128)(2,1)S(1)} %copy-done.2, bf16[3,256,2048]{2,1,0:T(8,128)(2,1)} %proj_ref.7, bf16[32,2048]{1,0:T(8,128)(2,1)S(1)} %copy-done.1, bf16[32,2048]{1,0:T(8,128)(2,1)S(1)} %collective-permute-done.13.refs_1_, ...), custom_call_target="tpu_custom_call", output_to_operand_aliasing={{}: (7, {})} | custom-call | flops 3840000000 | bytes 16318464 | tf_op jit(solution)/shard_map/finish/pallas_call | solution.py:401
  (73 shorter events, 8.0 us)
Async XLA Ops:
  0.6 51.5 %copy-start = (s32[64,3840]{1,0:T(8,128)S(1)}, s32[64,3840]{1,0:T(8,128)}, u32[]{:S(2)}) copy-start(s32[64,3840]{1,0:T(8,128)} %param.18) | copy-start | bytes 2949124
  3.2 16.4 %collective-permute-start = (bf16[2,32,2048]{2,1,0:T(8,128)(2,1)}, bf16[2,32,2048]{2,1,0:T(8,128)(2,1)}, u32[]{:S(2)}, u32[]{:S(2)}) collective-permute-start(bf16[2,32,2048]{2,1,0:T(8,128)(2,1)} %get-tuple-element.51), channel_id=1, source_target_pairs={{0,8},{8,0},{16,24},{24,16},{1,9},{9,1},{17,25},{25,17},{2,10},{10... | collective-permute-start | bytes 786440 | tf_op jit(solution)/shard_map/ppermute | solution.py:863
  3.3 17.4 %collective-permute-start.1 = (bf16[2,32,2048]{2,1,0:T(8,128)(2,1)}, bf16[2,32,2048]{2,1,0:T(8,128)(2,1)}, u32[]{:S(2)}, u32[]{:S(2)}) collective-permute-start(bf16[2,32,2048]{2,1,0:T(8,128)(2,1)} %get-tuple-element.52), channel_id=1, source_target_pairs={{0,16},{8,24},{16,0},{24,8},{1,17},{9,25},{17,1},{25,9},{2,18},{10... | collective-permute-start | bytes 786440 | tf_op jit(solution)/shard_map/ppermute | solution.py:863
  6.0 14.8 %collective-permute-start.2 = (bf16[2,32,2048]{2,1,0:T(8,128)(2,1)}, bf16[2,32,2048]{2,1,0:T(8,128)(2,1)}, u32[]{:S(2)}, u32[]{:S(2)}) collective-permute-start(bf16[2,32,2048]{2,1,0:T(8,128)(2,1)} %get-tuple-element.53), channel_id=1, source_target_pairs={{0,24},{8,16},{16,8},{24,0},{1,25},{9,17},{17,9},{25,1},{2,26},{10... | collective-permute-start | bytes 786440 | tf_op jit(solution)/shard_map/ppermute | solution.py:863
  9.2 20.3 %collective-permute-start.6 = (bf16[2,32,2048]{2,1,0:T(8,128)(2,1)}, bf16[2,32,2048]{2,1,0:T(8,128)(2,1)S(1)}, u32[]{:S(2)}, u32[]{:S(2)}) collective-permute-start(bf16[2,32,2048]{2,1,0:T(8,128)(2,1)} %get-tuple-element.64), channel_id=1, source_target_pairs={{0,8},{8,0},{16,24},{24,16},{1,9},{9,1},{17,25},{25,17},{2,10},{10... | collective-permute-start | bytes 786440 | tf_op jit(solution)/shard_map/ppermute | solution.py:863
  9.6 20.8 %collective-permute-start.7 = (bf16[2,32,2048]{2,1,0:T(8,128)(2,1)}, bf16[2,32,2048]{2,1,0:T(8,128)(2,1)S(1)}, u32[]{:S(2)}, u32[]{:S(2)}) collective-permute-start(bf16[2,32,2048]{2,1,0:T(8,128)(2,1)} %get-tuple-element.65), channel_id=1, source_target_pairs={{0,16},{8,24},{16,0},{24,8},{1,17},{9,25},{17,1},{25,9},{2,18},{10... | collective-permute-start | bytes 786440 | tf_op jit(solution)/shard_map/ppermute | solution.py:863
  13.7 7.0 %copy-start.11 = (bf16[64,2048]{1,0:T(8,128)(2,1)S(1)}, bf16[64,2048]{1,0:T(8,128)(2,1)}, u32[]{:S(2)}) copy-start(bf16[64,2048]{1,0:T(8,128)(2,1)} %get-tuple-element.60) | copy-start | bytes 786436
  13.8 7.1 %copy-start.10 = (bf16[64,2048]{1,0:T(8,128)(2,1)S(1)}, bf16[64,2048]{1,0:T(8,128)(2,1)}, u32[]{:S(2)}) copy-start(bf16[64,2048]{1,0:T(8,128)(2,1)} %get-tuple-element.61) | copy-start | bytes 786436
  13.8 30.9 %all-to-all-start.1 = ((bf16[8,128,512]{2,1,0:T(8,128)(2,1)}), bf16[8,128,512]{2,1,0:T(8,128)(2,1)S(1)}, u32[]{:S(2)}, u32[]{:S(2)}) async-start(bf16[8,128,512]{2,1,0:T(8,128)(2,1)} %by_track.1), calls=%async_computation.1 | async-start | bytes 2097152 | tf_op jit(solution)/shard_map/all_to_all | solution.py:903
  19.7 9.8 %copy-start.9 = (bf16[64,2048]{1,0:T(8,128)(2,1)S(1)}, bf16[64,2048]{1,0:T(8,128)(2,1)}, u32[]{:S(2)}) copy-start(bf16[64,2048]{1,0:T(8,128)(2,1)} %get-tuple-element.62) | copy-start | bytes 786436
  19.7 10.7 %collective-permute-start.8 = (bf16[2,32,2048]{2,1,0:T(8,128)(2,1)S(1)}, bf16[2,32,2048]{2,1,0:T(8,128)(2,1)S(1)}, u32[]{:S(2)}, u32[]{:S(2)}) collective-permute-start(bf16[2,32,2048]{2,1,0:T(8,128)(2,1)S(1)} %copy-done.13), channel_id=1, source_target_pairs={{0,24},{8,16},{16,8},{24,0},{1,25},{9,17},{17,9},{25,1},{2,26},{10... | collective-permute-start | bytes 786440 | tf_op jit(solution)/shard_map/ppermute | solution.py:863
  20.8 17.7 %collective-permute-start.3 = (bf16[64,2048]{1,0:T(8,128)(2,1)S(1)}, bf16[64,2048]{1,0:T(8,128)(2,1)S(1)}, u32[]{:S(2)}, u32[]{:S(2)}) collective-permute-start(bf16[64,2048]{1,0:T(8,128)(2,1)S(1)} %copy-done.11), channel_id=1, source_target_pairs={{0,8},{8,0},{16,24},{24,16},{1,9},{9,1},{17,25},{25,17},{2,10},{10... | collective-permute-start | bytes 786440 | tf_op jit(solution)/shard_map/ppermute | solution.py:863
  20.9 17.6 %collective-permute-start.4 = (bf16[64,2048]{1,0:T(8,128)(2,1)S(1)}, bf16[64,2048]{1,0:T(8,128)(2,1)S(1)}, u32[]{:S(2)}, u32[]{:S(2)}) collective-permute-start(bf16[64,2048]{1,0:T(8,128)(2,1)S(1)} %copy-done.10), channel_id=1, source_target_pairs={{0,16},{8,24},{16,0},{24,8},{1,17},{9,25},{17,1},{25,9},{2,18},{10... | collective-permute-start | bytes 786440 | tf_op jit(solution)/shard_map/ppermute | solution.py:863
  29.5 11.4 %collective-permute-start.5 = (bf16[64,2048]{1,0:T(8,128)(2,1)S(1)}, bf16[64,2048]{1,0:T(8,128)(2,1)S(1)}, u32[]{:S(2)}, u32[]{:S(2)}) collective-permute-start(bf16[64,2048]{1,0:T(8,128)(2,1)S(1)} %copy-done.9), channel_id=1, source_target_pairs={{0,24},{8,16},{16,8},{24,0},{1,25},{9,17},{17,9},{25,1},{2,26},{10... | collective-permute-start | bytes 786440 | tf_op jit(solution)/shard_map/ppermute | solution.py:863
  44.7 17.0 %collective-permute-start.9 = (bf16[8,128,512]{2,1,0:T(8,128)(2,1)S(1)}, bf16[8,128,512]{2,1,0:T(8,128)(2,1)S(1)}, u32[]{:S(2)}, u32[]{:S(2)}) collective-permute-start(bf16[8,128,512]{2,1,0:T(8,128)(2,1)S(1)} %all-to-all-done.1.mine_ref), channel_id=1, source_target_pairs={{0,8},{8,0},{16,24},{24,16},{1,9},{9,1},{17,25},{25,17},{2,10},{10... | collective-permute-start | bytes 3145736 | tf_op jit(solution)/shard_map/ppermute | solution.py:863
  46.2 15.5 %all-to-all-start = ((bf16[32,32,128]{2,1,0:T(8,128)(2,1)}), bf16[32,32,128]{2,1,0:T(8,128)(2,1)S(1)}, u32[]{:S(2)}, u32[]{:S(2)}) async-start(bf16[32,32,128]{2,1,0:T(8,128)(2,1)} %bitcast.15), calls=%async_computation | async-start | bytes 524288 | tf_op jit(solution)/shard_map/all_to_all | solution.py:914
  69.4 15.6 %all-to-all-start.2 = ((bf16[32,32,128]{2,1,0:T(8,128)(2,1)}), bf16[32,32,128]{2,1,0:T(8,128)(2,1)S(1)}, u32[]{:S(2)}, u32[]{:S(2)}) async-start(bf16[32,32,128]{2,1,0:T(8,128)(2,1)} %bitcast.14), calls=%async_computation.2 | async-start | bytes 524288 | tf_op jit(solution)/shard_map/all_to_all | solution.py:914
  72.0 2.7 %collective-permute-start.10 = (f32[8,128]{1,0:T(8,128)S(1)}, f32[8,128]{1,0:T(8,128)S(1)}, u32[]{:S(2)}, u32[]{:S(2)}) collective-permute-start(f32[8,128]{1,0:T(8,128)S(1)} %get-tuple-element.74), channel_id=1, source_target_pairs={{0,1},{1,0},{2,3},{3,2},{4,5},{5,4},{6,7},{7,6},{8,9},{9,8},{10,11... | collective-permute-start | bytes 12296 | tf_op jit(solution)/shard_map/ppermute | solution.py:928
  74.7 2.8 %collective-permute-start.11 = (f32[8,128]{1,0:T(8,128)S(1)}, f32[8,128]{1,0:T(8,128)S(1)}, u32[]{:S(2)}, u32[]{:S(2)}) collective-permute-start(f32[8,128]{1,0:T(8,128)S(1)} %add.19), channel_id=1, source_target_pairs={{0,2},{1,3},{2,0},{3,1},{4,6},{5,7},{6,4},{7,5},{8,10},{9,11},{10,... | collective-permute-start | bytes 12296 | tf_op jit(solution)/shard_map/ppermute | solution.py:928
  77.4 6.4 %collective-permute-start.12 = (f32[8,128]{1,0:T(8,128)S(1)}, f32[8,128]{1,0:T(8,128)S(1)}, u32[]{:S(2)}, u32[]{:S(2)}) collective-permute-start(f32[8,128]{1,0:T(8,128)S(1)} %add.20), channel_id=1, source_target_pairs={{0,4},{1,5},{2,6},{3,7},{4,0},{5,1},{6,2},{7,3},{8,12},{9,13},{10,... | collective-permute-start | bytes 12296 | tf_op jit(solution)/shard_map/ppermute | solution.py:928
  80.6 13.2 %collective-permute-start.16 = (bf16[64,2048]{1,0:T(8,128)(2,1)}, bf16[64,2048]{1,0:T(8,128)(2,1)S(1)}, u32[]{:S(2)}, u32[]{:S(2)}) collective-permute-start(bf16[64,2048]{1,0:T(8,128)(2,1)} %get-tuple-element.86), channel_id=1, source_target_pairs={{0,8},{8,0},{16,24},{24,16},{1,9},{9,1},{17,25},{25,17},{2,10},{10... | collective-permute-start | bytes 786440 | tf_op jit(solution)/shard_map/ppermute | solution.py:863
  82.2 19.2 %collective-permute-start.17 = (bf16[64,2048]{1,0:T(8,128)(2,1)}, bf16[64,2048]{1,0:T(8,128)(2,1)S(1)}, u32[]{:S(2)}, u32[]{:S(2)}) collective-permute-start(bf16[64,2048]{1,0:T(8,128)(2,1)} %get-tuple-element.87), channel_id=1, source_target_pairs={{0,16},{8,24},{16,0},{24,8},{1,17},{9,25},{17,1},{25,9},{2,18},{10... | collective-permute-start | bytes 786440 | tf_op jit(solution)/shard_map/ppermute | solution.py:863
  83.8 17.9 %collective-permute-start.18 = (bf16[64,2048]{1,0:T(8,128)(2,1)}, bf16[64,2048]{1,0:T(8,128)(2,1)S(1)}, u32[]{:S(2)}, u32[]{:S(2)}) collective-permute-start(bf16[64,2048]{1,0:T(8,128)(2,1)} %get-tuple-element.88), channel_id=1, source_target_pairs={{0,24},{8,16},{16,8},{24,0},{1,25},{9,17},{17,9},{25,1},{2,26},{10... | collective-permute-start | bytes 786440 | tf_op jit(solution)/shard_map/ppermute | solution.py:863
  91.9 10.9 %collective-permute-start.19 = (bf16[32,2304]{1,0:T(8,128)(2,1)}, bf16[32,2304]{1,0:T(8,128)(2,1)S(1)}, u32[]{:S(2)}, u32[]{:S(2)}) collective-permute-start(bf16[32,2304]{1,0:T(8,128)(2,1)} %get-tuple-element.95), channel_id=1, source_target_pairs={{0,8},{8,0},{16,24},{24,16},{1,9},{9,1},{17,25},{25,17},{2,10},{10... | collective-permute-start | bytes 442376 | tf_op jit(solution)/shard_map/ppermute | solution.py:863
  92.7 10.9 %collective-permute-start.20 = (bf16[32,2304]{1,0:T(8,128)(2,1)}, bf16[32,2304]{1,0:T(8,128)(2,1)S(1)}, u32[]{:S(2)}, u32[]{:S(2)}) collective-permute-start(bf16[32,2304]{1,0:T(8,128)(2,1)} %get-tuple-element.96), channel_id=1, source_target_pairs={{0,16},{8,24},{16,0},{24,8},{1,17},{9,25},{17,1},{25,9},{2,18},{10... | collective-permute-start | bytes 442376 | tf_op jit(solution)/shard_map/ppermute | solution.py:863
  93.8 9.8 %collective-permute-start.21 = (bf16[32,2304]{1,0:T(8,128)(2,1)}, bf16[32,2304]{1,0:T(8,128)(2,1)S(1)}, u32[]{:S(2)}, u32[]{:S(2)}) collective-permute-start(bf16[32,2304]{1,0:T(8,128)(2,1)} %get-tuple-element.97), channel_id=1, source_target_pairs={{0,24},{8,16},{16,8},{24,0},{1,25},{9,17},{17,9},{25,1},{2,26},{10... | collective-permute-start | bytes 442376 | tf_op jit(solution)/shard_map/ppermute | solution.py:863
  94.5 9.2 %copy-start.2 = (bf16[256,128]{1,0:T(8,128)(2,1)S(1)}, bf16[256,128]{1,0:T(8,128)(2,1)}, u32[]{:S(2)}) copy-start(bf16[256,128]{1,0:T(8,128)(2,1)} %constant.43.clone.refs_16_.refs_17_.spread_ref) | copy-start | bytes 196612
  94.5 9.2 %copy-start.3 = (bf16[64,2048]{1,0:T(8,128)(2,1)S(1)}, bf16[64,2048]{1,0:T(8,128)(2,1)}, u32[]{:S(2)}) copy-start(bf16[64,2048]{1,0:T(8,128)(2,1)} %get-tuple-element.85.refs_0_) | copy-start | bytes 786436
  94.5 9.2 %copy-start.4 = (bf16[32,2304]{1,0:T(8,128)(2,1)S(1)}, bf16[32,2304]{1,0:T(8,128)(2,1)}, u32[]{:S(2)}) copy-start(bf16[32,2304]{1,0:T(8,128)(2,1)} %get-tuple-element.94.refs_4_) | copy-start | bytes 442372
  101.4 5.9 %collective-permute-start.13 = (bf16[32,2048]{1,0:T(8,128)(2,1)}, bf16[32,2048]{1,0:T(8,128)(2,1)S(1)}, u32[]{:S(2)}, u32[]{:S(2)}) collective-permute-start(bf16[32,2048]{1,0:T(8,128)(2,1)} %get-tuple-element.82), channel_id=1, source_target_pairs={{0,8},{8,0},{16,24},{24,16},{1,9},{9,1},{17,25},{25,17},{2,10},{10... | collective-permute-start | bytes 393224 | tf_op jit(solution)/shard_map/ppermute | solution.py:863
  101.6 5.7 %collective-permute-start.14 = (bf16[32,2048]{1,0:T(8,128)(2,1)}, bf16[32,2048]{1,0:T(8,128)(2,1)S(1)}, u32[]{:S(2)}, u32[]{:S(2)}) collective-permute-start(bf16[32,2048]{1,0:T(8,128)(2,1)} %get-tuple-element.83), channel_id=1, source_target_pairs={{0,16},{8,24},{16,0},{24,8},{1,17},{9,25},{17,1},{25,9},{2,18},{10... | collective-permute-start | bytes 393224 | tf_op jit(solution)/shard_map/ppermute | solution.py:863
  102.8 7.0 %collective-permute-start.15 = (bf16[32,2048]{1,0:T(8,128)(2,1)}, bf16[32,2048]{1,0:T(8,128)(2,1)S(1)}, u32[]{:S(2)}, u32[]{:S(2)}) collective-permute-start(bf16[32,2048]{1,0:T(8,128)(2,1)} %get-tuple-element.84), channel_id=1, source_target_pairs={{0,24},{8,16},{16,8},{24,0},{1,25},{9,17},{17,9},{25,1},{2,26},{10... | collective-permute-start | bytes 393224 | tf_op jit(solution)/shard_map/ppermute | solution.py:863
  (9 other events, 25.9 us)

commit v5 on v4

--- a/solution.py
+++ b/solution.py
@@ -493,7 +493,7 @@
             pltpu.VMEM((peers, step, width), bf16),
             pltpu.VMEM((step // ROWS, outer * ROWS, 2 * LANES), bf16),
         ],
-        rows * outer * 0.001 * MICROSECOND, vmem=(peers,),
+        rows * outer * 0.001 * MICROSECOND, vmem=range(1, peers + 1),
     )
     return out[:peers], out[peers]
 
@@ -690,23 +690,28 @@
     )
 
 
-def head_grads(me, logits, sums, mine, other, counts, peers):
+def head_grads(me, logits, sums, mine, other, counts):
     groups, half, _ = mine.shape
     own = counts.shape[1]
+    peers = len(sums)
     seats = peers // 2
     pencil = half // seats
     bins = LANES // 2
     f32, bf16 = jnp.float32, jnp.bfloat16
 
-    def kernel(me_ref, logits_ref, sums_ref, mine_ref, other_ref, counts_ref, out_ref, loss_ref):
+    def kernel(me_ref, logits_ref, *refs):
+        sums_refs = refs[:peers]
+        mine_ref, other_ref, counts_ref, out_ref, loss_ref = refs[peers:]
         odd = me_ref[0] & 1
-        totals = sums_ref[0]
-        for seat in range(1, peers):
-            totals = totals + sums_ref[seat]
+        totals = [ref[...] for ref in sums_refs]
+        while len(totals) > 1:
+            totals = [totals[i] + totals[i + 1] for i in range(0, len(totals), 2)]
+        totals = totals[0]
         pred_total, obs_total, log_sum = totals[0:1], totals[1:2], totals[2:3]
         log_pred = jnp.log(pred_total)
         terms = total_weight * (pred_total - obs_total * log_pred) + obs_total * log_pred - log_sum
-        loss_ref[...] = jnp.broadcast_to(jnp.sum(terms, axis=1, keepdims=True), loss_ref.shape)
+        mean = jnp.sum(terms, axis=1, keepdims=True) / (peers * bins * groups * own)
+        loss_ref[...] = jnp.broadcast_to(mean, loss_ref.shape)
         ratio = obs_total / pred_total
         logits_here = logits_ref[...]
         rates = jax.nn.softplus(logits_here) + rate_floor
@@ -723,13 +728,13 @@
             part = part + lax.dot_general(right, in_right, across, preferred_element_type=f32)
             out_ref[:, pl.ds(place * seats, seats)] = part.astype(bf16).reshape(groups, seats, pencil // 2, LANES)
 
-    inputs = [logits, sums, mine, other, counts]
+    inputs = [logits, *sums, mine, other, counts]
     out = shape((groups, peers, pencil // 2, LANES), bf16)
     return call(
         kernel, "head_grads", me, 1, inputs, [whole(x) for x in inputs],
         [out, shape((8, LANES), f32)],
-        [pl.BlockSpec(out.shape, lambda i, me: (0, 0, 0, 0)), pl.BlockSpec((8, LANES), lambda i, me: (0, 0))],
-        [], 4 * bins * groups * peers * pencil * own, near=(0, 1, 2, 3, 4, 6),
+        [whole(out), pl.BlockSpec((8, LANES), lambda i, me: (0, 0))],
+        [], 4 * bins * groups * peers * pencil * own, near=(*range(peers + 4), peers + 5),
     )
 
 
@@ -757,7 +762,7 @@
     )
 
 
-def finish(me, projections, mixed_home, corr_home, spread, chunk, chunks, before):
+def finish(me, projections, mixed_home, corr_home, spread, chunk, chunks, before, loss):
     peers = len(corr_home)
     _, channels, width = projections.shape
     pencil = channels // peers
@@ -770,7 +775,11 @@
 
     def kernel(me_ref, spread_ref, proj_ref, *refs):
         mixed_refs, corr_refs = refs[: len(mixed_home)], refs[len(mixed_home) : len(mixed_home) + peers]
-        out_ref, pair, mixed_in, corr_in, done, query_done, lhs, sems, out_sems = refs[-9:]
+        pair, mixed_in, corr_in, done, query_done, lhs, sems, out_sems = refs[-8:]
+        if loss:
+            loss_ref, mean_ref = refs[len(mixed_home) + peers], refs[-9]
+            mean_ref[...] = loss_ref[0:1, 0:1]
+        out_ref = refs[-9 - len(loss)]
         place = lax.broadcasted_iota(jnp.int32, (ROWS, LANES), 1) // each
         zero = jnp.zeros((ROWS, LANES), f32)
 
@@ -831,9 +840,10 @@
             for plane in range(0 if with_query else 1, 3):
                 leave(k, plane).wait()
 
-    inputs = [spread, projections, *mixed_home, *corr_home]
+    inputs = [spread, projections, *mixed_home, *corr_home, *loss]
     in_specs = [whole(spread), pl.BlockSpec(memory_space=pltpu.HBM)]
-    in_specs += [pl.BlockSpec(memory_space=pl.ANY)] * (len(inputs) - 2)
+    in_specs += [pl.BlockSpec(memory_space=pl.ANY)] * (len(mixed_home) + peers)
+    in_specs += [whole(x) for x in loss]
     near = (0, *range(2, len(inputs)))
     aliases = {}
     if before is not None:
@@ -842,7 +852,8 @@
         in_specs.append(pl.BlockSpec(memory_space=pl.ANY))
     return call(
         kernel, "finish", me, 1, inputs, in_specs,
-        [shape((3, channels, width), f32)], [pl.BlockSpec(memory_space=pltpu.HBM)],
+        [shape((3, channels, width), f32)] + [shape((1, 1), f32)] * len(loss),
+        [pl.BlockSpec(memory_space=pltpu.HBM)] + [pl.BlockSpec((1, 1), lambda i, me: (0, 0))] * len(loss),
         [
             pltpu.VMEM((peers, 2, rows, width), bf16),
             pltpu.VMEM((peers, pencil if with_query else ROWS, width), bf16),
@@ -854,7 +865,7 @@
             pltpu.SemaphoreType.DMA((peers, 3)),
         ],
         rows * peers * 0.03 * MICROSECOND, aliases, near=near,
-    )[0]
+    )
 
 
 def swap(value, k, count):
@@ -920,23 +931,31 @@
     own_bias = lax.dynamic_slice_in_dim(head_bias, group * own_tracks, own_tracks).reshape(1, own_tracks)
     own_counts = lax.dynamic_slice_in_dim(counts, group * own_tracks, own_tracks, axis=1)
     logits, sums = head_rates(me, got, mine, other, own_bias, own_counts)
-    all_sums = lax.all_gather(sums, "seq")
-    part, loss = head_grads(me, logits, all_sums, mine, other, own_counts, peers)
+    all_sums = [swap(sums, k, peers) for k in range(peers)]
+    early, late = mixed_home[: peers - 1], mixed_home[peers - 1 :]
+    logits, early = lax.optimization_barrier((logits, early))
+    part, loss = head_grads(me, logits, all_sums, mine, other, own_counts)
     back = exchange(part)
+
     step = 1
     while step < groups:
         loss = loss + lax.ppermute(loss, "chan", [(i, i ^ step) for i in range(groups)])
         step *= 2
-    mean_loss = loss[0, 0] / (bins * peers * tracks)
-
+
+    back, loss, late = lax.optimization_barrier((back, loss, late))
+    mixed_home = [*early, *late]
     grad_rows, packed = sum_grads(me, back)
     grads = None
     corr_home = []
     for j in range(chunks):
         corr = correlate(me, queries, grad_rows, specs[j], skip, tables, spread, j * rows, None if j else packed)
+        grad_rows, _ = lax.optimization_barrier((grad_rows, corr))
         corr_home.append([swap(corr[k], k, peers) for k in range(peers)])
     for j in range(chunks):
-        grads = finish(me, projections, [] if j else mixed_home, corr_home[j], spread, j, chunks, grads)
+        ours = [] if j else mixed_home
+        grads, *rest = finish(me, projections, ours, corr_home[j], spread, j, chunks, grads, [] if j else [loss])
+        if not j:
+            mean_loss = rest[0].reshape(())
     return mean_loss, grads
 
 

time: 114 us -> 112 us (0.982)
  blocking collectives: 5.67 us -> 0 us
  starting transfers between devices: 36.7 us -> 41 us
  between operations: 2.73 us -> 1.05 us
    all_gather x1 -> x0, blocking collectives: 5.67 us -> none  [aligned(): all_sums = lax.all_gather(sums, 'seq')]
    ppermute x19 -> x22, starting transfers between devices: 17.5 us -> 22.1 us  [swap(): return lax.ppermute(value, 'seq', [(i, i ^ k) for i in range(count)])]
    all_to_all x2, waiting for transfers between devices: 9.37 us -> 7.58 us  [exchange(): lax.all_to_all(flat, ('chan', 'seq'), split_axis=0, concat_axis=0, tiled=...]
    ppermute x3, waiting for transfers between devices: 2.87 us -> 4.11 us  [aligned(): lax.ppermute(loss, 'chan', [(i, i ^ step) for i in range(groups)])]
    ppermute x19 -> x22, waiting for transfers between devices: 4.99 us -> 5.77 us  [swap(): return lax.ppermute(value, 'seq', [(i, i ^ k) for i in range(count)])]
  transfers between devices with their start and end apart: 25 -> 28, of which waited for: 5 -> 8; matrix products, arithmetic and copies ran while one was open for 1% -> 1% of each run, Pallas kernels for 36% -> 31%
where the time goes in v5:
time: 112 us; the launch traced here: 111 us
  Pallas kernels  48.5 us (43%)
  starting transfers between devices  41 us (37%)
  waiting for transfers between devices  17.5 us (16%)
  local copies, waits for them, and re-layouts  3.21 us (3%)
    pallas_call x13, Pallas kernels, call(): pl.pallas_call(kernel, name=name, grid_spec=pltpu.PrefetchScalarGridSpec(...  48.5 us
    ppermute x22, starting transfers between devices, swap(): return lax.ppermute(value, 'seq', [(i, i ^ k) for i in range(count)])  22.1 us
    all_to_all x2, starting transfers between devices, exchange(): lax.all_to_all(flat, ('chan', 'seq'), split_axis=0, concat_axis=0, tiled=...  8.39 us
    all_to_all x2, waiting for transfers between devices, exchange(): lax.all_to_all(flat, ('chan', 'seq'), split_axis=0, concat_axis=0, tiled=...  7.58 us
    ppermute x22, waiting for transfers between devices, swap(): return lax.ppermute(value, 'seq', [(i, i ^ k) for i in range(count)])  5.77 us
    all_to_all x1, starting transfers between devices, aligned(): mine = lax.all_to_all(mine, 'chan', split_axis=0, concat_axis=0, tiled=True)  5.7 us
    ppermute x3, starting transfers between devices, aligned(): lax.ppermute(loss, 'chan', [(i, i ^ step) for i in range(groups)])  4.81 us
    ppermute x3, waiting for transfers between devices, aligned(): lax.ppermute(loss, 'chan', [(i, i ^ step) for i in range(groups)])  4.11 us
  transfers between devices with their start and end apart: 28, of which 8 were waited for; matrix products, arithmetic and copies ran while one was open for 1% of the time, Pallas kernels for 31%

profile of v5, /device:TPU:1, one launch (start us, length us, event | category | flops | bytes accessed | tf_op | source)
XLA Modules:
  0.0 111.1 jit_solution(5867063574896621336)
XLA Ops:
  0.7 2.5 %lay_out.2 = (bf16[2,32,2048]{2,1,0:T(8,128)(2,1)}, bf16[2,32,2048]{2,1,0:T(8,128)(2,1)}, bf16[2,32,2048]{2,1,0:T(8,128)(2,1)}, bf16[2,32,2048]{2,1,0:T(8,128)(2,1)}) custom-call(s32[1]{0:T(128)} %bitcast.me_ref.refs_0_, bf16[3,256,2048]{2,1,0:T(8,128)(2,1)} %proj_ref.7, f32[256,2048]{1,0:T(8,128)} %taps_ref.3), custom_call_target="tpu_custom_call" | custom-call | flops 1920000000 | bytes 6291456 | tf_op jit(solution)/shard_map/lay_out/pallas_call | solution.py:401
  3.3 2.7 %collective-permute-start.1 = (bf16[2,32,2048]{2,1,0:T(8,128)(2,1)}, bf16[2,32,2048]{2,1,0:T(8,128)(2,1)S(1)}, u32[]{:S(2)}, u32[]{:S(2)}) collective-permute-start(bf16[2,32,2048]{2,1,0:T(8,128)(2,1)} %get-tuple-element.62), channel_id=1, source_target_pairs={{0,16},{8,24},{16,0},{24,8},{1,17},{9,25},{17,1},{25,9},{2,18},{10... | collective-permute-start | bytes 786440 | tf_op jit(solution)/shard_map/ppermute | solution.py:874
  6.0 3.1 %lay_out.3 = (bf16[2,32,2048]{2,1,0:T(8,128)(2,1)}, bf16[2,32,2048]{2,1,0:T(8,128)(2,1)}, bf16[2,32,2048]{2,1,0:T(8,128)(2,1)}, bf16[2,32,2048]{2,1,0:T(8,128)(2...) custom-call(s32[1]{0:T(128)} %bitcast.me_ref.refs_0_, ...), custom_call_target="tpu_custom_call" | custom-call | flops 1920000000 | bytes 7340032 | tf_op jit(solution)/shard_map/lay_out/pallas_call | solution.py:401
  9.5 1.4 %collective-permute-start.7 = (bf16[2,32,2048]{2,1,0:T(8,128)(2,1)}, bf16[2,32,2048]{2,1,0:T(8,128)(2,1)}, u32[]{:S(2)}, u32[]{:S(2)}) collective-permute-start(bf16[2,32,2048]{2,1,0:T(8,128)(2,1)} %get-tuple-element.75), channel_id=1, source_target_pairs={{0,16},{8,24},{16,0},{24,8},{1,17},{9,25},{17,1},{25,9},{2,18},{10... | collective-permute-start | bytes 786440 | tf_op jit(solution)/shard_map/ppermute | solution.py:874
  11.0 2.7 %by_track.1 = bf16[8,128,512]{2,1,0:T(8,128)(2,1)} custom-call(s32[1]{0:T(128)} %bitcast.me_ref.refs_0_, bf16[256,3840]{1,0:T(8,128)(2,1)} %weight_ref.1), custom_call_target="tpu_custom_call" | custom-call | flops 2000000000 | bytes 3014656 | tf_op jit(solution)/shard_map/by_track/pallas_call | solution.py:401
  13.7 5.7 %all-to-all-start.1 = ((bf16[8,128,512]{2,1,0:T(8,128)(2,1)}), bf16[8,128,512]{2,1,0:T(8,128)(2,1)S(1)}, u32[]{:S(2)}, u32[]{:S(2)}) async-start(bf16[8,128,512]{2,1,0:T(8,128)(2,1)} %by_track.1), calls=%async_computation.1 | async-start | bytes 2097152 | tf_op jit(solution)/shard_map/all_to_all | solution.py:914
  22.7 7.3 %long_convolution.2 = (f32[64,8192]{1,0:T(8,128)S(1)}, f32[2,256,256]{2,1,0:T(8,128)}, f32[2,256,256]{2,1,0:T(8,128)}, f32[2,256,256]{2,1,0:T(8,128)}, f32[2,256,256]{2,1,0:T(8,128)}) custom-call(s32[1]{0:T(128)} %bitcast.me_ref.refs_0_, bf16[2,32,2048]{2,1,0:T(8,128)(2,1)} %get-tuple-element.60.refs_1_, bf16[2,32,2048]{2,1,0:T(8,128)(2,1)} %copy-done.13, ...), custom_call_target="tpu_custom_call" | custom-call | flops 8192000000 | bytes 5832960 | tf_op jit(solution)/shard_map/long_convolution/pallas_call | solution.py:401
  31.7 7.3 %long_convolution.3 = (f32[64,8192]{1,0:T(8,128)S(1)}, f32[2,256,256]{2,1,0:T(8,128)}, f32[2,256,256]{2,1,0:T(8,128)}, f32[2,256,256]{2,1,0:T(8,128)}, f32[2,256,256]{2,1,0:T(8,128)}) custom-call(s32[1]{0:T(128)} %bitcast.me_ref.refs_0_, bf16[2,32,2048]{2,1,0:T(8,128)(2,1)} %get-tuple-element.73.refs_1_, ...), custom_call_target="tpu_custom_call", output_to_operand_aliasing={{0}: (11, {})} | custom-call | flops 8192000000 | bytes 7930112 | tf_op jit(solution)/shard_map/long_convolution/pallas_call | solution.py:401
  39.0 1.9 %collective-permute-done.5.refs_4_.refs_5_ = bf16[64,2048]{1,0:T(8,128)(2,1)S(1)} collective-permute-done((bf16[64,2048]{1,0:T(8,128)(2,1)S(1)}, bf16[64,2048]{1,0:T(8,128)(2,1)S(1)}, u32[]{:S(2)}, u32[]{:S(2)}) %collective-permute-start.5) | collective-permute-done | bytes 262176 | tf_op jit(solution)/shard_map/ppermute | solution.py:874
  40.9 2.8 %pool_bins.1 = (bf16[64,2048]{1,0:T(8,128)(2,1)}, bf16[64,2048]{1,0:T(8,128)(2,1)}, bf16[64,2048]{1,0:T(8,128)(2,1)}, bf16[64,2048]{1,0:T(8,128)(2,1)}, bf16[8,4,32,128]{3,2,1,0:T(8,128)(2,1)}) custom-call(s32[1]{0:T(128)} %bitcast.me_ref.refs_0_, bf16[64,2048]{1,0:T(8,128)(2,1)} %get-tuple-element.69.refs_1_.refs_2_, ...), custom_call_target="tpu_custom_call" | custom-call | flops 4096000000 | bytes 4521984 | tf_op jit(solution)/shard_map/pool_bins/pallas_call | solution.py:401
  44.4 1.7 %collective-permute-start.9 = (bf16[8,128,512]{2,1,0:T(8,128)(2,1)S(1)}, bf16[8,128,512]{2,1,0:T(8,128)(2,1)S(1)}, u32[]{:S(2)}, u32[]{:S(2)}) collective-permute-start(bf16[8,128,512]{2,1,0:T(8,128)(2,1)S(1)} %all-to-all-done.1.mine_ref.refs_4_), channel_id=1, source_target_pairs={{0,8},{8,0},{16,24},{24,16},{1,9},{9,1},{17,25},{25,17},{2,10},{10... | collective-permute-start | bytes 3145736 | tf_op jit(solution)/shard_map/ppermute | solution.py:874
  46.1 4.9 %all-to-all-start = ((bf16[32,32,128]{2,1,0:T(8,128)(2,1)}), bf16[32,32,128]{2,1,0:T(8,128)(2,1)S(1)}, u32[]{:S(2)}, u32[]{:S(2)}) async-start(bf16[32,32,128]{2,1,0:T(8,128)(2,1)} %bitcast.13), calls=%async_computation | async-start | bytes 524288 | tf_op jit(solution)/shard_map/all_to_all | solution.py:925
  51.3 1.5 %collective-permute-start.11 = (bf16[64,2048]{1,0:T(8,128)(2,1)}, bf16[64,2048]{1,0:T(8,128)(2,1)}, u32[]{:S(2)}, u32[]{:S(2)}) collective-permute-start(bf16[64,2048]{1,0:T(8,128)(2,1)} %get-tuple-element.85), channel_id=1, source_target_pairs={{0,16},{8,24},{16,0},{24,8},{1,17},{9,25},{17,1},{25,9},{2,18},{10... | collective-permute-start | bytes 786440 | tf_op jit(solution)/shard_map/ppermute | solution.py:874
  53.7 7.6 %all-to-all-done = bf16[32,32,128]{2,1,0:T(8,128)(2,1)S(1)} async-done(((bf16[32,32,128]{2,1,0:T(8,128)(2,1)}), bf16[32,32,128]{2,1,0:T(8,128)(2,1)S(1)}, u32[]{:S(2)}, u32[]{:S(2)}) %all-to-all-start) | async-done | bytes 262176 | tf_op jit(solution)/shard_map/all_to_all | solution.py:925
  62.5 1.5 %collective-permute-start.13 = (f32[8,480]{1,0:T(8,128)S(1)}, f32[8,480]{1,0:T(8,128)S(1)}, u32[]{:S(2)}, u32[]{:S(2)}) collective-permute-start(f32[8,480]{1,0:T(8,128)S(1)} %get-tuple-element.90.refs_0_), channel_id=1, source_target_pairs={{0,16},{8,24},{16,0},{24,8},{1,17},{9,25},{17,1},{25,9},{2,18},{10... | collective-permute-start | bytes 46088 | tf_op jit(solution)/shard_map/ppermute | solution.py:874
  64.2 1.3 %collective-permute-done.14.refs_3_ = f32[8,480]{1,0:T(8,128)S(1)} collective-permute-done((f32[8,480]{1,0:T(8,128)S(1)}, f32[8,480]{1,0:T(8,128)S(1)}, u32[]{:S(2)}, u32[]{:S(2)}) %collective-permute-start.14) | collective-permute-done | bytes 15392 | tf_op jit(solution)/shard_map/ppermute | solution.py:874
  65.5 1.5 %head_grads.1 = (bf16[8,4,32,128]{3,2,1,0:T(8,128)(2,1)}, f32[8,128]{1,0:T(8,128)S(1)}) custom-call(s32[1]{0:T(128)} %bitcast.me_ref.refs_0_, f32[64,480]{1,0:T(8,128)S(1)} %get-tuple-element.89.logits_ref, f32[8,480]{1,0:T(8,128)S(1)} %get-tuple-element.90.refs_0_, f32[8,480]{1,0:T(8,128)S(1)} %collective-permute-done.12.refs_1_, ...), custom_call_target="tpu_custom_call" | custom-call | flops 251658240 | bytes 2670592 | tf_op jit(solution)/shard_map/head_grads/pallas_call | solution.py:401
  66.9 3.5 %all-to-all-start.2 = ((bf16[32,32,128]{2,1,0:T(8,128)(2,1)}), bf16[32,32,128]{2,1,0:T(8,128)(2,1)S(1)}, u32[]{:S(2)}, u32[]{:S(2)}) async-start(bf16[32,32,128]{2,1,0:T(8,128)(2,1)} %bitcast.12), calls=%async_computation.2 | async-start | bytes 524288 | tf_op jit(solution)/shard_map/all_to_all | solution.py:925
  70.4 1.7 %collective-permute-start.18 = (bf16[64,2048]{1,0:T(8,128)(2,1)}, bf16[64,2048]{1,0:T(8,128)(2,1)S(1)}, u32[]{:S(2)}, u32[]{:S(2)}) collective-permute-start(bf16[64,2048]{1,0:T(8,128)(2,1)} %get-tuple-element.93), channel_id=1, source_target_pairs={{0,24},{8,16},{16,8},{24,0},{1,25},{9,17},{17,9},{25,1},{2,26},{10... | collective-permute-start | bytes 786440 | tf_op jit(solution)/shard_map/ppermute | solution.py:874
  72.1 1.2 %collective-permute-start.15 = (f32[8,128]{1,0:T(8,128)S(1)}, f32[8,128]{1,0:T(8,128)S(1)}, u32[]{:S(2)}, u32[]{:S(2)}) collective-permute-start(f32[8,128]{1,0:T(8,128)S(1)} %get-tuple-element.92), channel_id=1, source_target_pairs={{0,1},{1,0},{2,3},{3,2},{4,5},{5,4},{6,7},{7,6},{8,9},{9,8},{10,11... | collective-permute-start | bytes 12296 | tf_op jit(solution)/shard_map/ppermute | solution.py:942
  73.4 1.5 %collective-permute-done.15 = f32[8,128]{1,0:T(8,128)S(1)} collective-permute-done((f32[8,128]{1,0:T(8,128)S(1)}, f32[8,128]{1,0:T(8,128)S(1)}, u32[]{:S(2)}, u32[]{:S(2)}) %collective-permute-start.15) | collective-permute-done | bytes 4128 | tf_op jit(solution)/shard_map/ppermute | solution.py:942
  74.9 1.2 %collective-permute-start.16 = (f32[8,128]{1,0:T(8,128)S(1)}, f32[8,128]{1,0:T(8,128)S(1)}, u32[]{:S(2)}, u32[]{:S(2)}) collective-permute-start(f32[8,128]{1,0:T(8,128)S(1)} %add.19), channel_id=1, source_target_pairs={{0,2},{1,3},{2,0},{3,1},{4,6},{5,7},{6,4},{7,5},{8,10},{9,11},{10,... | collective-permute-start | bytes 12296 | tf_op jit(solution)/shard_map/ppermute | solution.py:942
  76.2 1.6 %collective-permute-done.16 = f32[8,128]{1,0:T(8,128)S(1)} collective-permute-done((f32[8,128]{1,0:T(8,128)S(1)}, f32[8,128]{1,0:T(8,128)S(1)}, u32[]{:S(2)}, u32[]{:S(2)}) %collective-permute-start.16) | collective-permute-done | bytes 4128 | tf_op jit(solution)/shard_map/ppermute | solution.py:942
  77.7 2.3 %collective-permute-start.17 = (f32[8,128]{1,0:T(8,128)S(1)}, f32[8,128]{1,0:T(8,128)S(1)}, u32[]{:S(2)}, u32[]{:S(2)}) collective-permute-start(f32[8,128]{1,0:T(8,128)S(1)} %add.20), channel_id=1, source_target_pairs={{0,4},{1,5},{2,6},{3,7},{4,0},{5,1},{6,2},{7,3},{8,12},{9,13},{10,... | collective-permute-start | bytes 12296 | tf_op jit(solution)/shard_map/ppermute | solution.py:942
  81.7 6.8 %long_correlation.2 = (bf16[32,2304]{1,0:T(8,128)(2,1)}, bf16[32,2304]{1,0:T(8,128)(2,1)}, bf16[32,2304]{1,0:T(8,128)(2,1)}, bf16[32,2304]{1,0:T(8,128)(2,1)}) custom-call(s32[1]{0:T(128)} %bitcast.me_ref.refs_0_, f32[4,32,128]{2,1,0:T(8,128)S(1)} %get-tuple-element.96.refs_1_, bf16[64,2048]{1,0:T(8,128)(2,1)} %get-tuple-element.69.refs_1_.refs_2_, ...), custom_call_target="tpu_custom_call" | custom-call | flops 8192000000 | bytes 4522240 | tf_op jit(solution)/shard_map/long_correlation/pallas_call | solution.py:401
  88.5 2.6 %collective-permute-start.19 = (bf16[32,2304]{1,0:T(8,128)(2,1)}, bf16[32,2304]{1,0:T(8,128)(2,1)S(1)}, u32[]{:S(2)}, u32[]{:S(2)}) collective-permute-start(bf16[32,2304]{1,0:T(8,128)(2,1)} %get-tuple-element.103), channel_id=1, source_target_pairs={{0,8},{8,0},{16,24},{24,16},{1,9},{9,1},{17,25},{25,17},{2,10},{10... | collective-permute-start | bytes 442376 | tf_op jit(solution)/shard_map/ppermute | solution.py:874
  91.2 1.7 %collective-permute-start.21 = (bf16[32,2304]{1,0:T(8,128)(2,1)}, bf16[32,2304]{1,0:T(8,128)(2,1)S(1)}, u32[]{:S(2)}, u32[]{:S(2)}) collective-permute-start(bf16[32,2304]{1,0:T(8,128)(2,1)} %get-tuple-element.105), channel_id=1, source_target_pairs={{0,24},{8,16},{16,8},{24,0},{1,25},{9,17},{17,9},{25,1},{2,26},{10... | collective-permute-start | bytes 442376 | tf_op jit(solution)/shard_map/ppermute | solution.py:874
  92.9 6.9 %long_correlation.3 = (bf16[32,2048]{1,0:T(8,128)(2,1)}, bf16[32,2048]{1,0:T(8,128)(2,1)}, bf16[32,2048]{1,0:T(8,128)(2,1)}, bf16[32,2048]{1,0:T(8,128)(2,1)}) custom-call(s32[1]{0:T(128)} %bitcast.me_ref.refs_0_, bf16[64,2048]{1,0:T(8,128)(2,1)} %get-tuple-element.69.refs_1_.refs_2_, bf16[64,2048]{1,0:T(8,128)(2,1)} %copy-done.3, ...), custom_call_target="tpu_custom_call" | custom-call | flops 8192000000 | bytes 4391168 | tf_op jit(solution)/shard_map/long_correlation/pallas_call | solution.py:401
  100.0 1.9 %collective-permute-start.24 = (bf16[32,2048]{1,0:T(8,128)(2,1)}, bf16[32,2048]{1,0:T(8,128)(2,1)S(1)}, u32[]{:S(2)}, u32[]{:S(2)}) collective-permute-start(bf16[32,2048]{1,0:T(8,128)(2,1)} %get-tuple-element.116), channel_id=1, source_target_pairs={{0,24},{8,16},{16,8},{24,0},{1,25},{9,17},{17,9},{25,1},{2,26},{10... | collective-permute-start | bytes 393224 | tf_op jit(solution)/shard_map/ppermute | solution.py:874
  102.0 4.2 %finish.2 = (f32[3,256,2048]{2,1,0:T(8,128)}, f32[1,1]{1,0:T(1,128)}) custom-call(s32[1]{0:T(128)} %bitcast.me_ref.refs_0_, bf16[256,128]{1,0:T(8,128)(2,1)S(1)} %copy-done.2, bf16[3,256,2048]{2,1,0:T(8,128)(2,1)} %proj_ref.7, bf16[64,2048]{1,0:T(8,128)(2,1)S(1)} %copy-done.6, bf16[64,2048]{1,0:T(8,128)(2,1)} %collective-permute-done.10.refs_1_, ...), custom_call_target="tpu_custom_call" | custom-call | flops 3840000000 | bytes 11145220 | tf_op jit(solution)/shard_map/finish/pallas_call | solution.py:401
  106.2 2.0 %collective-permute-done.24.refs_3_ = bf16[32,2048]{1,0:T(8,128)(2,1)S(1)} collective-permute-done((bf16[32,2048]{1,0:T(8,128)(2,1)}, bf16[32,2048]{1,0:T(8,128)(2,1)S(1)}, u32[]{:S(2)}, u32[]{:S(2)}) %collective-permute-start.24) | collective-permute-done | bytes 131104 | tf_op jit(solution)/shard_map/ppermute | solution.py:874
  108.2 2.8 %finish.3 = f32[3,256,2048]{2,1,0:T(8,128)} custom-call(s32[1]{0:T(128)} %bitcast.me_ref.refs_0_, bf16[256,128]{1,0:T(8,128)(2,1)S(1)} %copy-done.2, bf16[3,256,2048]{2,1,0:T(8,128)(2,1)} %proj_ref.7, bf16[32,2048]{1,0:T(8,128)(2,1)S(1)} %copy-done.1, bf16[32,2048]{1,0:T(8,128)(2,1)S(1)} %collective-permute-done.22.refs_1_, ...), custom_call_target="tpu_custom_call", output_to_operand_aliasing={{}: (7, {})} | custom-call | flops 3840000000 | bytes 16318464 | tf_op jit(solution)/shard_map/finish/pallas_call | solution.py:401
  (77 shorter events, 10.8 us)
Async XLA Ops:
  0.6 53.0 %copy-start = (s32[64,3840]{1,0:T(8,128)S(1)}, s32[64,3840]{1,0:T(8,128)}, u32[]{:S(2)}) copy-start(s32[64,3840]{1,0:T(8,128)} %param.18) | copy-start | bytes 2949124
  3.2 16.4 %collective-permute-start = (bf16[2,32,2048]{2,1,0:T(8,128)(2,1)}, bf16[2,32,2048]{2,1,0:T(8,128)(2,1)S(1)}, u32[]{:S(2)}, u32[]{:S(2)}) collective-permute-start(bf16[2,32,2048]{2,1,0:T(8,128)(2,1)} %get-tuple-element.61), channel_id=1, source_target_pairs={{0,8},{8,0},{16,24},{24,16},{1,9},{9,1},{17,25},{25,17},{2,10},{10... | collective-permute-start | bytes 786440 | tf_op jit(solution)/shard_map/ppermute | solution.py:874
  3.3 17.4 %collective-permute-start.1 = (bf16[2,32,2048]{2,1,0:T(8,128)(2,1)}, bf16[2,32,2048]{2,1,0:T(8,128)(2,1)S(1)}, u32[]{:S(2)}, u32[]{:S(2)}) collective-permute-start(bf16[2,32,2048]{2,1,0:T(8,128)(2,1)} %get-tuple-element.62), channel_id=1, source_target_pairs={{0,16},{8,24},{16,0},{24,8},{1,17},{9,25},{17,1},{25,9},{2,18},{10... | collective-permute-start | bytes 786440 | tf_op jit(solution)/shard_map/ppermute | solution.py:874
  6.0 14.7 %collective-permute-start.2 = (bf16[2,32,2048]{2,1,0:T(8,128)(2,1)}, bf16[2,32,2048]{2,1,0:T(8,128)(2,1)}, u32[]{:S(2)}, u32[]{:S(2)}) collective-permute-start(bf16[2,32,2048]{2,1,0:T(8,128)(2,1)} %get-tuple-element.63), channel_id=1, source_target_pairs={{0,24},{8,16},{16,8},{24,0},{1,25},{9,17},{17,9},{25,1},{2,26},{10... | collective-permute-start | bytes 786440 | tf_op jit(solution)/shard_map/ppermute | solution.py:874
  9.1 20.9 %collective-permute-start.6 = (bf16[2,32,2048]{2,1,0:T(8,128)(2,1)}, bf16[2,32,2048]{2,1,0:T(8,128)(2,1)S(1)}, u32[]{:S(2)}, u32[]{:S(2)}) collective-permute-start(bf16[2,32,2048]{2,1,0:T(8,128)(2,1)} %get-tuple-element.74), channel_id=1, source_target_pairs={{0,8},{8,0},{16,24},{24,16},{1,9},{9,1},{17,25},{25,17},{2,10},{10... | collective-permute-start | bytes 786440 | tf_op jit(solution)/shard_map/ppermute | solution.py:874
  9.5 21.4 %collective-permute-start.7 = (bf16[2,32,2048]{2,1,0:T(8,128)(2,1)}, bf16[2,32,2048]{2,1,0:T(8,128)(2,1)}, u32[]{:S(2)}, u32[]{:S(2)}) collective-permute-start(bf16[2,32,2048]{2,1,0:T(8,128)(2,1)} %get-tuple-element.75), channel_id=1, source_target_pairs={{0,16},{8,24},{16,0},{24,8},{1,17},{9,25},{17,1},{25,9},{2,18},{10... | collective-permute-start | bytes 786440 | tf_op jit(solution)/shard_map/ppermute | solution.py:874
  13.7 30.7 %all-to-all-start.1 = ((bf16[8,128,512]{2,1,0:T(8,128)(2,1)}), bf16[8,128,512]{2,1,0:T(8,128)(2,1)S(1)}, u32[]{:S(2)}, u32[]{:S(2)}) async-start(bf16[8,128,512]{2,1,0:T(8,128)(2,1)} %by_track.1), calls=%async_computation.1 | async-start | bytes 2097152 | tf_op jit(solution)/shard_map/all_to_all | solution.py:914
  19.6 10.4 %copy-start.9 = (bf16[64,2048]{1,0:T(8,128)(2,1)S(1)}, bf16[64,2048]{1,0:T(8,128)(2,1)}, u32[]{:S(2)}) copy-start(bf16[64,2048]{1,0:T(8,128)(2,1)} %get-tuple-element.72) | copy-start | bytes 786436
  19.6 11.4 %collective-permute-start.8 = (bf16[2,32,2048]{2,1,0:T(8,128)(2,1)}, bf16[2,32,2048]{2,1,0:T(8,128)(2,1)S(1)}, u32[]{:S(2)}, u32[]{:S(2)}) collective-permute-start(bf16[2,32,2048]{2,1,0:T(8,128)(2,1)} %get-tuple-element.76), channel_id=1, source_target_pairs={{0,24},{8,16},{16,8},{24,0},{1,25},{9,17},{17,9},{25,1},{2,26},{10... | collective-permute-start | bytes 786440 | tf_op jit(solution)/shard_map/ppermute | solution.py:874
  21.4 17.6 %collective-permute-start.3 = (bf16[64,2048]{1,0:T(8,128)(2,1)S(1)}, bf16[64,2048]{1,0:T(8,128)(2,1)S(1)}, u32[]{:S(2)}, u32[]{:S(2)}) collective-permute-start(bf16[64,2048]{1,0:T(8,128)(2,1)S(1)} %copy-done.11), channel_id=1, source_target_pairs={{0,8},{8,0},{16,24},{24,16},{1,9},{9,1},{17,25},{25,17},{2,10},{10... | collective-permute-start | bytes 786440 | tf_op jit(solution)/shard_map/ppermute | solution.py:874
  21.9 17.1 %collective-permute-start.4 = (bf16[64,2048]{1,0:T(8,128)(2,1)S(1)}, bf16[64,2048]{1,0:T(8,128)(2,1)S(1)}, u32[]{:S(2)}, u32[]{:S(2)}) collective-permute-start(bf16[64,2048]{1,0:T(8,128)(2,1)S(1)} %copy-done.10), channel_id=1, source_target_pairs={{0,16},{8,24},{16,0},{24,8},{1,17},{9,25},{17,1},{25,9},{2,18},{10... | collective-permute-start | bytes 786440 | tf_op jit(solution)/shard_map/ppermute | solution.py:874
  30.0 10.9 %collective-permute-start.5 = (bf16[64,2048]{1,0:T(8,128)(2,1)S(1)}, bf16[64,2048]{1,0:T(8,128)(2,1)S(1)}, u32[]{:S(2)}, u32[]{:S(2)}) collective-permute-start(bf16[64,2048]{1,0:T(8,128)(2,1)S(1)} %copy-done.9), channel_id=1, source_target_pairs={{0,24},{8,16},{16,8},{24,0},{1,25},{9,17},{17,9},{25,1},{2,26},{10... | collective-permute-start | bytes 786440 | tf_op jit(solution)/shard_map/ppermute | solution.py:874
  44.4 16.9 %collective-permute-start.9 = (bf16[8,128,512]{2,1,0:T(8,128)(2,1)S(1)}, bf16[8,128,512]{2,1,0:T(8,128)(2,1)S(1)}, u32[]{:S(2)}, u32[]{:S(2)}) collective-permute-start(bf16[8,128,512]{2,1,0:T(8,128)(2,1)S(1)} %all-to-all-done.1.mine_ref.refs_4_), channel_id=1, source_target_pairs={{0,8},{8,0},{16,24},{24,16},{1,9},{9,1},{17,25},{25,17},{2,10},{10... | collective-permute-start | bytes 3145736 | tf_op jit(solution)/shard_map/ppermute | solution.py:874
  46.1 15.2 %all-to-all-start = ((bf16[32,32,128]{2,1,0:T(8,128)(2,1)}), bf16[32,32,128]{2,1,0:T(8,128)(2,1)S(1)}, u32[]{:S(2)}, u32[]{:S(2)}) async-start(bf16[32,32,128]{2,1,0:T(8,128)(2,1)} %bitcast.13), calls=%async_computation | async-start | bytes 524288 | tf_op jit(solution)/shard_map/all_to_all | solution.py:925
  51.0 13.1 %collective-permute-start.10 = (bf16[64,2048]{1,0:T(8,128)(2,1)}, bf16[64,2048]{1,0:T(8,128)(2,1)}, u32[]{:S(2)}, u32[]{:S(2)}) collective-permute-start(bf16[64,2048]{1,0:T(8,128)(2,1)} %get-tuple-element.84), channel_id=1, source_target_pairs={{0,8},{8,0},{16,24},{24,16},{1,9},{9,1},{17,25},{25,17},{2,10},{10... | collective-permute-start | bytes 786440 | tf_op jit(solution)/shard_map/ppermute | solution.py:874
  51.3 12.8 %collective-permute-start.11 = (bf16[64,2048]{1,0:T(8,128)(2,1)}, bf16[64,2048]{1,0:T(8,128)(2,1)}, u32[]{:S(2)}, u32[]{:S(2)}) collective-permute-start(bf16[64,2048]{1,0:T(8,128)(2,1)} %get-tuple-element.85), channel_id=1, source_target_pairs={{0,16},{8,24},{16,0},{24,8},{1,17},{9,25},{17,1},{25,9},{2,18},{10... | collective-permute-start | bytes 786440 | tf_op jit(solution)/shard_map/ppermute | solution.py:874
  61.9 3.5 %collective-permute-start.14 = (f32[8,480]{1,0:T(8,128)S(1)}, f32[8,480]{1,0:T(8,128)S(1)}, u32[]{:S(2)}, u32[]{:S(2)}) collective-permute-start(f32[8,480]{1,0:T(8,128)S(1)} %get-tuple-element.90.refs_0_), channel_id=1, source_target_pairs={{0,24},{8,16},{16,8},{24,0},{1,25},{9,17},{17,9},{25,1},{2,26},{10... | collective-permute-start | bytes 46088 | tf_op jit(solution)/shard_map/ppermute | solution.py:874
  62.5 3.0 %collective-permute-start.13 = (f32[8,480]{1,0:T(8,128)S(1)}, f32[8,480]{1,0:T(8,128)S(1)}, u32[]{:S(2)}, u32[]{:S(2)}) collective-permute-start(f32[8,480]{1,0:T(8,128)S(1)} %get-tuple-element.90.refs_0_), channel_id=1, source_target_pairs={{0,16},{8,24},{16,0},{24,8},{1,17},{9,25},{17,1},{25,9},{2,18},{10... | collective-permute-start | bytes 46088 | tf_op jit(solution)/shard_map/ppermute | solution.py:874
  64.0 1.5 %collective-permute-start.12 = (f32[8,480]{1,0:T(8,128)S(1)}, f32[8,480]{1,0:T(8,128)S(1)}, u32[]{:S(2)}, u32[]{:S(2)}) collective-permute-start(f32[8,480]{1,0:T(8,128)S(1)} %get-tuple-element.90.refs_0_), channel_id=1, source_target_pairs={{0,8},{8,0},{16,24},{24,16},{1,9},{9,1},{17,25},{25,17},{2,10},{10... | collective-permute-start | bytes 46088 | tf_op jit(solution)/shard_map/ppermute | solution.py:874
  66.9 14.7 %all-to-all-start.2 = ((bf16[32,32,128]{2,1,0:T(8,128)(2,1)}), bf16[32,32,128]{2,1,0:T(8,128)(2,1)S(1)}, u32[]{:S(2)}, u32[]{:S(2)}) async-start(bf16[32,32,128]{2,1,0:T(8,128)(2,1)} %bitcast.12), calls=%async_computation.2 | async-start | bytes 524288 | tf_op jit(solution)/shard_map/all_to_all | solution.py:925
  70.4 11.2 %collective-permute-start.18 = (bf16[64,2048]{1,0:T(8,128)(2,1)}, bf16[64,2048]{1,0:T(8,128)(2,1)S(1)}, u32[]{:S(2)}, u32[]{:S(2)}) collective-permute-start(bf16[64,2048]{1,0:T(8,128)(2,1)} %get-tuple-element.93), channel_id=1, source_target_pairs={{0,24},{8,16},{16,8},{24,0},{1,25},{9,17},{17,9},{25,1},{2,26},{10... | collective-permute-start | bytes 786440 | tf_op jit(solution)/shard_map/ppermute | solution.py:874
  72.1 2.8 %collective-permute-start.15 = (f32[8,128]{1,0:T(8,128)S(1)}, f32[8,128]{1,0:T(8,128)S(1)}, u32[]{:S(2)}, u32[]{:S(2)}) collective-permute-start(f32[8,128]{1,0:T(8,128)S(1)} %get-tuple-element.92), channel_id=1, source_target_pairs={{0,1},{1,0},{2,3},{3,2},{4,5},{5,4},{6,7},{7,6},{8,9},{9,8},{10,11... | collective-permute-start | bytes 12296 | tf_op jit(solution)/shard_map/ppermute | solution.py:942
  74.9 2.8 %collective-permute-start.16 = (f32[8,128]{1,0:T(8,128)S(1)}, f32[8,128]{1,0:T(8,128)S(1)}, u32[]{:S(2)}, u32[]{:S(2)}) collective-permute-start(f32[8,128]{1,0:T(8,128)S(1)} %add.19), channel_id=1, source_target_pairs={{0,2},{1,3},{2,0},{3,1},{4,6},{5,7},{6,4},{7,5},{8,10},{9,11},{10,... | collective-permute-start | bytes 12296 | tf_op jit(solution)/shard_map/ppermute | solution.py:942
  77.7 3.4 %collective-permute-start.17 = (f32[8,128]{1,0:T(8,128)S(1)}, f32[8,128]{1,0:T(8,128)S(1)}, u32[]{:S(2)}, u32[]{:S(2)}) collective-permute-start(f32[8,128]{1,0:T(8,128)S(1)} %add.20), channel_id=1, source_target_pairs={{0,4},{1,5},{2,6},{3,7},{4,0},{5,1},{6,2},{7,3},{8,12},{9,13},{10,... | collective-permute-start | bytes 12296 | tf_op jit(solution)/shard_map/ppermute | solution.py:942
  88.5 11.5 %collective-permute-start.19 = (bf16[32,2304]{1,0:T(8,128)(2,1)}, bf16[32,2304]{1,0:T(8,128)(2,1)S(1)}, u32[]{:S(2)}, u32[]{:S(2)}) collective-permute-start(bf16[32,2304]{1,0:T(8,128)(2,1)} %get-tuple-element.103), channel_id=1, source_target_pairs={{0,8},{8,0},{16,24},{24,16},{1,9},{9,1},{17,25},{25,17},{2,10},{10... | collective-permute-start | bytes 442376 | tf_op jit(solution)/shard_map/ppermute | solution.py:874
  91.1 10.8 %collective-permute-start.20 = (bf16[32,2304]{1,0:T(8,128)(2,1)}, bf16[32,2304]{1,0:T(8,128)(2,1)S(1)}, u32[]{:S(2)}, u32[]{:S(2)}) collective-permute-start(bf16[32,2304]{1,0:T(8,128)(2,1)} %get-tuple-element.104), channel_id=1, source_target_pairs={{0,16},{8,24},{16,0},{24,8},{1,17},{9,25},{17,1},{25,9},{2,18},{10... | collective-permute-start | bytes 442376 | tf_op jit(solution)/shard_map/ppermute | solution.py:874
  91.2 10.8 %collective-permute-start.21 = (bf16[32,2304]{1,0:T(8,128)(2,1)}, bf16[32,2304]{1,0:T(8,128)(2,1)S(1)}, u32[]{:S(2)}, u32[]{:S(2)}) collective-permute-start(bf16[32,2304]{1,0:T(8,128)(2,1)} %get-tuple-element.105), channel_id=1, source_target_pairs={{0,24},{8,16},{16,8},{24,0},{1,25},{9,17},{17,9},{25,1},{2,26},{10... | collective-permute-start | bytes 442376 | tf_op jit(solution)/shard_map/ppermute | solution.py:874
  92.8 9.1 %copy-start.6 = (bf16[64,2048]{1,0:T(8,128)(2,1)S(1)}, bf16[64,2048]{1,0:T(8,128)(2,1)}, u32[]{:S(2)}) copy-start(bf16[64,2048]{1,0:T(8,128)(2,1)} %get-tuple-element.86.refs_0_) | copy-start | bytes 786436
  92.8 9.1 %copy-start.7 = (bf16[32,2304]{1,0:T(8,128)(2,1)S(1)}, bf16[32,2304]{1,0:T(8,128)(2,1)}, u32[]{:S(2)}) copy-start(bf16[32,2304]{1,0:T(8,128)(2,1)} %get-tuple-element.102.refs_4_) | copy-start | bytes 442372
  99.7 6.4 %collective-permute-start.22 = (bf16[32,2048]{1,0:T(8,128)(2,1)}, bf16[32,2048]{1,0:T(8,128)(2,1)S(1)}, u32[]{:S(2)}, u32[]{:S(2)}) collective-permute-start(bf16[32,2048]{1,0:T(8,128)(2,1)} %get-tuple-element.114), channel_id=1, source_target_pairs={{0,8},{8,0},{16,24},{24,16},{1,9},{9,1},{17,25},{25,17},{2,10},{10... | collective-permute-start | bytes 393224 | tf_op jit(solution)/shard_map/ppermute | solution.py:874
  100.0 6.2 %collective-permute-start.23 = (bf16[32,2048]{1,0:T(8,128)(2,1)}, bf16[32,2048]{1,0:T(8,128)(2,1)S(1)}, u32[]{:S(2)}, u32[]{:S(2)}) collective-permute-start(bf16[32,2048]{1,0:T(8,128)(2,1)} %get-tuple-element.115), channel_id=1, source_target_pairs={{0,16},{8,24},{16,0},{24,8},{1,17},{9,25},{17,1},{25,9},{2,18},{10... | collective-permute-start | bytes 393224 | tf_op jit(solution)/shard_map/ppermute | solution.py:874
  100.0 8.2 %collective-permute-start.24 = (bf16[32,2048]{1,0:T(8,128)(2,1)}, bf16[32,2048]{1,0:T(8,128)(2,1)S(1)}, u32[]{:S(2)}, u32[]{:S(2)}) collective-permute-start(bf16[32,2048]{1,0:T(8,128)(2,1)} %get-tuple-element.116), channel_id=1, source_target_pairs={{0,24},{8,16},{16,8},{24,0},{1,25},{9,17},{17,9},{25,1},{2,26},{10... | collective-permute-start | bytes 393224 | tf_op jit(solution)/shard_map/ppermute | solution.py:874
  (12 other events, 52.6 us)

commit v6 on v5

--- a/solution.py
+++ b/solution.py
@@ -29,6 +29,19 @@
     high = table.astype(ml_dtypes.bfloat16)
     low = (table - high.astype(np.float64)).astype(ml_dtypes.bfloat16)
     return high, low
+
+
+def kind_scale(table):
+    values = np.unique(np.abs(table))
+    factors = np.linspace(1.0, 2.0, 4001)
+
+    def lost(factor):
+        scaled = table[: LANES // 2] * factor
+        return np.sum((scaled - split_bf16(scaled)[0].astype(np.float64)) ** 2) / factor**2
+
+    rough = [np.sum((values * f - split_bf16(values * f)[0].astype(np.float64)) ** 2) / f**2 for f in factors]
+    best = np.argsort(rough, kind="stable")[:8]
+    return float(min((factors[i] for i in best), key=lost))
 
 
 def radices(outer):
@@ -47,11 +60,15 @@
     backward = np.block([[wr, -wi], [wi, wr]]) / length
     k1 = np.arange(outer)[:, None]
     twist = 2.0 * np.pi * (k1 - SHIFT) * idx[None, :] / length
+    scale = kind_scale(forward)
     f_hi, f_lo = split_bf16(forward)
     b_hi, b_lo = split_bf16(backward)
     return dict(
         fwd=[f_hi, f_lo],
         bwd=[b_hi, b_lo],
+        scale=scale,
+        fwd_scaled=[split_bf16(forward * scale)[0]],
+        bwd_scaled=[split_bf16(backward * scale)[0]],
         twist=np.stack([np.cos(twist), -np.sin(twist)]).astype(np.float32),
     )
 
@@ -137,6 +154,9 @@
 
 def lane_transform(lhs, table_refs):
     high = lhs[0]
+    if len(table_refs) == 1:
+        table = table_refs[0][...]
+        return dot(high, table) + dot(lhs[1], table)
     table_high, table_low = table_refs[0][...], table_refs[1][...]
     return dot(high, table_high) + (dot(lhs[1], table_high) + dot(high, table_low))
 
@@ -182,7 +202,7 @@
         store(b, alpha, re, im)
 
 
-def back_first_pass(parts, outer, emit):
+def back_first_pass(parts, outer, emit, scale=1.0):
     ra, rb = radices(outer)
     for b in range(rb):
         values = [(parts[0, b, alpha], parts[1, b, alpha]) for alpha in range(ra)]
@@ -190,8 +210,11 @@
         for a in range(ra):
             angle = -2.0 * math.pi * a * SHIFT / ra
             re, im = out[a]
-            c, s = math.cos(angle), math.sin(angle)
-            emit(rb * a + b, re if a == 0 else re * c - im * s)
+            c, s = math.cos(angle) * scale, math.sin(angle) * scale
+            if a == 0:
+                emit(rb * a + b, re if scale == 1.0 else re * scale)
+            else:
+                emit(rb * a + b, re * c - im * s)
 
 
 def put_product(re, im, lhs, start):
@@ -303,15 +326,15 @@
         outs[k][...] = rows_out[me ^ k]
 
 
-def corr_kernel(peers, outer, packed, me_ref, *refs):
+def corr_kernel(peers, outer, packed, scale, me_ref, *refs):
     if packed:
         packed_ref, refs = refs[0], refs[1:]
     queries = refs[:peers]
     refs, spec_refs = refs[: peers] + refs[peers + SPECTRA :], refs[peers : peers + SPECTRA]
-    grad_ref, skip_ref, *tables, twist_ref, spread_ref = refs[peers : peers + 8]
-    fwd_ref, bwd_ref = tables[:2], tables[2:]
-    outs = refs[peers + 8 : 2 * peers + 8]
-    rows_in, lhs_g, gated, parts_g, parts_y, lhs, rows_out = refs[2 * peers + 8 :]
+    grad_ref, skip_ref, *tables, twist_ref, spread_ref = refs[peers : peers + 6]
+    fwd_ref, bwd_ref = tables[:1], tables[1:]
+    outs = refs[peers + 6 : 2 * peers + 6]
+    rows_in, lhs_g, gated, parts_g, parts_y, lhs, rows_out = refs[2 * peers + 6 :]
     me = me_ref[0]
     ra, rb = radices(outer)
     per = outer // peers
@@ -365,7 +388,7 @@
         lanes = slice((n1 % per) * LANES, (n1 % per + 1) * LANES)
         rows_out[n1 // per, :, lanes] = (value + skip * load_g(n1)).astype(jnp.bfloat16)
 
-    back_first_pass(parts_y, outer, emit)
+    back_first_pass(parts_y, outer, emit, scale)
     step, steps = pl.program_id(0), pl.num_programs(0)
     for k in range(peers):
         outs[k][:, : per * LANES] = rows_out[me ^ k]
@@ -509,7 +532,7 @@
     chunk = rb * ROWS
     first = start // ROWS
     f32, bf16 = jnp.float32, jnp.bfloat16
-    fwd, bwd, twist = tables["fwd"], tables["bwd"], tables["twist"]
+    fwd, bwd, twist = tables["fwd_scaled"], tables["bwd_scaled"], tables["twist"]
     in_specs = [by_rows(width, start=first)] * peers + [
         *[pl.BlockSpec((1, *part.shape[1:]), lambda i, me: (i, 0, 0)) for part in spec],
         by_rows(bins, start=first),
@@ -528,7 +551,7 @@
     ]
 
     def kernel(*refs):
-        corr_kernel(peers, outer, packed is not None, *refs)
+        corr_kernel(peers, outer, packed is not None, 1.0 / tables["scale"] ** 2, *refs)
 
     inputs = [*queries, *spec, grad_pooled, skip, *fwd, *bwd, twist, spread]
     sent = width
@@ -536,11 +559,11 @@
         sent = width + packed.shape[1] // (rows // 2) * LANES
         inputs = [packed, *inputs]
         in_specs = [whole(packed), *in_specs]
-    near = len(inputs) - 8
+    near = len(inputs) - 6
     return call(
         kernel, "long_correlation", me, rows // ROWS, inputs, in_specs,
         [shape((rows, sent), bf16)] * peers, [by_rows(sent)] * peers,
-        scratch, rows * outer * 0.004 * MICROSECOND, near=(0, near, near + 1) if packed is not None else (near, near + 1),
+        scratch, rows * outer * 0.004 * MICROSECOND, near=((0,) if packed is not None else ()) + (near, near + 1, *range(len(inputs), len(inputs) + peers)),
     )
 
 

time: 112 us -> 109 us (0.973)
  Pallas kernels: 48.5 us -> 45.8 us
    pallas_call x13, Pallas kernels: 48.5 us -> 45.8 us  [call(): pl.pallas_call(kernel, name=name, grid_spec=pltpu.PrefetchScalarGridSpec(...]
where the time goes in v6:
time: 109 us; the launch traced here: 108 us
  Pallas kernels  45.8 us (42%)
  starting transfers between devices  40.9 us (38%)
  waiting for transfers between devices  17.3 us (16%)
  local copies, waits for them, and re-layouts  3.2 us (3%)
    pallas_call x13, Pallas kernels, call(): pl.pallas_call(kernel, name=name, grid_spec=pltpu.PrefetchScalarGridSpec(...  45.8 us
    ppermute x22, starting transfers between devices, swap(): return lax.ppermute(value, 'seq', [(i, i ^ k) for i in range(count)])  22.1 us
    all_to_all x2, starting transfers between devices, exchange(): lax.all_to_all(flat, ('chan', 'seq'), split_axis=0, concat_axis=0, tiled=...  8.38 us
    all_to_all x2, waiting for transfers between devices, exchange(): lax.all_to_all(flat, ('chan', 'seq'), split_axis=0, concat_axis=0, tiled=...  7.58 us
    all_to_all x1, starting transfers between devices, aligned(): mine = lax.all_to_all(mine, 'chan', split_axis=0, concat_axis=0, tiled=True)  5.7 us
    ppermute x22, waiting for transfers between devices, swap(): return lax.ppermute(value, 'seq', [(i, i ^ k) for i in range(count)])  5.59 us
    ppermute x3, starting transfers between devices, aligned(): lax.ppermute(loss, 'chan', [(i, i ^ step) for i in range(groups)])  4.81 us
    ppermute x3, waiting for transfers between devices, aligned(): lax.ppermute(loss, 'chan', [(i, i ^ step) for i in range(groups)])  4.11 us
  transfers between devices with their start and end apart: 28, of which 8 were waited for; matrix products, arithmetic and copies ran while one was open for 1% of the time, Pallas kernels for 31%

profile of v6, /device:TPU:1, one launch (start us, length us, event | category | flops | bytes accessed | tf_op | source)
XLA Modules:
  0.0 108.3 jit_solution(3569590848786061835)
XLA Ops:
  0.7 2.5 %lay_out.2 = (bf16[2,32,2048]{2,1,0:T(8,128)(2,1)}, bf16[2,32,2048]{2,1,0:T(8,128)(2,1)}, bf16[2,32,2048]{2,1,0:T(8,128)(2,1)}, bf16[2,32,2048]{2,1,0:T(8,128)(2,1)}) custom-call(s32[1]{0:T(128)} %bitcast.me_ref.refs_0_, bf16[3,256,2048]{2,1,0:T(8,128)(2,1)} %proj_ref.7, f32[256,2048]{1,0:T(8,128)} %taps_ref.3), custom_call_target="tpu_custom_call" | custom-call | flops 1920000000 | bytes 6291456 | tf_op jit(solution)/shard_map/lay_out/pallas_call | solution.py:424
  3.3 2.7 %collective-permute-start.1 = (bf16[2,32,2048]{2,1,0:T(8,128)(2,1)}, bf16[2,32,2048]{2,1,0:T(8,128)(2,1)S(1)}, u32[]{:S(2)}, u32[]{:S(2)}) collective-permute-start(bf16[2,32,2048]{2,1,0:T(8,128)(2,1)} %get-tuple-element.62), channel_id=1, source_target_pairs={{0,16},{8,24},{16,0},{24,8},{1,17},{9,25},{17,1},{25,9},{2,18},{10... | collective-permute-start | bytes 786440 | tf_op jit(solution)/shard_map/ppermute | solution.py:897
  6.0 3.0 %lay_out.3 = (bf16[2,32,2048]{2,1,0:T(8,128)(2,1)}, bf16[2,32,2048]{2,1,0:T(8,128)(2,1)}, bf16[2,32,2048]{2,1,0:T(8,128)(2,1)}, bf16[2,32,2048]{2,1,0:T(8,128)(2...) custom-call(s32[1]{0:T(128)} %bitcast.me_ref.refs_0_, ...), custom_call_target="tpu_custom_call" | custom-call | flops 1920000000 | bytes 7340032 | tf_op jit(solution)/shard_map/lay_out/pallas_call | solution.py:424
  9.5 1.4 %collective-permute-start.7 = (bf16[2,32,2048]{2,1,0:T(8,128)(2,1)}, bf16[2,32,2048]{2,1,0:T(8,128)(2,1)}, u32[]{:S(2)}, u32[]{:S(2)}) collective-permute-start(bf16[2,32,2048]{2,1,0:T(8,128)(2,1)} %get-tuple-element.75), channel_id=1, source_target_pairs={{0,16},{8,24},{16,0},{24,8},{1,17},{9,25},{17,1},{25,9},{2,18},{10... | collective-permute-start | bytes 786440 | tf_op jit(solution)/shard_map/ppermute | solution.py:897
  11.0 2.7 %by_track.1 = bf16[8,128,512]{2,1,0:T(8,128)(2,1)} custom-call(s32[1]{0:T(128)} %bitcast.me_ref.refs_0_, bf16[256,3840]{1,0:T(8,128)(2,1)} %weight_ref.1), custom_call_target="tpu_custom_call" | custom-call | flops 2000000000 | bytes 3014656 | tf_op jit(solution)/shard_map/by_track/pallas_call | solution.py:424
  13.7 5.7 %all-to-all-start.1 = ((bf16[8,128,512]{2,1,0:T(8,128)(2,1)}), bf16[8,128,512]{2,1,0:T(8,128)(2,1)S(1)}, u32[]{:S(2)}, u32[]{:S(2)}) async-start(bf16[8,128,512]{2,1,0:T(8,128)(2,1)} %by_track.1), calls=%async_computation.1 | async-start | bytes 2097152 | tf_op jit(solution)/shard_map/all_to_all | solution.py:937
  22.7 7.3 %long_convolution.2 = (f32[64,8192]{1,0:T(8,128)S(1)}, f32[2,256,256]{2,1,0:T(8,128)}, f32[2,256,256]{2,1,0:T(8,128)}, f32[2,256,256]{2,1,0:T(8,128)}, f32[2,256,256]{2,1,0:T(8,128)}) custom-call(s32[1]{0:T(128)} %bitcast.me_ref.refs_0_, bf16[2,32,2048]{2,1,0:T(8,128)(2,1)} %get-tuple-element.60.refs_1_, bf16[2,32,2048]{2,1,0:T(8,128)(2,1)} %copy-done.11, ...), custom_call_target="tpu_custom_call" | custom-call | flops 8192000000 | bytes 5832960 | tf_op jit(solution)/shard_map/long_convolution/pallas_call | solution.py:424
  31.7 7.3 %long_convolution.3 = (f32[64,8192]{1,0:T(8,128)S(1)}, f32[2,256,256]{2,1,0:T(8,128)}, f32[2,256,256]{2,1,0:T(8,128)}, f32[2,256,256]{2,1,0:T(8,128)}, f32[2,256,256]{2,1,0:T(8,128)}) custom-call(s32[1]{0:T(128)} %bitcast.me_ref.refs_0_, bf16[2,32,2048]{2,1,0:T(8,128)(2,1)} %get-tuple-element.73.refs_1_, ...), custom_call_target="tpu_custom_call", output_to_operand_aliasing={{0}: (11, {})} | custom-call | flops 8192000000 | bytes 7930112 | tf_op jit(solution)/shard_map/long_convolution/pallas_call | solution.py:424
  39.0 1.9 %collective-permute-done.5.refs_4_.refs_5_ = bf16[64,2048]{1,0:T(8,128)(2,1)S(1)} collective-permute-done((bf16[64,2048]{1,0:T(8,128)(2,1)S(1)}, bf16[64,2048]{1,0:T(8,128)(2,1)S(1)}, u32[]{:S(2)}, u32[]{:S(2)}) %collective-permute-start.5) | collective-permute-done | bytes 262176 | tf_op jit(solution)/shard_map/ppermute | solution.py:897
  40.9 2.7 %pool_bins.1 = (bf16[64,2048]{1,0:T(8,128)(2,1)}, bf16[64,2048]{1,0:T(8,128)(2,1)}, bf16[64,2048]{1,0:T(8,128)(2,1)}, bf16[64,2048]{1,0:T(8,128)(2,1)}, bf16[8,4,32,128]{3,2,1,0:T(8,128)(2,1)}) custom-call(s32[1]{0:T(128)} %bitcast.me_ref.refs_0_, bf16[64,2048]{1,0:T(8,128)(2,1)} %get-tuple-element.69.refs_1_.refs_2_, ...), custom_call_target="tpu_custom_call" | custom-call | flops 4096000000 | bytes 4521984 | tf_op jit(solution)/shard_map/pool_bins/pallas_call | solution.py:424
  44.3 1.7 %collective-permute-start.9 = (bf16[8,128,512]{2,1,0:T(8,128)(2,1)S(1)}, bf16[8,128,512]{2,1,0:T(8,128)(2,1)S(1)}, u32[]{:S(2)}, u32[]{:S(2)}) collective-permute-start(bf16[8,128,512]{2,1,0:T(8,128)(2,1)S(1)} %all-to-all-done.1.mine_ref.refs_4_), channel_id=1, source_target_pairs={{0,8},{8,0},{16,24},{24,16},{1,9},{9,1},{17,25},{25,17},{2,10},{10... | collective-permute-start | bytes 3145736 | tf_op jit(solution)/shard_map/ppermute | solution.py:897
  46.1 4.9 %all-to-all-start = ((bf16[32,32,128]{2,1,0:T(8,128)(2,1)}), bf16[32,32,128]{2,1,0:T(8,128)(2,1)S(1)}, u32[]{:S(2)}, u32[]{:S(2)}) async-start(bf16[32,32,128]{2,1,0:T(8,128)(2,1)} %bitcast.13), calls=%async_computation | async-start | bytes 524288 | tf_op jit(solution)/shard_map/all_to_all | solution.py:948
  51.3 1.5 %collective-permute-start.11 = (bf16[64,2048]{1,0:T(8,128)(2,1)}, bf16[64,2048]{1,0:T(8,128)(2,1)}, u32[]{:S(2)}, u32[]{:S(2)}) collective-permute-start(bf16[64,2048]{1,0:T(8,128)(2,1)} %get-tuple-element.85), channel_id=1, source_target_pairs={{0,16},{8,24},{16,0},{24,8},{1,17},{9,25},{17,1},{25,9},{2,18},{10... | collective-permute-start | bytes 786440 | tf_op jit(solution)/shard_map/ppermute | solution.py:897
  53.7 7.6 %all-to-all-done = bf16[32,32,128]{2,1,0:T(8,128)(2,1)S(1)} async-done(((bf16[32,32,128]{2,1,0:T(8,128)(2,1)}), bf16[32,32,128]{2,1,0:T(8,128)(2,1)S(1)}, u32[]{:S(2)}, u32[]{:S(2)}) %all-to-all-start) | async-done | bytes 262176 | tf_op jit(solution)/shard_map/all_to_all | solution.py:948
  62.4 1.5 %collective-permute-start.13 = (f32[8,480]{1,0:T(8,128)S(1)}, f32[8,480]{1,0:T(8,128)S(1)}, u32[]{:S(2)}, u32[]{:S(2)}) collective-permute-start(f32[8,480]{1,0:T(8,128)S(1)} %get-tuple-element.90.refs_0_), channel_id=1, source_target_pairs={{0,16},{8,24},{16,0},{24,8},{1,17},{9,25},{17,1},{25,9},{2,18},{10... | collective-permute-start | bytes 46088 | tf_op jit(solution)/shard_map/ppermute | solution.py:897
  64.1 1.3 %collective-permute-done.14.refs_3_ = f32[8,480]{1,0:T(8,128)S(1)} collective-permute-done((f32[8,480]{1,0:T(8,128)S(1)}, f32[8,480]{1,0:T(8,128)S(1)}, u32[]{:S(2)}, u32[]{:S(2)}) %collective-permute-start.14) | collective-permute-done | bytes 15392 | tf_op jit(solution)/shard_map/ppermute | solution.py:897
  65.4 1.5 %head_grads.1 = (bf16[8,4,32,128]{3,2,1,0:T(8,128)(2,1)}, f32[8,128]{1,0:T(8,128)S(1)}) custom-call(s32[1]{0:T(128)} %bitcast.me_ref.refs_0_, f32[64,480]{1,0:T(8,128)S(1)} %get-tuple-element.89.logits_ref, f32[8,480]{1,0:T(8,128)S(1)} %get-tuple-element.90.refs_0_, f32[8,480]{1,0:T(8,128)S(1)} %collective-permute-done.12.refs_1_, ...), custom_call_target="tpu_custom_call" | custom-call | flops 251658240 | bytes 2670592 | tf_op jit(solution)/shard_map/head_grads/pallas_call | solution.py:424
  66.9 3.5 %all-to-all-start.2 = ((bf16[32,32,128]{2,1,0:T(8,128)(2,1)}), bf16[32,32,128]{2,1,0:T(8,128)(2,1)S(1)}, u32[]{:S(2)}, u32[]{:S(2)}) async-start(bf16[32,32,128]{2,1,0:T(8,128)(2,1)} %bitcast.12), calls=%async_computation.2 | async-start | bytes 524288 | tf_op jit(solution)/shard_map/all_to_all | solution.py:948
  70.4 1.7 %collective-permute-start.18 = (bf16[64,2048]{1,0:T(8,128)(2,1)}, bf16[64,2048]{1,0:T(8,128)(2,1)S(1)}, u32[]{:S(2)}, u32[]{:S(2)}) collective-permute-start(bf16[64,2048]{1,0:T(8,128)(2,1)} %get-tuple-element.93), channel_id=1, source_target_pairs={{0,24},{8,16},{16,8},{24,0},{1,25},{9,17},{17,9},{25,1},{2,26},{10... | collective-permute-start | bytes 786440 | tf_op jit(solution)/shard_map/ppermute | solution.py:897
  72.1 1.2 %collective-permute-start.15 = (f32[8,128]{1,0:T(8,128)S(1)}, f32[8,128]{1,0:T(8,128)S(1)}, u32[]{:S(2)}, u32[]{:S(2)}) collective-permute-start(f32[8,128]{1,0:T(8,128)S(1)} %get-tuple-element.92), channel_id=1, source_target_pairs={{0,1},{1,0},{2,3},{3,2},{4,5},{5,4},{6,7},{7,6},{8,9},{9,8},{10,11... | collective-permute-start | bytes 12296 | tf_op jit(solution)/shard_map/ppermute | solution.py:965
  73.3 1.5 %collective-permute-done.15 = f32[8,128]{1,0:T(8,128)S(1)} collective-permute-done((f32[8,128]{1,0:T(8,128)S(1)}, f32[8,128]{1,0:T(8,128)S(1)}, u32[]{:S(2)}, u32[]{:S(2)}) %collective-permute-start.15) | collective-permute-done | bytes 4128 | tf_op jit(solution)/shard_map/ppermute | solution.py:965
  74.9 1.2 %collective-permute-start.16 = (f32[8,128]{1,0:T(8,128)S(1)}, f32[8,128]{1,0:T(8,128)S(1)}, u32[]{:S(2)}, u32[]{:S(2)}) collective-permute-start(f32[8,128]{1,0:T(8,128)S(1)} %add.19), channel_id=1, source_target_pairs={{0,2},{1,3},{2,0},{3,1},{4,6},{5,7},{6,4},{7,5},{8,10},{9,11},{10,... | collective-permute-start | bytes 12296 | tf_op jit(solution)/shard_map/ppermute | solution.py:965
  76.1 1.6 %collective-permute-done.16 = f32[8,128]{1,0:T(8,128)S(1)} collective-permute-done((f32[8,128]{1,0:T(8,128)S(1)}, f32[8,128]{1,0:T(8,128)S(1)}, u32[]{:S(2)}, u32[]{:S(2)}) %collective-permute-start.16) | collective-permute-done | bytes 4128 | tf_op jit(solution)/shard_map/ppermute | solution.py:965
  77.7 2.3 %collective-permute-start.17 = (f32[8,128]{1,0:T(8,128)S(1)}, f32[8,128]{1,0:T(8,128)S(1)}, u32[]{:S(2)}, u32[]{:S(2)}) collective-permute-start(f32[8,128]{1,0:T(8,128)S(1)} %add.20), channel_id=1, source_target_pairs={{0,4},{1,5},{2,6},{3,7},{4,0},{5,1},{6,2},{7,3},{8,12},{9,13},{10,... | collective-permute-start | bytes 12296 | tf_op jit(solution)/shard_map/ppermute | solution.py:965
  81.7 5.5 %long_correlation.2 = (bf16[32,2304]{1,0:T(8,128)(2,1)S(1)}, bf16[32,2304]{1,0:T(8,128)(2,1)S(1)}, bf16[32,2304]{1,0:T(8,128)(2,1)S(1)}, bf16[32,2304]{1,0:T(8,128)(2,1)S(1)}) custom-call(s32[1]{0:T(128)} %bitcast.me_ref.refs_0_, f32[4,32,128]{2,1,0:T(8,128)S(1)} %get-tuple-element.96.refs_1_, bf16[64,2048]{1,0:T(8,128)(2,1)} %get-tuple-element.69.refs_1_.refs_2_, ...), custom_call_target="tpu_custom_call" | custom-call | flops 8192000000 | bytes 4260096 | tf_op jit(solution)/shard_map/long_correlation/pallas_call | solution.py:424
  87.2 2.6 %collective-permute-start.19 = (bf16[32,2304]{1,0:T(8,128)(2,1)S(1)}, bf16[32,2304]{1,0:T(8,128)(2,1)S(1)}, u32[]{:S(2)}, u32[]{:S(2)}) collective-permute-start(bf16[32,2304]{1,0:T(8,128)(2,1)S(1)} %get-tuple-element.103), channel_id=1, source_target_pairs={{0,8},{8,0},{16,24},{24,16},{1,9},{9,1},{17,25},{25,17},{2,10},{10... | collective-permute-start | bytes 442376 | tf_op jit(solution)/shard_map/ppermute | solution.py:897
  89.8 1.7 %collective-permute-start.21 = (bf16[32,2304]{1,0:T(8,128)(2,1)S(1)}, bf16[32,2304]{1,0:T(8,128)(2,1)S(1)}, u32[]{:S(2)}, u32[]{:S(2)}) collective-permute-start(bf16[32,2304]{1,0:T(8,128)(2,1)S(1)} %get-tuple-element.105), channel_id=1, source_target_pairs={{0,24},{8,16},{16,8},{24,0},{1,25},{9,17},{17,9},{25,1},{2,26},{10... | collective-permute-start | bytes 442376 | tf_op jit(solution)/shard_map/ppermute | solution.py:897
  91.5 5.6 %long_correlation.3 = (bf16[32,2048]{1,0:T(8,128)(2,1)S(1)}, bf16[32,2048]{1,0:T(8,128)(2,1)S(1)}, bf16[32,2048]{1,0:T(8,128)(2,1)S(1)}, bf16[32,2048]{1,0:T(8,128)(2,1)S(1)}) custom-call(s32[1]{0:T(128)} %bitcast.me_ref.refs_0_, bf16[64,2048]{1,0:T(8,128)(2,1)} %get-tuple-element.69.refs_1_.refs_2_, bf16[64,2048]{1,0:T(8,128)(2,1)} %copy-done.2, ...), custom_call_target="tpu_custom_call" | custom-call | flops 8192000000 | bytes 4129024 | tf_op jit(solution)/shard_map/long_correlation/pallas_call | solution.py:424
  97.4 1.9 %collective-permute-start.24 = (bf16[32,2048]{1,0:T(8,128)(2,1)S(1)}, bf16[32,2048]{1,0:T(8,128)(2,1)S(1)}, u32[]{:S(2)}, u32[]{:S(2)}) collective-permute-start(bf16[32,2048]{1,0:T(8,128)(2,1)S(1)} %get-tuple-element.116), channel_id=1, source_target_pairs={{0,24},{8,16},{16,8},{24,0},{1,25},{9,17},{17,9},{25,1},{2,26},{10... | collective-permute-start | bytes 393224 | tf_op jit(solution)/shard_map/ppermute | solution.py:897
  99.3 4.2 %finish.2 = (f32[3,256,2048]{2,1,0:T(8,128)}, f32[1,1]{1,0:T(1,128)}) custom-call(s32[1]{0:T(128)} %bitcast.me_ref.refs_0_, bf16[256,128]{1,0:T(8,128)(2,1)S(1)} %copy-done.1, bf16[3,256,2048]{2,1,0:T(8,128)(2,1)} %proj_ref.7, bf16[64,2048]{1,0:T(8,128)(2,1)S(1)} %copy-done.5, bf16[64,2048]{1,0:T(8,128)(2,1)} %collective-permute-done.10.refs_1_, ...), custom_call_target="tpu_custom_call" | custom-call | flops 3840000000 | bytes 11145220 | tf_op jit(solution)/shard_map/finish/pallas_call | solution.py:424
  103.5 1.8 %collective-permute-done.24.refs_3_ = bf16[32,2048]{1,0:T(8,128)(2,1)S(1)} collective-permute-done((bf16[32,2048]{1,0:T(8,128)(2,1)S(1)}, bf16[32,2048]{1,0:T(8,128)(2,1)S(1)}, u32[]{:S(2)}, u32[]{:S(2)}) %collective-permute-start.24) | collective-permute-done | bytes 131104 | tf_op jit(solution)/shard_map/ppermute | solution.py:897
  105.4 2.7 %finish.3 = f32[3,256,2048]{2,1,0:T(8,128)} custom-call(s32[1]{0:T(128)} %bitcast.me_ref.refs_0_, bf16[256,128]{1,0:T(8,128)(2,1)S(1)} %copy-done.1, bf16[3,256,2048]{2,1,0:T(8,128)(2,1)} %proj_ref.7, bf16[32,2048]{1,0:T(8,128)(2,1)S(1)} %get-tuple-element.113.refs_0_, ...), custom_call_target="tpu_custom_call", output_to_operand_aliasing={{}: (7, {})} | custom-call | flops 3840000000 | bytes 16318464 | tf_op jit(solution)/shard_map/finish/pallas_call | solution.py:424
  (73 shorter events, 10.8 us)
Async XLA Ops:
  0.6 52.9 %copy-start = (s32[64,3840]{1,0:T(8,128)S(1)}, s32[64,3840]{1,0:T(8,128)}, u32[]{:S(2)}) copy-start(s32[64,3840]{1,0:T(8,128)} %param.20) | copy-start | bytes 2949124
  3.2 16.4 %collective-permute-start = (bf16[2,32,2048]{2,1,0:T(8,128)(2,1)}, bf16[2,32,2048]{2,1,0:T(8,128)(2,1)S(1)}, u32[]{:S(2)}, u32[]{:S(2)}) collective-permute-start(bf16[2,32,2048]{2,1,0:T(8,128)(2,1)} %get-tuple-element.61), channel_id=1, source_target_pairs={{0,8},{8,0},{16,24},{24,16},{1,9},{9,1},{17,25},{25,17},{2,10},{10... | collective-permute-start | bytes 786440 | tf_op jit(solution)/shard_map/ppermute | solution.py:897
  3.3 17.4 %collective-permute-start.1 = (bf16[2,32,2048]{2,1,0:T(8,128)(2,1)}, bf16[2,32,2048]{2,1,0:T(8,128)(2,1)S(1)}, u32[]{:S(2)}, u32[]{:S(2)}) collective-permute-start(bf16[2,32,2048]{2,1,0:T(8,128)(2,1)} %get-tuple-element.62), channel_id=1, source_target_pairs={{0,16},{8,24},{16,0},{24,8},{1,17},{9,25},{17,1},{25,9},{2,18},{10... | collective-permute-start | bytes 786440 | tf_op jit(solution)/shard_map/ppermute | solution.py:897
  6.0 14.7 %collective-permute-start.2 = (bf16[2,32,2048]{2,1,0:T(8,128)(2,1)}, bf16[2,32,2048]{2,1,0:T(8,128)(2,1)}, u32[]{:S(2)}, u32[]{:S(2)}) collective-permute-start(bf16[2,32,2048]{2,1,0:T(8,128)(2,1)} %get-tuple-element.63), channel_id=1, source_target_pairs={{0,24},{8,16},{16,8},{24,0},{1,25},{9,17},{17,9},{25,1},{2,26},{10... | collective-permute-start | bytes 786440 | tf_op jit(solution)/shard_map/ppermute | solution.py:897
  9.1 20.9 %collective-permute-start.6 = (bf16[2,32,2048]{2,1,0:T(8,128)(2,1)}, bf16[2,32,2048]{2,1,0:T(8,128)(2,1)S(1)}, u32[]{:S(2)}, u32[]{:S(2)}) collective-permute-start(bf16[2,32,2048]{2,1,0:T(8,128)(2,1)} %get-tuple-element.74), channel_id=1, source_target_pairs={{0,8},{8,0},{16,24},{24,16},{1,9},{9,1},{17,25},{25,17},{2,10},{10... | collective-permute-start | bytes 786440 | tf_op jit(solution)/shard_map/ppermute | solution.py:897
  9.5 21.4 %collective-permute-start.7 = (bf16[2,32,2048]{2,1,0:T(8,128)(2,1)}, bf16[2,32,2048]{2,1,0:T(8,128)(2,1)}, u32[]{:S(2)}, u32[]{:S(2)}) collective-permute-start(bf16[2,32,2048]{2,1,0:T(8,128)(2,1)} %get-tuple-element.75), channel_id=1, source_target_pairs={{0,16},{8,24},{16,0},{24,8},{1,17},{9,25},{17,1},{25,9},{2,18},{10... | collective-permute-start | bytes 786440 | tf_op jit(solution)/shard_map/ppermute | solution.py:897
  13.7 8.2 %copy-start.8 = (bf16[64,2048]{1,0:T(8,128)(2,1)S(1)}, bf16[64,2048]{1,0:T(8,128)(2,1)}, u32[]{:S(2)}) copy-start(bf16[64,2048]{1,0:T(8,128)(2,1)} %get-tuple-element.71) | copy-start | bytes 786436
  13.7 30.7 %all-to-all-start.1 = ((bf16[8,128,512]{2,1,0:T(8,128)(2,1)}), bf16[8,128,512]{2,1,0:T(8,128)(2,1)S(1)}, u32[]{:S(2)}, u32[]{:S(2)}) async-start(bf16[8,128,512]{2,1,0:T(8,128)(2,1)} %by_track.1), calls=%async_computation.1 | async-start | bytes 2097152 | tf_op jit(solution)/shard_map/all_to_all | solution.py:937
  19.6 10.4 %copy-start.7 = (bf16[64,2048]{1,0:T(8,128)(2,1)S(1)}, bf16[64,2048]{1,0:T(8,128)(2,1)}, u32[]{:S(2)}) copy-start(bf16[64,2048]{1,0:T(8,128)(2,1)} %get-tuple-element.72) | copy-start | bytes 786436
  19.6 11.4 %collective-permute-start.8 = (bf16[2,32,2048]{2,1,0:T(8,128)(2,1)}, bf16[2,32,2048]{2,1,0:T(8,128)(2,1)S(1)}, u32[]{:S(2)}, u32[]{:S(2)}) collective-permute-start(bf16[2,32,2048]{2,1,0:T(8,128)(2,1)} %get-tuple-element.76), channel_id=1, source_target_pairs={{0,24},{8,16},{16,8},{24,0},{1,25},{9,17},{17,9},{25,1},{2,26},{10... | collective-permute-start | bytes 786440 | tf_op jit(solution)/shard_map/ppermute | solution.py:897
  21.4 17.6 %collective-permute-start.3 = (bf16[64,2048]{1,0:T(8,128)(2,1)S(1)}, bf16[64,2048]{1,0:T(8,128)(2,1)S(1)}, u32[]{:S(2)}, u32[]{:S(2)}) collective-permute-start(bf16[64,2048]{1,0:T(8,128)(2,1)S(1)} %copy-done.9), channel_id=1, source_target_pairs={{0,8},{8,0},{16,24},{24,16},{1,9},{9,1},{17,25},{25,17},{2,10},{10... | collective-permute-start | bytes 786440 | tf_op jit(solution)/shard_map/ppermute | solution.py:897
  21.9 17.1 %collective-permute-start.4 = (bf16[64,2048]{1,0:T(8,128)(2,1)S(1)}, bf16[64,2048]{1,0:T(8,128)(2,1)S(1)}, u32[]{:S(2)}, u32[]{:S(2)}) collective-permute-start(bf16[64,2048]{1,0:T(8,128)(2,1)S(1)} %copy-done.8), channel_id=1, source_target_pairs={{0,16},{8,24},{16,0},{24,8},{1,17},{9,25},{17,1},{25,9},{2,18},{10... | collective-permute-start | bytes 786440 | tf_op jit(solution)/shard_map/ppermute | solution.py:897
  30.0 10.9 %collective-permute-start.5 = (bf16[64,2048]{1,0:T(8,128)(2,1)S(1)}, bf16[64,2048]{1,0:T(8,128)(2,1)S(1)}, u32[]{:S(2)}, u32[]{:S(2)}) collective-permute-start(bf16[64,2048]{1,0:T(8,128)(2,1)S(1)} %copy-done.7), channel_id=1, source_target_pairs={{0,24},{8,16},{16,8},{24,0},{1,25},{9,17},{17,9},{25,1},{2,26},{10... | collective-permute-start | bytes 786440 | tf_op jit(solution)/shard_map/ppermute | solution.py:897
  44.3 16.9 %collective-permute-start.9 = (bf16[8,128,512]{2,1,0:T(8,128)(2,1)S(1)}, bf16[8,128,512]{2,1,0:T(8,128)(2,1)S(1)}, u32[]{:S(2)}, u32[]{:S(2)}) collective-permute-start(bf16[8,128,512]{2,1,0:T(8,128)(2,1)S(1)} %all-to-all-done.1.mine_ref.refs_4_), channel_id=1, source_target_pairs={{0,8},{8,0},{16,24},{24,16},{1,9},{9,1},{17,25},{25,17},{2,10},{10... | collective-permute-start | bytes 3145736 | tf_op jit(solution)/shard_map/ppermute | solution.py:897
  46.1 15.2 %all-to-all-start = ((bf16[32,32,128]{2,1,0:T(8,128)(2,1)}), bf16[32,32,128]{2,1,0:T(8,128)(2,1)S(1)}, u32[]{:S(2)}, u32[]{:S(2)}) async-start(bf16[32,32,128]{2,1,0:T(8,128)(2,1)} %bitcast.13), calls=%async_computation | async-start | bytes 524288 | tf_op jit(solution)/shard_map/all_to_all | solution.py:948
  51.0 13.1 %collective-permute-start.10 = (bf16[64,2048]{1,0:T(8,128)(2,1)}, bf16[64,2048]{1,0:T(8,128)(2,1)}, u32[]{:S(2)}, u32[]{:S(2)}) collective-permute-start(bf16[64,2048]{1,0:T(8,128)(2,1)} %get-tuple-element.84), channel_id=1, source_target_pairs={{0,8},{8,0},{16,24},{24,16},{1,9},{9,1},{17,25},{25,17},{2,10},{10... | collective-permute-start | bytes 786440 | tf_op jit(solution)/shard_map/ppermute | solution.py:897
  51.3 12.8 %collective-permute-start.11 = (bf16[64,2048]{1,0:T(8,128)(2,1)}, bf16[64,2048]{1,0:T(8,128)(2,1)}, u32[]{:S(2)}, u32[]{:S(2)}) collective-permute-start(bf16[64,2048]{1,0:T(8,128)(2,1)} %get-tuple-element.85), channel_id=1, source_target_pairs={{0,16},{8,24},{16,0},{24,8},{1,17},{9,25},{17,1},{25,9},{2,18},{10... | collective-permute-start | bytes 786440 | tf_op jit(solution)/shard_map/ppermute | solution.py:897
  61.9 3.5 %collective-permute-start.14 = (f32[8,480]{1,0:T(8,128)S(1)}, f32[8,480]{1,0:T(8,128)S(1)}, u32[]{:S(2)}, u32[]{:S(2)}) collective-permute-start(f32[8,480]{1,0:T(8,128)S(1)} %get-tuple-element.90.refs_0_), channel_id=1, source_target_pairs={{0,24},{8,16},{16,8},{24,0},{1,25},{9,17},{17,9},{25,1},{2,26},{10... | collective-permute-start | bytes 46088 | tf_op jit(solution)/shard_map/ppermute | solution.py:897
  62.4 3.0 %collective-permute-start.13 = (f32[8,480]{1,0:T(8,128)S(1)}, f32[8,480]{1,0:T(8,128)S(1)}, u32[]{:S(2)}, u32[]{:S(2)}) collective-permute-start(f32[8,480]{1,0:T(8,128)S(1)} %get-tuple-element.90.refs_0_), channel_id=1, source_target_pairs={{0,16},{8,24},{16,0},{24,8},{1,17},{9,25},{17,1},{25,9},{2,18},{10... | collective-permute-start | bytes 46088 | tf_op jit(solution)/shard_map/ppermute | solution.py:897
  63.9 1.5 %collective-permute-start.12 = (f32[8,480]{1,0:T(8,128)S(1)}, f32[8,480]{1,0:T(8,128)S(1)}, u32[]{:S(2)}, u32[]{:S(2)}) collective-permute-start(f32[8,480]{1,0:T(8,128)S(1)} %get-tuple-element.90.refs_0_), channel_id=1, source_target_pairs={{0,8},{8,0},{16,24},{24,16},{1,9},{9,1},{17,25},{25,17},{2,10},{10... | collective-permute-start | bytes 46088 | tf_op jit(solution)/shard_map/ppermute | solution.py:897
  66.9 14.7 %all-to-all-start.2 = ((bf16[32,32,128]{2,1,0:T(8,128)(2,1)}), bf16[32,32,128]{2,1,0:T(8,128)(2,1)S(1)}, u32[]{:S(2)}, u32[]{:S(2)}) async-start(bf16[32,32,128]{2,1,0:T(8,128)(2,1)} %bitcast.12), calls=%async_computation.2 | async-start | bytes 524288 | tf_op jit(solution)/shard_map/all_to_all | solution.py:948
  70.4 11.2 %collective-permute-start.18 = (bf16[64,2048]{1,0:T(8,128)(2,1)}, bf16[64,2048]{1,0:T(8,128)(2,1)S(1)}, u32[]{:S(2)}, u32[]{:S(2)}) collective-permute-start(bf16[64,2048]{1,0:T(8,128)(2,1)} %get-tuple-element.93), channel_id=1, source_target_pairs={{0,24},{8,16},{16,8},{24,0},{1,25},{9,17},{17,9},{25,1},{2,26},{10... | collective-permute-start | bytes 786440 | tf_op jit(solution)/shard_map/ppermute | solution.py:897
  72.1 2.8 %collective-permute-start.15 = (f32[8,128]{1,0:T(8,128)S(1)}, f32[8,128]{1,0:T(8,128)S(1)}, u32[]{:S(2)}, u32[]{:S(2)}) collective-permute-start(f32[8,128]{1,0:T(8,128)S(1)} %get-tuple-element.92), channel_id=1, source_target_pairs={{0,1},{1,0},{2,3},{3,2},{4,5},{5,4},{6,7},{7,6},{8,9},{9,8},{10,11... | collective-permute-start | bytes 12296 | tf_op jit(solution)/shard_map/ppermute | solution.py:965
  74.9 2.8 %collective-permute-start.16 = (f32[8,128]{1,0:T(8,128)S(1)}, f32[8,128]{1,0:T(8,128)S(1)}, u32[]{:S(2)}, u32[]{:S(2)}) collective-permute-start(f32[8,128]{1,0:T(8,128)S(1)} %add.19), channel_id=1, source_target_pairs={{0,2},{1,3},{2,0},{3,1},{4,6},{5,7},{6,4},{7,5},{8,10},{9,11},{10,... | collective-permute-start | bytes 12296 | tf_op jit(solution)/shard_map/ppermute | solution.py:965
  77.7 3.4 %collective-permute-start.17 = (f32[8,128]{1,0:T(8,128)S(1)}, f32[8,128]{1,0:T(8,128)S(1)}, u32[]{:S(2)}, u32[]{:S(2)}) collective-permute-start(f32[8,128]{1,0:T(8,128)S(1)} %add.20), channel_id=1, source_target_pairs={{0,4},{1,5},{2,6},{3,7},{4,0},{5,1},{6,2},{7,3},{8,12},{9,13},{10,... | collective-permute-start | bytes 12296 | tf_op jit(solution)/shard_map/ppermute | solution.py:965
  87.2 10.2 %collective-permute-start.19 = (bf16[32,2304]{1,0:T(8,128)(2,1)S(1)}, bf16[32,2304]{1,0:T(8,128)(2,1)S(1)}, u32[]{:S(2)}, u32[]{:S(2)}) collective-permute-start(bf16[32,2304]{1,0:T(8,128)(2,1)S(1)} %get-tuple-element.103), channel_id=1, source_target_pairs={{0,8},{8,0},{16,24},{24,16},{1,9},{9,1},{17,25},{25,17},{2,10},{10... | collective-permute-start | bytes 442376 | tf_op jit(solution)/shard_map/ppermute | solution.py:897
  89.8 9.5 %collective-permute-start.20 = (bf16[32,2304]{1,0:T(8,128)(2,1)S(1)}, bf16[32,2304]{1,0:T(8,128)(2,1)S(1)}, u32[]{:S(2)}, u32[]{:S(2)}) collective-permute-start(bf16[32,2304]{1,0:T(8,128)(2,1)S(1)} %get-tuple-element.104), channel_id=1, source_target_pairs={{0,16},{8,24},{16,0},{24,8},{1,17},{9,25},{17,1},{25,9},{2,18},{10... | collective-permute-start | bytes 442376 | tf_op jit(solution)/shard_map/ppermute | solution.py:897
  89.8 9.5 %collective-permute-start.21 = (bf16[32,2304]{1,0:T(8,128)(2,1)S(1)}, bf16[32,2304]{1,0:T(8,128)(2,1)S(1)}, u32[]{:S(2)}, u32[]{:S(2)}) collective-permute-start(bf16[32,2304]{1,0:T(8,128)(2,1)S(1)} %get-tuple-element.105), channel_id=1, source_target_pairs={{0,24},{8,16},{16,8},{24,0},{1,25},{9,17},{17,9},{25,1},{2,26},{10... | collective-permute-start | bytes 442376 | tf_op jit(solution)/shard_map/ppermute | solution.py:897
  91.5 7.8 %copy-start.5 = (bf16[64,2048]{1,0:T(8,128)(2,1)S(1)}, bf16[64,2048]{1,0:T(8,128)(2,1)}, u32[]{:S(2)}) copy-start(bf16[64,2048]{1,0:T(8,128)(2,1)} %get-tuple-element.86.refs_0_) | copy-start | bytes 786436
  97.1 6.4 %collective-permute-start.22 = (bf16[32,2048]{1,0:T(8,128)(2,1)S(1)}, bf16[32,2048]{1,0:T(8,128)(2,1)S(1)}, u32[]{:S(2)}, u32[]{:S(2)}) collective-permute-start(bf16[32,2048]{1,0:T(8,128)(2,1)S(1)} %get-tuple-element.114), channel_id=1, source_target_pairs={{0,8},{8,0},{16,24},{24,16},{1,9},{9,1},{17,25},{25,17},{2,10},{10... | collective-permute-start | bytes 393224 | tf_op jit(solution)/shard_map/ppermute | solution.py:897
  97.3 6.2 %collective-permute-start.23 = (bf16[32,2048]{1,0:T(8,128)(2,1)S(1)}, bf16[32,2048]{1,0:T(8,128)(2,1)S(1)}, u32[]{:S(2)}, u32[]{:S(2)}) collective-permute-start(bf16[32,2048]{1,0:T(8,128)(2,1)S(1)} %get-tuple-element.115), channel_id=1, source_target_pairs={{0,16},{8,24},{16,0},{24,8},{1,17},{9,25},{17,1},{25,9},{2,18},{10... | collective-permute-start | bytes 393224 | tf_op jit(solution)/shard_map/ppermute | solution.py:897
  97.4 8.0 %collective-permute-start.24 = (bf16[32,2048]{1,0:T(8,128)(2,1)S(1)}, bf16[32,2048]{1,0:T(8,128)(2,1)S(1)}, u32[]{:S(2)}, u32[]{:S(2)}) collective-permute-start(bf16[32,2048]{1,0:T(8,128)(2,1)S(1)} %get-tuple-element.116), channel_id=1, source_target_pairs={{0,24},{8,16},{16,8},{24,0},{1,25},{9,17},{17,9},{25,1},{2,26},{10... | collective-permute-start | bytes 393224 | tf_op jit(solution)/shard_map/ppermute | solution.py:897
  (10 other events, 34.8 us)

commit v7 on v6

--- a/solution.py
+++ b/solution.py
@@ -567,18 +567,29 @@
     )
 
 
-def lay_out(me, projections, filter_taps, peers, chunk, chunks):
-    last = chunk == chunks - 1
+def lay_out(me, projections, filter_taps, peers, chunks, jobs, with_query):
     _, channels, width = projections.shape
     pencil = channels // peers
     rows = pencil // chunks
     f32, bf16 = jnp.float32, jnp.bfloat16
-    order = list(range(peers))[::-1]
+    count = len(jobs)
+    query_count = peers if with_query else 0
 
     def kernel(me_ref, proj_ref, taps_ref, *refs):
-        outs = refs[:peers]
-        queries = refs[peers:-7]
+        outs, queries = refs[:count], refs[count:-7]
         pair, taps, laid, passing, sems, out_sems, query_sems = refs[-7:]
+
+        def fetch(i):
+            chunk, k = jobs[i]
+            here = pl.ds(pl.multiple_of((me_ref[0] ^ k) * pencil + chunk * rows, rows), rows)
+            return (
+                pltpu.make_async_copy(proj_ref.at[1, here], pair.at[i, 0], sems.at[i, 0]),
+                pltpu.make_async_copy(proj_ref.at[2, here], pair.at[i, 1], sems.at[i, 1]),
+                pltpu.make_async_copy(taps_ref.at[here], taps.at[i], sems.at[i, 2]),
+            )
+
+        def leave(i):
+            return pltpu.make_async_copy(laid.at[i], outs[i], out_sems.at[i])
 
         def take(k):
             block = pl.ds(pl.multiple_of((me_ref[0] ^ k) * pencil, pencil), pencil)
@@ -587,57 +598,43 @@
         def hand_on(k):
             return pltpu.make_async_copy(passing.at[k], queries[k], query_sems.at[k, 1])
 
-
-        def fetch(k):
-            here = pl.ds(pl.multiple_of((me_ref[0] ^ k) * pencil + chunk * rows, rows), rows)
-            return (
-                pltpu.make_async_copy(proj_ref.at[1, here], pair.at[k, 0], sems.at[k, 0]),
-                pltpu.make_async_copy(proj_ref.at[2, here], pair.at[k, 1], sems.at[k, 1]),
-                pltpu.make_async_copy(taps_ref.at[here], taps.at[k], sems.at[k, 2]),
-            )
-
-        def leave(k):
-            return pltpu.make_async_copy(laid.at[k], outs[k], out_sems.at[k])
-
-        for k in order:
-            for copy in fetch(k):
+        for i in range(count):
+            for copy in fetch(i):
                 copy.start()
-        for k in range(len(queries)):
+        for k in range(query_count):
             take(k).start()
-        for k in order:
-            keyed, valued, lags = fetch(k)
+        for i in range(count):
+            keyed, valued, lags = fetch(i)
             keyed.wait()
             valued.wait()
-            laid[k, 0] = (pair[k, 0].astype(f32) * pair[k, 1].astype(f32)).astype(bf16)
+            laid[i, 0] = (pair[i, 0].astype(f32) * pair[i, 1].astype(f32)).astype(bf16)
             lags.wait()
-            laid[k, 1] = taps[k].astype(bf16)
-            leave(k).start()
-        for k in range(len(queries)):
+            laid[i, 1] = taps[i].astype(bf16)
+            leave(i).start()
+        for k in range(query_count):
             take(k).wait()
             hand_on(k).start()
-        for k in order:
-            leave(k).wait()
-        for k in range(len(queries)):
+        for i in range(count):
+            leave(i).wait()
+        for k in range(query_count):
             hand_on(k).wait()
 
-    out_shapes = [shape((2, rows, width), bf16)] * peers
-    if last:
-        out_shapes += [shape((pencil, width), bf16)] * peers
+    out_shapes = [shape((2, rows, width), bf16)] * count + [shape((pencil, width), bf16)] * query_count
     return call(
         kernel, "lay_out", me, 1, [projections, filter_taps],
         [pl.BlockSpec(memory_space=pltpu.HBM)] * 2,
         out_shapes,
         [pl.BlockSpec(memory_space=pltpu.HBM)] * len(out_shapes),
         [
-            pltpu.VMEM((peers, 2, rows, width), bf16),
-            pltpu.VMEM((peers, rows, width), f32),
-            pltpu.VMEM((peers, 2, rows, width), bf16),
-            pltpu.VMEM((peers, pencil, width), bf16),
-            pltpu.SemaphoreType.DMA((peers, 3)),
-            pltpu.SemaphoreType.DMA((peers,)),
-            pltpu.SemaphoreType.DMA((peers, 2)),
+            pltpu.VMEM((count, 2, rows, width), bf16),
+            pltpu.VMEM((count, rows, width), f32),
+            pltpu.VMEM((count, 2, rows, width), bf16),
+            pltpu.VMEM((max(query_count, 1), pencil, width), bf16),
+            pltpu.SemaphoreType.DMA((count, 3)),
+            pltpu.SemaphoreType.DMA((count,)),
+            pltpu.SemaphoreType.DMA((max(query_count, 1), 2)),
         ],
-        rows * peers * 0.015 * MICROSECOND,
+        rows * count * 0.015 * MICROSECOND,
     )
 
 
@@ -924,12 +921,15 @@
     tables = transform_tables(length)
     gather, spread = pool_tables()
 
-    laid, me_next = [], me
-    for j in range(chunks):
-        laid.append(lay_out(me_next, projections, filter_taps, peers, j, chunks))
-        me_next, _ = lax.optimization_barrier((me, laid[j]))
-    pieces = [[swap(laid[j][k], k, peers) for k in range(peers)] for j in range(chunks)]
-    held_back, _ = lax.optimization_barrier((laid[-1][peers:], pieces[0]))
+    first = [(0, k) for k in range(peers // 2, peers)]
+    others = [(0, k) for k in range(peers // 2)] + [(j, k) for j in range(1, chunks) for k in range(peers)]
+    far = lay_out(me, projections, filter_taps, peers, chunks, first, False)
+    me_next, _ = lax.optimization_barrier((me, far))
+    rest = lay_out(me_next, projections, filter_taps, peers, chunks, others, True)
+    me_next, _ = lax.optimization_barrier((me, rest))
+    laid = dict(zip(first + others, [*far, *rest]))
+    pieces = [[swap(laid[j, k], k, peers) for k in range(peers)] for j in range(chunks)]
+    held_back, _ = lax.optimization_barrier((rest[len(others) :], pieces[0]))
     queries = [swap(held_back[k], k, peers) for k in range(peers)]
     skip = lax.dynamic_index_in_dim(skip_gain.reshape(peers, pencil, 1), seat, axis=0, keepdims=False)
 

time: 109 us -> 108 us (level)
  starting transfers between devices: 40.9 us -> 39.1 us
    all_to_all x2, starting transfers between devices: 8.38 us -> 6.79 us  [exchange(): lax.all_to_all(flat, ('chan', 'seq'), split_axis=0, concat_axis=0, tiled=...]
    all_to_all x1, waiting for transfers between devices: 0.01 us -> 1.25 us  [aligned(): mine = lax.all_to_all(mine, 'chan', split_axis=0, concat_axis=0, tiled=True)]
  transfers between devices with their start and end apart: 28 -> 28, of which waited for: 8 -> 9; matrix products, arithmetic and copies ran while one was open for 1% -> 1% of each run, Pallas kernels for 31% -> 32%
where the time goes in v7:
time: 108 us; the launch traced here: 107 us
  Pallas kernels  46 us (43%)
  starting transfers between devices  39.1 us (36%)
  waiting for transfers between devices  17.9 us (17%)
  local copies, waits for them, and re-layouts  3.17 us (3%)
    pallas_call x13, Pallas kernels, call(): pl.pallas_call(kernel, name=name, grid_spec=pltpu.PrefetchScalarGridSpec(...  46 us
    ppermute x22, starting transfers between devices, swap(): return lax.ppermute(value, 'seq', [(i, i ^ k) for i in range(count)])  21.8 us
    all_to_all x2, waiting for transfers between devices, exchange(): lax.all_to_all(flat, ('chan', 'seq'), split_axis=0, concat_axis=0, tiled=...  7.58 us
    all_to_all x2, starting transfers between devices, exchange(): lax.all_to_all(flat, ('chan', 'seq'), split_axis=0, concat_axis=0, tiled=...  6.79 us
    all_to_all x1, starting transfers between devices, aligned(): mine = lax.all_to_all(mine, 'chan', split_axis=0, concat_axis=0, tiled=True)  5.7 us
    ppermute x22, waiting for transfers between devices, swap(): return lax.ppermute(value, 'seq', [(i, i ^ k) for i in range(count)])  4.94 us
    ppermute x3, starting transfers between devices, aligned(): lax.ppermute(loss, 'chan', [(i, i ^ step) for i in range(groups)])  4.81 us
    ppermute x3, waiting for transfers between devices, aligned(): lax.ppermute(loss, 'chan', [(i, i ^ step) for i in range(groups)])  4.11 us
  transfers between devices with their start and end apart: 28, of which 9 were waited for; matrix products, arithmetic and copies ran while one was open for 1% of the time, Pallas kernels for 32%

profile of v7, /device:TPU:1, one launch (start us, length us, event | category | flops | bytes accessed | tf_op | source)
XLA Modules:
  0.0 107.2 jit_solution(16568716842605103270)
XLA Ops:
  0.7 2.1 %lay_out.2 = (bf16[2,32,2048]{2,1,0:T(8,128)(2,1)}, bf16[2,32,2048]{2,1,0:T(8,128)(2,1)}) custom-call(s32[1]{0:T(128)} %bitcast.me_ref.refs_0_, bf16[3,256,2048]{2,1,0:T(8,128)(2,1)} %proj_ref.7, f32[256,2048]{1,0:T(8,128)} %taps_ref.3), custom_call_target="tpu_custom_call" | custom-call | flops 960000000 | bytes 5767168 | tf_op jit(solution)/shard_map/lay_out/pallas_call | solution.py:424
  2.8 2.1 %collective-permute-start.1 = (bf16[2,32,2048]{2,1,0:T(8,128)(2,1)}, bf16[2,32,2048]{2,1,0:T(8,128)(2,1)S(1)}, u32[]{:S(2)}, u32[]{:S(2)}) collective-permute-start(bf16[2,32,2048]{2,1,0:T(8,128)(2,1)} %get-tuple-element.60), channel_id=1, source_target_pairs={{0,16},{8,24},{16,0},{24,8},{1,17},{9,25},{17,1},{25,9},{2,18},{10... | collective-permute-start | bytes 786440 | tf_op jit(solution)/shard_map/ppermute | solution.py:894
  5.5 3.7 %lay_out.3 = (bf16[2,32,2048]{2,1,0:T(8,128)(2,1)}, bf16[2,32,2048]{2,1,0:T(8,128)(2,1)}, bf16[2,32,2048]{2,1,0:T(8,128)(2,1)}, bf16[2,32,2048]{2,1,0:T(8,128)(2...) custom-call(s32[1]{0:T(128)} %bitcast.me_ref.refs_0_, ...), custom_call_target="tpu_custom_call" | custom-call | flops 2880000000 | bytes 7864320 | tf_op jit(solution)/shard_map/lay_out/pallas_call | solution.py:424
  9.8 1.7 %collective-permute-start.7 = (bf16[2,32,2048]{2,1,0:T(8,128)(2,1)}, bf16[2,32,2048]{2,1,0:T(8,128)(2,1)}, u32[]{:S(2)}, u32[]{:S(2)}) collective-permute-start(bf16[2,32,2048]{2,1,0:T(8,128)(2,1)} %get-tuple-element.75), channel_id=1, source_target_pairs={{0,16},{8,24},{16,0},{24,8},{1,17},{9,25},{17,1},{25,9},{2,18},{10... | collective-permute-start | bytes 786440 | tf_op jit(solution)/shard_map/ppermute | solution.py:894
  11.4 2.7 %by_track.1 = bf16[8,128,512]{2,1,0:T(8,128)(2,1)} custom-call(s32[1]{0:T(128)} %bitcast.me_ref.refs_0_, bf16[256,3840]{1,0:T(8,128)(2,1)} %weight_ref.1), custom_call_target="tpu_custom_call" | custom-call | flops 2000000000 | bytes 3014656 | tf_op jit(solution)/shard_map/by_track/pallas_call | solution.py:424
  14.1 5.7 %all-to-all-start.1 = ((bf16[8,128,512]{2,1,0:T(8,128)(2,1)}), bf16[8,128,512]{2,1,0:T(8,128)(2,1)S(1)}, u32[]{:S(2)}, u32[]{:S(2)}) async-start(bf16[8,128,512]{2,1,0:T(8,128)(2,1)} %by_track.1), calls=%async_computation.1 | async-start | bytes 2097152 | tf_op jit(solution)/shard_map/all_to_all | solution.py:937
  22.8 7.3 %long_convolution.2 = (f32[64,8192]{1,0:T(8,128)S(1)}, f32[2,256,256]{2,1,0:T(8,128)}, f32[2,256,256]{2,1,0:T(8,128)}, f32[2,256,256]{2,1,0:T(8,128)}, f32[2,256,256]{2,1,0:T(8,128)}) custom-call(s32[1]{0:T(128)} %bitcast.me_ref.refs_0_, bf16[2,32,2048]{2,1,0:T(8,128)(2,1)} %get-tuple-element.67.refs_1_, bf16[2,32,2048]{2,1,0:T(8,128)(2,1)} %collective-permute-done.refs_2_, ...), custom_call_target="tpu_custom_call" | custom-call | flops 8192000000 | bytes 5832960 | tf_op jit(solution)/shard_map/long_convolution/pallas_call | solution.py:424
  31.8 7.3 %long_convolution.3 = (f32[64,8192]{1,0:T(8,128)S(1)}, f32[2,256,256]{2,1,0:T(8,128)}, f32[2,256,256]{2,1,0:T(8,128)}, f32[2,256,256]{2,1,0:T(8,128)}, f32[2,256,256]{2,1,0:T(8,128)}) custom-call(s32[1]{0:T(128)} %bitcast.me_ref.refs_0_, bf16[2,32,2048]{2,1,0:T(8,128)(2,1)} %get-tuple-element.73.refs_1_, ...), custom_call_target="tpu_custom_call", output_to_operand_aliasing={{0}: (11, {})} | custom-call | flops 8192000000 | bytes 7930112 | tf_op jit(solution)/shard_map/long_convolution/pallas_call | solution.py:424
  39.2 1.2 %collective-permute-done.5.refs_4_.refs_5_ = bf16[64,2048]{1,0:T(8,128)(2,1)S(1)} collective-permute-done((bf16[64,2048]{1,0:T(8,128)(2,1)S(1)}, bf16[64,2048]{1,0:T(8,128)(2,1)S(1)}, u32[]{:S(2)}, u32[]{:S(2)}) %collective-permute-start.5) | collective-permute-done | bytes 262176 | tf_op jit(solution)/shard_map/ppermute | solution.py:894
  40.4 2.8 %pool_bins.1 = (bf16[64,2048]{1,0:T(8,128)(2,1)}, bf16[64,2048]{1,0:T(8,128)(2,1)}, bf16[64,2048]{1,0:T(8,128)(2,1)}, bf16[64,2048]{1,0:T(8,128)(2,1)}, bf16[8,4,32,128]{3,2,1,0:T(8,128)(2,1)}) custom-call(s32[1]{0:T(128)} %bitcast.me_ref.refs_0_, bf16[64,2048]{1,0:T(8,128)(2,1)} %get-tuple-element.69.refs_1_.refs_2_, ...), custom_call_target="tpu_custom_call" | custom-call | flops 4096000000 | bytes 4521984 | tf_op jit(solution)/shard_map/pool_bins/pallas_call | solution.py:424
  43.9 1.2 %all-to-all-done.1.mine_ref.refs_4_ = bf16[8,128,512]{2,1,0:T(8,128)(2,1)S(1)} async-done(((bf16[8,128,512]{2,1,0:T(8,128)(2,1)}), bf16[8,128,512]{2,1,0:T(8,128)(2,1)S(1)}, u32[]{:S(2)}, u32[]{:S(2)}) %all-to-all-start.1) | async-done | bytes 1048608 | tf_op jit(solution)/shard_map/all_to_all | solution.py:937
  45.1 1.4 %collective-permute-start.9 = (bf16[8,128,512]{2,1,0:T(8,128)(2,1)S(1)}, bf16[8,128,512]{2,1,0:T(8,128)(2,1)S(1)}, u32[]{:S(2)}, u32[]{:S(2)}) collective-permute-start(bf16[8,128,512]{2,1,0:T(8,128)(2,1)S(1)} %all-to-all-done.1.mine_ref.refs_4_), channel_id=1, source_target_pairs={{0,8},{8,0},{16,24},{24,16},{1,9},{9,1},{17,25},{25,17},{2,10},{10... | collective-permute-start | bytes 3145736 | tf_op jit(solution)/shard_map/ppermute | solution.py:894
  46.5 3.3 %all-to-all-start = ((bf16[32,32,128]{2,1,0:T(8,128)(2,1)}), bf16[32,32,128]{2,1,0:T(8,128)(2,1)S(1)}, u32[]{:S(2)}, u32[]{:S(2)}) async-start(bf16[32,32,128]{2,1,0:T(8,128)(2,1)} %bitcast.13), calls=%async_computation | async-start | bytes 524288 | tf_op jit(solution)/shard_map/all_to_all | solution.py:948
  50.2 1.5 %collective-permute-start.11 = (bf16[64,2048]{1,0:T(8,128)(2,1)}, bf16[64,2048]{1,0:T(8,128)(2,1)}, u32[]{:S(2)}, u32[]{:S(2)}) collective-permute-start(bf16[64,2048]{1,0:T(8,128)(2,1)} %get-tuple-element.85), channel_id=1, source_target_pairs={{0,16},{8,24},{16,0},{24,8},{1,17},{9,25},{17,1},{25,9},{2,18},{10... | collective-permute-start | bytes 786440 | tf_op jit(solution)/shard_map/ppermute | solution.py:894
  52.6 7.6 %all-to-all-done = bf16[32,32,128]{2,1,0:T(8,128)(2,1)S(1)} async-done(((bf16[32,32,128]{2,1,0:T(8,128)(2,1)}), bf16[32,32,128]{2,1,0:T(8,128)(2,1)S(1)}, u32[]{:S(2)}, u32[]{:S(2)}) %all-to-all-start) | async-done | bytes 262176 | tf_op jit(solution)/shard_map/all_to_all | solution.py:948
  61.3 1.5 %collective-permute-start.13 = (f32[8,480]{1,0:T(8,128)S(1)}, f32[8,480]{1,0:T(8,128)S(1)}, u32[]{:S(2)}, u32[]{:S(2)}) collective-permute-start(f32[8,480]{1,0:T(8,128)S(1)} %get-tuple-element.90.refs_0_), channel_id=1, source_target_pairs={{0,16},{8,24},{16,0},{24,8},{1,17},{9,25},{17,1},{25,9},{2,18},{10... | collective-permute-start | bytes 46088 | tf_op jit(solution)/shard_map/ppermute | solution.py:894
  63.0 1.3 %collective-permute-done.14.refs_3_ = f32[8,480]{1,0:T(8,128)S(1)} collective-permute-done((f32[8,480]{1,0:T(8,128)S(1)}, f32[8,480]{1,0:T(8,128)S(1)}, u32[]{:S(2)}, u32[]{:S(2)}) %collective-permute-start.14) | collective-permute-done | bytes 15392 | tf_op jit(solution)/shard_map/ppermute | solution.py:894
  64.3 1.5 %head_grads.1 = (bf16[8,4,32,128]{3,2,1,0:T(8,128)(2,1)}, f32[8,128]{1,0:T(8,128)S(1)}) custom-call(s32[1]{0:T(128)} %bitcast.me_ref.refs_0_, f32[64,480]{1,0:T(8,128)S(1)} %get-tuple-element.89.logits_ref, f32[8,480]{1,0:T(8,128)S(1)} %get-tuple-element.90.refs_0_, f32[8,480]{1,0:T(8,128)S(1)} %collective-permute-done.12.refs_1_, ...), custom_call_target="tpu_custom_call" | custom-call | flops 251658240 | bytes 2670592 | tf_op jit(solution)/shard_map/head_grads/pallas_call | solution.py:424
  65.8 3.5 %all-to-all-start.2 = ((bf16[32,32,128]{2,1,0:T(8,128)(2,1)}), bf16[32,32,128]{2,1,0:T(8,128)(2,1)S(1)}, u32[]{:S(2)}, u32[]{:S(2)}) async-start(bf16[32,32,128]{2,1,0:T(8,128)(2,1)} %bitcast.12), calls=%async_computation.2 | async-start | bytes 524288 | tf_op jit(solution)/shard_map/all_to_all | solution.py:948
  69.3 1.7 %collective-permute-start.18 = (bf16[64,2048]{1,0:T(8,128)(2,1)}, bf16[64,2048]{1,0:T(8,128)(2,1)S(1)}, u32[]{:S(2)}, u32[]{:S(2)}) collective-permute-start(bf16[64,2048]{1,0:T(8,128)(2,1)} %get-tuple-element.93), channel_id=1, source_target_pairs={{0,24},{8,16},{16,8},{24,0},{1,25},{9,17},{17,9},{25,1},{2,26},{10... | collective-permute-start | bytes 786440 | tf_op jit(solution)/shard_map/ppermute | solution.py:894
  72.2 1.5 %collective-permute-done.15 = f32[8,128]{1,0:T(8,128)S(1)} collective-permute-done((f32[8,128]{1,0:T(8,128)S(1)}, f32[8,128]{1,0:T(8,128)S(1)}, u32[]{:S(2)}, u32[]{:S(2)}) %collective-permute-start.15) | collective-permute-done | bytes 4128 | tf_op jit(solution)/shard_map/ppermute | solution.py:965
  73.7 1.2 %collective-permute-start.16 = (f32[8,128]{1,0:T(8,128)S(1)}, f32[8,128]{1,0:T(8,128)S(1)}, u32[]{:S(2)}, u32[]{:S(2)}) collective-permute-start(f32[8,128]{1,0:T(8,128)S(1)} %add.19), channel_id=1, source_target_pairs={{0,2},{1,3},{2,0},{3,1},{4,6},{5,7},{6,4},{7,5},{8,10},{9,11},{10,... | collective-permute-start | bytes 12296 | tf_op jit(solution)/shard_map/ppermute | solution.py:965
  75.0 1.6 %collective-permute-done.16 = f32[8,128]{1,0:T(8,128)S(1)} collective-permute-done((f32[8,128]{1,0:T(8,128)S(1)}, f32[8,128]{1,0:T(8,128)S(1)}, u32[]{:S(2)}, u32[]{:S(2)}) %collective-permute-start.16) | collective-permute-done | bytes 4128 | tf_op jit(solution)/shard_map/ppermute | solution.py:965
  76.6 2.3 %collective-permute-start.17 = (f32[8,128]{1,0:T(8,128)S(1)}, f32[8,128]{1,0:T(8,128)S(1)}, u32[]{:S(2)}, u32[]{:S(2)}) collective-permute-start(f32[8,128]{1,0:T(8,128)S(1)} %add.20), channel_id=1, source_target_pairs={{0,4},{1,5},{2,6},{3,7},{4,0},{5,1},{6,2},{7,3},{8,12},{9,13},{10,... | collective-permute-start | bytes 12296 | tf_op jit(solution)/shard_map/ppermute | solution.py:965
  80.6 5.5 %long_correlation.2 = (bf16[32,2304]{1,0:T(8,128)(2,1)S(1)}, bf16[32,2304]{1,0:T(8,128)(2,1)S(1)}, bf16[32,2304]{1,0:T(8,128)(2,1)S(1)}, bf16[32,2304]{1,0:T(8,128)(2,1)S(1)}) custom-call(s32[1]{0:T(128)} %bitcast.me_ref.refs_0_, f32[4,32,128]{2,1,0:T(8,128)S(1)} %get-tuple-element.96.refs_1_, bf16[64,2048]{1,0:T(8,128)(2,1)} %get-tuple-element.69.refs_1_.refs_2_, ...), custom_call_target="tpu_custom_call" | custom-call | flops 8192000000 | bytes 4260096 | tf_op jit(solution)/shard_map/long_correlation/pallas_call | solution.py:424
  86.1 2.6 %collective-permute-start.19 = (bf16[32,2304]{1,0:T(8,128)(2,1)S(1)}, bf16[32,2304]{1,0:T(8,128)(2,1)S(1)}, u32[]{:S(2)}, u32[]{:S(2)}) collective-permute-start(bf16[32,2304]{1,0:T(8,128)(2,1)S(1)} %get-tuple-element.103), channel_id=1, source_target_pairs={{0,8},{8,0},{16,24},{24,16},{1,9},{9,1},{17,25},{25,17},{2,10},{10... | collective-permute-start | bytes 442376 | tf_op jit(solution)/shard_map/ppermute | solution.py:894
  88.7 1.7 %collective-permute-start.21 = (bf16[32,2304]{1,0:T(8,128)(2,1)S(1)}, bf16[32,2304]{1,0:T(8,128)(2,1)S(1)}, u32[]{:S(2)}, u32[]{:S(2)}) collective-permute-start(bf16[32,2304]{1,0:T(8,128)(2,1)S(1)} %get-tuple-element.105), channel_id=1, source_target_pairs={{0,24},{8,16},{16,8},{24,0},{1,25},{9,17},{17,9},{25,1},{2,26},{10... | collective-permute-start | bytes 442376 | tf_op jit(solution)/shard_map/ppermute | solution.py:894
  90.4 5.6 %long_correlation.3 = (bf16[32,2048]{1,0:T(8,128)(2,1)S(1)}, bf16[32,2048]{1,0:T(8,128)(2,1)S(1)}, bf16[32,2048]{1,0:T(8,128)(2,1)S(1)}, bf16[32,2048]{1,0:T(8,128)(2,1)S(1)}) custom-call(s32[1]{0:T(128)} %bitcast.me_ref.refs_0_, bf16[64,2048]{1,0:T(8,128)(2,1)} %get-tuple-element.69.refs_1_.refs_2_, bf16[64,2048]{1,0:T(8,128)(2,1)} %copy-done.2, ...), custom_call_target="tpu_custom_call" | custom-call | flops 8192000000 | bytes 4129024 | tf_op jit(solution)/shard_map/long_correlation/pallas_call | solution.py:424
  96.3 1.9 %collective-permute-start.24 = (bf16[32,2048]{1,0:T(8,128)(2,1)S(1)}, bf16[32,2048]{1,0:T(8,128)(2,1)S(1)}, u32[]{:S(2)}, u32[]{:S(2)}) collective-permute-start(bf16[32,2048]{1,0:T(8,128)(2,1)S(1)} %get-tuple-element.116), channel_id=1, source_target_pairs={{0,24},{8,16},{16,8},{24,0},{1,25},{9,17},{17,9},{25,1},{2,26},{10... | collective-permute-start | bytes 393224 | tf_op jit(solution)/shard_map/ppermute | solution.py:894
  98.2 4.2 %finish.2 = (f32[3,256,2048]{2,1,0:T(8,128)}, f32[1,1]{1,0:T(1,128)}) custom-call(s32[1]{0:T(128)} %bitcast.me_ref.refs_0_, bf16[256,128]{1,0:T(8,128)(2,1)S(1)} %copy-done.1, bf16[3,256,2048]{2,1,0:T(8,128)(2,1)} %proj_ref.7, bf16[64,2048]{1,0:T(8,128)(2,1)S(1)} %copy-done.5, bf16[64,2048]{1,0:T(8,128)(2,1)} %collective-permute-done.10.refs_1_, ...), custom_call_target="tpu_custom_call" | custom-call | flops 3840000000 | bytes 11145220 | tf_op jit(solution)/shard_map/finish/pallas_call | solution.py:424
  102.4 1.8 %collective-permute-done.24.refs_3_ = bf16[32,2048]{1,0:T(8,128)(2,1)S(1)} collective-permute-done((bf16[32,2048]{1,0:T(8,128)(2,1)S(1)}, bf16[32,2048]{1,0:T(8,128)(2,1)S(1)}, u32[]{:S(2)}, u32[]{:S(2)}) %collective-permute-start.24) | collective-permute-done | bytes 131104 | tf_op jit(solution)/shard_map/ppermute | solution.py:894
  104.3 2.7 %finish.3 = f32[3,256,2048]{2,1,0:T(8,128)} custom-call(s32[1]{0:T(128)} %bitcast.me_ref.refs_0_, bf16[256,128]{1,0:T(8,128)(2,1)S(1)} %copy-done.1, bf16[3,256,2048]{2,1,0:T(8,128)(2,1)} %proj_ref.7, bf16[32,2048]{1,0:T(8,128)(2,1)S(1)} %get-tuple-element.113.refs_0_, ...), custom_call_target="tpu_custom_call", output_to_operand_aliasing={{}: (7, {})} | custom-call | flops 3840000000 | bytes 16318464 | tf_op jit(solution)/shard_map/finish/pallas_call | solution.py:424
  (73 shorter events, 12.3 us)
Async XLA Ops:
  0.6 51.8 %copy-start = (s32[64,3840]{1,0:T(8,128)S(1)}, s32[64,3840]{1,0:T(8,128)}, u32[]{:S(2)}) copy-start(s32[64,3840]{1,0:T(8,128)} %param.20) | copy-start | bytes 2949124
  2.8 17.3 %collective-permute-start.1 = (bf16[2,32,2048]{2,1,0:T(8,128)(2,1)}, bf16[2,32,2048]{2,1,0:T(8,128)(2,1)S(1)}, u32[]{:S(2)}, u32[]{:S(2)}) collective-permute-start(bf16[2,32,2048]{2,1,0:T(8,128)(2,1)} %get-tuple-element.60), channel_id=1, source_target_pairs={{0,16},{8,24},{16,0},{24,8},{1,17},{9,25},{17,1},{25,9},{2,18},{10... | collective-permute-start | bytes 786440 | tf_op jit(solution)/shard_map/ppermute | solution.py:894
  4.9 16.0 %collective-permute-start.2 = (bf16[2,32,2048]{2,1,0:T(8,128)(2,1)}, bf16[2,32,2048]{2,1,0:T(8,128)(2,1)S(1)}, u32[]{:S(2)}, u32[]{:S(2)}) collective-permute-start(bf16[2,32,2048]{2,1,0:T(8,128)(2,1)} %get-tuple-element.61), channel_id=1, source_target_pairs={{0,24},{8,16},{16,8},{24,0},{1,25},{9,17},{17,9},{25,1},{2,26},{10... | collective-permute-start | bytes 786440 | tf_op jit(solution)/shard_map/ppermute | solution.py:894
  9.2 11.7 %collective-permute-start = (bf16[2,32,2048]{2,1,0:T(8,128)(2,1)}, bf16[2,32,2048]{2,1,0:T(8,128)(2,1)}, u32[]{:S(2)}, u32[]{:S(2)}) collective-permute-start(bf16[2,32,2048]{2,1,0:T(8,128)(2,1)} %get-tuple-element.68), channel_id=1, source_target_pairs={{0,8},{8,0},{16,24},{24,16},{1,9},{9,1},{17,25},{25,17},{2,10},{10... | collective-permute-start | bytes 786440 | tf_op jit(solution)/shard_map/ppermute | solution.py:894
  9.6 20.6 %collective-permute-start.6 = (bf16[2,32,2048]{2,1,0:T(8,128)(2,1)}, bf16[2,32,2048]{2,1,0:T(8,128)(2,1)S(1)}, u32[]{:S(2)}, u32[]{:S(2)}) collective-permute-start(bf16[2,32,2048]{2,1,0:T(8,128)(2,1)} %get-tuple-element.74), channel_id=1, source_target_pairs={{0,8},{8,0},{16,24},{24,16},{1,9},{9,1},{17,25},{25,17},{2,10},{10... | collective-permute-start | bytes 786440 | tf_op jit(solution)/shard_map/ppermute | solution.py:894
  9.8 21.4 %collective-permute-start.7 = (bf16[2,32,2048]{2,1,0:T(8,128)(2,1)}, bf16[2,32,2048]{2,1,0:T(8,128)(2,1)}, u32[]{:S(2)}, u32[]{:S(2)}) collective-permute-start(bf16[2,32,2048]{2,1,0:T(8,128)(2,1)} %get-tuple-element.75), channel_id=1, source_target_pairs={{0,16},{8,24},{16,0},{24,8},{1,17},{9,25},{17,1},{25,9},{2,18},{10... | collective-permute-start | bytes 786440 | tf_op jit(solution)/shard_map/ppermute | solution.py:894
  14.1 7.9 %copy-start.8 = (bf16[64,2048]{1,0:T(8,128)(2,1)S(1)}, bf16[64,2048]{1,0:T(8,128)(2,1)}, u32[]{:S(2)}) copy-start(bf16[64,2048]{1,0:T(8,128)(2,1)} %get-tuple-element.71) | copy-start | bytes 786436
  14.1 31.0 %all-to-all-start.1 = ((bf16[8,128,512]{2,1,0:T(8,128)(2,1)}), bf16[8,128,512]{2,1,0:T(8,128)(2,1)S(1)}, u32[]{:S(2)}, u32[]{:S(2)}) async-start(bf16[8,128,512]{2,1,0:T(8,128)(2,1)} %by_track.1), calls=%async_computation.1 | async-start | bytes 2097152 | tf_op jit(solution)/shard_map/all_to_all | solution.py:937
  20.0 10.1 %copy-start.7 = (bf16[64,2048]{1,0:T(8,128)(2,1)S(1)}, bf16[64,2048]{1,0:T(8,128)(2,1)}, u32[]{:S(2)}) copy-start(bf16[64,2048]{1,0:T(8,128)(2,1)} %get-tuple-element.72) | copy-start | bytes 786436
  20.0 11.1 %collective-permute-start.8 = (bf16[2,32,2048]{2,1,0:T(8,128)(2,1)}, bf16[2,32,2048]{2,1,0:T(8,128)(2,1)S(1)}, u32[]{:S(2)}, u32[]{:S(2)}) collective-permute-start(bf16[2,32,2048]{2,1,0:T(8,128)(2,1)} %get-tuple-element.76), channel_id=1, source_target_pairs={{0,24},{8,16},{16,8},{24,0},{1,25},{9,17},{17,9},{25,1},{2,26},{10... | collective-permute-start | bytes 786440 | tf_op jit(solution)/shard_map/ppermute | solution.py:894
  21.6 17.6 %collective-permute-start.3 = (bf16[64,2048]{1,0:T(8,128)(2,1)S(1)}, bf16[64,2048]{1,0:T(8,128)(2,1)S(1)}, u32[]{:S(2)}, u32[]{:S(2)}) collective-permute-start(bf16[64,2048]{1,0:T(8,128)(2,1)S(1)} %copy-done.9), channel_id=1, source_target_pairs={{0,8},{8,0},{16,24},{24,16},{1,9},{9,1},{17,25},{25,17},{2,10},{10... | collective-permute-start | bytes 786440 | tf_op jit(solution)/shard_map/ppermute | solution.py:894
  22.0 17.1 %collective-permute-start.4 = (bf16[64,2048]{1,0:T(8,128)(2,1)S(1)}, bf16[64,2048]{1,0:T(8,128)(2,1)S(1)}, u32[]{:S(2)}, u32[]{:S(2)}) collective-permute-start(bf16[64,2048]{1,0:T(8,128)(2,1)S(1)} %copy-done.8), channel_id=1, source_target_pairs={{0,16},{8,24},{16,0},{24,8},{1,17},{9,25},{17,1},{25,9},{2,18},{10... | collective-permute-start | bytes 786440 | tf_op jit(solution)/shard_map/ppermute | solution.py:894
  30.2 10.2 %collective-permute-start.5 = (bf16[64,2048]{1,0:T(8,128)(2,1)S(1)}, bf16[64,2048]{1,0:T(8,128)(2,1)S(1)}, u32[]{:S(2)}, u32[]{:S(2)}) collective-permute-start(bf16[64,2048]{1,0:T(8,128)(2,1)S(1)} %copy-done.7), channel_id=1, source_target_pairs={{0,24},{8,16},{16,8},{24,0},{1,25},{9,17},{17,9},{25,1},{2,26},{10... | collective-permute-start | bytes 786440 | tf_op jit(solution)/shard_map/ppermute | solution.py:894
  45.1 15.0 %collective-permute-start.9 = (bf16[8,128,512]{2,1,0:T(8,128)(2,1)S(1)}, bf16[8,128,512]{2,1,0:T(8,128)(2,1)S(1)}, u32[]{:S(2)}, u32[]{:S(2)}) collective-permute-start(bf16[8,128,512]{2,1,0:T(8,128)(2,1)S(1)} %all-to-all-done.1.mine_ref.refs_4_), channel_id=1, source_target_pairs={{0,8},{8,0},{16,24},{24,16},{1,9},{9,1},{17,25},{25,17},{2,10},{10... | collective-permute-start | bytes 3145736 | tf_op jit(solution)/shard_map/ppermute | solution.py:894
  46.5 13.6 %all-to-all-start = ((bf16[32,32,128]{2,1,0:T(8,128)(2,1)}), bf16[32,32,128]{2,1,0:T(8,128)(2,1)S(1)}, u32[]{:S(2)}, u32[]{:S(2)}) async-start(bf16[32,32,128]{2,1,0:T(8,128)(2,1)} %bitcast.13), calls=%async_computation | async-start | bytes 524288 | tf_op jit(solution)/shard_map/all_to_all | solution.py:948
  49.9 13.1 %collective-permute-start.10 = (bf16[64,2048]{1,0:T(8,128)(2,1)}, bf16[64,2048]{1,0:T(8,128)(2,1)}, u32[]{:S(2)}, u32[]{:S(2)}) collective-permute-start(bf16[64,2048]{1,0:T(8,128)(2,1)} %get-tuple-element.84), channel_id=1, source_target_pairs={{0,8},{8,0},{16,24},{24,16},{1,9},{9,1},{17,25},{25,17},{2,10},{10... | collective-permute-start | bytes 786440 | tf_op jit(solution)/shard_map/ppermute | solution.py:894
  50.2 12.8 %collective-permute-start.11 = (bf16[64,2048]{1,0:T(8,128)(2,1)}, bf16[64,2048]{1,0:T(8,128)(2,1)}, u32[]{:S(2)}, u32[]{:S(2)}) collective-permute-start(bf16[64,2048]{1,0:T(8,128)(2,1)} %get-tuple-element.85), channel_id=1, source_target_pairs={{0,16},{8,24},{16,0},{24,8},{1,17},{9,25},{17,1},{25,9},{2,18},{10... | collective-permute-start | bytes 786440 | tf_op jit(solution)/shard_map/ppermute | solution.py:894
  60.8 3.5 %collective-permute-start.14 = (f32[8,480]{1,0:T(8,128)S(1)}, f32[8,480]{1,0:T(8,128)S(1)}, u32[]{:S(2)}, u32[]{:S(2)}) collective-permute-start(f32[8,480]{1,0:T(8,128)S(1)} %get-tuple-element.90.refs_0_), channel_id=1, source_target_pairs={{0,24},{8,16},{16,8},{24,0},{1,25},{9,17},{17,9},{25,1},{2,26},{10... | collective-permute-start | bytes 46088 | tf_op jit(solution)/shard_map/ppermute | solution.py:894
  61.3 3.0 %collective-permute-start.13 = (f32[8,480]{1,0:T(8,128)S(1)}, f32[8,480]{1,0:T(8,128)S(1)}, u32[]{:S(2)}, u32[]{:S(2)}) collective-permute-start(f32[8,480]{1,0:T(8,128)S(1)} %get-tuple-element.90.refs_0_), channel_id=1, source_target_pairs={{0,16},{8,24},{16,0},{24,8},{1,17},{9,25},{17,1},{25,9},{2,18},{10... | collective-permute-start | bytes 46088 | tf_op jit(solution)/shard_map/ppermute | solution.py:894
  62.8 1.5 %collective-permute-start.12 = (f32[8,480]{1,0:T(8,128)S(1)}, f32[8,480]{1,0:T(8,128)S(1)}, u32[]{:S(2)}, u32[]{:S(2)}) collective-permute-start(f32[8,480]{1,0:T(8,128)S(1)} %get-tuple-element.90.refs_0_), channel_id=1, source_target_pairs={{0,8},{8,0},{16,24},{24,16},{1,9},{9,1},{17,25},{25,17},{2,10},{10... | collective-permute-start | bytes 46088 | tf_op jit(solution)/shard_map/ppermute | solution.py:894
  65.8 14.7 %all-to-all-start.2 = ((bf16[32,32,128]{2,1,0:T(8,128)(2,1)}), bf16[32,32,128]{2,1,0:T(8,128)(2,1)S(1)}, u32[]{:S(2)}, u32[]{:S(2)}) async-start(bf16[32,32,128]{2,1,0:T(8,128)(2,1)} %bitcast.12), calls=%async_computation.2 | async-start | bytes 524288 | tf_op jit(solution)/shard_map/all_to_all | solution.py:948
  69.3 11.2 %collective-permute-start.18 = (bf16[64,2048]{1,0:T(8,128)(2,1)}, bf16[64,2048]{1,0:T(8,128)(2,1)S(1)}, u32[]{:S(2)}, u32[]{:S(2)}) collective-permute-start(bf16[64,2048]{1,0:T(8,128)(2,1)} %get-tuple-element.93), channel_id=1, source_target_pairs={{0,24},{8,16},{16,8},{24,0},{1,25},{9,17},{17,9},{25,1},{2,26},{10... | collective-permute-start | bytes 786440 | tf_op jit(solution)/shard_map/ppermute | solution.py:894
  71.0 2.8 %collective-permute-start.15 = (f32[8,128]{1,0:T(8,128)S(1)}, f32[8,128]{1,0:T(8,128)S(1)}, u32[]{:S(2)}, u32[]{:S(2)}) collective-permute-start(f32[8,128]{1,0:T(8,128)S(1)} %get-tuple-element.92), channel_id=1, source_target_pairs={{0,1},{1,0},{2,3},{3,2},{4,5},{5,4},{6,7},{7,6},{8,9},{9,8},{10,11... | collective-permute-start | bytes 12296 | tf_op jit(solution)/shard_map/ppermute | solution.py:965
  73.7 2.8 %collective-permute-start.16 = (f32[8,128]{1,0:T(8,128)S(1)}, f32[8,128]{1,0:T(8,128)S(1)}, u32[]{:S(2)}, u32[]{:S(2)}) collective-permute-start(f32[8,128]{1,0:T(8,128)S(1)} %add.19), channel_id=1, source_target_pairs={{0,2},{1,3},{2,0},{3,1},{4,6},{5,7},{6,4},{7,5},{8,10},{9,11},{10,... | collective-permute-start | bytes 12296 | tf_op jit(solution)/shard_map/ppermute | solution.py:965
  76.6 3.4 %collective-permute-start.17 = (f32[8,128]{1,0:T(8,128)S(1)}, f32[8,128]{1,0:T(8,128)S(1)}, u32[]{:S(2)}, u32[]{:S(2)}) collective-permute-start(f32[8,128]{1,0:T(8,128)S(1)} %add.20), channel_id=1, source_target_pairs={{0,4},{1,5},{2,6},{3,7},{4,0},{5,1},{6,2},{7,3},{8,12},{9,13},{10,... | collective-permute-start | bytes 12296 | tf_op jit(solution)/shard_map/ppermute | solution.py:965
  86.1 10.2 %collective-permute-start.19 = (bf16[32,2304]{1,0:T(8,128)(2,1)S(1)}, bf16[32,2304]{1,0:T(8,128)(2,1)S(1)}, u32[]{:S(2)}, u32[]{:S(2)}) collective-permute-start(bf16[32,2304]{1,0:T(8,128)(2,1)S(1)} %get-tuple-element.103), channel_id=1, source_target_pairs={{0,8},{8,0},{16,24},{24,16},{1,9},{9,1},{17,25},{25,17},{2,10},{10... | collective-permute-start | bytes 442376 | tf_op jit(solution)/shard_map/ppermute | solution.py:894
  88.7 9.5 %collective-permute-start.20 = (bf16[32,2304]{1,0:T(8,128)(2,1)S(1)}, bf16[32,2304]{1,0:T(8,128)(2,1)S(1)}, u32[]{:S(2)}, u32[]{:S(2)}) collective-permute-start(bf16[32,2304]{1,0:T(8,128)(2,1)S(1)} %get-tuple-element.104), channel_id=1, source_target_pairs={{0,16},{8,24},{16,0},{24,8},{1,17},{9,25},{17,1},{25,9},{2,18},{10... | collective-permute-start | bytes 442376 | tf_op jit(solution)/shard_map/ppermute | solution.py:894
  88.7 9.5 %collective-permute-start.21 = (bf16[32,2304]{1,0:T(8,128)(2,1)S(1)}, bf16[32,2304]{1,0:T(8,128)(2,1)S(1)}, u32[]{:S(2)}, u32[]{:S(2)}) collective-permute-start(bf16[32,2304]{1,0:T(8,128)(2,1)S(1)} %get-tuple-element.105), channel_id=1, source_target_pairs={{0,24},{8,16},{16,8},{24,0},{1,25},{9,17},{17,9},{25,1},{2,26},{10... | collective-permute-start | bytes 442376 | tf_op jit(solution)/shard_map/ppermute | solution.py:894
  90.4 7.8 %copy-start.5 = (bf16[64,2048]{1,0:T(8,128)(2,1)S(1)}, bf16[64,2048]{1,0:T(8,128)(2,1)}, u32[]{:S(2)}) copy-start(bf16[64,2048]{1,0:T(8,128)(2,1)} %get-tuple-element.86.refs_0_) | copy-start | bytes 786436
  96.0 6.4 %collective-permute-start.22 = (bf16[32,2048]{1,0:T(8,128)(2,1)S(1)}, bf16[32,2048]{1,0:T(8,128)(2,1)S(1)}, u32[]{:S(2)}, u32[]{:S(2)}) collective-permute-start(bf16[32,2048]{1,0:T(8,128)(2,1)S(1)} %get-tuple-element.114), channel_id=1, source_target_pairs={{0,8},{8,0},{16,24},{24,16},{1,9},{9,1},{17,25},{25,17},{2,10},{10... | collective-permute-start | bytes 393224 | tf_op jit(solution)/shard_map/ppermute | solution.py:894
  96.2 6.2 %collective-permute-start.23 = (bf16[32,2048]{1,0:T(8,128)(2,1)S(1)}, bf16[32,2048]{1,0:T(8,128)(2,1)S(1)}, u32[]{:S(2)}, u32[]{:S(2)}) collective-permute-start(bf16[32,2048]{1,0:T(8,128)(2,1)S(1)} %get-tuple-element.115), channel_id=1, source_target_pairs={{0,16},{8,24},{16,0},{24,8},{1,17},{9,25},{17,1},{25,9},{2,18},{10... | collective-permute-start | bytes 393224 | tf_op jit(solution)/shard_map/ppermute | solution.py:894
  96.3 8.0 %collective-permute-start.24 = (bf16[32,2048]{1,0:T(8,128)(2,1)S(1)}, bf16[32,2048]{1,0:T(8,128)(2,1)S(1)}, u32[]{:S(2)}, u32[]{:S(2)}) collective-permute-start(bf16[32,2048]{1,0:T(8,128)(2,1)S(1)} %get-tuple-element.116), channel_id=1, source_target_pairs={{0,24},{8,16},{16,8},{24,0},{1,25},{9,17},{17,9},{25,1},{2,26},{10... | collective-permute-start | bytes 393224 | tf_op jit(solution)/shard_map/ppermute | solution.py:894
  (10 other events, 32.9 us)

commit v8 on v7

--- a/solution.py
+++ b/solution.py
@@ -626,15 +626,15 @@
         out_shapes,
         [pl.BlockSpec(memory_space=pltpu.HBM)] * len(out_shapes),
         [
-            pltpu.VMEM((count, 2, rows, width), bf16),
-            pltpu.VMEM((count, rows, width), f32),
-            pltpu.VMEM((count, 2, rows, width), bf16),
+            pltpu.VMEM((max(count, 1), 2, rows, width), bf16),
+            pltpu.VMEM((max(count, 1), rows, width), f32),
+            pltpu.VMEM((max(count, 1), 2, rows, width), bf16),
             pltpu.VMEM((max(query_count, 1), pencil, width), bf16),
-            pltpu.SemaphoreType.DMA((count, 3)),
-            pltpu.SemaphoreType.DMA((count,)),
+            pltpu.SemaphoreType.DMA((max(count, 1), 3)),
+            pltpu.SemaphoreType.DMA((max(count, 1),)),
             pltpu.SemaphoreType.DMA((max(query_count, 1), 2)),
         ],
-        rows * count * 0.015 * MICROSECOND,
+        max(rows * count * 0.015, 2.0) * MICROSECOND,
     )
 
 
@@ -925,11 +925,12 @@
     others = [(0, k) for k in range(peers // 2)] + [(j, k) for j in range(1, chunks) for k in range(peers)]
     far = lay_out(me, projections, filter_taps, peers, chunks, first, False)
     me_next, _ = lax.optimization_barrier((me, far))
-    rest = lay_out(me_next, projections, filter_taps, peers, chunks, others, True)
+    rest = lay_out(me_next, projections, filter_taps, peers, chunks, others, False)
     me_next, _ = lax.optimization_barrier((me, rest))
     laid = dict(zip(first + others, [*far, *rest]))
     pieces = [[swap(laid[j, k], k, peers) for k in range(peers)] for j in range(chunks)]
-    held_back, _ = lax.optimization_barrier((rest[len(others) :], pieces[0]))
+    me_query, _ = lax.optimization_barrier((me, pieces[0]))
+    held_back = lay_out(me_query, projections, filter_taps, peers, chunks, [], True)
     queries = [swap(held_back[k], k, peers) for k in range(peers)]
     skip = lax.dynamic_index_in_dim(skip_gain.reshape(peers, pencil, 1), seat, axis=0, keepdims=False)
 

time: 108 us -> 108 us (level)
  waiting for transfers between devices: 17.9 us -> 16.1 us
  Pallas kernels: 46 us -> 47.5 us
    pallas_call x13 -> x14, Pallas kernels: 46 us -> 47.5 us  [call(): pl.pallas_call(kernel, name=name, grid_spec=pltpu.PrefetchScalarGridSpec(...]
    ppermute x22, waiting for transfers between devices: 4.94 us -> 3.72 us  [swap(): return lax.ppermute(value, 'seq', [(i, i ^ k) for i in range(count)])]
  transfers between devices with their start and end apart: 28 -> 28, of which waited for: 9 -> 8; matrix products, arithmetic and copies ran while one was open for 1% -> 1% of each run, Pallas kernels for 32% -> 33%
where the time goes in v8:
time: 108 us; the launch traced here: 107 us
  Pallas kernels  47.5 us (44%)
  starting transfers between devices  39.9 us (37%)
  waiting for transfers between devices  16.1 us (15%)
  local copies, waits for them, and re-layouts  2.58 us (2%)
  between operations  1.1 us (1%)
    pallas_call x14, Pallas kernels, call(): pl.pallas_call(kernel, name=name, grid_spec=pltpu.PrefetchScalarGridSpec(...  47.5 us
    ppermute x22, starting transfers between devices, swap(): return lax.ppermute(value, 'seq', [(i, i ^ k) for i in range(count)])  21.8 us
    all_to_all x2, starting transfers between devices, exchange(): lax.all_to_all(flat, ('chan', 'seq'), split_axis=0, concat_axis=0, tiled=...  7.65 us
    all_to_all x2, waiting for transfers between devices, exchange(): lax.all_to_all(flat, ('chan', 'seq'), split_axis=0, concat_axis=0, tiled=...  7.58 us
    all_to_all x1, starting transfers between devices, aligned(): mine = lax.all_to_all(mine, 'chan', split_axis=0, concat_axis=0, tiled=True)  5.7 us
    ppermute x3, starting transfers between devices, aligned(): lax.ppermute(loss, 'chan', [(i, i ^ step) for i in range(groups)])  4.81 us
    ppermute x3, waiting for transfers between devices, aligned(): lax.ppermute(loss, 'chan', [(i, i ^ step) for i in range(groups)])  4.11 us
    ppermute x22, waiting for transfers between devices, swap(): return lax.ppermute(value, 'seq', [(i, i ^ k) for i in range(count)])  3.72 us
  transfers between devices with their start and end apart: 28, of which 8 were waited for; matrix products, arithmetic and copies ran while one was open for 1% of the time, Pallas kernels for 33%

profile of v8, /device:TPU:1, one launch (start us, length us, event | category | flops | bytes accessed | tf_op | source)
XLA Modules:
  0.0 107.2 jit_solution(3227334643354892930)
XLA Ops:
  0.7 2.1 %lay_out.3 = (bf16[2,32,2048]{2,1,0:T(8,128)(2,1)}, bf16[2,32,2048]{2,1,0:T(8,128)(2,1)}) custom-call(s32[1]{0:T(128)} %bitcast.me_ref.refs_0_, bf16[3,256,2048]{2,1,0:T(8,128)(2,1)} %proj_ref.9, f32[256,2048]{1,0:T(8,128)} %taps_ref.5), custom_call_target="tpu_custom_call" | custom-call | flops 2000000000 | bytes 5767168 | tf_op jit(solution)/shard_map/lay_out/pallas_call | solution.py:424
  2.8 2.1 %collective-permute-start.1 = (bf16[2,32,2048]{2,1,0:T(8,128)(2,1)}, bf16[2,32,2048]{2,1,0:T(8,128)(2,1)S(1)}, u32[]{:S(2)}, u32[]{:S(2)}) collective-permute-start(bf16[2,32,2048]{2,1,0:T(8,128)(2,1)} %get-tuple-element.57), channel_id=1, source_target_pairs={{0,16},{8,24},{16,0},{24,8},{1,17},{9,25},{17,1},{25,9},{2,18},{10... | collective-permute-start | bytes 786440 | tf_op jit(solution)/shard_map/ppermute | solution.py:894
  5.5 2.8 %lay_out.4 = (bf16[2,32,2048]{2,1,0:T(8,128)(2,1)}, bf16[2,32,2048]{2,1,0:T(8,128)(2,1)}, bf16[2,32,2048]{2,1,0:T(8,128)(2,1)}, bf16[2,32,2048]{2,1,0:T(8,128)(2...) custom-call(s32[1]{0:T(128)} %bitcast.me_ref.refs_0_, bf16[3,256,2048]{2,1,0:T(8,128)(2,1)} %proj_ref.9, ...), custom_call_target="tpu_custom_call" | custom-call | flops 2880000000 | bytes 6815744 | tf_op jit(solution)/shard_map/lay_out/pallas_call | solution.py:424
  9.0 1.7 %collective-permute-start.7 = (bf16[2,32,2048]{2,1,0:T(8,128)(2,1)}, bf16[2,32,2048]{2,1,0:T(8,128)(2,1)S(1)}, u32[]{:S(2)}, u32[]{:S(2)}) collective-permute-start(bf16[2,32,2048]{2,1,0:T(8,128)(2,1)} %get-tuple-element.69), channel_id=1, source_target_pairs={{0,16},{8,24},{16,0},{24,8},{1,17},{9,25},{17,1},{25,9},{2,18},{10... | collective-permute-start | bytes 786440 | tf_op jit(solution)/shard_map/ppermute | solution.py:894
  10.6 2.7 %by_track.1 = bf16[8,128,512]{2,1,0:T(8,128)(2,1)} custom-call(s32[1]{0:T(128)} %bitcast.me_ref.refs_0_, bf16[256,3840]{1,0:T(8,128)(2,1)} %weight_ref.1), custom_call_target="tpu_custom_call" | custom-call | flops 2000000000 | bytes 3014656 | tf_op jit(solution)/shard_map/by_track/pallas_call | solution.py:424
  13.3 5.7 %all-to-all-start.1 = ((bf16[8,128,512]{2,1,0:T(8,128)(2,1)}), bf16[8,128,512]{2,1,0:T(8,128)(2,1)S(1)}, u32[]{:S(2)}, u32[]{:S(2)}) async-start(bf16[8,128,512]{2,1,0:T(8,128)(2,1)} %by_track.1), calls=%async_computation.1 | async-start | bytes 2097152 | tf_op jit(solution)/shard_map/all_to_all | solution.py:938
  20.1 2.1 %lay_out.5 = (bf16[64,2048]{1,0:T(8,128)(2,1)}, bf16[64,2048]{1,0:T(8,128)(2,1)}, bf16[64,2048]{1,0:T(8,128)(2,1)}, bf16[64,2048]{1,0:T(8,128)(2,1)}) custom-call(s32[1]{0:T(128)} %bitcast.me_ref.refs_0_, bf16[3,256,2048]{2,1,0:T(8,128)(2,1)} %proj_ref.9, f32[256,2048]{1,0:T(8,128)} %taps_ref.5), custom_call_target="tpu_custom_call" | custom-call | flops 2000000000 | bytes 6291456 | tf_op jit(solution)/shard_map/lay_out/pallas_call | solution.py:424
  22.3 1.3 %collective-permute-start.4 = (bf16[64,2048]{1,0:T(8,128)(2,1)}, bf16[64,2048]{1,0:T(8,128)(2,1)S(1)}, u32[]{:S(2)}, u32[]{:S(2)}) collective-permute-start(bf16[64,2048]{1,0:T(8,128)(2,1)} %get-tuple-element.65), channel_id=1, source_target_pairs={{0,16},{8,24},{16,0},{24,8},{1,17},{9,25},{17,1},{25,9},{2,18},{10... | collective-permute-start | bytes 786440 | tf_op jit(solution)/shard_map/ppermute | solution.py:894
  23.6 7.3 %long_convolution.2 = (f32[64,8192]{1,0:T(8,128)S(1)}, f32[2,256,256]{2,1,0:T(8,128)}, f32[2,256,256]{2,1,0:T(8,128)}, f32[2,256,256]{2,1,0:T(8,128)}, f32[2,256,256]{2,1,0:T(8,128)}) custom-call(s32[1]{0:T(128)} %bitcast.me_ref.refs_0_, bf16[2,32,2048]{2,1,0:T(8,128)(2,1)} %get-tuple-element.60.refs_1_, bf16[2,32,2048]{2,1,0:T(8,128)(2,1)} %collective-permute-done.refs_2_, ...), custom_call_target="tpu_custom_call" | custom-call | flops 8192000000 | bytes 5832960 | tf_op jit(solution)/shard_map/long_convolution/pallas_call | solution.py:424
  32.7 7.3 %long_convolution.3 = (f32[64,8192]{1,0:T(8,128)S(1)}, f32[2,256,256]{2,1,0:T(8,128)}, f32[2,256,256]{2,1,0:T(8,128)}, f32[2,256,256]{2,1,0:T(8,128)}, f32[2,256,256]{2,1,0:T(8,128)}) custom-call(s32[1]{0:T(128)} %bitcast.me_ref.refs_0_, bf16[2,32,2048]{2,1,0:T(8,128)(2,1)} %get-tuple-element.67.refs_1_, ...), custom_call_target="tpu_custom_call", output_to_operand_aliasing={{0}: (11, {})} | custom-call | flops 8192000000 | bytes 7930112 | tf_op jit(solution)/shard_map/long_convolution/pallas_call | solution.py:424
  40.0 2.9 %pool_bins.1 = (bf16[64,2048]{1,0:T(8,128)(2,1)}, bf16[64,2048]{1,0:T(8,128)(2,1)}, bf16[64,2048]{1,0:T(8,128)(2,1)}, bf16[64,2048]{1,0:T(8,128)(2,1)}, bf16[8,4,32,128]{3,2,1,0:T(8,128)(2,1)}) custom-call(s32[1]{0:T(128)} %bitcast.me_ref.refs_0_, bf16[64,2048]{1,0:T(8,128)(2,1)} %get-tuple-element.63.refs_1_.refs_2_, ...), custom_call_target="tpu_custom_call" | custom-call | flops 4096000000 | bytes 4521984 | tf_op jit(solution)/shard_map/pool_bins/pallas_call | solution.py:424
  44.3 1.4 %collective-permute-start.9 = (bf16[8,128,512]{2,1,0:T(8,128)(2,1)S(1)}, bf16[8,128,512]{2,1,0:T(8,128)(2,1)S(1)}, u32[]{:S(2)}, u32[]{:S(2)}) collective-permute-start(bf16[8,128,512]{2,1,0:T(8,128)(2,1)S(1)} %all-to-all-done.1.mine_ref.refs_4_), channel_id=1, source_target_pairs={{0,8},{8,0},{16,24},{24,16},{1,9},{9,1},{17,25},{25,17},{2,10},{10... | collective-permute-start | bytes 3145736 | tf_op jit(solution)/shard_map/ppermute | solution.py:894
  45.7 4.2 %all-to-all-start = ((bf16[32,32,128]{2,1,0:T(8,128)(2,1)}), bf16[32,32,128]{2,1,0:T(8,128)(2,1)S(1)}, u32[]{:S(2)}, u32[]{:S(2)}) async-start(bf16[32,32,128]{2,1,0:T(8,128)(2,1)} %bitcast.13), calls=%async_computation | async-start | bytes 524288 | tf_op jit(solution)/shard_map/all_to_all | solution.py:949
  50.2 1.5 %collective-permute-start.11 = (bf16[64,2048]{1,0:T(8,128)(2,1)}, bf16[64,2048]{1,0:T(8,128)(2,1)}, u32[]{:S(2)}, u32[]{:S(2)}) collective-permute-start(bf16[64,2048]{1,0:T(8,128)(2,1)} %get-tuple-element.79), channel_id=1, source_target_pairs={{0,16},{8,24},{16,0},{24,8},{1,17},{9,25},{17,1},{25,9},{2,18},{10... | collective-permute-start | bytes 786440 | tf_op jit(solution)/shard_map/ppermute | solution.py:894
  52.6 7.6 %all-to-all-done = bf16[32,32,128]{2,1,0:T(8,128)(2,1)S(1)} async-done(((bf16[32,32,128]{2,1,0:T(8,128)(2,1)}), bf16[32,32,128]{2,1,0:T(8,128)(2,1)S(1)}, u32[]{:S(2)}, u32[]{:S(2)}) %all-to-all-start) | async-done | bytes 262176 | tf_op jit(solution)/shard_map/all_to_all | solution.py:949
  61.3 1.5 %collective-permute-start.13 = (f32[8,480]{1,0:T(8,128)S(1)}, f32[8,480]{1,0:T(8,128)S(1)}, u32[]{:S(2)}, u32[]{:S(2)}) collective-permute-start(f32[8,480]{1,0:T(8,128)S(1)} %get-tuple-element.84.refs_0_), channel_id=1, source_target_pairs={{0,16},{8,24},{16,0},{24,8},{1,17},{9,25},{17,1},{25,9},{2,18},{10... | collective-permute-start | bytes 46088 | tf_op jit(solution)/shard_map/ppermute | solution.py:894
  63.0 1.3 %collective-permute-done.14.refs_3_ = f32[8,480]{1,0:T(8,128)S(1)} collective-permute-done((f32[8,480]{1,0:T(8,128)S(1)}, f32[8,480]{1,0:T(8,128)S(1)}, u32[]{:S(2)}, u32[]{:S(2)}) %collective-permute-start.14) | collective-permute-done | bytes 15392 | tf_op jit(solution)/shard_map/ppermute | solution.py:894
  64.4 1.5 %head_grads.1 = (bf16[8,4,32,128]{3,2,1,0:T(8,128)(2,1)}, f32[8,128]{1,0:T(8,128)S(1)}) custom-call(s32[1]{0:T(128)} %bitcast.me_ref.refs_0_, f32[64,480]{1,0:T(8,128)S(1)} %get-tuple-element.83.logits_ref, f32[8,480]{1,0:T(8,128)S(1)} %get-tuple-element.84.refs_0_, f32[8,480]{1,0:T(8,128)S(1)} %collective-permute-done.12.refs_1_, ...), custom_call_target="tpu_custom_call" | custom-call | flops 251658240 | bytes 2670592 | tf_op jit(solution)/shard_map/head_grads/pallas_call | solution.py:424
  65.8 3.5 %all-to-all-start.2 = ((bf16[32,32,128]{2,1,0:T(8,128)(2,1)}), bf16[32,32,128]{2,1,0:T(8,128)(2,1)S(1)}, u32[]{:S(2)}, u32[]{:S(2)}) async-start(bf16[32,32,128]{2,1,0:T(8,128)(2,1)} %bitcast.12), calls=%async_computation.2 | async-start | bytes 524288 | tf_op jit(solution)/shard_map/all_to_all | solution.py:949
  69.3 1.7 %collective-permute-start.18 = (bf16[64,2048]{1,0:T(8,128)(2,1)}, bf16[64,2048]{1,0:T(8,128)(2,1)S(1)}, u32[]{:S(2)}, u32[]{:S(2)}) collective-permute-start(bf16[64,2048]{1,0:T(8,128)(2,1)} %get-tuple-element.87), channel_id=1, source_target_pairs={{0,24},{8,16},{16,8},{24,0},{1,25},{9,17},{17,9},{25,1},{2,26},{10... | collective-permute-start | bytes 786440 | tf_op jit(solution)/shard_map/ppermute | solution.py:894
  72.3 1.5 %collective-permute-done.15 = f32[8,128]{1,0:T(8,128)S(1)} collective-permute-done((f32[8,128]{1,0:T(8,128)S(1)}, f32[8,128]{1,0:T(8,128)S(1)}, u32[]{:S(2)}, u32[]{:S(2)}) %collective-permute-start.15) | collective-permute-done | bytes 4128 | tf_op jit(solution)/shard_map/ppermute | solution.py:966
  73.8 1.2 %collective-permute-start.16 = (f32[8,128]{1,0:T(8,128)S(1)}, f32[8,128]{1,0:T(8,128)S(1)}, u32[]{:S(2)}, u32[]{:S(2)}) collective-permute-start(f32[8,128]{1,0:T(8,128)S(1)} %add.19), channel_id=1, source_target_pairs={{0,2},{1,3},{2,0},{3,1},{4,6},{5,7},{6,4},{7,5},{8,10},{9,11},{10,... | collective-permute-start | bytes 12296 | tf_op jit(solution)/shard_map/ppermute | solution.py:966
  75.0 1.6 %collective-permute-done.16 = f32[8,128]{1,0:T(8,128)S(1)} collective-permute-done((f32[8,128]{1,0:T(8,128)S(1)}, f32[8,128]{1,0:T(8,128)S(1)}, u32[]{:S(2)}, u32[]{:S(2)}) %collective-permute-start.16) | collective-permute-done | bytes 4128 | tf_op jit(solution)/shard_map/ppermute | solution.py:966
  76.6 2.3 %collective-permute-start.17 = (f32[8,128]{1,0:T(8,128)S(1)}, f32[8,128]{1,0:T(8,128)S(1)}, u32[]{:S(2)}, u32[]{:S(2)}) collective-permute-start(f32[8,128]{1,0:T(8,128)S(1)} %add.20), channel_id=1, source_target_pairs={{0,4},{1,5},{2,6},{3,7},{4,0},{5,1},{6,2},{7,3},{8,12},{9,13},{10,... | collective-permute-start | bytes 12296 | tf_op jit(solution)/shard_map/ppermute | solution.py:966
  80.6 5.5 %long_correlation.2 = (bf16[32,2304]{1,0:T(8,128)(2,1)S(1)}, bf16[32,2304]{1,0:T(8,128)(2,1)S(1)}, bf16[32,2304]{1,0:T(8,128)(2,1)S(1)}, bf16[32,2304]{1,0:T(8,128)(2,1)S(1)}) custom-call(s32[1]{0:T(128)} %bitcast.me_ref.refs_0_, f32[4,32,128]{2,1,0:T(8,128)S(1)} %get-tuple-element.90.refs_1_, bf16[64,2048]{1,0:T(8,128)(2,1)} %get-tuple-element.63.refs_1_.refs_2_, ...), custom_call_target="tpu_custom_call" | custom-call | flops 8192000000 | bytes 4260096 | tf_op jit(solution)/shard_map/long_correlation/pallas_call | solution.py:424
  86.1 2.6 %collective-permute-start.19 = (bf16[32,2304]{1,0:T(8,128)(2,1)S(1)}, bf16[32,2304]{1,0:T(8,128)(2,1)S(1)}, u32[]{:S(2)}, u32[]{:S(2)}) collective-permute-start(bf16[32,2304]{1,0:T(8,128)(2,1)S(1)} %get-tuple-element.97), channel_id=1, source_target_pairs={{0,8},{8,0},{16,24},{24,16},{1,9},{9,1},{17,25},{25,17},{2,10},{10... | collective-permute-start | bytes 442376 | tf_op jit(solution)/shard_map/ppermute | solution.py:894
  88.8 1.7 %collective-permute-start.21 = (bf16[32,2304]{1,0:T(8,128)(2,1)S(1)}, bf16[32,2304]{1,0:T(8,128)(2,1)S(1)}, u32[]{:S(2)}, u32[]{:S(2)}) collective-permute-start(bf16[32,2304]{1,0:T(8,128)(2,1)S(1)} %get-tuple-element.99), channel_id=1, source_target_pairs={{0,24},{8,16},{16,8},{24,0},{1,25},{9,17},{17,9},{25,1},{2,26},{10... | collective-permute-start | bytes 442376 | tf_op jit(solution)/shard_map/ppermute | solution.py:894
  90.4 5.6 %long_correlation.3 = (bf16[32,2048]{1,0:T(8,128)(2,1)S(1)}, bf16[32,2048]{1,0:T(8,128)(2,1)S(1)}, bf16[32,2048]{1,0:T(8,128)(2,1)S(1)}, bf16[32,2048]{1,0:T(8,128)(2,1)S(1)}) custom-call(s32[1]{0:T(128)} %bitcast.me_ref.refs_0_, bf16[64,2048]{1,0:T(8,128)(2,1)} %get-tuple-element.63.refs_1_.refs_2_, bf16[64,2048]{1,0:T(8,128)(2,1)} %copy-done.2, ...), custom_call_target="tpu_custom_call" | custom-call | flops 8192000000 | bytes 4129024 | tf_op jit(solution)/shard_map/long_correlation/pallas_call | solution.py:424
  96.3 1.9 %collective-permute-start.24 = (bf16[32,2048]{1,0:T(8,128)(2,1)S(1)}, bf16[32,2048]{1,0:T(8,128)(2,1)S(1)}, u32[]{:S(2)}, u32[]{:S(2)}) collective-permute-start(bf16[32,2048]{1,0:T(8,128)(2,1)S(1)} %get-tuple-element.110), channel_id=1, source_target_pairs={{0,24},{8,16},{16,8},{24,0},{1,25},{9,17},{17,9},{25,1},{2,26},{10... | collective-permute-start | bytes 393224 | tf_op jit(solution)/shard_map/ppermute | solution.py:894
  98.3 4.2 %finish.2 = (f32[3,256,2048]{2,1,0:T(8,128)}, f32[1,1]{1,0:T(1,128)}) custom-call(s32[1]{0:T(128)} %bitcast.me_ref.refs_0_, bf16[256,128]{1,0:T(8,128)(2,1)S(1)} %copy-done.1, bf16[3,256,2048]{2,1,0:T(8,128)(2,1)} %proj_ref.9, bf16[64,2048]{1,0:T(8,128)(2,1)S(1)} %copy-done.5, bf16[64,2048]{1,0:T(8,128)(2,1)} %collective-permute-done.10.refs_1_, ...), custom_call_target="tpu_custom_call" | custom-call | flops 3840000000 | bytes 11145220 | tf_op jit(solution)/shard_map/finish/pallas_call | solution.py:424
  102.5 1.8 %collective-permute-done.24.refs_3_ = bf16[32,2048]{1,0:T(8,128)(2,1)S(1)} collective-permute-done((bf16[32,2048]{1,0:T(8,128)(2,1)S(1)}, bf16[32,2048]{1,0:T(8,128)(2,1)S(1)}, u32[]{:S(2)}, u32[]{:S(2)}) %collective-permute-start.24) | collective-permute-done | bytes 131104 | tf_op jit(solution)/shard_map/ppermute | solution.py:894
  104.3 2.7 %finish.3 = f32[3,256,2048]{2,1,0:T(8,128)} custom-call(s32[1]{0:T(128)} %bitcast.me_ref.refs_0_, bf16[256,128]{1,0:T(8,128)(2,1)S(1)} %copy-done.1, bf16[3,256,2048]{2,1,0:T(8,128)(2,1)} %proj_ref.9, bf16[32,2048]{1,0:T(8,128)(2,1)S(1)} %get-tuple-element.107.refs_0_, ...), custom_call_target="tpu_custom_call", output_to_operand_aliasing={{}: (7, {})} | custom-call | flops 3840000000 | bytes 16318464 | tf_op jit(solution)/shard_map/finish/pallas_call | solution.py:424
  (74 shorter events, 11.2 us)
Async XLA Ops:
  0.6 51.9 %copy-start = (s32[64,3840]{1,0:T(8,128)S(1)}, s32[64,3840]{1,0:T(8,128)}, u32[]{:S(2)}) copy-start(s32[64,3840]{1,0:T(8,128)} %param.20) | copy-start | bytes 2949124
  2.8 16.4 %collective-permute-start.1 = (bf16[2,32,2048]{2,1,0:T(8,128)(2,1)}, bf16[2,32,2048]{2,1,0:T(8,128)(2,1)S(1)}, u32[]{:S(2)}, u32[]{:S(2)}) collective-permute-start(bf16[2,32,2048]{2,1,0:T(8,128)(2,1)} %get-tuple-element.57), channel_id=1, source_target_pairs={{0,16},{8,24},{16,0},{24,8},{1,17},{9,25},{17,1},{25,9},{2,18},{10... | collective-permute-start | bytes 786440 | tf_op jit(solution)/shard_map/ppermute | solution.py:894
  4.9 15.2 %collective-permute-start.2 = (bf16[2,32,2048]{2,1,0:T(8,128)(2,1)}, bf16[2,32,2048]{2,1,0:T(8,128)(2,1)S(1)}, u32[]{:S(2)}, u32[]{:S(2)}) collective-permute-start(bf16[2,32,2048]{2,1,0:T(8,128)(2,1)} %get-tuple-element.58), channel_id=1, source_target_pairs={{0,24},{8,16},{16,8},{24,0},{1,25},{9,17},{17,9},{25,1},{2,26},{10... | collective-permute-start | bytes 786440 | tf_op jit(solution)/shard_map/ppermute | solution.py:894
  8.4 11.7 %collective-permute-start = (bf16[2,32,2048]{2,1,0:T(8,128)(2,1)}, bf16[2,32,2048]{2,1,0:T(8,128)(2,1)}, u32[]{:S(2)}, u32[]{:S(2)}) collective-permute-start(bf16[2,32,2048]{2,1,0:T(8,128)(2,1)} %get-tuple-element.61), channel_id=1, source_target_pairs={{0,8},{8,0},{16,24},{24,16},{1,9},{9,1},{17,25},{25,17},{2,10},{10... | collective-permute-start | bytes 786440 | tf_op jit(solution)/shard_map/ppermute | solution.py:894
  8.8 22.1 %collective-permute-start.6 = (bf16[2,32,2048]{2,1,0:T(8,128)(2,1)}, bf16[2,32,2048]{2,1,0:T(8,128)(2,1)S(1)}, u32[]{:S(2)}, u32[]{:S(2)}) collective-permute-start(bf16[2,32,2048]{2,1,0:T(8,128)(2,1)} %get-tuple-element.68), channel_id=1, source_target_pairs={{0,8},{8,0},{16,24},{24,16},{1,9},{9,1},{17,25},{25,17},{2,10},{10... | collective-permute-start | bytes 786440 | tf_op jit(solution)/shard_map/ppermute | solution.py:894
  9.0 22.9 %collective-permute-start.7 = (bf16[2,32,2048]{2,1,0:T(8,128)(2,1)}, bf16[2,32,2048]{2,1,0:T(8,128)(2,1)S(1)}, u32[]{:S(2)}, u32[]{:S(2)}) collective-permute-start(bf16[2,32,2048]{2,1,0:T(8,128)(2,1)} %get-tuple-element.69), channel_id=1, source_target_pairs={{0,16},{8,24},{16,0},{24,8},{1,17},{9,25},{17,1},{25,9},{2,18},{10... | collective-permute-start | bytes 786440 | tf_op jit(solution)/shard_map/ppermute | solution.py:894
  13.3 31.0 %all-to-all-start.1 = ((bf16[8,128,512]{2,1,0:T(8,128)(2,1)}), bf16[8,128,512]{2,1,0:T(8,128)(2,1)S(1)}, u32[]{:S(2)}, u32[]{:S(2)}) async-start(bf16[8,128,512]{2,1,0:T(8,128)(2,1)} %by_track.1), calls=%async_computation.1 | async-start | bytes 2097152 | tf_op jit(solution)/shard_map/all_to_all | solution.py:938
  19.2 12.6 %collective-permute-start.8 = (bf16[2,32,2048]{2,1,0:T(8,128)(2,1)S(1)}, bf16[2,32,2048]{2,1,0:T(8,128)(2,1)S(1)}, u32[]{:S(2)}, u32[]{:S(2)}) collective-permute-start(bf16[2,32,2048]{2,1,0:T(8,128)(2,1)S(1)} %copy-done.9), channel_id=1, source_target_pairs={{0,24},{8,16},{16,8},{24,0},{1,25},{9,17},{17,9},{25,1},{2,26},{10... | collective-permute-start | bytes 786440 | tf_op jit(solution)/shard_map/ppermute | solution.py:894
  22.2 17.7 %collective-permute-start.3 = (bf16[64,2048]{1,0:T(8,128)(2,1)}, bf16[64,2048]{1,0:T(8,128)(2,1)S(1)}, u32[]{:S(2)}, u32[]{:S(2)}) collective-permute-start(bf16[64,2048]{1,0:T(8,128)(2,1)} %get-tuple-element.64), channel_id=1, source_target_pairs={{0,8},{8,0},{16,24},{24,16},{1,9},{9,1},{17,25},{25,17},{2,10},{10... | collective-permute-start | bytes 786440 | tf_op jit(solution)/shard_map/ppermute | solution.py:894
  22.3 8.6 %copy-start.13 = (bf16[64,2048]{1,0:T(8,128)(2,1)S(1)}, bf16[64,2048]{1,0:T(8,128)(2,1)}, u32[]{:S(2)}) copy-start(bf16[64,2048]{1,0:T(8,128)(2,1)} %get-tuple-element.66) | copy-start | bytes 786436
  22.3 17.7 %collective-permute-start.4 = (bf16[64,2048]{1,0:T(8,128)(2,1)}, bf16[64,2048]{1,0:T(8,128)(2,1)S(1)}, u32[]{:S(2)}, u32[]{:S(2)}) collective-permute-start(bf16[64,2048]{1,0:T(8,128)(2,1)} %get-tuple-element.65), channel_id=1, source_target_pairs={{0,16},{8,24},{16,0},{24,8},{1,17},{9,25},{17,1},{25,9},{2,18},{10... | collective-permute-start | bytes 786440 | tf_op jit(solution)/shard_map/ppermute | solution.py:894
  30.9 9.1 %collective-permute-start.5 = (bf16[64,2048]{1,0:T(8,128)(2,1)S(1)}, bf16[64,2048]{1,0:T(8,128)(2,1)S(1)}, u32[]{:S(2)}, u32[]{:S(2)}) collective-permute-start(bf16[64,2048]{1,0:T(8,128)(2,1)S(1)} %copy-done.13), channel_id=1, source_target_pairs={{0,24},{8,16},{16,8},{24,0},{1,25},{9,17},{17,9},{25,1},{2,26},{10... | collective-permute-start | bytes 786440 | tf_op jit(solution)/shard_map/ppermute | solution.py:894
  44.3 15.9 %collective-permute-start.9 = (bf16[8,128,512]{2,1,0:T(8,128)(2,1)S(1)}, bf16[8,128,512]{2,1,0:T(8,128)(2,1)S(1)}, u32[]{:S(2)}, u32[]{:S(2)}) collective-permute-start(bf16[8,128,512]{2,1,0:T(8,128)(2,1)S(1)} %all-to-all-done.1.mine_ref.refs_4_), channel_id=1, source_target_pairs={{0,8},{8,0},{16,24},{24,16},{1,9},{9,1},{17,25},{25,17},{2,10},{10... | collective-permute-start | bytes 3145736 | tf_op jit(solution)/shard_map/ppermute | solution.py:894
  45.7 14.4 %all-to-all-start = ((bf16[32,32,128]{2,1,0:T(8,128)(2,1)}), bf16[32,32,128]{2,1,0:T(8,128)(2,1)S(1)}, u32[]{:S(2)}, u32[]{:S(2)}) async-start(bf16[32,32,128]{2,1,0:T(8,128)(2,1)} %bitcast.13), calls=%async_computation | async-start | bytes 524288 | tf_op jit(solution)/shard_map/all_to_all | solution.py:949
  49.9 13.1 %collective-permute-start.10 = (bf16[64,2048]{1,0:T(8,128)(2,1)}, bf16[64,2048]{1,0:T(8,128)(2,1)}, u32[]{:S(2)}, u32[]{:S(2)}) collective-permute-start(bf16[64,2048]{1,0:T(8,128)(2,1)} %get-tuple-element.78), channel_id=1, source_target_pairs={{0,8},{8,0},{16,24},{24,16},{1,9},{9,1},{17,25},{25,17},{2,10},{10... | collective-permute-start | bytes 786440 | tf_op jit(solution)/shard_map/ppermute | solution.py:894
  50.2 12.8 %collective-permute-start.11 = (bf16[64,2048]{1,0:T(8,128)(2,1)}, bf16[64,2048]{1,0:T(8,128)(2,1)}, u32[]{:S(2)}, u32[]{:S(2)}) collective-permute-start(bf16[64,2048]{1,0:T(8,128)(2,1)} %get-tuple-element.79), channel_id=1, source_target_pairs={{0,16},{8,24},{16,0},{24,8},{1,17},{9,25},{17,1},{25,9},{2,18},{10... | collective-permute-start | bytes 786440 | tf_op jit(solution)/shard_map/ppermute | solution.py:894
  60.8 3.5 %collective-permute-start.14 = (f32[8,480]{1,0:T(8,128)S(1)}, f32[8,480]{1,0:T(8,128)S(1)}, u32[]{:S(2)}, u32[]{:S(2)}) collective-permute-start(f32[8,480]{1,0:T(8,128)S(1)} %get-tuple-element.84.refs_0_), channel_id=1, source_target_pairs={{0,24},{8,16},{16,8},{24,0},{1,25},{9,17},{17,9},{25,1},{2,26},{10... | collective-permute-start | bytes 46088 | tf_op jit(solution)/shard_map/ppermute | solution.py:894
  61.3 3.0 %collective-permute-start.13 = (f32[8,480]{1,0:T(8,128)S(1)}, f32[8,480]{1,0:T(8,128)S(1)}, u32[]{:S(2)}, u32[]{:S(2)}) collective-permute-start(f32[8,480]{1,0:T(8,128)S(1)} %get-tuple-element.84.refs_0_), channel_id=1, source_target_pairs={{0,16},{8,24},{16,0},{24,8},{1,17},{9,25},{17,1},{25,9},{2,18},{10... | collective-permute-start | bytes 46088 | tf_op jit(solution)/shard_map/ppermute | solution.py:894
  62.9 1.5 %collective-permute-start.12 = (f32[8,480]{1,0:T(8,128)S(1)}, f32[8,480]{1,0:T(8,128)S(1)}, u32[]{:S(2)}, u32[]{:S(2)}) collective-permute-start(f32[8,480]{1,0:T(8,128)S(1)} %get-tuple-element.84.refs_0_), channel_id=1, source_target_pairs={{0,8},{8,0},{16,24},{24,16},{1,9},{9,1},{17,25},{25,17},{2,10},{10... | collective-permute-start | bytes 46088 | tf_op jit(solution)/shard_map/ppermute | solution.py:894
  65.8 14.7 %all-to-all-start.2 = ((bf16[32,32,128]{2,1,0:T(8,128)(2,1)}), bf16[32,32,128]{2,1,0:T(8,128)(2,1)S(1)}, u32[]{:S(2)}, u32[]{:S(2)}) async-start(bf16[32,32,128]{2,1,0:T(8,128)(2,1)} %bitcast.12), calls=%async_computation.2 | async-start | bytes 524288 | tf_op jit(solution)/shard_map/all_to_all | solution.py:949
  69.3 11.2 %collective-permute-start.18 = (bf16[64,2048]{1,0:T(8,128)(2,1)}, bf16[64,2048]{1,0:T(8,128)(2,1)S(1)}, u32[]{:S(2)}, u32[]{:S(2)}) collective-permute-start(bf16[64,2048]{1,0:T(8,128)(2,1)} %get-tuple-element.87), channel_id=1, source_target_pairs={{0,24},{8,16},{16,8},{24,0},{1,25},{9,17},{17,9},{25,1},{2,26},{10... | collective-permute-start | bytes 786440 | tf_op jit(solution)/shard_map/ppermute | solution.py:894
  71.0 2.8 %collective-permute-start.15 = (f32[8,128]{1,0:T(8,128)S(1)}, f32[8,128]{1,0:T(8,128)S(1)}, u32[]{:S(2)}, u32[]{:S(2)}) collective-permute-start(f32[8,128]{1,0:T(8,128)S(1)} %get-tuple-element.86), channel_id=1, source_target_pairs={{0,1},{1,0},{2,3},{3,2},{4,5},{5,4},{6,7},{7,6},{8,9},{9,8},{10,11... | collective-permute-start | bytes 12296 | tf_op jit(solution)/shard_map/ppermute | solution.py:966
  73.8 2.8 %collective-permute-start.16 = (f32[8,128]{1,0:T(8,128)S(1)}, f32[8,128]{1,0:T(8,128)S(1)}, u32[]{:S(2)}, u32[]{:S(2)}) collective-permute-start(f32[8,128]{1,0:T(8,128)S(1)} %add.19), channel_id=1, source_target_pairs={{0,2},{1,3},{2,0},{3,1},{4,6},{5,7},{6,4},{7,5},{8,10},{9,11},{10,... | collective-permute-start | bytes 12296 | tf_op jit(solution)/shard_map/ppermute | solution.py:966
  76.6 3.4 %collective-permute-start.17 = (f32[8,128]{1,0:T(8,128)S(1)}, f32[8,128]{1,0:T(8,128)S(1)}, u32[]{:S(2)}, u32[]{:S(2)}) collective-permute-start(f32[8,128]{1,0:T(8,128)S(1)} %add.20), channel_id=1, source_target_pairs={{0,4},{1,5},{2,6},{3,7},{4,0},{5,1},{6,2},{7,3},{8,12},{9,13},{10,... | collective-permute-start | bytes 12296 | tf_op jit(solution)/shard_map/ppermute | solution.py:966
  86.1 10.2 %collective-permute-start.19 = (bf16[32,2304]{1,0:T(8,128)(2,1)S(1)}, bf16[32,2304]{1,0:T(8,128)(2,1)S(1)}, u32[]{:S(2)}, u32[]{:S(2)}) collective-permute-start(bf16[32,2304]{1,0:T(8,128)(2,1)S(1)} %get-tuple-element.97), channel_id=1, source_target_pairs={{0,8},{8,0},{16,24},{24,16},{1,9},{9,1},{17,25},{25,17},{2,10},{10... | collective-permute-start | bytes 442376 | tf_op jit(solution)/shard_map/ppermute | solution.py:894
  88.7 9.6 %collective-permute-start.20 = (bf16[32,2304]{1,0:T(8,128)(2,1)S(1)}, bf16[32,2304]{1,0:T(8,128)(2,1)S(1)}, u32[]{:S(2)}, u32[]{:S(2)}) collective-permute-start(bf16[32,2304]{1,0:T(8,128)(2,1)S(1)} %get-tuple-element.98), channel_id=1, source_target_pairs={{0,16},{8,24},{16,0},{24,8},{1,17},{9,25},{17,1},{25,9},{2,18},{10... | collective-permute-start | bytes 442376 | tf_op jit(solution)/shard_map/ppermute | solution.py:894
  88.8 9.5 %collective-permute-start.21 = (bf16[32,2304]{1,0:T(8,128)(2,1)S(1)}, bf16[32,2304]{1,0:T(8,128)(2,1)S(1)}, u32[]{:S(2)}, u32[]{:S(2)}) collective-permute-start(bf16[32,2304]{1,0:T(8,128)(2,1)S(1)} %get-tuple-element.99), channel_id=1, source_target_pairs={{0,24},{8,16},{16,8},{24,0},{1,25},{9,17},{17,9},{25,1},{2,26},{10... | collective-permute-start | bytes 442376 | tf_op jit(solution)/shard_map/ppermute | solution.py:894
  90.4 7.8 %copy-start.1 = (bf16[256,128]{1,0:T(8,128)(2,1)S(1)}, bf16[256,128]{1,0:T(8,128)(2,1)}, u32[]{:S(2)}) copy-start(bf16[256,128]{1,0:T(8,128)(2,1)} %constant.45.clone.refs_15_.spread_ref.refs_14_) | copy-start | bytes 196612
  90.4 7.9 %copy-start.5 = (bf16[64,2048]{1,0:T(8,128)(2,1)S(1)}, bf16[64,2048]{1,0:T(8,128)(2,1)}, u32[]{:S(2)}) copy-start(bf16[64,2048]{1,0:T(8,128)(2,1)} %get-tuple-element.80.refs_0_) | copy-start | bytes 786436
  96.1 6.4 %collective-permute-start.22 = (bf16[32,2048]{1,0:T(8,128)(2,1)S(1)}, bf16[32,2048]{1,0:T(8,128)(2,1)S(1)}, u32[]{:S(2)}, u32[]{:S(2)}) collective-permute-start(bf16[32,2048]{1,0:T(8,128)(2,1)S(1)} %get-tuple-element.108), channel_id=1, source_target_pairs={{0,8},{8,0},{16,24},{24,16},{1,9},{9,1},{17,25},{25,17},{2,10},{10... | collective-permute-start | bytes 393224 | tf_op jit(solution)/shard_map/ppermute | solution.py:894
  96.3 6.2 %collective-permute-start.23 = (bf16[32,2048]{1,0:T(8,128)(2,1)S(1)}, bf16[32,2048]{1,0:T(8,128)(2,1)S(1)}, u32[]{:S(2)}, u32[]{:S(2)}) collective-permute-start(bf16[32,2048]{1,0:T(8,128)(2,1)S(1)} %get-tuple-element.109), channel_id=1, source_target_pairs={{0,16},{8,24},{16,0},{24,8},{1,17},{9,25},{17,1},{25,9},{2,18},{10... | collective-permute-start | bytes 393224 | tf_op jit(solution)/shard_map/ppermute | solution.py:894
  96.3 8.0 %collective-permute-start.24 = (bf16[32,2048]{1,0:T(8,128)(2,1)S(1)}, bf16[32,2048]{1,0:T(8,128)(2,1)S(1)}, u32[]{:S(2)}, u32[]{:S(2)}) collective-permute-start(bf16[32,2048]{1,0:T(8,128)(2,1)S(1)} %get-tuple-element.110), channel_id=1, source_target_pairs={{0,24},{8,16},{16,8},{24,0},{1,25},{9,17},{17,9},{25,1},{2,26},{10... | collective-permute-start | bytes 393224 | tf_op jit(solution)/shard_map/ppermute | solution.py:894
  (10 other events, 25.8 us)

commit v9 on v7

--- a/solution.py
+++ b/solution.py
@@ -21,7 +21,7 @@
 
 VMEM_LIMIT = 20 * 1024 * 1024
 CHUNKS = 2
-SPECTRA = 4
+SPECTRA = 1
 MOST_GROUPS = 16
 
 

time: 108 us -> 108 us (level)
  transfers between devices with their start and end apart: 28 -> 28, of which waited for: 9 -> 9; matrix products, arithmetic and copies ran while one was open for 1% -> 1% of each run, Pallas kernels for 32% -> 31%
where the time goes in v9:
time: 108 us; the launch traced here: 107 us
  Pallas kernels  45.3 us (42%)
  starting transfers between devices  39.1 us (36%)
  waiting for transfers between devices  18.4 us (17%)
  local copies, waits for them, and re-layouts  3.2 us (3%)
    pallas_call x13, Pallas kernels, call(): pl.pallas_call(kernel, name=name, grid_spec=pltpu.PrefetchScalarGridSpec(...  45.3 us
    ppermute x22, starting transfers between devices, swap(): return lax.ppermute(value, 'seq', [(i, i ^ k) for i in range(count)])  21.8 us
    all_to_all x2, waiting for transfers between devices, exchange(): lax.all_to_all(flat, ('chan', 'seq'), split_axis=0, concat_axis=0, tiled=...  7.58 us
    all_to_all x2, starting transfers between devices, exchange(): lax.all_to_all(flat, ('chan', 'seq'), split_axis=0, concat_axis=0, tiled=...  6.85 us
    all_to_all x1, starting transfers between devices, aligned(): mine = lax.all_to_all(mine, 'chan', split_axis=0, concat_axis=0, tiled=True)  5.7 us
    ppermute x22, waiting for transfers between devices, swap(): return lax.ppermute(value, 'seq', [(i, i ^ k) for i in range(count)])  5.32 us
    ppermute x3, starting transfers between devices, aligned(): lax.ppermute(loss, 'chan', [(i, i ^ step) for i in range(groups)])  4.81 us
    ppermute x3, waiting for transfers between devices, aligned(): lax.ppermute(loss, 'chan', [(i, i ^ step) for i in range(groups)])  4.11 us
  transfers between devices with their start and end apart: 28, of which 9 were waited for; matrix products, arithmetic and copies ran while one was open for 1% of the time, Pallas kernels for 31%

profile of v9, /device:TPU:1, one launch (start us, length us, event | category | flops | bytes accessed | tf_op | source)
XLA Modules:
  0.0 107.1 jit_solution(13291939701186664096)
XLA Ops:
  0.7 2.1 %lay_out.2 = (bf16[2,32,2048]{2,1,0:T(8,128)(2,1)}, bf16[2,32,2048]{2,1,0:T(8,128)(2,1)}) custom-call(s32[1]{0:T(128)} %bitcast.me_ref.refs_0_, bf16[3,256,2048]{2,1,0:T(8,128)(2,1)} %proj_ref.7, f32[256,2048]{1,0:T(8,128)} %taps_ref.3), custom_call_target="tpu_custom_call" | custom-call | flops 960000000 | bytes 5767168 | tf_op jit(solution)/shard_map/lay_out/pallas_call | solution.py:424
  2.8 2.1 %collective-permute-start.1 = (bf16[2,32,2048]{2,1,0:T(8,128)(2,1)}, bf16[2,32,2048]{2,1,0:T(8,128)(2,1)S(1)}, u32[]{:S(2)}, u32[]{:S(2)}) collective-permute-start(bf16[2,32,2048]{2,1,0:T(8,128)(2,1)} %get-tuple-element.54), channel_id=1, source_target_pairs={{0,16},{8,24},{16,0},{24,8},{1,17},{9,25},{17,1},{25,9},{2,18},{10... | collective-permute-start | bytes 786440 | tf_op jit(solution)/shard_map/ppermute | solution.py:894
  5.5 3.6 %lay_out.3 = (bf16[2,32,2048]{2,1,0:T(8,128)(2,1)}, bf16[2,32,2048]{2,1,0:T(8,128)(2,1)}, bf16[2,32,2048]{2,1,0:T(8,128)(2,1)}, bf16[2,32,2048]{2,1,0:T(8,128)(2...) custom-call(s32[1]{0:T(128)} %bitcast.me_ref.refs_0_, ...), custom_call_target="tpu_custom_call" | custom-call | flops 2880000000 | bytes 7864320 | tf_op jit(solution)/shard_map/lay_out/pallas_call | solution.py:424
  9.7 1.7 %collective-permute-start.7 = (bf16[2,32,2048]{2,1,0:T(8,128)(2,1)}, bf16[2,32,2048]{2,1,0:T(8,128)(2,1)}, u32[]{:S(2)}, u32[]{:S(2)}) collective-permute-start(bf16[2,32,2048]{2,1,0:T(8,128)(2,1)} %get-tuple-element.69), channel_id=1, source_target_pairs={{0,16},{8,24},{16,0},{24,8},{1,17},{9,25},{17,1},{25,9},{2,18},{10... | collective-permute-start | bytes 786440 | tf_op jit(solution)/shard_map/ppermute | solution.py:894
  11.4 2.7 %by_track.1 = bf16[8,128,512]{2,1,0:T(8,128)(2,1)} custom-call(s32[1]{0:T(128)} %bitcast.me_ref.refs_0_, bf16[256,3840]{1,0:T(8,128)(2,1)} %weight_ref.1), custom_call_target="tpu_custom_call" | custom-call | flops 2000000000 | bytes 3014656 | tf_op jit(solution)/shard_map/by_track/pallas_call | solution.py:424
  14.1 5.7 %all-to-all-start.1 = ((bf16[8,128,512]{2,1,0:T(8,128)(2,1)}), bf16[8,128,512]{2,1,0:T(8,128)(2,1)S(1)}, u32[]{:S(2)}, u32[]{:S(2)}) async-start(bf16[8,128,512]{2,1,0:T(8,128)(2,1)} %by_track.1), calls=%async_computation.1 | async-start | bytes 2097152 | tf_op jit(solution)/shard_map/all_to_all | solution.py:937
  22.9 7.0 %long_convolution.2 = (f32[64,8192]{1,0:T(8,128)S(1)}, f32[2,1024,256]{2,1,0:T(8,128)}) custom-call(s32[1]{0:T(128)} %bitcast.me_ref.refs_0_, bf16[2,32,2048]{2,1,0:T(8,128)(2,1)} %get-tuple-element.61.refs_1_, bf16[2,32,2048]{2,1,0:T(8,128)(2,1)} %collective-permute-done.refs_2_, bf16[2,32,2048]{2,1,0:T(8,128)(2,1)} %copy-done.11, ...), custom_call_target="tpu_custom_call" | custom-call | flops 8192000000 | bytes 5832960 | tf_op jit(solution)/shard_map/long_convolution/pallas_call | solution.py:424
  31.6 7.0 %long_convolution.3 = (f32[64,8192]{1,0:T(8,128)S(1)}, f32[2,1024,256]{2,1,0:T(8,128)}) custom-call(s32[1]{0:T(128)} %bitcast.me_ref.refs_0_, bf16[2,32,2048]{2,1,0:T(8,128)(2,1)} %get-tuple-element.67.refs_1_, bf16[2,32,2048]{2,1,0:T(8,128)(2,1)} %collective-permute-done.6.refs_2_, ...), custom_call_target="tpu_custom_call", output_to_operand_aliasing={{0}: (11, {})} | custom-call | flops 8192000000 | bytes 7930112 | tf_op jit(solution)/shard_map/long_convolution/pallas_call | solution.py:424
  38.6 1.6 %collective-permute-done.5.refs_4_.refs_5_ = bf16[64,2048]{1,0:T(8,128)(2,1)S(1)} collective-permute-done((bf16[64,2048]{1,0:T(8,128)(2,1)S(1)}, bf16[64,2048]{1,0:T(8,128)(2,1)S(1)}, u32[]{:S(2)}, u32[]{:S(2)}) %collective-permute-start.5) | collective-permute-done | bytes 262176 | tf_op jit(solution)/shard_map/ppermute | solution.py:894
  40.2 2.8 %pool_bins.1 = (bf16[64,2048]{1,0:T(8,128)(2,1)}, bf16[64,2048]{1,0:T(8,128)(2,1)}, bf16[64,2048]{1,0:T(8,128)(2,1)}, bf16[64,2048]{1,0:T(8,128)(2,1)}, bf16[8,4,32,128]{3,2,1,0:T(8,128)(2,1)}) custom-call(s32[1]{0:T(128)} %bitcast.me_ref.refs_0_, bf16[64,2048]{1,0:T(8,128)(2,1)} %get-tuple-element.63.refs_1_.refs_2_, ...), custom_call_target="tpu_custom_call" | custom-call | flops 4096000000 | bytes 4521984 | tf_op jit(solution)/shard_map/pool_bins/pallas_call | solution.py:424
  43.7 1.4 %all-to-all-done.1.mine_ref.refs_4_ = bf16[8,128,512]{2,1,0:T(8,128)(2,1)S(1)} async-done(((bf16[8,128,512]{2,1,0:T(8,128)(2,1)}), bf16[8,128,512]{2,1,0:T(8,128)(2,1)S(1)}, u32[]{:S(2)}, u32[]{:S(2)}) %all-to-all-start.1) | async-done | bytes 1048608 | tf_op jit(solution)/shard_map/all_to_all | solution.py:937
  45.1 1.4 %collective-permute-start.9 = (bf16[8,128,512]{2,1,0:T(8,128)(2,1)S(1)}, bf16[8,128,512]{2,1,0:T(8,128)(2,1)S(1)}, u32[]{:S(2)}, u32[]{:S(2)}) collective-permute-start(bf16[8,128,512]{2,1,0:T(8,128)(2,1)S(1)} %all-to-all-done.1.mine_ref.refs_4_), channel_id=1, source_target_pairs={{0,8},{8,0},{16,24},{24,16},{1,9},{9,1},{17,25},{25,17},{2,10},{10... | collective-permute-start | bytes 3145736 | tf_op jit(solution)/shard_map/ppermute | solution.py:894
  46.5 3.4 %all-to-all-start = ((bf16[32,32,128]{2,1,0:T(8,128)(2,1)}), bf16[32,32,128]{2,1,0:T(8,128)(2,1)S(1)}, u32[]{:S(2)}, u32[]{:S(2)}) async-start(bf16[32,32,128]{2,1,0:T(8,128)(2,1)} %bitcast.13), calls=%async_computation | async-start | bytes 524288 | tf_op jit(solution)/shard_map/all_to_all | solution.py:948
  50.2 1.5 %collective-permute-start.11 = (bf16[64,2048]{1,0:T(8,128)(2,1)}, bf16[64,2048]{1,0:T(8,128)(2,1)}, u32[]{:S(2)}, u32[]{:S(2)}) collective-permute-start(bf16[64,2048]{1,0:T(8,128)(2,1)} %get-tuple-element.79), channel_id=1, source_target_pairs={{0,16},{8,24},{16,0},{24,8},{1,17},{9,25},{17,1},{25,9},{2,18},{10... | collective-permute-start | bytes 786440 | tf_op jit(solution)/shard_map/ppermute | solution.py:894
  52.6 7.6 %all-to-all-done = bf16[32,32,128]{2,1,0:T(8,128)(2,1)S(1)} async-done(((bf16[32,32,128]{2,1,0:T(8,128)(2,1)}), bf16[32,32,128]{2,1,0:T(8,128)(2,1)S(1)}, u32[]{:S(2)}, u32[]{:S(2)}) %all-to-all-start) | async-done | bytes 262176 | tf_op jit(solution)/shard_map/all_to_all | solution.py:948
  61.4 1.5 %collective-permute-start.13 = (f32[8,480]{1,0:T(8,128)S(1)}, f32[8,480]{1,0:T(8,128)S(1)}, u32[]{:S(2)}, u32[]{:S(2)}) collective-permute-start(f32[8,480]{1,0:T(8,128)S(1)} %get-tuple-element.84.refs_0_), channel_id=1, source_target_pairs={{0,16},{8,24},{16,0},{24,8},{1,17},{9,25},{17,1},{25,9},{2,18},{10... | collective-permute-start | bytes 46088 | tf_op jit(solution)/shard_map/ppermute | solution.py:894
  63.1 1.3 %collective-permute-done.14.refs_3_ = f32[8,480]{1,0:T(8,128)S(1)} collective-permute-done((f32[8,480]{1,0:T(8,128)S(1)}, f32[8,480]{1,0:T(8,128)S(1)}, u32[]{:S(2)}, u32[]{:S(2)}) %collective-permute-start.14) | collective-permute-done | bytes 15392 | tf_op jit(solution)/shard_map/ppermute | solution.py:894
  64.4 1.5 %head_grads.1 = (bf16[8,4,32,128]{3,2,1,0:T(8,128)(2,1)}, f32[8,128]{1,0:T(8,128)S(1)}) custom-call(s32[1]{0:T(128)} %bitcast.me_ref.refs_0_, f32[64,480]{1,0:T(8,128)S(1)} %get-tuple-element.83.logits_ref, f32[8,480]{1,0:T(8,128)S(1)} %get-tuple-element.84.refs_0_, f32[8,480]{1,0:T(8,128)S(1)} %collective-permute-done.12.refs_1_, ...), custom_call_target="tpu_custom_call" | custom-call | flops 251658240 | bytes 2670592 | tf_op jit(solution)/shard_map/head_grads/pallas_call | solution.py:424
  65.8 3.5 %all-to-all-start.2 = ((bf16[32,32,128]{2,1,0:T(8,128)(2,1)}), bf16[32,32,128]{2,1,0:T(8,128)(2,1)S(1)}, u32[]{:S(2)}, u32[]{:S(2)}) async-start(bf16[32,32,128]{2,1,0:T(8,128)(2,1)} %bitcast.12), calls=%async_computation.2 | async-start | bytes 524288 | tf_op jit(solution)/shard_map/all_to_all | solution.py:948
  69.3 1.7 %collective-permute-start.18 = (bf16[64,2048]{1,0:T(8,128)(2,1)}, bf16[64,2048]{1,0:T(8,128)(2,1)S(1)}, u32[]{:S(2)}, u32[]{:S(2)}) collective-permute-start(bf16[64,2048]{1,0:T(8,128)(2,1)} %get-tuple-element.87), channel_id=1, source_target_pairs={{0,24},{8,16},{16,8},{24,0},{1,25},{9,17},{17,9},{25,1},{2,26},{10... | collective-permute-start | bytes 786440 | tf_op jit(solution)/shard_map/ppermute | solution.py:894
  72.2 1.5 %collective-permute-done.15 = f32[8,128]{1,0:T(8,128)S(1)} collective-permute-done((f32[8,128]{1,0:T(8,128)S(1)}, f32[8,128]{1,0:T(8,128)S(1)}, u32[]{:S(2)}, u32[]{:S(2)}) %collective-permute-start.15) | collective-permute-done | bytes 4128 | tf_op jit(solution)/shard_map/ppermute | solution.py:965
  73.8 1.2 %collective-permute-start.16 = (f32[8,128]{1,0:T(8,128)S(1)}, f32[8,128]{1,0:T(8,128)S(1)}, u32[]{:S(2)}, u32[]{:S(2)}) collective-permute-start(f32[8,128]{1,0:T(8,128)S(1)} %add.19), channel_id=1, source_target_pairs={{0,2},{1,3},{2,0},{3,1},{4,6},{5,7},{6,4},{7,5},{8,10},{9,11},{10,... | collective-permute-start | bytes 12296 | tf_op jit(solution)/shard_map/ppermute | solution.py:965
  75.0 1.6 %collective-permute-done.16 = f32[8,128]{1,0:T(8,128)S(1)} collective-permute-done((f32[8,128]{1,0:T(8,128)S(1)}, f32[8,128]{1,0:T(8,128)S(1)}, u32[]{:S(2)}, u32[]{:S(2)}) %collective-permute-start.16) | collective-permute-done | bytes 4128 | tf_op jit(solution)/shard_map/ppermute | solution.py:965
  76.6 2.3 %collective-permute-start.17 = (f32[8,128]{1,0:T(8,128)S(1)}, f32[8,128]{1,0:T(8,128)S(1)}, u32[]{:S(2)}, u32[]{:S(2)}) collective-permute-start(f32[8,128]{1,0:T(8,128)S(1)} %add.20), channel_id=1, source_target_pairs={{0,4},{1,5},{2,6},{3,7},{4,0},{5,1},{6,2},{7,3},{8,12},{9,13},{10,... | collective-permute-start | bytes 12296 | tf_op jit(solution)/shard_map/ppermute | solution.py:965
  80.6 5.4 %long_correlation.2 = (bf16[32,2304]{1,0:T(8,128)(2,1)S(1)}, bf16[32,2304]{1,0:T(8,128)(2,1)S(1)}, bf16[32,2304]{1,0:T(8,128)(2,1)S(1)}, bf16[32,2304]{1,0:T(8,128)(2,1)S(1)}) custom-call(s32[1]{0:T(128)} %bitcast.me_ref.refs_0_, f32[4,32,128]{2,1,0:T(8,128)S(1)} %get-tuple-element.90.refs_1_, bf16[64,2048]{1,0:T(8,128)(2,1)} %get-tuple-element.63.refs_1_.refs_2_, ...), custom_call_target="tpu_custom_call" | custom-call | flops 8192000000 | bytes 4260096 | tf_op jit(solution)/shard_map/long_correlation/pallas_call | solution.py:424
  86.0 2.6 %collective-permute-start.19 = (bf16[32,2304]{1,0:T(8,128)(2,1)S(1)}, bf16[32,2304]{1,0:T(8,128)(2,1)S(1)}, u32[]{:S(2)}, u32[]{:S(2)}) collective-permute-start(bf16[32,2304]{1,0:T(8,128)(2,1)S(1)} %get-tuple-element.94), channel_id=1, source_target_pairs={{0,8},{8,0},{16,24},{24,16},{1,9},{9,1},{17,25},{25,17},{2,10},{10... | collective-permute-start | bytes 442376 | tf_op jit(solution)/shard_map/ppermute | solution.py:894
  88.7 1.7 %collective-permute-start.21 = (bf16[32,2304]{1,0:T(8,128)(2,1)S(1)}, bf16[32,2304]{1,0:T(8,128)(2,1)S(1)}, u32[]{:S(2)}, u32[]{:S(2)}) collective-permute-start(bf16[32,2304]{1,0:T(8,128)(2,1)S(1)} %get-tuple-element.96), channel_id=1, source_target_pairs={{0,24},{8,16},{16,8},{24,0},{1,25},{9,17},{17,9},{25,1},{2,26},{10... | collective-permute-start | bytes 442376 | tf_op jit(solution)/shard_map/ppermute | solution.py:894
  90.3 5.6 %long_correlation.3 = (bf16[32,2048]{1,0:T(8,128)(2,1)S(1)}, bf16[32,2048]{1,0:T(8,128)(2,1)S(1)}, bf16[32,2048]{1,0:T(8,128)(2,1)S(1)}, bf16[32,2048]{1,0:T(8,128)(2,1)S(1)}) custom-call(s32[1]{0:T(128)} %bitcast.me_ref.refs_0_, bf16[64,2048]{1,0:T(8,128)(2,1)} %get-tuple-element.63.refs_1_.refs_2_, bf16[64,2048]{1,0:T(8,128)(2,1)} %copy-done.2, ...), custom_call_target="tpu_custom_call" | custom-call | flops 8192000000 | bytes 4129024 | tf_op jit(solution)/shard_map/long_correlation/pallas_call | solution.py:424
  96.2 1.9 %collective-permute-start.24 = (bf16[32,2048]{1,0:T(8,128)(2,1)S(1)}, bf16[32,2048]{1,0:T(8,128)(2,1)S(1)}, u32[]{:S(2)}, u32[]{:S(2)}) collective-permute-start(bf16[32,2048]{1,0:T(8,128)(2,1)S(1)} %get-tuple-element.104), channel_id=1, source_target_pairs={{0,24},{8,16},{16,8},{24,0},{1,25},{9,17},{17,9},{25,1},{2,26},{10... | collective-permute-start | bytes 393224 | tf_op jit(solution)/shard_map/ppermute | solution.py:894
  98.1 4.2 %finish.2 = (f32[3,256,2048]{2,1,0:T(8,128)}, f32[1,1]{1,0:T(1,128)}) custom-call(s32[1]{0:T(128)} %bitcast.me_ref.refs_0_, bf16[256,128]{1,0:T(8,128)(2,1)S(1)} %copy-done.1, bf16[3,256,2048]{2,1,0:T(8,128)(2,1)} %proj_ref.7, bf16[64,2048]{1,0:T(8,128)(2,1)S(1)} %copy-done.5, bf16[64,2048]{1,0:T(8,128)(2,1)} %collective-permute-done.10.refs_1_, ...), custom_call_target="tpu_custom_call" | custom-call | flops 3840000000 | bytes 11145220 | tf_op jit(solution)/shard_map/finish/pallas_call | solution.py:424
  102.3 1.8 %collective-permute-done.24.refs_3_ = bf16[32,2048]{1,0:T(8,128)(2,1)S(1)} collective-permute-done((bf16[32,2048]{1,0:T(8,128)(2,1)S(1)}, bf16[32,2048]{1,0:T(8,128)(2,1)S(1)}, u32[]{:S(2)}, u32[]{:S(2)}) %collective-permute-start.24) | collective-permute-done | bytes 131104 | tf_op jit(solution)/shard_map/ppermute | solution.py:894
  104.2 2.7 %finish.3 = f32[3,256,2048]{2,1,0:T(8,128)} custom-call(s32[1]{0:T(128)} %bitcast.me_ref.refs_0_, bf16[256,128]{1,0:T(8,128)(2,1)S(1)} %copy-done.1, bf16[3,256,2048]{2,1,0:T(8,128)(2,1)} %proj_ref.7, bf16[32,2048]{1,0:T(8,128)(2,1)S(1)} %get-tuple-element.101.refs_0_, ...), custom_call_target="tpu_custom_call", output_to_operand_aliasing={{}: (7, {})} | custom-call | flops 3840000000 | bytes 16318464 | tf_op jit(solution)/shard_map/finish/pallas_call | solution.py:424
  (73 shorter events, 12.4 us)
Async XLA Ops:
  0.6 51.9 %copy-start = (s32[64,3840]{1,0:T(8,128)S(1)}, s32[64,3840]{1,0:T(8,128)}, u32[]{:S(2)}) copy-start(s32[64,3840]{1,0:T(8,128)} %param.20) | copy-start | bytes 2949124
  2.8 17.2 %collective-permute-start.1 = (bf16[2,32,2048]{2,1,0:T(8,128)(2,1)}, bf16[2,32,2048]{2,1,0:T(8,128)(2,1)S(1)}, u32[]{:S(2)}, u32[]{:S(2)}) collective-permute-start(bf16[2,32,2048]{2,1,0:T(8,128)(2,1)} %get-tuple-element.54), channel_id=1, source_target_pairs={{0,16},{8,24},{16,0},{24,8},{1,17},{9,25},{17,1},{25,9},{2,18},{10... | collective-permute-start | bytes 786440 | tf_op jit(solution)/shard_map/ppermute | solution.py:894
  4.9 16.0 %collective-permute-start.2 = (bf16[2,32,2048]{2,1,0:T(8,128)(2,1)}, bf16[2,32,2048]{2,1,0:T(8,128)(2,1)S(1)}, u32[]{:S(2)}, u32[]{:S(2)}) collective-permute-start(bf16[2,32,2048]{2,1,0:T(8,128)(2,1)} %get-tuple-element.55), channel_id=1, source_target_pairs={{0,24},{8,16},{16,8},{24,0},{1,25},{9,17},{17,9},{25,1},{2,26},{10... | collective-permute-start | bytes 786440 | tf_op jit(solution)/shard_map/ppermute | solution.py:894
  9.2 11.7 %collective-permute-start = (bf16[2,32,2048]{2,1,0:T(8,128)(2,1)}, bf16[2,32,2048]{2,1,0:T(8,128)(2,1)}, u32[]{:S(2)}, u32[]{:S(2)}) collective-permute-start(bf16[2,32,2048]{2,1,0:T(8,128)(2,1)} %get-tuple-element.62), channel_id=1, source_target_pairs={{0,8},{8,0},{16,24},{24,16},{1,9},{9,1},{17,25},{25,17},{2,10},{10... | collective-permute-start | bytes 786440 | tf_op jit(solution)/shard_map/ppermute | solution.py:894
  9.5 20.3 %collective-permute-start.6 = (bf16[2,32,2048]{2,1,0:T(8,128)(2,1)}, bf16[2,32,2048]{2,1,0:T(8,128)(2,1)}, u32[]{:S(2)}, u32[]{:S(2)}) collective-permute-start(bf16[2,32,2048]{2,1,0:T(8,128)(2,1)} %get-tuple-element.68), channel_id=1, source_target_pairs={{0,8},{8,0},{16,24},{24,16},{1,9},{9,1},{17,25},{25,17},{2,10},{10... | collective-permute-start | bytes 786440 | tf_op jit(solution)/shard_map/ppermute | solution.py:894
  9.7 21.1 %collective-permute-start.7 = (bf16[2,32,2048]{2,1,0:T(8,128)(2,1)}, bf16[2,32,2048]{2,1,0:T(8,128)(2,1)}, u32[]{:S(2)}, u32[]{:S(2)}) collective-permute-start(bf16[2,32,2048]{2,1,0:T(8,128)(2,1)} %get-tuple-element.69), channel_id=1, source_target_pairs={{0,16},{8,24},{16,0},{24,8},{1,17},{9,25},{17,1},{25,9},{2,18},{10... | collective-permute-start | bytes 786440 | tf_op jit(solution)/shard_map/ppermute | solution.py:894
  14.1 8.0 %copy-start.8 = (bf16[64,2048]{1,0:T(8,128)(2,1)S(1)}, bf16[64,2048]{1,0:T(8,128)(2,1)}, u32[]{:S(2)}) copy-start(bf16[64,2048]{1,0:T(8,128)(2,1)} %get-tuple-element.65) | copy-start | bytes 786436
  14.1 31.0 %all-to-all-start.1 = ((bf16[8,128,512]{2,1,0:T(8,128)(2,1)}), bf16[8,128,512]{2,1,0:T(8,128)(2,1)S(1)}, u32[]{:S(2)}, u32[]{:S(2)}) async-start(bf16[8,128,512]{2,1,0:T(8,128)(2,1)} %by_track.1), calls=%async_computation.1 | async-start | bytes 2097152 | tf_op jit(solution)/shard_map/all_to_all | solution.py:937
  20.0 9.9 %copy-start.7 = (bf16[64,2048]{1,0:T(8,128)(2,1)S(1)}, bf16[64,2048]{1,0:T(8,128)(2,1)}, u32[]{:S(2)}) copy-start(bf16[64,2048]{1,0:T(8,128)(2,1)} %get-tuple-element.66) | copy-start | bytes 786436
  20.0 10.8 %collective-permute-start.8 = (bf16[2,32,2048]{2,1,0:T(8,128)(2,1)S(1)}, bf16[2,32,2048]{2,1,0:T(8,128)(2,1)S(1)}, u32[]{:S(2)}, u32[]{:S(2)}) collective-permute-start(bf16[2,32,2048]{2,1,0:T(8,128)(2,1)S(1)} %copy-done.10), channel_id=1, source_target_pairs={{0,24},{8,16},{16,8},{24,0},{1,25},{9,17},{17,9},{25,1},{2,26},{10... | collective-permute-start | bytes 786440 | tf_op jit(solution)/shard_map/ppermute | solution.py:894
  21.6 17.0 %collective-permute-start.3 = (bf16[64,2048]{1,0:T(8,128)(2,1)S(1)}, bf16[64,2048]{1,0:T(8,128)(2,1)S(1)}, u32[]{:S(2)}, u32[]{:S(2)}) collective-permute-start(bf16[64,2048]{1,0:T(8,128)(2,1)S(1)} %copy-done.9), channel_id=1, source_target_pairs={{0,8},{8,0},{16,24},{24,16},{1,9},{9,1},{17,25},{25,17},{2,10},{10... | collective-permute-start | bytes 786440 | tf_op jit(solution)/shard_map/ppermute | solution.py:894
  22.1 16.5 %collective-permute-start.4 = (bf16[64,2048]{1,0:T(8,128)(2,1)S(1)}, bf16[64,2048]{1,0:T(8,128)(2,1)S(1)}, u32[]{:S(2)}, u32[]{:S(2)}) collective-permute-start(bf16[64,2048]{1,0:T(8,128)(2,1)S(1)} %copy-done.8), channel_id=1, source_target_pairs={{0,16},{8,24},{16,0},{24,8},{1,17},{9,25},{17,1},{25,9},{2,18},{10... | collective-permute-start | bytes 786440 | tf_op jit(solution)/shard_map/ppermute | solution.py:894
  29.9 10.3 %collective-permute-start.5 = (bf16[64,2048]{1,0:T(8,128)(2,1)S(1)}, bf16[64,2048]{1,0:T(8,128)(2,1)S(1)}, u32[]{:S(2)}, u32[]{:S(2)}) collective-permute-start(bf16[64,2048]{1,0:T(8,128)(2,1)S(1)} %copy-done.7), channel_id=1, source_target_pairs={{0,24},{8,16},{16,8},{24,0},{1,25},{9,17},{17,9},{25,1},{2,26},{10... | collective-permute-start | bytes 786440 | tf_op jit(solution)/shard_map/ppermute | solution.py:894
  45.1 15.1 %collective-permute-start.9 = (bf16[8,128,512]{2,1,0:T(8,128)(2,1)S(1)}, bf16[8,128,512]{2,1,0:T(8,128)(2,1)S(1)}, u32[]{:S(2)}, u32[]{:S(2)}) collective-permute-start(bf16[8,128,512]{2,1,0:T(8,128)(2,1)S(1)} %all-to-all-done.1.mine_ref.refs_4_), channel_id=1, source_target_pairs={{0,8},{8,0},{16,24},{24,16},{1,9},{9,1},{17,25},{25,17},{2,10},{10... | collective-permute-start | bytes 3145736 | tf_op jit(solution)/shard_map/ppermute | solution.py:894
  46.5 13.6 %all-to-all-start = ((bf16[32,32,128]{2,1,0:T(8,128)(2,1)}), bf16[32,32,128]{2,1,0:T(8,128)(2,1)S(1)}, u32[]{:S(2)}, u32[]{:S(2)}) async-start(bf16[32,32,128]{2,1,0:T(8,128)(2,1)} %bitcast.13), calls=%async_computation | async-start | bytes 524288 | tf_op jit(solution)/shard_map/all_to_all | solution.py:948
  49.9 13.1 %collective-permute-start.10 = (bf16[64,2048]{1,0:T(8,128)(2,1)}, bf16[64,2048]{1,0:T(8,128)(2,1)}, u32[]{:S(2)}, u32[]{:S(2)}) collective-permute-start(bf16[64,2048]{1,0:T(8,128)(2,1)} %get-tuple-element.78), channel_id=1, source_target_pairs={{0,8},{8,0},{16,24},{24,16},{1,9},{9,1},{17,25},{25,17},{2,10},{10... | collective-permute-start | bytes 786440 | tf_op jit(solution)/shard_map/ppermute | solution.py:894
  50.2 12.8 %collective-permute-start.11 = (bf16[64,2048]{1,0:T(8,128)(2,1)}, bf16[64,2048]{1,0:T(8,128)(2,1)}, u32[]{:S(2)}, u32[]{:S(2)}) collective-permute-start(bf16[64,2048]{1,0:T(8,128)(2,1)} %get-tuple-element.79), channel_id=1, source_target_pairs={{0,16},{8,24},{16,0},{24,8},{1,17},{9,25},{17,1},{25,9},{2,18},{10... | collective-permute-start | bytes 786440 | tf_op jit(solution)/shard_map/ppermute | solution.py:894
  60.8 3.5 %collective-permute-start.14 = (f32[8,480]{1,0:T(8,128)S(1)}, f32[8,480]{1,0:T(8,128)S(1)}, u32[]{:S(2)}, u32[]{:S(2)}) collective-permute-start(f32[8,480]{1,0:T(8,128)S(1)} %get-tuple-element.84.refs_0_), channel_id=1, source_target_pairs={{0,24},{8,16},{16,8},{24,0},{1,25},{9,17},{17,9},{25,1},{2,26},{10... | collective-permute-start | bytes 46088 | tf_op jit(solution)/shard_map/ppermute | solution.py:894
  61.4 3.0 %collective-permute-start.13 = (f32[8,480]{1,0:T(8,128)S(1)}, f32[8,480]{1,0:T(8,128)S(1)}, u32[]{:S(2)}, u32[]{:S(2)}) collective-permute-start(f32[8,480]{1,0:T(8,128)S(1)} %get-tuple-element.84.refs_0_), channel_id=1, source_target_pairs={{0,16},{8,24},{16,0},{24,8},{1,17},{9,25},{17,1},{25,9},{2,18},{10... | collective-permute-start | bytes 46088 | tf_op jit(solution)/shard_map/ppermute | solution.py:894
  62.9 1.5 %collective-permute-start.12 = (f32[8,480]{1,0:T(8,128)S(1)}, f32[8,480]{1,0:T(8,128)S(1)}, u32[]{:S(2)}, u32[]{:S(2)}) collective-permute-start(f32[8,480]{1,0:T(8,128)S(1)} %get-tuple-element.84.refs_0_), channel_id=1, source_target_pairs={{0,8},{8,0},{16,24},{24,16},{1,9},{9,1},{17,25},{25,17},{2,10},{10... | collective-permute-start | bytes 46088 | tf_op jit(solution)/shard_map/ppermute | solution.py:894
  65.8 14.7 %all-to-all-start.2 = ((bf16[32,32,128]{2,1,0:T(8,128)(2,1)}), bf16[32,32,128]{2,1,0:T(8,128)(2,1)S(1)}, u32[]{:S(2)}, u32[]{:S(2)}) async-start(bf16[32,32,128]{2,1,0:T(8,128)(2,1)} %bitcast.12), calls=%async_computation.2 | async-start | bytes 524288 | tf_op jit(solution)/shard_map/all_to_all | solution.py:948
  69.3 11.2 %collective-permute-start.18 = (bf16[64,2048]{1,0:T(8,128)(2,1)}, bf16[64,2048]{1,0:T(8,128)(2,1)S(1)}, u32[]{:S(2)}, u32[]{:S(2)}) collective-permute-start(bf16[64,2048]{1,0:T(8,128)(2,1)} %get-tuple-element.87), channel_id=1, source_target_pairs={{0,24},{8,16},{16,8},{24,0},{1,25},{9,17},{17,9},{25,1},{2,26},{10... | collective-permute-start | bytes 786440 | tf_op jit(solution)/shard_map/ppermute | solution.py:894
  71.0 2.8 %collective-permute-start.15 = (f32[8,128]{1,0:T(8,128)S(1)}, f32[8,128]{1,0:T(8,128)S(1)}, u32[]{:S(2)}, u32[]{:S(2)}) collective-permute-start(f32[8,128]{1,0:T(8,128)S(1)} %get-tuple-element.86), channel_id=1, source_target_pairs={{0,1},{1,0},{2,3},{3,2},{4,5},{5,4},{6,7},{7,6},{8,9},{9,8},{10,11... | collective-permute-start | bytes 12296 | tf_op jit(solution)/shard_map/ppermute | solution.py:965
  73.8 2.8 %collective-permute-start.16 = (f32[8,128]{1,0:T(8,128)S(1)}, f32[8,128]{1,0:T(8,128)S(1)}, u32[]{:S(2)}, u32[]{:S(2)}) collective-permute-start(f32[8,128]{1,0:T(8,128)S(1)} %add.19), channel_id=1, source_target_pairs={{0,2},{1,3},{2,0},{3,1},{4,6},{5,7},{6,4},{7,5},{8,10},{9,11},{10,... | collective-permute-start | bytes 12296 | tf_op jit(solution)/shard_map/ppermute | solution.py:965
  76.6 3.4 %collective-permute-start.17 = (f32[8,128]{1,0:T(8,128)S(1)}, f32[8,128]{1,0:T(8,128)S(1)}, u32[]{:S(2)}, u32[]{:S(2)}) collective-permute-start(f32[8,128]{1,0:T(8,128)S(1)} %add.20), channel_id=1, source_target_pairs={{0,4},{1,5},{2,6},{3,7},{4,0},{5,1},{6,2},{7,3},{8,12},{9,13},{10,... | collective-permute-start | bytes 12296 | tf_op jit(solution)/shard_map/ppermute | solution.py:965
  86.0 10.2 %collective-permute-start.19 = (bf16[32,2304]{1,0:T(8,128)(2,1)S(1)}, bf16[32,2304]{1,0:T(8,128)(2,1)S(1)}, u32[]{:S(2)}, u32[]{:S(2)}) collective-permute-start(bf16[32,2304]{1,0:T(8,128)(2,1)S(1)} %get-tuple-element.94), channel_id=1, source_target_pairs={{0,8},{8,0},{16,24},{24,16},{1,9},{9,1},{17,25},{25,17},{2,10},{10... | collective-permute-start | bytes 442376 | tf_op jit(solution)/shard_map/ppermute | solution.py:894
  88.6 9.5 %collective-permute-start.20 = (bf16[32,2304]{1,0:T(8,128)(2,1)S(1)}, bf16[32,2304]{1,0:T(8,128)(2,1)S(1)}, u32[]{:S(2)}, u32[]{:S(2)}) collective-permute-start(bf16[32,2304]{1,0:T(8,128)(2,1)S(1)} %get-tuple-element.95), channel_id=1, source_target_pairs={{0,16},{8,24},{16,0},{24,8},{1,17},{9,25},{17,1},{25,9},{2,18},{10... | collective-permute-start | bytes 442376 | tf_op jit(solution)/shard_map/ppermute | solution.py:894
  88.7 9.5 %collective-permute-start.21 = (bf16[32,2304]{1,0:T(8,128)(2,1)S(1)}, bf16[32,2304]{1,0:T(8,128)(2,1)S(1)}, u32[]{:S(2)}, u32[]{:S(2)}) collective-permute-start(bf16[32,2304]{1,0:T(8,128)(2,1)S(1)} %get-tuple-element.96), channel_id=1, source_target_pairs={{0,24},{8,16},{16,8},{24,0},{1,25},{9,17},{17,9},{25,1},{2,26},{10... | collective-permute-start | bytes 442376 | tf_op jit(solution)/shard_map/ppermute | solution.py:894
  90.3 7.8 %copy-start.5 = (bf16[64,2048]{1,0:T(8,128)(2,1)S(1)}, bf16[64,2048]{1,0:T(8,128)(2,1)}, u32[]{:S(2)}) copy-start(bf16[64,2048]{1,0:T(8,128)(2,1)} %get-tuple-element.80.refs_0_) | copy-start | bytes 786436
  95.9 6.4 %collective-permute-start.22 = (bf16[32,2048]{1,0:T(8,128)(2,1)S(1)}, bf16[32,2048]{1,0:T(8,128)(2,1)S(1)}, u32[]{:S(2)}, u32[]{:S(2)}) collective-permute-start(bf16[32,2048]{1,0:T(8,128)(2,1)S(1)} %get-tuple-element.102), channel_id=1, source_target_pairs={{0,8},{8,0},{16,24},{24,16},{1,9},{9,1},{17,25},{25,17},{2,10},{10... | collective-permute-start | bytes 393224 | tf_op jit(solution)/shard_map/ppermute | solution.py:894
  96.1 6.2 %collective-permute-start.23 = (bf16[32,2048]{1,0:T(8,128)(2,1)S(1)}, bf16[32,2048]{1,0:T(8,128)(2,1)S(1)}, u32[]{:S(2)}, u32[]{:S(2)}) collective-permute-start(bf16[32,2048]{1,0:T(8,128)(2,1)S(1)} %get-tuple-element.103), channel_id=1, source_target_pairs={{0,16},{8,24},{16,0},{24,8},{1,17},{9,25},{17,1},{25,9},{2,18},{10... | collective-permute-start | bytes 393224 | tf_op jit(solution)/shard_map/ppermute | solution.py:894
  96.2 8.0 %collective-permute-start.24 = (bf16[32,2048]{1,0:T(8,128)(2,1)S(1)}, bf16[32,2048]{1,0:T(8,128)(2,1)S(1)}, u32[]{:S(2)}, u32[]{:S(2)}) collective-permute-start(bf16[32,2048]{1,0:T(8,128)(2,1)S(1)} %get-tuple-element.104), channel_id=1, source_target_pairs={{0,24},{8,16},{16,8},{24,0},{1,25},{9,17},{17,9},{25,1},{2,26},{10... | collective-permute-start | bytes 393224 | tf_op jit(solution)/shard_map/ppermute | solution.py:894
  (10 other events, 38.8 us)
